TPU v7x, 128 devices: a whole 4x4x4 slice. The times are simulated.
128 devices in a mesh: vocab: 16 (over y, z), tokens: 8 (over x, core).
Axes of the slice: x: 4, y: 4, z: 4, core: 2. Of those that a mesh axis runs over, the one named last changes fastest.
Arguments:
- teacher_logits: bfloat16 [2048, 65536], P('tokens', 'vocab'), may hold values from -300 to 350
- student_hidden: bfloat16 [2048, 4096], P('tokens'), may hold values from -18 to 18
- student_unembed: bfloat16 [4096, 32768], P(None, 'vocab'), may hold values from -8 to 8
- tile_weights: bfloat16 [256, 512, 512], P('vocab', 'tokens'), may hold values from 0.0009994507 to 1
- tile_pairs: int32 [256, 2], P('vocab'), may hold values from 0 to 127, as said below
- tile_count: int32 [16], P('vocab'), may hold values from 1 to 16, as said below
Outputs:
- grad_hidden: bfloat16 [2048, 4096], P('tokens', 'vocab')
- divergence: float32 [2048], P('tokens')
Inputs may be any that keep to these rules, and one draw needn't show every extreme that they name: `tile_pairs`: row i belongs to vocab index k = i // 16. Its first entry, the teacher block, lies in k * 8 to (k + 1) * 8 - 1; its second, the student block b, has (b % 4) // 1 equal to k % 4. Dead slots follow the same rule. `tile_count`: entry k counts the live slots of vocab index k, which are its first ones.
All inputs are finite; a program needn't handle non-finite values.
Results may differ from a plain program's by a relative error of at most 0.015.
Values may be sent and summed in bfloat16 or wider, within the bound.
No kernel may reach another device: no remote copies, remote signals or barrier semaphores. Data moves between devices by JAX's collectives and lax.ppermute only.
A program may use at most 192 MiB of HBM per device.

v0:
```python
import jax
import jax.numpy as jnp
from jax import lax
from jax.sharding import PartitionSpec as P


def joined(shard, axis, combine):
    everything = jax.tree.map(lambda part: lax.all_gather(part, axis), shard)
    first = jax.tree.map(lambda part: part[0], everything)

    def turn(k, so_far):
        return combine(so_far, jax.tree.map(lambda part: part[k], everything))

    return lax.fori_loop(1, lax.axis_size(axis), turn, first)


def merge_softmax(former, latter):
    highest = jnp.maximum(former[0], latter[0])
    summed = former[1] * jnp.exp(former[0] - highest) + latter[1] * jnp.exp(latter[0] - highest)
    others = tuple(
        (first_term + second_term for first_term, second_term in zip(former[2:], latter[2:]))
    )
    return (highest, summed) + others


def shards(teacher_logits, student_hidden, student_unembed, tile_weights, tile_pairs, tile_count):
    vocab_index = lax.axis_index("vocab")
    vocab_size = lax.axis_size("vocab")
    row_count = teacher_logits.shape[0]
    teacher_cols = teacher_logits.shape[1]
    block_width = tile_weights.shape[2]
    student_cols = student_unembed.shape[1]
    local_blocks = student_cols // block_width
    teacher_f32 = teacher_logits.astype(jnp.float32)
    local_peak = jnp.max(teacher_f32, axis=1)
    local_mass = jnp.sum(jnp.exp(teacher_f32 - local_peak[:, None]), axis=1)
    teacher_peak, teacher_mass = joined((local_peak, local_mass), "vocab", merge_softmax)
    teacher_probs = (jnp.exp(teacher_f32 - teacher_peak[:, None]) / teacher_mass[:, None]).astype(
        jnp.bfloat16
    )
    first_block = vocab_index * (teacher_cols // block_width)
    live_tiles = tile_count[0]
    student_block = tile_pairs[:, 1]
    buffer_count = vocab_size * local_blocks
    empty = jnp.zeros((buffer_count, row_count, block_width), jnp.float32)
    shard_piece = lax.all_gather(tile_weights, "tokens", axis=1, tiled=True)
    piece_rows = shard_piece.shape[1]

    def tile_step(slot_index, running):
        teacher_block = tile_pairs[slot_index, 0] - first_block
        columns = lax.dynamic_slice_in_dim(
            teacher_probs, teacher_block * block_width, piece_rows, 1
        )
        weights = lax.dynamic_index_in_dim(shard_piece, slot_index, 0, keepdims=False)
        product = jnp.dot(columns, weights, preferred_element_type=jnp.float32)
        target_index = student_block[slot_index]
        current = lax.dynamic_index_in_dim(running, target_index, 0, keepdims=False)
        return lax.dynamic_update_index_in_dim(running, current + product, target_index, 0)

    placed = lax.fori_loop(0, live_tiles, tile_step, empty)
    student_logits = jnp.dot(student_hidden, student_unembed, preferred_element_type=jnp.float32)
    speak_local = jnp.max(student_logits, axis=1)
    smass_local = jnp.sum(jnp.exp(student_logits - speak_local[:, None]), axis=1)
    received = lax.psum_scatter(
        placed.astype(jnp.bfloat16), "vocab", scatter_dimension=0, tiled=True
    ).astype(jnp.float32)
    raw_target = received.transpose(1, 0, 2).reshape(row_count, student_cols)
    positive = raw_target > 0
    entropy_local = jnp.sum(
        jnp.where(positive, raw_target * jnp.log(jnp.where(positive, raw_target, 1.0)), 0.0), axis=1
    )
    cross_local = jnp.sum(raw_target * student_logits, axis=1)
    row_total = jnp.sum(raw_target, axis=1)
    student_peak, student_mass, target_total, entropy_sum, cross_sum = joined(
        (speak_local, smass_local, row_total, entropy_local, cross_local), "vocab", merge_softmax
    )
    floored = jnp.maximum(target_total, 1.0)
    mass_share = target_total / floored
    student_probs = jnp.exp(student_logits - student_peak[:, None]) / student_mass[:, None]
    logit_grad = (mass_share[:, None] * student_probs - raw_target / floored[:, None]).astype(
        jnp.bfloat16
    )
    grad_part = lax.psum_scatter(
        lax.dot_general(
            student_unembed,
            logit_grad,
            (((1,), (1,)), ((), ())),
            preferred_element_type=jnp.float32,
        ).astype(jnp.bfloat16),
        "vocab",
        scatter_dimension=0,
        tiled=True,
    ).astype(jnp.float32)
    grad_hidden = grad_part.T.astype(jnp.bfloat16)
    log_norm = student_peak + jnp.log(student_mass)
    divergence = (
        (entropy_sum - cross_sum) / floored - mass_share * jnp.log(floored) + mass_share * log_norm
    )
    return (grad_hidden, divergence)


def solution(mesh):
    return jax.shard_map(
        shards,
        mesh=mesh,
        in_specs=(
            P("tokens", "vocab"),
            P("tokens", None),
            P(None, "vocab"),
            P("vocab", "tokens", None),
            P("vocab", None),
            P("vocab"),
        ),
        out_specs=(P("tokens", "vocab"), P("tokens")),
        check_vma=False,
    )
```

profile of v0, /device:TPU:1, one launch (start us, length us, event | category | flops | bytes accessed | tf_op | source)
XLA Modules:
  0.0 506.7 jit_solution(12949959245999868607)
XLA Ops:
  8.0 2.0 reduce_max.28
  9.9 2.4 fusion.8
  12.4 21.3 %all-gather.10 = f32[16,1,256]{2,1,0:T(1,128)S(1)} all-gather(f32[1,1,256]{2,1,0:T(1,128)S(1)} %bitcast.133), channel_id=5, replica_groups=mesh['vocab'=16,'tokens'=8] {'vocab'}, dimensions={0}, use_global_device_ids=true | all-gather | bytes 17408 | tf_op jit(solution)/shard_map/all_gather | solution.py:8
  33.7 19.6 %all-gather.9 = f32[16,1,256]{2,1,0:T(1,128)S(1)} all-gather(f32[1,1,256]{2,1,0:T(1,128)S(1)} %bitcast.132), channel_id=4, replica_groups=mesh['vocab'=16,'tokens'=8] {'vocab'}, dimensions={0}, use_global_device_ids=true | all-gather | bytes 17408 | tf_op jit(solution)/shard_map/all_gather | solution.py:8
  53.3 0.9 while.50
  54.2 3.9 fusion.11
  58.1 5.0 all-gather.16.cloned.1.call-done
  63.1 11.3 %broadcast_in_dim.11 = f32[64,256,512]{2,1,0:T(8,128)} broadcast(f32[]{:T(128)} %constant.109.clone.1), dimensions={} | broadcast | bytes 33554436 | tf_op jit(solution)/shard_map/broadcast_in_dim | solution.py:45
  74.3 8.0 %while.51 = (s32[]{:T(128)}, f32[64,256,512]{2,1,0:T(8,128)}, s32[]{:T(128)}, s32[16]{0:T(128)S(1)}, s32[16,2]{0,1:T(2,128)S(1)}, /*index=5*/s32[]{:T(128)}, bf1...) while((s32[]{:T(128)}, f32[64,256,512]{2,1,0:T(8,128)}, ...), condition=%wide.region_7.8_spmd, body=%wide.region_6.7_spmd.sunk | while | flops 134348816 | bytes 2883883 | solution.py:60
  77.2 1.1 constant_dynamic-slice_fusion.16
  79.4 2.2 fusion.32
  82.3 17.3 %convert_element_type.28 = bf16[64,256,512]{2,1,0:T(8,128)(2,1)} convert(f32[64,256,512]{2,1,0:T(8,128)} %get-tuple-element.448) | non-fusion elementwise | flops 8388608 | bytes 50331648 | tf_op jit(solution)/shard_map/convert_element_type | solution.py:65
  99.7 9.6 %fusion.23 = (f32[256]{0:T(256)S(1)}, f32[256,2048]{1,0:T(8,128)}) fusion(bf16[256,4096]{1,0:T(8,128)(2,1)S(1)} %copy-done, bf16[4096,2048]{1,0:T(8,128)(2,1)} %param.14), kind=kOutput, calls=%fused_computation.54 | convolution fusion | flops 4295491584 | bytes 20972544 | tf_op jit(solution)/shard_map/dot_general | solution.py:61
  109.3 128.6 %all-gather.7 = f32[16,1,256]{2,1,0:T(1,128)S(1)} all-gather(f32[1,1,256]{2,1,0:T(1,128)S(1)} %bitcast.134), channel_id=2, replica_groups=mesh['vocab'=16,'tokens'=8] {'vocab'}, dimensions={0}, use_global_device_ids=true | all-gather | bytes 17408 | tf_op jit(solution)/shard_map/all_gather | solution.py:8
  237.9 80.7 %reduce-scatter.3.cloned.1.call-done = bf16[4,256,512]{2,1,0:T(8,128)(2,1)} async-done(((bf16[64,256,512]{2,1,0:T(8,128)(2,1)}), bf16[4,256,512]{2,1,0:T(8,128)(2,1)}) %reduce-scatter.3.cloned.1.call-update) | async-done | bytes 1048592 | tf_op jit(solution)/shard_map/reduce_scatter | solution.py:64
  318.6 1.5 convert_bitcast_fusion
  320.3 2.1 copy-done.4
  323.0 17.8 %all-gather.8 = f32[16,1,256]{2,1,0:T(1,128)S(1)} all-gather(f32[1,1,256]{2,1,0:T(1,128)S(1)} %bitcast.136), channel_id=3, replica_groups=mesh['vocab'=16,'tokens'=8] {'vocab'}, dimensions={0}, use_global_device_ids=true | all-gather | bytes 17408 | tf_op jit(solution)/shard_map/all_gather | solution.py:8
  340.9 15.4 %all-gather.13 = f32[16,1,256]{2,1,0:T(1,128)S(1)} all-gather(f32[1,1,256]{2,1,0:T(1,128)S(1)} %bitcast.135), channel_id=8, replica_groups=mesh['vocab'=16,'tokens'=8] {'vocab'}, dimensions={0}, use_global_device_ids=true | all-gather | bytes 17408 | tf_op jit(solution)/shard_map/all_gather | solution.py:8
  356.5 17.4 %all-gather.11 = f32[16,1,256]{2,1,0:T(1,128)S(1)} all-gather(f32[1,1,256]{2,1,0:T(1,128)S(1)} %bitcast.138), channel_id=6, replica_groups=mesh['vocab'=16,'tokens'=8] {'vocab'}, dimensions={0}, use_global_device_ids=true | all-gather | bytes 17408 | tf_op jit(solution)/shard_map/all_gather | solution.py:8
  374.5 15.8 %all-gather.12 = f32[16,1,256]{2,1,0:T(1,128)S(1)} all-gather(f32[1,1,256]{2,1,0:T(1,128)S(1)} %bitcast.137), channel_id=7, replica_groups=mesh['vocab'=16,'tokens'=8] {'vocab'}, dimensions={0}, use_global_device_ids=true | all-gather | bytes 17408 | tf_op jit(solution)/shard_map/all_gather | solution.py:8
  390.4 2.1 while.52
  393.0 13.5 %fusion.6 = bf16[4096,256]{0,1:T(8,128)(2,1)} fusion(bf16[4096,2048]{1,0:T(8,128)(2,1)} %param.14, f32[256,2048]{1,0:T(8,128)} %bitcast.110, f32[256,2048]{1,0:T(8,128)} %get-tuple-element.518, f32[256]{0:T(256)S(1)} %get-tuple-element.516, f32[256]{0:T(256)S(1)} %get-tuple-element.451, f32[256]{0:T(256)S(1)} %get-tuple-element.450, ...), kind=kOutput, calls=%fused_computation.21 | convolution fusion | flops 4299161600 | bytes 23072768 | tf_op jit(solution)/shard_map/dot_general | solution.py:84
  406.6 93.7 %reduce-scatter.5.cloned.1.call-done = bf16[256,256]{0,1:T(8,128)(2,1)} async-done(((bf16[4096,256]{0,1:T(8,128)(2,1)}), bf16[256,256]{0,1:T(8,128)(2,1)}) %reduce-scatter.5.cloned.1.call-update) | async-done | bytes 131088 | tf_op jit(solution)/shard_map/reduce_scatter | solution.py:83
  (178 shorter events, 6.0 us)
Async XLA Ops:
  7.2 92.5 %copy-start = (bf16[256,4096]{1,0:T(8,128)(2,1)S(1)}, bf16[256,4096]{1,0:T(8,128)(2,1)}, u32[]{:S(2)}) copy-start(bf16[256,4096]{1,0:T(8,128)(2,1)} %param.13) | copy-start | bytes 6291460
  7.2 55.9 %all-gather.16.cloned.1.call-start = ((), (), s32[]{:S(2)}) async-start(), calls=%async_computation.2 | async-start | bytes 9437184 | tf_op jit(solution)/shard_map/all_gather | solution.py:46
  7.9 45.4 %copy-start.6 = (s32[16,2]{0,1:T(2,128)S(1)}, s32[16,2]{0,1:T(2,128)}, u32[]{:S(2)}) copy-start(s32[16,2]{0,1:T(2,128)} %param.16) | copy-start | bytes 388
  7.9 310.6 %reduce-scatter.3.cloned.1.call-start = ((), (), s32[]{:S(2)}) async-start(), calls=%async_computation.3 | async-start | bytes 17825792 | tf_op jit(solution)/shard_map/reduce_scatter | solution.py:64
  99.6 400.6 %reduce-scatter.5.cloned.1.call-start = ((), (), s32[]{:S(2)}) async-start(), calls=%async_computation.4 | async-start | bytes 2228224 | tf_op jit(solution)/shard_map/reduce_scatter | solution.py:83
  237.9 82.4 %copy-start.5 = (f32[16,1,256]{2,1,0:T(1,128)}, f32[16,1,256]{2,1,0:T(1,128)S(1)}, u32[]{:S(2)}) copy-start(f32[16,1,256]{2,1,0:T(1,128)S(1)} %all-gather.7) | copy-start | bytes 49156
  320.1 2.4 copy-start.4
  320.3 2.7 copy-start.3
  322.4 33.8 %copy-start.2 = (bf16[4,256,512]{2,1,0:T(8,128)(2,1)S(1)}, bf16[4,256,512]{2,1,0:T(8,128)(2,1)}, u32[]{:S(2)}) copy-start(bf16[4,256,512]{2,1,0:T(8,128)(2,1)} %reduce-scatter.3.cloned.1.call-done) | copy-start | bytes 3145732
  323.0 67.3 %slice-start = ((f32[16,1,256]{2,1,0:T(1,128)}), f32[1,1,256]{2,1,0:T(1,128)S(1)}, s32[]{:S(2)}) async-start(f32[16,1,256]{2,1,0:T(1,128)} %copy-done.5), calls=%async_computation.5 | async-start | bytes 2048 | tf_op jit(solution)/shard_map/slice | solution.py:9
  393.0 107.2 %copy-start.1 = (bf16[256,4096]{1,0:T(8,128)(2,1)S(1)}, bf16[256,4096]{1,0:T(8,128)(2,1)}, u32[]{:S(2)}) copy-start(bf16[256,4096]{1,0:T(8,128)(2,1)} %param.13) | copy-start | bytes 6291460
Sparse Core Ops, SparseCore 0:
  9.7 53.3 all-gather.15
  99.8 218.7 reduce-scatter.2
  406.7 93.4 reduce-scatter.4
where the time goes:
time: 510 us; the launch traced here: 507 us
  blocking collectives  236 us (46%)
  waiting for transfers between devices  180 us (35%)
  other arithmetic  30.2 us (6%)
  matrix products  25.4 us (5%)
  local copies, waits for them, and re-layouts  16.5 us (3%)
  between operations  13.9 us (3%)
    all_gather x7, blocking collectives, joined(): everything = jax.tree.map(lambda part: lax.all_gather(part, axis), shard)  236 us
    reduce_scatter x1, waiting for transfers between devices, shards(): lax.psum_scatter(lax.dot_general(student_unembed, logit_grad, (((1,), (1,...  93.7 us
    reduce_scatter x1, waiting for transfers between devices, shards(): lax.psum_scatter(placed.astype(jnp.bfloat16), 'vocab', scatter_dimension=...  80.7 us
    convert_element_type x1, other arithmetic, shards(): placed.astype(jnp.bfloat16)  17.3 us
    dot_general x1, matrix products, shards(): lax.dot_general(student_unembed, logit_grad, (((1,), (1,)), ((), ())), pr...  13.5 us
    broadcast_in_dim x1, local copies, waits for them, and re-layouts, shards(): empty = jnp.zeros((buffer_count, row_count, block_width), jnp.float32)  11.3 us
  transfers between devices with their start and end apart: 3, of which 3 were waited for; matrix products, arithmetic and copies ran while one was open for 4% of the time, Pallas kernels for 0%

commit v1 on v0

v1 whole, which is shorter than its diff:
```python
import functools

import jax
import jax.numpy as jnp
from jax import lax
from jax.experimental import pallas as pl
from jax.experimental.pallas import tpu as pltpu
from jax.sharding import Mesh
from jax.sharding import PartitionSpec as P

F32 = jnp.float32
BF16 = jnp.bfloat16
SIDE = 4
WIDTHS = (128, 128, 128, 128)
VMEM = pl.BlockSpec(memory_space=pltpu.VMEM)
SMEM = pl.BlockSpec(memory_space=pltpu.SMEM)
LIMIT = 40 * 1024 * 1024


def params():
    return pltpu.CompilerParams(vmem_limit_bytes=LIMIT)


def cost(flops, moved, transcendentals=0):
    return pl.CostEstimate(flops=flops, bytes_accessed=moved, transcendentals=transcendentals)


def send(value, axis, step):
    return lax.ppermute(value, axis, [(i, (i + step) % SIDE) for i in range(SIDE)])


def thirds(value):
    high = value.astype(BF16).astype(F32)
    rest = value - high
    middle = rest.astype(BF16).astype(F32)
    return high, middle, rest - middle


def product_kernel(place, pairs, count, probs, weights, *rest):
    outs, total = rest[:SIDE], rest[SIDE]
    block = weights.shape[0] * 64
    width = weights.shape[2]
    vocab_y = place[0]
    first_block = (vocab_y * SIDE + place[1]) * (probs.shape[1] // block)
    total[...] = jnp.zeros_like(total)

    def tile(slot, carry):
        teacher = pairs[slot, 0] - first_block
        owner = pairs[slot, 1] // SIDE
        columns = probs[:, pl.ds(pl.multiple_of(teacher * block, block), block)]
        rows = weights[:, pl.ds(pl.multiple_of(slot * 64, 64), 64), :].reshape(block, width)
        total[owner] += jnp.dot(columns, rows, preferred_element_type=F32)
        return carry

    lax.fori_loop(0, count[0], tile, 0)
    for step in range(SIDE):
        start = lax.rem(vocab_y + step, SIDE) * SIDE
        for z in range(SIDE):
            outs[step][z] = total[start + z].astype(BF16)


def products(place, pairs, count, probs, weights):
    rows, width = probs.shape[0], weights.shape[2]
    return pl.pallas_call(
        product_kernel,
        out_shape=[jax.ShapeDtypeStruct((SIDE, rows, width), BF16)] * SIDE,
        in_specs=[SMEM, SMEM, SMEM, VMEM, VMEM],
        out_specs=[VMEM] * SIDE,
        scratch_shapes=[pltpu.VMEM((SIDE * SIDE, rows, width), F32)],
        compiler_params=params(),
        cost_estimate=cost(16 * 2 * rows * 512 * width, 2 * probs.size + 2 * weights.size + 32 * rows * width),
        name="tile_products",
    )(place, pairs, count, probs, weights)


def stats_kernel(*refs):
    parts, out = refs[:-1], refs[-1]
    peaks = [part[:, 0, :] for part in parts]
    peak = functools.reduce(jnp.maximum, [jnp.max(v, axis=0, keepdims=True) for v in peaks])
    speaks = [part[:, 3, :] for part in parts]
    speak = functools.reduce(jnp.maximum, [jnp.max(v, axis=0, keepdims=True) for v in speaks])
    mass = jnp.zeros_like(peak)
    total = jnp.zeros_like(peak)
    smass = jnp.zeros_like(peak)
    scales = []
    for part, own, sown in zip(parts, peaks, speaks):
        factor = jnp.exp(own - peak)
        scales.append(factor[0:1])
        mass += jnp.sum(part[:, 1, :] * factor, axis=0, keepdims=True)
        total += jnp.sum(part[:, 2, :] * factor, axis=0, keepdims=True)
        smass += jnp.sum(part[:, 4, :] * jnp.exp(sown - speak), axis=0, keepdims=True)
    total = total / mass
    floored = jnp.maximum(total, 1.0)
    share = total / floored
    table = [s / mass for s in scales] + [1.0 / floored, share / smass, speak, speak + jnp.log(smass)]
    table = jnp.concatenate(table + [jnp.zeros((128 - len(table), peak.shape[1]), F32)], axis=0)
    out[...] = table.T


def statistics(parts):
    rows = parts[0].shape[2]
    return pl.pallas_call(
        stats_kernel,
        out_shape=jax.ShapeDtypeStruct((rows, 128), F32),
        in_specs=[VMEM] * SIDE,
        out_specs=VMEM,
        compiler_params=params(),
        cost_estimate=cost(16 * rows * 20, 64 * 8 * rows, 32 * rows),
        name="row_stats",
    )(*parts)


def merge_kernel(place, table, *refs):
    parts, outs = refs[:SIDE], refs[SIDE:]
    for step in range(SIDE):
        z = lax.rem(place[1] + step, SIDE)
        value = table[:, 0:1] * parts[0][z].astype(F32)
        for d in range(1, SIDE):
            value += table[:, d : d + 1] * parts[d][z].astype(F32)
        outs[step][...] = value.astype(BF16)


def merged(place, table, parts):
    _, rows, width = parts[0].shape
    return pl.pallas_call(
        merge_kernel,
        out_shape=[jax.ShapeDtypeStruct((rows, width), BF16)] * SIDE,
        in_specs=[SMEM] + [VMEM] * (1 + SIDE),
        out_specs=[VMEM] * SIDE,
        compiler_params=params(),
        cost_estimate=cost(32 * rows * width, 40 * rows * width),
        name="merge_targets",
    )(place, table, *parts)


def gradient_kernel(offset, place, table, logits, *refs):
    parts, grad, loss = refs[:SIDE], refs[SIDE], refs[SIDE + 1]
    width = parts[0].shape[1]
    inverse, share, peak, norm = (table[:, c : c + 1] for c in range(4, 8))
    terms = jnp.zeros(parts[0].shape, F32)
    for step in range(SIDE):
        block = lax.rem(place[1] + SIDE - step, SIDE)
        scores = logits[:, pl.ds(pl.multiple_of(block * 512 + offset, 128), width)]
        target = parts[step][...].astype(F32) * inverse
        positive = target > 0
        entropy = jnp.where(positive, target * jnp.log(jnp.where(positive, target, 1.0)), 0.0)
        terms += entropy - target * (scores - norm)
        value = share * jnp.exp(scores - peak) - target
        grad[block] = value.T.astype(BF16)
    loss[...] = jnp.broadcast_to(jnp.sum(terms.T, axis=0, keepdims=True), loss.shape)


def gradients(offset, place, table, logits, parts):
    rows, width = parts[0].shape
    return pl.pallas_call(
        functools.partial(gradient_kernel, offset),
        out_shape=[
            jax.ShapeDtypeStruct((SIDE, width, rows), BF16),
            jax.ShapeDtypeStruct((8, rows), F32),
        ],
        in_specs=[SMEM] + [VMEM] * (2 + SIDE),
        out_specs=[VMEM, VMEM],
        compiler_params=params(),
        cost_estimate=cost(60 * rows * width, 16 * rows * width + 4 * logits.size, 8 * rows * width),
        name="logit_grad",
    )(place, table, logits, *parts)


def hidden_kernel(chunks, place, unembed, *refs):
    grads, losses = refs[:chunks], refs[chunks : 2 * chunks]
    first = refs[2 * chunks : 2 * chunks + SIDE]
    second = refs[2 * chunks + SIDE : 2 * chunks + 2 * SIDE]
    turned = refs[2 * chunks + 2 * SIDE]
    index = pl.program_id(0)
    rows = turned.shape[1]

    @pl.when(index == 0)
    def _():
        offset = 0
        loss = jnp.zeros((1, rows), F32)
        for part, term in zip(grads, losses):
            width = part.shape[1]
            for block in range(SIDE):
                turned[block * 512 + offset : block * 512 + offset + width, :] = part[block]
            offset += width
            loss += term[0:1]
        packed = jnp.concatenate(list(thirds(loss)) + [jnp.zeros((13, rows), F32)], axis=0).astype(BF16)
        for out in first:
            out[512:528, :] = packed

    result = jnp.dot(unembed[...], turned[...], preferred_element_type=F32).astype(BF16)
    for half in range(2):
        owner = index * 2 + half
        owner_y, owner_z = owner // SIDE, lax.rem(owner, SIDE)
        top = result[half * 256 : half * 256 + 128]
        low = result[half * 256 + 128 : half * 256 + 256]
        for step in range(SIDE):

            @pl.when(lax.rem(place[0] + step, SIDE) == owner_y)
            def _():
                first[step][pl.ds(pl.multiple_of(owner_z * 128, 128), 128), :] = top

            @pl.when(lax.rem(place[1] + step, SIDE) == owner_z)
            def _():
                second[step][pl.ds(pl.multiple_of(owner_y * 128, 128), 128), :] = low


def hidden_parts(place, unembed, grads, losses):
    chunks = len(grads)
    width, cols = unembed.shape
    rows = grads[0].shape[2]
    whole = lambda shape: pl.BlockSpec(shape, lambda i: (0,) * len(shape))
    return pl.pallas_call(
        functools.partial(hidden_kernel, chunks),
        grid=(8,),
        out_shape=[jax.ShapeDtypeStruct((528, rows), BF16)] * SIDE
        + [jax.ShapeDtypeStruct((512, rows), BF16)] * SIDE,
        in_specs=[SMEM, pl.BlockSpec((width // 8, cols), lambda i: (i, 0))]
        + [whole(g.shape) for g in grads]
        + [whole(v.shape) for v in losses],
        out_specs=[whole((528, rows))] * SIDE + [whole((512, rows))] * SIDE,
        scratch_shapes=[pltpu.VMEM((cols, rows), BF16)],
        compiler_params=params(),
        cost_estimate=cost(2 * width * cols * rows, 2 * width * cols + 4 * width * rows),
        name="hidden_grad",
    )(place, unembed, *grads, *losses)


def packed_loss(place_index, parts, at, ordered):
    for step in range(SIDE):
        piece = parts[step][at : at + 16, :].astype(F32)
        ordered[lax.rem(place_index + SIDE - step, SIDE)] = piece[0:1] + piece[1:2] + piece[2:3]
    return ((ordered[0] + ordered[1]) + ordered[2]) + ordered[3]


def middle_kernel(place, *refs):
    first, second = refs[:SIDE], refs[SIDE : 2 * SIDE]
    first_out, second_out = refs[2 * SIDE : 3 * SIDE], refs[3 * SIDE : 4 * SIDE]
    ordered = refs[4 * SIDE]
    rows = ordered.shape[2]
    loss = packed_loss(place[0], first, 512, ordered)
    packed = jnp.concatenate(list(thirds(loss)) + [jnp.zeros((13, rows), F32)], axis=0).astype(BF16)
    for step in range(SIDE):
        at = pl.ds(pl.multiple_of(lax.rem(place[1] + step, SIDE) * 128, 128), 128)
        value = first[0][at, :].astype(F32)
        for part in first[1:]:
            value += part[at, :].astype(F32)
        first_out[step][0:128, :] = value.astype(BF16)
        first_out[step][128:144, :] = packed
        at = pl.ds(pl.multiple_of(lax.rem(place[0] + step, SIDE) * 128, 128), 128)
        value = second[0][at, :].astype(F32)
        for part in second[1:]:
            value += part[at, :].astype(F32)
        second_out[step][...] = value.astype(BF16)


def middle(place, first, second):
    rows = first[0].shape[1]
    return pl.pallas_call(
        middle_kernel,
        out_shape=[jax.ShapeDtypeStruct((144, rows), BF16)] * SIDE
        + [jax.ShapeDtypeStruct((128, rows), BF16)] * SIDE,
        in_specs=[SMEM] + [VMEM] * (2 * SIDE),
        out_specs=[VMEM] * (2 * SIDE),
        scratch_shapes=[pltpu.VMEM((SIDE, 1, rows), F32)],
        compiler_params=params(),
        cost_estimate=cost(8 * 512 * rows, 20 * 512 * rows),
        name="merge_grads",
    )(place, *first, *second)


def last_kernel(place, *refs):
    first, second = refs[:SIDE], refs[SIDE : 2 * SIDE]
    grad, loss, ordered = refs[2 * SIDE :]
    loss[...] = jnp.broadcast_to(packed_loss(place[1], first, 128, ordered), loss.shape)
    top = first[0][0:128, :].astype(F32)
    low = second[0][...].astype(F32)
    for a, b in zip(first[1:], second[1:]):
        top += a[0:128, :].astype(F32)
        low += b[...].astype(F32)
    grad[:, 0:128] = top.T.astype(BF16)
    grad[:, 128:256] = low.T.astype(BF16)


def last(place, first, second):
    rows = first[0].shape[1]
    return pl.pallas_call(
        last_kernel,
        out_shape=[jax.ShapeDtypeStruct((rows, 256), BF16), jax.ShapeDtypeStruct((8, rows), F32)],
        in_specs=[SMEM] + [VMEM] * (2 * SIDE),
        out_specs=[VMEM, VMEM],
        scratch_shapes=[pltpu.VMEM((SIDE, 1, rows), F32)],
        compiler_params=params(),
        cost_estimate=cost(8 * 256 * rows, 20 * 256 * rows),
        name="last_sum",
    )(place, *first, *second)


def shards(teacher_logits, student_hidden, student_unembed, tile_weights, tile_pairs, tile_count):
    place = jnp.stack([lax.axis_index("vy"), lax.axis_index("vz")]).astype(jnp.int32)
    rows = teacher_logits.shape[0]
    slots, shard_rows, block = tile_weights.shape

    row_sums = jnp.sum(tile_weights.astype(F32), axis=2)
    high = lax.reduce_precision(row_sums, 8, 7)
    mid = lax.reduce_precision(row_sums - high, 8, 7)
    low = row_sums - high - mid
    gathered = []
    offset = 0
    for index, width in enumerate(WIDTHS):
        piece = tile_weights[:, :, offset : offset + width].reshape(slots * shard_rows, width)
        if index == 1:
            extra = jnp.stack([high, mid, low]).astype(BF16).reshape(-1, width)
            extra = jnp.pad(extra, ((0, -extra.shape[0] % 16), (0, 0)))
            piece = jnp.concatenate([piece, extra], axis=0)
        gathered.append(lax.all_gather(piece, ("tx", "tc"), axis=0))
        offset += width

    teacher = teacher_logits.astype(F32)
    peak = jnp.max(teacher, axis=1)
    shifted = jnp.exp(teacher - peak[:, None])
    mass = jnp.sum(shifted, axis=1)
    probs = shifted.astype(BF16)

    logits = jnp.dot(student_hidden, student_unembed, preferred_element_type=F32)
    speak = jnp.max(logits, axis=1)
    smass = jnp.sum(jnp.exp(logits - speak[:, None]), axis=1)

    extra = gathered[1][:, slots * shard_rows :, :].reshape(8, -1)[:, : 3 * slots * shard_rows]
    sums = jnp.sum(extra.reshape(8, 3, slots, shard_rows).astype(F32), axis=1)
    sums = sums.transpose(1, 0, 2).reshape(slots, block)
    blocks = teacher.shape[1] // block
    live = jnp.arange(slots) < tile_count[0]
    chosen = (tile_pairs[:, 0] % blocks)[:, None] == jnp.arange(blocks)[None, :]
    chosen = jnp.where(live[:, None], chosen, False)
    spread = jnp.sum(jnp.where(chosen[:, :, None], sums[:, None, :], 0.0), axis=0).reshape(-1)
    total = jnp.sum(probs.astype(F32) * spread[None, :], axis=1)

    own = jnp.stack([peak, mass, total, speak, smass, smass, smass, smass])
    column = jnp.stack([own] + [send(own, "vz", step) for step in (1, 2, 3)])
    table = statistics([column] + [send(column, "vy", step) for step in (1, 2, 3)])

    grads, losses = [], []
    offset = 0
    for weights, width in zip(gathered, WIDTHS):
        parts = products(place, tile_pairs, tile_count, probs, weights)
        parts = [parts[0]] + [send(parts[step], "vy", step) for step in (1, 2, 3)]
        parts = merged(place, table, parts)
        parts = [parts[0]] + [send(parts[step], "vz", step) for step in (1, 2, 3)]
        grad, loss = gradients(offset, place, table, logits, parts)
        grads.append(grad)
        losses.append(loss)
        offset += width

    parts = hidden_parts(place, student_unembed, grads, losses)
    first, second = parts[:SIDE], parts[SIDE:]
    first = [first[0]] + [send(first[step], "vy", step) for step in (1, 2, 3)]
    second = [second[0]] + [send(second[step], "vz", step) for step in (1, 2, 3)]
    parts = middle(place, first, second)
    first, second = parts[:SIDE], parts[SIDE:]
    first = [first[0]] + [send(first[step], "vz", step) for step in (1, 2, 3)]
    second = [second[0]] + [send(second[step], "vy", step) for step in (1, 2, 3)]
    grad_hidden, loss = last(place, first, second)
    return grad_hidden, loss[0]


def solution(mesh):
    grid = Mesh(mesh.devices.reshape(SIDE, SIDE, SIDE, 2), ("vy", "vz", "tx", "tc"))
    vocab, tokens = ("vy", "vz"), ("tx", "tc")
    return jax.shard_map(
        shards,
        mesh=grid,
        in_specs=(
            P(tokens, vocab),
            P(tokens, None),
            P(None, vocab),
            P(vocab, tokens, None),
            P(vocab, None),
            P(vocab),
        ),
        out_specs=(P(tokens, vocab), P(tokens)),
        check_vma=False,
    )
```

time: 510 us -> 214 us (0.42)
  blocking collectives: 236 us -> 0 us
  waiting for transfers between devices: 180 us -> 64.2 us
  starting transfers between devices: 0.12 us -> 62.2 us
  Pallas kernels: 0 us -> 32.8 us
  other arithmetic: 30.2 us -> 9.15 us
  matrix products: 25.4 us -> 9.63 us
    all_gather x7 -> x0, blocking collectives: 236 us -> none  [joined(): everything = jax.tree.map(lambda part: lax.all_gather(part, axis), shard)]
    reduce_scatter x2 -> x0, waiting for transfers between devices: 174 us -> none  [the longest x1 93.7 us: shards(): lax.psum_scatter(lax.dot_general(student_unembed, logit_grad, (((1,), (1,...]
    ppermute x0 -> x42, starting transfers between devices: none -> 62.1 us  [send(): lax.ppermute(value, axis, [(i, (i + step) % SIDE) for i in range(SIDE)])]
    all_gather x1 -> x4, waiting for transfers between devices: 4.95 us -> 49.9 us  [shards(): gathered.append(lax.all_gather(piece, ('tx', 'tc'), axis=0))]
    pallas_call x0 -> x16, Pallas kernels: none -> 32.8 us  [the longest x1 11.5 us: hidden_parts(): pl.pallas_call(functools.partial(hidden_kernel, chunks), grid=(8,), out_s...]
    convert_element_type x2 -> x1, other arithmetic: 21.3 us -> 0.01 us  [shards(): sums = jnp.sum(extra.reshape(8, 3, slots, shard_rows).astype(F32), axis=1)]
    dot_general x3 -> x1, matrix products: 25.4 us -> 9.63 us  [shards(): jnp.dot(student_hidden, student_unembed, preferred_element_type=F32)]
    ppermute x0 -> x42, waiting for transfers between devices: none -> 12.4 us  [send(): lax.ppermute(value, axis, [(i, (i + step) % SIDE) for i in range(SIDE)])]
  transfers between devices with their start and end apart: 3 -> 46, of which waited for: 3 -> 10; matrix products, arithmetic and copies ran while one was open for 4% -> 8% of each run, Pallas kernels for 0% -> 9%
where the time goes in v1:
time: 214 us; the launch traced here: 210 us
  waiting for transfers between devices  64.2 us (30%)
  starting transfers between devices  62.2 us (29%)
  Pallas kernels  32.8 us (15%)
  local copies, waits for them, and re-layouts  17.5 us (8%)
  between operations  14.7 us (7%)
  matrix products  9.63 us (5%)
  other arithmetic  9.15 us (4%)
    ppermute x42, starting transfers between devices, send(): lax.ppermute(value, axis, [(i, (i + step) % SIDE) for i in range(SIDE)])  62.1 us
    all_gather x4, waiting for transfers between devices, shards(): gathered.append(lax.all_gather(piece, ('tx', 'tc'), axis=0))  49.9 us
    unnamed x32, local copies, waits for them, and re-layouts  14.5 us
    ppermute x42, waiting for transfers between devices, send(): lax.ppermute(value, axis, [(i, (i + step) % SIDE) for i in range(SIDE)])  12.4 us
    pallas_call x1, Pallas kernels, hidden_parts(): pl.pallas_call(functools.partial(hidden_kernel, chunks), grid=(8,), out_s...  11.5 us
    dot_general x1, matrix products, shards(): jnp.dot(student_hidden, student_unembed, preferred_element_type=F32)  9.63 us
    pallas_call x4, Pallas kernels, products(): pl.pallas_call(product_kernel, out_shape=[jax.ShapeDtypeStruct((SIDE, row...  7.95 us
    pallas_call x4, Pallas kernels, merged(): pl.pallas_call(merge_kernel, out_shape=[jax.ShapeDtypeStruct((rows, width...  6.69 us
  transfers between devices with their start and end apart: 46, of which 10 were waited for; matrix products, arithmetic and copies ran while one was open for 8% of the time, Pallas kernels for 9%

profile of v1, /device:TPU:1, one launch (start us, length us, event | category | flops | bytes accessed | tf_op | source)
XLA Modules:
  0.0 210.3 jit_solution(14218737900920526759)
XLA Ops:
  8.8 2.1 %fusion.9 = (bf16[16,64,128]{2,1,0:T(8,128)(2,1)}, bf16[16,64,128]{2,1,0:T(8,128)(2,1)}, bf16[16,64,128]{2,1,0:T(8,128)(2,1)S(1)}, bf16[16,64,128]{2,1,0:T(8,128)(2,1)}) fusion(bf16[16,64,512]{2,1,0:T(8,128)(2,1)} %param.9), kind=kLoop, calls=%fused_computation.29 | loop fusion | bytes 2097152 | tf_op jit(solution)/shard_map/slice | solution.py:311
  16.8 9.6 %fusion.10 = (f32[256]{0:T(256)S(1)}, f32[256,2048]{1,0:T(8,128)}) fusion(bf16[256,4096]{1,0:T(8,128)(2,1)S(1)} %copy-done, bf16[4096,2048]{1,0:T(8,128)(2,1)} %unembed.1), kind=kOutput, calls=%fused_computation.30 | convolution fusion | flops 4295491584 | bytes 20972544 | tf_op jit(solution)/shard_map/dot_general | solution.py:325
  26.4 14.4 %all-gather.12.cloned.1.call-done = bf16[8448,128]{1,0:T(8,128)(2,1)} async-done(((bf16[1056,128]{1,0:T(8,128)(2,1)}), bf16[8448,128]{1,0:T(8,128)(2,1)}) %all-gather.12.cloned.1.call-update) | async-done | bytes 2162704 | tf_op jit(solution)/shard_map/all_gather | solution.py:316
  42.1 4.1 %multiply_reduce_fusion = (f32[256]{0:T(256)S(1)}, bf16[256,4096]{1,0:T(8,128)(2,1)}, f32[256]{0:T(256)S(1)}) fusion(f32[4096]{0:T(1024)S(1)} %bitcast.46, f32[256]{0:T(256)S(1)} %reduce_max.32, bf16[256,4096]{1,0:T(8,128)(2,1)} %param.6), kind=kLoop, calls=%fused_computation | loop fusion | flops 7339520 | bytes 4213760 | tf_op jit(solution)/shard_map/reduce_sum | solution.py:337
  46.2 21.9 %all-gather.6.cloned.1.call-done.weights = bf16[8,1024,128]{2,1,0:T(8,128)(2,1)} async-done(((bf16[1,1024,128]{2,1,0:T(8,128)(2,1)}), bf16[8,1024,128]{2,1,0:T(8,128)(2,1)}) %all-gather.6.cloned.1.call-update) | async-done | bytes 2097168 | tf_op jit(solution)/shard_map/all_gather | solution.py:316
  71.2 2.2 %tile_products.4 = (bf16[4,256,128]{2,1,0:T(8,128)(2,1)S(1)}, bf16[4,256,128]{2,1,0:T(8,128)(2,1)}, bf16[4,256,128]{2,1,0:T(8,128)(2,1)}, bf16[4,256,128]{2,1,0:T(8,128)(2,1)}) custom-call(s32[2]{0:T(128)S(1)} %pad_add_fusion.place, s32[16,2]{1,0:T(8,128)S(1)} %copy.22.pairs, s32[1]{0:T(128)} %copy.30.count, bf16[256,4096]{1,0:T(8,128)(2,1)S(1)} %copy-done.1, ...), custom_call_target="tpu_custom_call" | custom-call | flops 536870912 | bytes 5242880 | tf_op jit(solution)/shard_map/tile_products/pallas_call | solution.py:64
  74.4 2.4 %collective-permute-start.7 = (bf16[4,256,128]{2,1,0:T(8,128)(2,1)}, bf16[4,256,128]{2,1,0:T(8,128)(2,1)S(1)}, u32[]{:S(2)}, u32[]{:S(2)}) collective-permute-start(bf16[4,256,128]{2,1,0:T(8,128)(2,1)} %get-tuple-element.62), channel_id=1, source_target_pairs={{0,64},{32,96},{64,0},{96,32},{1,65},{33,97},{65,1},{97,33},{2,66}... | collective-permute-start | bytes 786440 | tf_op jit(solution)/shard_map/ppermute | solution.py:29
  77.3 3.0 %collective-permute-start.2 = (f32[8,256]{1,0:T(8,128)S(1)}, f32[8,256]{1,0:T(8,128)S(1)}, u32[]{:S(2)}, u32[]{:S(2)}) collective-permute-start(f32[8,256]{1,0:T(8,128)S(1)} %stack.58), channel_id=1, source_target_pairs={{0,24},{8,0},{16,8},{24,16},{1,25},{9,1},{17,9},{25,17},{2,26},{10... | collective-permute-start | bytes 24584 | tf_op jit(solution)/shard_map/ppermute | solution.py:29
  82.2 2.1 %collective-permute-done.1 = f32[8,256]{1,0:T(8,128)S(1)} collective-permute-done((f32[8,256]{1,0:T(8,128)S(1)}, f32[8,256]{1,0:T(8,128)S(1)}, u32[]{:S(2)}, u32[]{:S(2)}) %collective-permute-start.1) | collective-permute-done | bytes 8224 | tf_op jit(solution)/shard_map/ppermute | solution.py:29
  91.3 2.2 %tile_products.5 = (bf16[4,256,128]{2,1,0:T(8,128)(2,1)S(1)}, bf16[4,256,128]{2,1,0:T(8,128)(2,1)}, bf16[4,256,128]{2,1,0:T(8,128)(2,1)}, bf16[4,256,128]{2,1,0:T(8,128)(2,1)}) custom-call(s32[2]{0:T(128)S(1)} %pad_add_fusion.place, s32[16,2]{1,0:T(8,128)S(1)} %copy.22.pairs, s32[1]{0:T(128)} %copy.30.count, bf16[256,4096]{1,0:T(8,128)(2,1)S(1)} %copy-done.2, ...), custom_call_target="tpu_custom_call" | custom-call | flops 536870912 | bytes 5308416 | tf_op jit(solution)/shard_map/tile_products/pallas_call | solution.py:64
  95.0 2.4 %collective-permute-start.5 = (f32[4,8,256]{2,1,0:T(8,128)S(1)}, f32[4,8,256]{2,1,0:T(8,128)S(1)}, u32[]{:S(2)}, u32[]{:S(2)}) collective-permute-start(f32[4,8,256]{2,1,0:T(8,128)S(1)} %pad_maximum_fusion.refs_0_), channel_id=1, source_target_pairs={{0,96},{32,0},{64,32},{96,64},{1,97},{33,1},{65,33},{97,65},{2,98}... | collective-permute-start | bytes 98312 | tf_op jit(solution)/shard_map/ppermute | solution.py:29
  100.6 2.2 %tile_products.6 = (bf16[4,256,128]{2,1,0:T(8,128)(2,1)S(1)}, bf16[4,256,128]{2,1,0:T(8,128)(2,1)}, bf16[4,256,128]{2,1,0:T(8,128)(2,1)}, bf16[4,256,128]{2,1,0:T(8,128)(2,1)}) custom-call(s32[2]{0:T(128)S(1)} %pad_add_fusion.place, s32[16,2]{1,0:T(8,128)S(1)} %copy.22.pairs, s32[1]{0:T(128)} %copy.30.count, bf16[256,4096]{1,0:T(8,128)(2,1)S(1)} %copy-done.3, ...), custom_call_target="tpu_custom_call" | custom-call | flops 536870912 | bytes 5242880 | tf_op jit(solution)/shard_map/tile_products/pallas_call | solution.py:64
  105.3 2.6 %collective-permute-start.19 = (bf16[4,256,128]{2,1,0:T(8,128)(2,1)}, bf16[4,256,128]{2,1,0:T(8,128)(2,1)}, u32[]{:S(2)}, u32[]{:S(2)}) collective-permute-start(bf16[4,256,128]{2,1,0:T(8,128)(2,1)} %get-tuple-element.80), channel_id=1, source_target_pairs={{0,64},{32,96},{64,0},{96,32},{1,65},{33,97},{65,1},{97,33},{2,66}... | collective-permute-start | bytes 786440 | tf_op jit(solution)/shard_map/ppermute | solution.py:29
  108.6 13.7 %all-gather.10.cloned.1.call-done.weights = bf16[8,1024,128]{2,1,0:T(8,128)(2,1)} async-done(((bf16[1,1024,128]{2,1,0:T(8,128)(2,1)}), bf16[8,1024,128]{2,1,0:T(8,128)(2,1)}) %all-gather.10.cloned.1.call-update) | async-done | bytes 2097168 | tf_op jit(solution)/shard_map/all_gather | solution.py:316
  128.1 2.5 %collective-permute-start.25 = (bf16[4,256,128]{2,1,0:T(8,128)(2,1)S(1)}, bf16[4,256,128]{2,1,0:T(8,128)(2,1)S(1)}, u32[]{:S(2)}, u32[]{:S(2)}) collective-permute-start(bf16[4,256,128]{2,1,0:T(8,128)(2,1)S(1)} %get-tuple-element.89), channel_id=1, source_target_pairs={{0,64},{32,96},{64,0},{96,32},{1,65},{33,97},{65,1},{97,33},{2,66}... | collective-permute-start | bytes 786440 | tf_op jit(solution)/shard_map/ppermute | solution.py:29
  133.8 2.4 %collective-permute-start.9 = (bf16[256,128]{1,0:T(8,128)(2,1)S(1)}, bf16[256,128]{1,0:T(8,128)(2,1)S(1)}, u32[]{:S(2)}, u32[]{:S(2)}) collective-permute-start(bf16[256,128]{1,0:T(8,128)(2,1)S(1)} %get-tuple-element.65), channel_id=1, source_target_pairs={{0,8},{8,16},{16,24},{24,0},{1,9},{9,17},{17,25},{25,1},{2,10},{10... | collective-permute-start | bytes 196616 | tf_op jit(solution)/shard_map/ppermute | solution.py:29
  136.2 2.7 %collective-permute-start.10 = (bf16[256,128]{1,0:T(8,128)(2,1)S(1)}, bf16[256,128]{1,0:T(8,128)(2,1)S(1)}, u32[]{:S(2)}, u32[]{:S(2)}) collective-permute-start(bf16[256,128]{1,0:T(8,128)(2,1)S(1)} %get-tuple-element.66), channel_id=1, source_target_pairs={{0,16},{8,24},{16,0},{24,8},{1,17},{9,25},{17,1},{25,9},{2,18},{10... | collective-permute-start | bytes 196616 | tf_op jit(solution)/shard_map/ppermute | solution.py:29
  142.5 4.8 %collective-permute-start.11 = (bf16[256,128]{1,0:T(8,128)(2,1)S(1)}, bf16[256,128]{1,0:T(8,128)(2,1)S(1)}, u32[]{:S(2)}, u32[]{:S(2)}) collective-permute-start(bf16[256,128]{1,0:T(8,128)(2,1)S(1)} %get-tuple-element.67), channel_id=1, source_target_pairs={{0,24},{8,0},{16,8},{24,16},{1,25},{9,1},{17,9},{25,17},{2,26},{10... | collective-permute-start | bytes 196616 | tf_op jit(solution)/shard_map/ppermute | solution.py:29
  153.7 2.1 collective-permute-start.23
  162.8 11.5 %hidden_grad.1 = (bf16[528,256]{1,0:T(8,128)(2,1)S(1)}, bf16[528,256]{1,0:T(8,128)(2,1)S(1)}, bf16[528,256]{1,0:T(8,128)(2,1)S(1)}, bf16[528,256]{1,0:T(8,128)(2...) custom-call(s32[2]{0:T(128)S(1)} %pad_add_fusion.place, ...), custom_call_target="tpu_custom_call" | custom-call | flops 4294967296 | bytes 20971520 | tf_op jit(solution)/shard_map/hidden_grad/pallas_call | solution.py:213
  178.3 2.4 %collective-permute-start.34 = (bf16[512,256]{1,0:T(8,128)(2,1)S(1)}, bf16[512,256]{1,0:T(8,128)(2,1)S(1)}, u32[]{:S(2)}, u32[]{:S(2)}) collective-permute-start(bf16[512,256]{1,0:T(8,128)(2,1)S(1)} %get-tuple-element.106), channel_id=1, source_target_pairs={{0,16},{8,24},{16,0},{24,8},{1,17},{9,25},{17,1},{25,9},{2,18},{10... | collective-permute-start | bytes 786440 | tf_op jit(solution)/shard_map/ppermute | solution.py:29
  182.1 5.0 %collective-permute-done.34.refs_6_ = bf16[512,256]{1,0:T(8,128)(2,1)S(1)} collective-permute-done((bf16[512,256]{1,0:T(8,128)(2,1)S(1)}, bf16[512,256]{1,0:T(8,128)(2,1)S(1)}, u32[]{:S(2)}, u32[]{:S(2)}) %collective-permute-start.34) | collective-permute-done | bytes 262176 | tf_op jit(solution)/shard_map/ppermute | solution.py:29
  190.4 2.1 %collective-permute-start.37 = (bf16[144,256]{1,0:T(8,128)(2,1)S(1)}, bf16[144,256]{1,0:T(8,128)(2,1)S(1)}, u32[]{:S(2)}, u32[]{:S(2)}) collective-permute-start(bf16[144,256]{1,0:T(8,128)(2,1)S(1)} %get-tuple-element.110), channel_id=1, source_target_pairs={{0,16},{8,24},{16,0},{24,8},{1,17},{9,25},{17,1},{25,9},{2,18},{10... | collective-permute-start | bytes 221192 | tf_op jit(solution)/shard_map/ppermute | solution.py:29
  194.4 4.0 %collective-permute-start.40 = (bf16[128,256]{1,0:T(8,128)(2,1)S(1)}, bf16[128,256]{1,0:T(8,128)(2,1)S(1)}, u32[]{:S(2)}, u32[]{:S(2)}) collective-permute-start(bf16[128,256]{1,0:T(8,128)(2,1)S(1)} %get-tuple-element.114), channel_id=1, source_target_pairs={{0,64},{32,96},{64,0},{96,32},{1,65},{33,97},{65,1},{97,33},{2,66}... | collective-permute-start | bytes 196616 | tf_op jit(solution)/shard_map/ppermute | solution.py:29
  (144 shorter events, 71.0 us)
Async XLA Ops:
  7.2 33.6 %all-gather.12.cloned.1.call-start = ((), (), s32[]{:S(2)}) async-start(), calls=%async_computation.3 | async-start | bytes 2433024 | tf_op jit(solution)/shard_map/all_gather | solution.py:316
  11.8 56.3 %all-gather.6.cloned.1.call-start = ((), (), s32[]{:S(2)}) async-start(), calls=%async_computation | async-start | bytes 2359296 | tf_op jit(solution)/shard_map/all_gather | solution.py:316
  12.6 84.9 %all-gather.8.cloned.1.call-start = ((), (), s32[]{:S(2)}) async-start(), calls=%async_computation.1 | async-start | bytes 2359296 | tf_op jit(solution)/shard_map/all_gather | solution.py:316
  13.3 109.0 %all-gather.10.cloned.1.call-start = ((), (), s32[]{:S(2)}) async-start(), calls=%async_computation.2 | async-start | bytes 2359296 | tf_op jit(solution)/shard_map/all_gather | solution.py:316
  73.4 30.4 %collective-permute-start.6 = (bf16[4,256,128]{2,1,0:T(8,128)(2,1)}, bf16[4,256,128]{2,1,0:T(8,128)(2,1)S(1)}, u32[]{:S(2)}, u32[]{:S(2)}) collective-permute-start(bf16[4,256,128]{2,1,0:T(8,128)(2,1)} %get-tuple-element.61), channel_id=1, source_target_pairs={{0,32},{32,64},{64,96},{96,0},{1,33},{33,65},{65,97},{97,1},{2,34}... | collective-permute-start | bytes 786440 | tf_op jit(solution)/shard_map/ppermute | solution.py:29
  74.4 30.3 %collective-permute-start.7 = (bf16[4,256,128]{2,1,0:T(8,128)(2,1)}, bf16[4,256,128]{2,1,0:T(8,128)(2,1)S(1)}, u32[]{:S(2)}, u32[]{:S(2)}) collective-permute-start(bf16[4,256,128]{2,1,0:T(8,128)(2,1)} %get-tuple-element.62), channel_id=1, source_target_pairs={{0,64},{32,96},{64,0},{96,32},{1,65},{33,97},{65,1},{97,33},{2,66}... | collective-permute-start | bytes 786440 | tf_op jit(solution)/shard_map/ppermute | solution.py:29
  93.5 11.8 %collective-permute-start.8 = (bf16[4,256,128]{2,1,0:T(8,128)(2,1)}, bf16[4,256,128]{2,1,0:T(8,128)(2,1)}, u32[]{:S(2)}, u32[]{:S(2)}) collective-permute-start(bf16[4,256,128]{2,1,0:T(8,128)(2,1)} %get-tuple-element.63), channel_id=1, source_target_pairs={{0,96},{32,0},{64,32},{96,64},{1,97},{33,1},{65,33},{97,65},{2,98}... | collective-permute-start | bytes 786440 | tf_op jit(solution)/shard_map/ppermute | solution.py:29
  94.7 13.2 %collective-permute-start.12 = (bf16[4,256,128]{2,1,0:T(8,128)(2,1)}, bf16[4,256,128]{2,1,0:T(8,128)(2,1)S(1)}, u32[]{:S(2)}, u32[]{:S(2)}) collective-permute-start(bf16[4,256,128]{2,1,0:T(8,128)(2,1)} %get-tuple-element.70), channel_id=1, source_target_pairs={{0,32},{32,64},{64,96},{96,0},{1,33},{33,65},{65,97},{97,1},{2,34}... | collective-permute-start | bytes 786440 | tf_op jit(solution)/shard_map/ppermute | solution.py:29
  103.5 23.3 %collective-permute-start.13 = (bf16[4,256,128]{2,1,0:T(8,128)(2,1)}, bf16[4,256,128]{2,1,0:T(8,128)(2,1)}, u32[]{:S(2)}, u32[]{:S(2)}) collective-permute-start(bf16[4,256,128]{2,1,0:T(8,128)(2,1)} %get-tuple-element.71), channel_id=1, source_target_pairs={{0,64},{32,96},{64,0},{96,32},{1,65},{33,97},{65,1},{97,33},{2,66}... | collective-permute-start | bytes 786440 | tf_op jit(solution)/shard_map/ppermute | solution.py:29
  103.9 24.2 %collective-permute-start.14 = (bf16[4,256,128]{2,1,0:T(8,128)(2,1)}, bf16[4,256,128]{2,1,0:T(8,128)(2,1)}, u32[]{:S(2)}, u32[]{:S(2)}) collective-permute-start(bf16[4,256,128]{2,1,0:T(8,128)(2,1)} %get-tuple-element.72), channel_id=1, source_target_pairs={{0,96},{32,0},{64,32},{96,64},{1,97},{33,1},{65,33},{97,65},{2,98}... | collective-permute-start | bytes 786440 | tf_op jit(solution)/shard_map/ppermute | solution.py:29
  104.7 25.8 %collective-permute-start.18 = (bf16[4,256,128]{2,1,0:T(8,128)(2,1)}, bf16[4,256,128]{2,1,0:T(8,128)(2,1)}, u32[]{:S(2)}, u32[]{:S(2)}) collective-permute-start(bf16[4,256,128]{2,1,0:T(8,128)(2,1)} %get-tuple-element.79), channel_id=1, source_target_pairs={{0,32},{32,64},{64,96},{96,0},{1,33},{33,65},{65,97},{97,1},{2,34}... | collective-permute-start | bytes 786440 | tf_op jit(solution)/shard_map/ppermute | solution.py:29
  105.3 28.4 %collective-permute-start.19 = (bf16[4,256,128]{2,1,0:T(8,128)(2,1)}, bf16[4,256,128]{2,1,0:T(8,128)(2,1)}, u32[]{:S(2)}, u32[]{:S(2)}) collective-permute-start(bf16[4,256,128]{2,1,0:T(8,128)(2,1)} %get-tuple-element.80), channel_id=1, source_target_pairs={{0,64},{32,96},{64,0},{96,32},{1,65},{33,97},{65,1},{97,33},{2,66}... | collective-permute-start | bytes 786440 | tf_op jit(solution)/shard_map/ppermute | solution.py:29
  108.0 28.2 %collective-permute-start.20 = (bf16[4,256,128]{2,1,0:T(8,128)(2,1)}, bf16[4,256,128]{2,1,0:T(8,128)(2,1)}, u32[]{:S(2)}, u32[]{:S(2)}) collective-permute-start(bf16[4,256,128]{2,1,0:T(8,128)(2,1)} %get-tuple-element.81), channel_id=1, source_target_pairs={{0,96},{32,0},{64,32},{96,64},{1,97},{33,1},{65,33},{97,65},{2,98}... | collective-permute-start | bytes 786440 | tf_op jit(solution)/shard_map/ppermute | solution.py:29
  126.9 15.6 %collective-permute-start.24 = (bf16[4,256,128]{2,1,0:T(8,128)(2,1)S(1)}, bf16[4,256,128]{2,1,0:T(8,128)(2,1)S(1)}, u32[]{:S(2)}, u32[]{:S(2)}) collective-permute-start(bf16[4,256,128]{2,1,0:T(8,128)(2,1)S(1)} %get-tuple-element.88), channel_id=1, source_target_pairs={{0,32},{32,64},{64,96},{96,0},{1,33},{33,65},{65,97},{97,1},{2,34}... | collective-permute-start | bytes 786440 | tf_op jit(solution)/shard_map/ppermute | solution.py:29
  128.1 19.2 %collective-permute-start.25 = (bf16[4,256,128]{2,1,0:T(8,128)(2,1)S(1)}, bf16[4,256,128]{2,1,0:T(8,128)(2,1)S(1)}, u32[]{:S(2)}, u32[]{:S(2)}) collective-permute-start(bf16[4,256,128]{2,1,0:T(8,128)(2,1)S(1)} %get-tuple-element.89), channel_id=1, source_target_pairs={{0,64},{32,96},{64,0},{96,32},{1,65},{33,97},{65,1},{97,33},{2,66}... | collective-permute-start | bytes 786440 | tf_op jit(solution)/shard_map/ppermute | solution.py:29
  130.6 16.7 %collective-permute-start.26 = (bf16[4,256,128]{2,1,0:T(8,128)(2,1)S(1)}, bf16[4,256,128]{2,1,0:T(8,128)(2,1)S(1)}, u32[]{:S(2)}, u32[]{:S(2)}) collective-permute-start(bf16[4,256,128]{2,1,0:T(8,128)(2,1)S(1)} %get-tuple-element.90), channel_id=1, source_target_pairs={{0,96},{32,0},{64,32},{96,64},{1,97},{33,1},{65,33},{97,65},{2,98}... | collective-permute-start | bytes 786440 | tf_op jit(solution)/shard_map/ppermute | solution.py:29
  133.8 14.7 %collective-permute-start.9 = (bf16[256,128]{1,0:T(8,128)(2,1)S(1)}, bf16[256,128]{1,0:T(8,128)(2,1)S(1)}, u32[]{:S(2)}, u32[]{:S(2)}) collective-permute-start(bf16[256,128]{1,0:T(8,128)(2,1)S(1)} %get-tuple-element.65), channel_id=1, source_target_pairs={{0,8},{8,16},{16,24},{24,0},{1,9},{9,17},{17,25},{25,1},{2,10},{10... | collective-permute-start | bytes 196616 | tf_op jit(solution)/shard_map/ppermute | solution.py:29
  136.2 13.8 %collective-permute-start.10 = (bf16[256,128]{1,0:T(8,128)(2,1)S(1)}, bf16[256,128]{1,0:T(8,128)(2,1)S(1)}, u32[]{:S(2)}, u32[]{:S(2)}) collective-permute-start(bf16[256,128]{1,0:T(8,128)(2,1)S(1)} %get-tuple-element.66), channel_id=1, source_target_pairs={{0,16},{8,24},{16,0},{24,8},{1,17},{9,25},{17,1},{25,9},{2,18},{10... | collective-permute-start | bytes 196616 | tf_op jit(solution)/shard_map/ppermute | solution.py:29
  175.6 11.8 %collective-permute-start.30 = (bf16[528,256]{1,0:T(8,128)(2,1)S(1)}, bf16[528,256]{1,0:T(8,128)(2,1)S(1)}, u32[]{:S(2)}, u32[]{:S(2)}) collective-permute-start(bf16[528,256]{1,0:T(8,128)(2,1)S(1)} %get-tuple-element.101), channel_id=1, source_target_pairs={{0,32},{32,64},{64,96},{96,0},{1,33},{33,65},{65,97},{97,1},{2,34}... | collective-permute-start | bytes 811016 | tf_op jit(solution)/shard_map/ppermute | solution.py:29
  175.6 11.8 %collective-permute-start.31 = (bf16[528,256]{1,0:T(8,128)(2,1)S(1)}, bf16[528,256]{1,0:T(8,128)(2,1)S(1)}, u32[]{:S(2)}, u32[]{:S(2)}) collective-permute-start(bf16[528,256]{1,0:T(8,128)(2,1)S(1)} %get-tuple-element.102), channel_id=1, source_target_pairs={{0,64},{32,96},{64,0},{96,32},{1,65},{33,97},{65,1},{97,33},{2,66}... | collective-permute-start | bytes 811016 | tf_op jit(solution)/shard_map/ppermute | solution.py:29
  176.5 10.8 %collective-permute-start.32 = (bf16[528,256]{1,0:T(8,128)(2,1)S(1)}, bf16[528,256]{1,0:T(8,128)(2,1)S(1)}, u32[]{:S(2)}, u32[]{:S(2)}) collective-permute-start(bf16[528,256]{1,0:T(8,128)(2,1)S(1)} %get-tuple-element.103), channel_id=1, source_target_pairs={{0,96},{32,0},{64,32},{96,64},{1,97},{33,1},{65,33},{97,65},{2,98}... | collective-permute-start | bytes 811016 | tf_op jit(solution)/shard_map/ppermute | solution.py:29
  188.3 10.2 %collective-permute-start.39 = (bf16[128,256]{1,0:T(8,128)(2,1)S(1)}, bf16[128,256]{1,0:T(8,128)(2,1)S(1)}, u32[]{:S(2)}, u32[]{:S(2)}) collective-permute-start(bf16[128,256]{1,0:T(8,128)(2,1)S(1)} %get-tuple-element.113), channel_id=1, source_target_pairs={{0,32},{32,64},{64,96},{96,0},{1,33},{33,65},{65,97},{97,1},{2,34}... | collective-permute-start | bytes 196616 | tf_op jit(solution)/shard_map/ppermute | solution.py:29
  188.9 12.9 %collective-permute-start.36 = (bf16[144,256]{1,0:T(8,128)(2,1)S(1)}, bf16[144,256]{1,0:T(8,128)(2,1)S(1)}, u32[]{:S(2)}, u32[]{:S(2)}) collective-permute-start(bf16[144,256]{1,0:T(8,128)(2,1)S(1)} %get-tuple-element.109), channel_id=1, source_target_pairs={{0,8},{8,16},{16,24},{24,0},{1,9},{9,17},{17,25},{25,1},{2,10},{10... | collective-permute-start | bytes 221192 | tf_op jit(solution)/shard_map/ppermute | solution.py:29
  190.4 11.5 %collective-permute-start.37 = (bf16[144,256]{1,0:T(8,128)(2,1)S(1)}, bf16[144,256]{1,0:T(8,128)(2,1)S(1)}, u32[]{:S(2)}, u32[]{:S(2)}) collective-permute-start(bf16[144,256]{1,0:T(8,128)(2,1)S(1)} %get-tuple-element.110), channel_id=1, source_target_pairs={{0,16},{8,24},{16,0},{24,8},{1,17},{9,25},{17,1},{25,9},{2,18},{10... | collective-permute-start | bytes 221192 | tf_op jit(solution)/shard_map/ppermute | solution.py:29
  (36 other events, 224.0 us)
Sparse Core Ops, SparseCore 0:
  11.9 28.8 all-gather.11
  42.5 25.4 all-gather.5
  69.8 25.4 all-gather.7
  96.8 25.4 all-gather.9

commit v2 on v1

--- a/solution.py
+++ b/solution.py
@@ -11,14 +11,15 @@
 F32 = jnp.float32
 BF16 = jnp.bfloat16
 SIDE = 4
-WIDTHS = (128, 128, 128, 128)
+WIDTHS = (256, 256)
 VMEM = pl.BlockSpec(memory_space=pltpu.VMEM)
 SMEM = pl.BlockSpec(memory_space=pltpu.SMEM)
-LIMIT = 40 * 1024 * 1024
-
-
-def params():
-    return pltpu.CompilerParams(vmem_limit_bytes=LIMIT)
+ANY = pl.BlockSpec(memory_space=pl.ANY)
+MIB = 1024 * 1024
+
+
+def params(mib=16):
+    return pltpu.CompilerParams(vmem_limit_bytes=mib * MIB)
 
 
 def cost(flops, moved, transcendentals=0):
@@ -27,6 +28,10 @@
 
 def send(value, axis, step):
     return lax.ppermute(value, axis, [(i, (i + step) % SIDE) for i in range(SIDE)])
+
+
+def swap(value):
+    return lax.ppermute(value, "tc", [(0, 1), (1, 0)])
 
 
 def thirds(value):
@@ -36,13 +41,78 @@
     return high, middle, rest - middle
 
 
-def product_kernel(place, pairs, count, probs, weights, *rest):
-    outs, total = rest[:SIDE], rest[SIDE]
+def prepare_kernel(weights, piece):
+    slots, shard_rows, _ = weights.shape
+    width = piece.shape[1]
+    rows = slots * shard_rows
+    piece[0:rows, :] = weights[:, :, 0:width].reshape(rows, width)
+    sums = jnp.sum(weights[...].astype(F32), axis=2, keepdims=True).reshape(rows, 1)
+    line = jnp.broadcast_to(sums, (rows, 128)).T[0:1]
+    lines = jnp.concatenate(list(thirds(line)) + [jnp.zeros((5, rows), F32)], axis=0)
+    extra = jnp.concatenate([lines[:, i * 128 : (i + 1) * 128] for i in range(8)], axis=0)
+    if width > 128:
+        extra = jnp.concatenate([extra, jnp.zeros((64, width - 128), F32)], axis=1)
+    piece[rows : rows + 64, :] = extra.astype(BF16)
+
+
+def prepared(weights, width):
+    slots, shard_rows, _ = weights.shape
+    return pl.pallas_call(
+        prepare_kernel,
+        out_shape=jax.ShapeDtypeStruct((slots * shard_rows + 64, width), BF16),
+        in_specs=[VMEM],
+        out_specs=VMEM,
+        compiler_params=params(),
+        cost_estimate=cost(2 * weights.size, 3 * weights.size),
+        name="prepare_weights",
+    )(weights)
+
+
+def slice_kernel(offset, weights, *refs):
+    piece = refs[-1]
+    piece[...] = weights[:, :, offset : offset + piece.shape[1]].reshape(piece.shape)
+
+
+def sliced(weights, offset, width, behind):
+    slots, shard_rows, _ = weights.shape
+    return pl.pallas_call(
+        functools.partial(slice_kernel, offset),
+        out_shape=jax.ShapeDtypeStruct((slots * shard_rows, width), BF16),
+        in_specs=[VMEM] + [ANY] * len(behind),
+        out_specs=VMEM,
+        compiler_params=params(),
+        cost_estimate=cost(0, 3 * weights.size),
+        name="slice_weights",
+    )(weights, *behind)
+
+
+def product_kernel(with_totals, place, pairs, count, probs, *rest):
+    pieces, rest = rest[: 2 * SIDE], rest[2 * SIDE :]
+    if with_totals:
+        before, rest = rest[0], rest[1:]
+    outs, rest = rest[:SIDE], rest[SIDE:]
+    if with_totals:
+        after, sums, line = rest[0], rest[3], rest[4]
+        rest = rest[1:]
+    weights, total = rest[:2]
     block = weights.shape[0] * 64
     width = weights.shape[2]
     vocab_y = place[0]
     first_block = (vocab_y * SIDE + place[1]) * (probs.shape[1] // block)
     total[...] = jnp.zeros_like(total)
+    for step in range(SIDE):
+        at = lax.rem(place[2] + SIDE - step, SIDE) * 2
+        weights[at + place[3]] = pieces[step][...]
+        weights[at + 1 - place[3]] = pieces[SIDE + step][...]
+    if with_totals:
+        line[...] = jnp.zeros_like(line)
+        lane = lax.broadcasted_iota(jnp.int32, (64, 128), 1)
+        for pair in range(SIDE):
+            even = weights[2 * pair, 1024:1088, 0:128].astype(F32)
+            odd = weights[2 * pair + 1, 1024:1088, 0:128].astype(F32)
+            lanes = slice(pair * 128, pair * 128 + 128)
+            sums[0, :, lanes] = jnp.where(lane < 64, even, pltpu.roll(odd, 64, 1))
+            sums[1, :, lanes] = jnp.where(lane < 64, pltpu.roll(even, 64, 1), odd)
 
     def tile(slot, carry):
         teacher = pairs[slot, 0] - first_block
@@ -50,6 +120,11 @@
         columns = probs[:, pl.ds(pl.multiple_of(teacher * block, block), block)]
         rows = weights[:, pl.ds(pl.multiple_of(slot * 64, 64), 64), :].reshape(block, width)
         total[owner] += jnp.dot(columns, rows, preferred_element_type=F32)
+        if with_totals:
+            row_sums = sums[lax.rem(slot, 2), pl.ds(pl.multiple_of(slot // 2 * 8, 8), 8), :]
+            line[...] += lax.dot_general(
+                row_sums.astype(BF16), columns, (((1,), (1,)), ((), ())), preferred_element_type=F32
+            )
         return carry
 
     lax.fori_loop(0, count[0], tile, 0)
@@ -57,20 +132,37 @@
         start = lax.rem(vocab_y + step, SIDE) * SIDE
         for z in range(SIDE):
             outs[step][z] = total[start + z].astype(BF16)
-
-
-def products(place, pairs, count, probs, weights):
-    rows, width = probs.shape[0], weights.shape[2]
-    return pl.pallas_call(
-        product_kernel,
-        out_shape=[jax.ShapeDtypeStruct((SIDE, rows, width), BF16)] * SIDE,
-        in_specs=[SMEM, SMEM, SMEM, VMEM, VMEM],
-        out_specs=[VMEM] * SIDE,
-        scratch_shapes=[pltpu.VMEM((SIDE * SIDE, rows, width), F32)],
-        compiler_params=params(),
-        cost_estimate=cost(16 * 2 * rows * 512 * width, 2 * probs.size + 2 * weights.size + 32 * rows * width),
+    if with_totals:
+        value = line[0:1] + line[1:2] + line[2:3]
+        index = lax.broadcasted_iota(jnp.int32, before.shape, 0)
+        after[...] = jnp.where(index == 2, jnp.broadcast_to(value, before.shape), before[...])
+
+
+def products(place, pairs, count, probs, pieces, before=None):
+    rows = probs.shape[0]
+    depth, width = pieces[0].shape
+    outs = [jax.ShapeDtypeStruct((SIDE, rows, width), BF16)] * SIDE
+    scratch = [
+        pltpu.VMEM((2 * SIDE, depth, width), BF16),
+        pltpu.VMEM((SIDE * SIDE, rows, width), F32),
+    ]
+    extra = []
+    if before is not None:
+        outs = outs + [jax.ShapeDtypeStruct((8, rows), F32)]
+        scratch += [pltpu.VMEM((2, 64, 512), F32), pltpu.VMEM((8, rows), F32)]
+        extra = [before]
+    return pl.pallas_call(
+        functools.partial(product_kernel, before is not None),
+        out_shape=outs,
+        in_specs=[SMEM, SMEM, SMEM] + [VMEM] * (1 + 2 * SIDE + len(extra)),
+        out_specs=[VMEM] * len(outs),
+        scratch_shapes=scratch,
+        compiler_params=params(24),
+        cost_estimate=cost(
+            16 * 2 * rows * 512 * width, 2 * probs.size + 16 * depth * width + 32 * rows * width
+        ),
         name="tile_products",
-    )(place, pairs, count, probs, weights)
+    )(place, pairs, count, probs, *pieces, *extra)
 
 
 def stats_kernel(*refs):
@@ -297,25 +389,7 @@
 
 
 def shards(teacher_logits, student_hidden, student_unembed, tile_weights, tile_pairs, tile_count):
-    place = jnp.stack([lax.axis_index("vy"), lax.axis_index("vz")]).astype(jnp.int32)
-    rows = teacher_logits.shape[0]
-    slots, shard_rows, block = tile_weights.shape
-
-    row_sums = jnp.sum(tile_weights.astype(F32), axis=2)
-    high = lax.reduce_precision(row_sums, 8, 7)
-    mid = lax.reduce_precision(row_sums - high, 8, 7)
-    low = row_sums - high - mid
-    gathered = []
-    offset = 0
-    for index, width in enumerate(WIDTHS):
-        piece = tile_weights[:, :, offset : offset + width].reshape(slots * shard_rows, width)
-        if index == 1:
-            extra = jnp.stack([high, mid, low]).astype(BF16).reshape(-1, width)
-            extra = jnp.pad(extra, ((0, -extra.shape[0] % 16), (0, 0)))
-            piece = jnp.concatenate([piece, extra], axis=0)
-        gathered.append(lax.all_gather(piece, ("tx", "tc"), axis=0))
-        offset += width
-
+    place = jnp.stack([lax.axis_index("vy"), lax.axis_index("vz"), lax.axis_index("tx"), lax.axis_index("tc")]).astype(jnp.int32)
     teacher = teacher_logits.astype(F32)
     peak = jnp.max(teacher, axis=1)
     shifted = jnp.exp(teacher - peak[:, None])
@@ -326,24 +400,29 @@
     speak = jnp.max(logits, axis=1)
     smass = jnp.sum(jnp.exp(logits - speak[:, None]), axis=1)
 
-    extra = gathered[1][:, slots * shard_rows :, :].reshape(8, -1)[:, : 3 * slots * shard_rows]
-    sums = jnp.sum(extra.reshape(8, 3, slots, shard_rows).astype(F32), axis=1)
-    sums = sums.transpose(1, 0, 2).reshape(slots, block)
-    blocks = teacher.shape[1] // block
-    live = jnp.arange(slots) < tile_count[0]
-    chosen = (tile_pairs[:, 0] % blocks)[:, None] == jnp.arange(blocks)[None, :]
-    chosen = jnp.where(live[:, None], chosen, False)
-    spread = jnp.sum(jnp.where(chosen[:, :, None], sums[:, None, :], 0.0), axis=0).reshape(-1)
-    total = jnp.sum(probs.astype(F32) * spread[None, :], axis=1)
-
-    own = jnp.stack([peak, mass, total, speak, smass, smass, smass, smass])
+    gathered = []
+    offset = 0
+    for index, width in enumerate(WIDTHS):
+        if index == 0:
+            piece = prepared(tile_weights, width)
+        else:
+            piece = sliced(tile_weights, offset, width, [pieces[2], mass, smass])
+        pieces = [piece] + [send(piece, "tx", step) for step in (1, 2, 3)]
+        gathered.append(pieces + [swap(piece) for piece in pieces])
+        offset += width
+
+    blank = jnp.zeros_like(peak)
+    before = jnp.stack([peak, mass, blank, speak, smass, blank, blank, blank])
+    outs = []
+    for pieces in gathered:
+        outs.append(products(place, tile_pairs, tile_count, probs, pieces, None if outs else before))
+    own = outs[0][SIDE]
     column = jnp.stack([own] + [send(own, "vz", step) for step in (1, 2, 3)])
     table = statistics([column] + [send(column, "vy", step) for step in (1, 2, 3)])
 
     grads, losses = [], []
     offset = 0
-    for weights, width in zip(gathered, WIDTHS):
-        parts = products(place, tile_pairs, tile_count, probs, weights)
+    for parts, width in zip(outs, WIDTHS):
         parts = [parts[0]] + [send(parts[step], "vy", step) for step in (1, 2, 3)]
         parts = merged(place, table, parts)
         parts = [parts[0]] + [send(parts[step], "vz", step) for step in (1, 2, 3)]

time: 214 us -> 194 us (0.907)
  the two profiles are of different devices: /device:TPU:1 before, /device:TPU:0 now
where the time goes in v2:
time: 194 us; the launch traced here: 193 us
  starting transfers between devices  78.1 us (40%)
  waiting for transfers between devices  63.5 us (33%)
  Pallas kernels  23.1 us (12%)
  local copies, waits for them, and re-layouts  10.2 us (5%)
  matrix products  9.61 us (5%)
  other arithmetic  6.36 us (3%)
    ppermute x36, starting transfers between devices, send(): lax.ppermute(value, axis, [(i, (i + step) % SIDE) for i in range(SIDE)])  76.3 us
    ppermute x36, waiting for transfers between devices, send(): lax.ppermute(value, axis, [(i, (i + step) % SIDE) for i in range(SIDE)])  63.5 us
    dot_general x1, matrix products, shards(): jnp.dot(student_hidden, student_unembed, preferred_element_type=F32)  9.61 us
    unnamed x19, local copies, waits for them, and re-layouts  9.61 us
    pallas_call x1, Pallas kernels, hidden_parts(): pl.pallas_call(functools.partial(hidden_kernel, chunks), grid=(8,), out_s...  8.05 us
    pallas_call x2, Pallas kernels, products(): pl.pallas_call(functools.partial(product_kernel, before is not None), out...  6.01 us
    reduce_sum x1, other arithmetic, shards(): mass = jnp.sum(shifted, axis=1)  3.89 us
  transfers between devices with their start and end apart: 44, of which 15 were waited for; matrix products, arithmetic and copies ran while one was open for 8% of the time, Pallas kernels for 6%

profile of v2, /device:TPU:0, one launch (start us, length us, event | category | flops | bytes accessed | tf_op | source)
XLA Modules:
  0.0 192.5 jit_solution(8425606837134293082)
XLA Ops:
  2.5 2.9 %collective-permute-start.2 = (bf16[1088,256]{1,0:T(8,128)(2,1)S(1)}, bf16[1088,256]{1,0:T(8,128)(2,1)}, u32[]{:S(2)}, u32[]{:S(2)}) collective-permute-start(bf16[1088,256]{1,0:T(8,128)(2,1)S(1)} %prepare_weights.1.rest_0_), channel_id=1, source_target_pairs={{0,6},{2,0},{4,2},{6,4},{1,7},{3,1},{5,3},{7,5},{8,14},{10,8},{12,... | collective-permute-start | bytes 1671176 | tf_op jit(solution)/shard_map/ppermute | solution.py:30
  7.1 9.6 %fusion.2 = (f32[256]{0:T(256)S(1)}, f32[256,2048]{1,0:T(8,128)}) fusion(bf16[256,4096]{1,0:T(8,128)(2,1)S(1)} %copy-done, bf16[4096,2048]{1,0:T(8,128)(2,1)} %unembed.1), kind=kOutput, calls=%fused_computation.6 | convolution fusion | flops 4295491584 | bytes 20972544 | tf_op jit(solution)/shard_map/dot_general | solution.py:399
  18.6 3.9 %fusion = (f32[256]{0:T(256)S(1)}, bf16[256,4096]{1,0:T(8,128)(2,1)}) fusion(bf16[256,4096]{1,0:T(8,128)(2,1)} %param.6, f32[256]{0:T(256)S(1)} %reduce_max.28), kind=kLoop, calls=%fused_computation.1 | loop fusion | flops 4194048 | bytes 4196352 | tf_op jit(solution)/shard_map/reduce_sum | solution.py:396
  24.6 8.5 %collective-permute-start.21 = (bf16[1024,256]{1,0:T(8,128)(2,1)}, bf16[1024,256]{1,0:T(8,128)(2,1)}, u32[]{:S(2)}, u32[]{:S(2)}) collective-permute-start(bf16[1024,256]{1,0:T(8,128)(2,1)} %slice_weights.1.rest_0_), channel_id=1, source_target_pairs={{0,6},{2,0},{4,2},{6,4},{1,7},{3,1},{5,3},{7,5},{8,14},{10,8},{12,... | collective-permute-start | bytes 1572872 | tf_op jit(solution)/shard_map/ppermute | solution.py:30
  35.5 20.1 %collective-permute-done.21.rest_3_ = bf16[1024,256]{1,0:T(8,128)(2,1)} collective-permute-done((bf16[1024,256]{1,0:T(8,128)(2,1)}, bf16[1024,256]{1,0:T(8,128)(2,1)}, u32[]{:S(2)}, u32[]{:S(2)}) %collective-permute-start.21) | collective-permute-done | bytes 524320 | tf_op jit(solution)/shard_map/ppermute | solution.py:30
  56.1 3.2 %collective-permute-done.19.rest_1_ = bf16[1024,256]{1,0:T(8,128)(2,1)} collective-permute-done((bf16[1024,256]{1,0:T(8,128)(2,1)}, bf16[1024,256]{1,0:T(8,128)(2,1)}, u32[]{:S(2)}, u32[]{:S(2)}) %collective-permute-start.19) | collective-permute-done | bytes 524320 | tf_op jit(solution)/shard_map/ppermute | solution.py:30
  62.5 3.2 %tile_products.2 = (bf16[4,256,256]{2,1,0:T(8,128)(2,1)S(1)}, bf16[4,256,256]{2,1,0:T(8,128)(2,1)S(1)}, bf16[4,256,256]{2,1,0:T(8,128)(2,1)S(1)}, bf16[4,256,256]{2,1,0:T(8,128)(2,1)S(1)}, f32[8,256]{1,0:T(8,128)S(1)}) custom-call(s32[4]{0:T(128)S(1)} %pad_add_fusion.place, s32[16,2]{1,0:T(8,128)S(1)} %copy.8.pairs, s32[1]{0:T(128)S(6)} %copy.10.count, ...), custom_call_target="tpu_custom_call" | custom-call | flops 1073741824 | bytes 8650752 | tf_op jit(solution)/shard_map/tile_products/pallas_call | solution.py:154
  65.6 4.5 %collective-permute-start.9 = (f32[8,256]{1,0:T(8,128)S(1)}, f32[8,256]{1,0:T(8,128)S(1)}, u32[]{:S(2)}, u32[]{:S(2)}) collective-permute-start(f32[8,256]{1,0:T(8,128)S(1)} %get-tuple-element.41), channel_id=1, source_target_pairs={{0,24},{8,0},{16,8},{24,16},{1,25},{9,1},{17,9},{25,17},{2,26},{10... | collective-permute-start | bytes 24584 | tf_op jit(solution)/shard_map/ppermute | solution.py:30
  71.5 6.1 %collective-permute-start.8 = (f32[8,256]{1,0:T(8,128)S(1)}, f32[8,256]{1,0:T(8,128)S(1)}, u32[]{:S(2)}, u32[]{:S(2)}) collective-permute-start(f32[8,256]{1,0:T(8,128)S(1)} %get-tuple-element.41), channel_id=1, source_target_pairs={{0,16},{8,24},{16,0},{24,8},{1,17},{9,25},{17,1},{25,9},{2,18},{10... | collective-permute-start | bytes 24584 | tf_op jit(solution)/shard_map/ppermute | solution.py:30
  80.7 3.4 %collective-permute-done.7 = f32[8,256]{1,0:T(8,128)S(1)} collective-permute-done((f32[8,256]{1,0:T(8,128)S(1)}, f32[8,256]{1,0:T(8,128)S(1)}, u32[]{:S(2)}, u32[]{:S(2)}) %collective-permute-start.7) | collective-permute-done | bytes 8224 | tf_op jit(solution)/shard_map/ppermute | solution.py:30
  84.1 3.2 %collective-permute-start.12 = (f32[4,8,256]{2,1,0:T(8,128)S(1)}, f32[4,8,256]{2,1,0:T(8,128)S(1)}, u32[]{:S(2)}, u32[]{:S(2)}) collective-permute-start(f32[4,8,256]{2,1,0:T(8,128)S(1)} %pad_maximum_fusion.refs_0_), channel_id=1, source_target_pairs={{0,96},{32,0},{64,32},{96,64},{1,97},{33,1},{65,33},{97,65},{2,98}... | collective-permute-start | bytes 98312 | tf_op jit(solution)/shard_map/ppermute | solution.py:30
  89.0 3.6 %collective-permute-start.14 = (bf16[4,256,256]{2,1,0:T(8,128)(2,1)S(1)}, bf16[4,256,256]{2,1,0:T(8,128)(2,1)S(1)}, u32[]{:S(2)}, u32[]{:S(2)}) collective-permute-start(bf16[4,256,256]{2,1,0:T(8,128)(2,1)S(1)} %get-tuple-element.44), channel_id=1, source_target_pairs={{0,64},{32,96},{64,0},{96,32},{1,65},{33,97},{65,1},{97,33},{2,66}... | collective-permute-start | bytes 1572872 | tf_op jit(solution)/shard_map/ppermute | solution.py:30
  92.5 5.7 %collective-permute-start.15 = (bf16[4,256,256]{2,1,0:T(8,128)(2,1)S(1)}, bf16[4,256,256]{2,1,0:T(8,128)(2,1)S(1)}, u32[]{:S(2)}, u32[]{:S(2)}) collective-permute-start(bf16[4,256,256]{2,1,0:T(8,128)(2,1)S(1)} %get-tuple-element.45), channel_id=1, source_target_pairs={{0,96},{32,0},{64,32},{96,64},{1,97},{33,1},{65,33},{97,65},{2,98}... | collective-permute-start | bytes 1572872 | tf_op jit(solution)/shard_map/ppermute | solution.py:30
  98.2 2.9 %collective-permute-start.11 = (f32[4,8,256]{2,1,0:T(8,128)S(1)}, f32[4,8,256]{2,1,0:T(8,128)S(1)}, u32[]{:S(2)}, u32[]{:S(2)}) collective-permute-start(f32[4,8,256]{2,1,0:T(8,128)S(1)} %pad_maximum_fusion.refs_0_), channel_id=1, source_target_pairs={{0,64},{32,96},{64,0},{96,32},{1,65},{33,97},{65,1},{97,33},{2,66}... | collective-permute-start | bytes 98312 | tf_op jit(solution)/shard_map/ppermute | solution.py:30
  101.1 2.8 %tile_products.3 = (bf16[4,256,256]{2,1,0:T(8,128)(2,1)S(1)}, bf16[4,256,256]{2,1,0:T(8,128)(2,1)S(1)}, bf16[4,256,256]{2,1,0:T(8,128)(2,1)S(1)}, bf16[4,256,256]{2,1,0:T(8,128)(2,1)S(1)}) custom-call(s32[4]{0:T(128)S(1)} %pad_add_fusion.place, s32[16,2]{1,0:T(8,128)S(1)} %copy.8.pairs, s32[1]{0:T(128)S(6)} %copy.10.count, bf16[256,4096]{1,0:T(8,128)(2,1)S(1)} %copy-done.4, ...), custom_call_target="tpu_custom_call" | custom-call | flops 1073741824 | bytes 8388608 | tf_op jit(solution)/shard_map/tile_products/pallas_call | solution.py:154
  104.0 8.3 %collective-permute-done.11.refs_2_ = f32[4,8,256]{2,1,0:T(8,128)S(1)} collective-permute-done((f32[4,8,256]{2,1,0:T(8,128)S(1)}, f32[4,8,256]{2,1,0:T(8,128)S(1)}, u32[]{:S(2)}, u32[]{:S(2)}) %collective-permute-start.11) | collective-permute-done | bytes 32800 | tf_op jit(solution)/shard_map/ppermute | solution.py:30
  112.2 5.4 %collective-permute-start.26 = (bf16[4,256,256]{2,1,0:T(8,128)(2,1)S(1)}, bf16[4,256,256]{2,1,0:T(8,128)(2,1)S(1)}, u32[]{:S(2)}, u32[]{:S(2)}) collective-permute-start(bf16[4,256,256]{2,1,0:T(8,128)(2,1)S(1)} %get-tuple-element.52), channel_id=1, source_target_pairs={{0,32},{32,64},{64,96},{96,0},{1,33},{33,65},{65,97},{97,1},{2,34}... | collective-permute-start | bytes 1572872 | tf_op jit(solution)/shard_map/ppermute | solution.py:30
  124.7 8.6 %collective-permute-done.26.refs_1_ = bf16[4,256,256]{2,1,0:T(8,128)(2,1)S(1)} collective-permute-done((bf16[4,256,256]{2,1,0:T(8,128)(2,1)S(1)}, bf16[4,256,256]{2,1,0:T(8,128)(2,1)S(1)}, u32[]{:S(2)}, u32[]{:S(2)}) %collective-permute-start.26) | collective-permute-done | bytes 524320 | tf_op jit(solution)/shard_map/ppermute | solution.py:30
  146.8 5.8 %copy-done.5 = bf16[4096,2048]{1,0:T(8,128)(2,1)S(1)} copy-done((bf16[4096,2048]{1,0:T(8,128)(2,1)S(1)}, bf16[4096,2048]{1,0:T(8,128)(2,1)}, u32[]{:S(2)}) %copy-start.5) | copy-done | bytes 16777240
  152.6 8.0 %hidden_grad.1 = (bf16[528,256]{1,0:T(8,128)(2,1)S(1)}, bf16[528,256]{1,0:T(8,128)(2,1)S(1)}, bf16[528,256]{1,0:T(8,128)(2,1)S(1)}, bf16[528,256]{1,0:T(8,128)(2...) custom-call(s32[4]{0:T(128)S(1)} %pad_add_fusion.place, ...), custom_call_target="tpu_custom_call" | custom-call | flops 4294967296 | bytes 20971520 | tf_op jit(solution)/shard_map/hidden_grad/pallas_call | solution.py:305
  162.7 3.5 %collective-permute-start.33 = (bf16[528,256]{1,0:T(8,128)(2,1)S(1)}, bf16[528,256]{1,0:T(8,128)(2,1)S(1)}, u32[]{:S(2)}, u32[]{:S(2)}) collective-permute-start(bf16[528,256]{1,0:T(8,128)(2,1)S(1)} %get-tuple-element.64), channel_id=1, source_target_pairs={{0,64},{32,96},{64,0},{96,32},{1,65},{33,97},{65,1},{97,33},{2,66}... | collective-permute-start | bytes 811016 | tf_op jit(solution)/shard_map/ppermute | solution.py:30
  166.2 2.9 %collective-permute-start.36 = (bf16[512,256]{1,0:T(8,128)(2,1)S(1)}, bf16[512,256]{1,0:T(8,128)(2,1)S(1)}, u32[]{:S(2)}, u32[]{:S(2)}) collective-permute-start(bf16[512,256]{1,0:T(8,128)(2,1)S(1)} %get-tuple-element.68), channel_id=1, source_target_pairs={{0,16},{8,24},{16,0},{24,8},{1,17},{9,25},{17,1},{25,9},{2,18},{10... | collective-permute-start | bytes 786440 | tf_op jit(solution)/shard_map/ppermute | solution.py:30
  174.0 3.3 %collective-permute-done.37.refs_7_ = bf16[512,256]{1,0:T(8,128)(2,1)S(1)} collective-permute-done((bf16[512,256]{1,0:T(8,128)(2,1)S(1)}, bf16[512,256]{1,0:T(8,128)(2,1)S(1)}, u32[]{:S(2)}, u32[]{:S(2)}) %collective-permute-start.37) | collective-permute-done | bytes 262176 | tf_op jit(solution)/shard_map/ppermute | solution.py:30
  187.6 3.0 %collective-permute-done.42.refs_6_ = bf16[128,256]{1,0:T(8,128)(2,1)S(1)} collective-permute-done((bf16[128,256]{1,0:T(8,128)(2,1)S(1)}, bf16[128,256]{1,0:T(8,128)(2,1)S(1)}, u32[]{:S(2)}, u32[]{:S(2)}) %collective-permute-start.42) | collective-permute-done | bytes 65568 | tf_op jit(solution)/shard_map/ppermute | solution.py:30
  (106 shorter events, 58.7 us)
Async XLA Ops:
  2.4 32.5 %collective-permute-start.3 = (bf16[1088,256]{1,0:T(8,128)(2,1)S(1)}, bf16[1088,256]{1,0:T(8,128)(2,1)}, u32[]{:S(2)}, u32[]{:S(2)}) collective-permute-start(bf16[1088,256]{1,0:T(8,128)(2,1)S(1)} %prepare_weights.1.rest_0_), channel_id=1, source_target_pairs={{0,1},{1,0},{2,3},{3,2},{4,5},{5,4},{6,7},{7,6},{8,9},{9,8},{10,11... | collective-permute-start | bytes 1671176 | tf_op jit(solution)/shard_map/ppermute | solution.py:34
  2.5 32.4 %collective-permute-start.2 = (bf16[1088,256]{1,0:T(8,128)(2,1)S(1)}, bf16[1088,256]{1,0:T(8,128)(2,1)}, u32[]{:S(2)}, u32[]{:S(2)}) collective-permute-start(bf16[1088,256]{1,0:T(8,128)(2,1)S(1)} %prepare_weights.1.rest_0_), channel_id=1, source_target_pairs={{0,6},{2,0},{4,2},{6,4},{1,7},{3,1},{5,3},{7,5},{8,14},{10,8},{12,... | collective-permute-start | bytes 1671176 | tf_op jit(solution)/shard_map/ppermute | solution.py:30
  5.4 17.6 %collective-permute-start.1 = (bf16[1088,256]{1,0:T(8,128)(2,1)S(1)}, bf16[1088,256]{1,0:T(8,128)(2,1)S(1)}, u32[]{:S(2)}, u32[]{:S(2)}) collective-permute-start(bf16[1088,256]{1,0:T(8,128)(2,1)S(1)} %prepare_weights.1.rest_0_), channel_id=1, source_target_pairs={{0,4},{2,6},{4,0},{6,2},{1,5},{3,7},{5,1},{7,3},{8,12},{10,14},{12... | collective-permute-start | bytes 1671176 | tf_op jit(solution)/shard_map/ppermute | solution.py:30
  6.2 28.8 %collective-permute-start = (bf16[1088,256]{1,0:T(8,128)(2,1)S(1)}, bf16[1088,256]{1,0:T(8,128)(2,1)}, u32[]{:S(2)}, u32[]{:S(2)}) collective-permute-start(bf16[1088,256]{1,0:T(8,128)(2,1)S(1)} %prepare_weights.1.rest_0_), channel_id=1, source_target_pairs={{0,2},{2,4},{4,6},{6,0},{1,3},{3,5},{5,7},{7,1},{8,10},{10,12},{12... | collective-permute-start | bytes 1671176 | tf_op jit(solution)/shard_map/ppermute | solution.py:30
  24.6 31.0 %collective-permute-start.21 = (bf16[1024,256]{1,0:T(8,128)(2,1)}, bf16[1024,256]{1,0:T(8,128)(2,1)}, u32[]{:S(2)}, u32[]{:S(2)}) collective-permute-start(bf16[1024,256]{1,0:T(8,128)(2,1)} %slice_weights.1.rest_0_), channel_id=1, source_target_pairs={{0,6},{2,0},{4,2},{6,4},{1,7},{3,1},{5,3},{7,5},{8,14},{10,8},{12,... | collective-permute-start | bytes 1572872 | tf_op jit(solution)/shard_map/ppermute | solution.py:30
  33.1 22.5 %collective-permute-start.20 = (bf16[1024,256]{1,0:T(8,128)(2,1)}, bf16[1024,256]{1,0:T(8,128)(2,1)}, u32[]{:S(2)}, u32[]{:S(2)}) collective-permute-start(bf16[1024,256]{1,0:T(8,128)(2,1)} %slice_weights.1.rest_0_), channel_id=1, source_target_pairs={{0,4},{2,6},{4,0},{6,2},{1,5},{3,7},{5,1},{7,3},{8,12},{10,14},{12... | collective-permute-start | bytes 1572872 | tf_op jit(solution)/shard_map/ppermute | solution.py:30
  34.9 24.4 %collective-permute-start.19 = (bf16[1024,256]{1,0:T(8,128)(2,1)}, bf16[1024,256]{1,0:T(8,128)(2,1)}, u32[]{:S(2)}, u32[]{:S(2)}) collective-permute-start(bf16[1024,256]{1,0:T(8,128)(2,1)} %slice_weights.1.rest_0_), channel_id=1, source_target_pairs={{0,2},{2,4},{4,6},{6,0},{1,3},{3,5},{5,7},{7,1},{8,10},{10,12},{12... | collective-permute-start | bytes 1572872 | tf_op jit(solution)/shard_map/ppermute | solution.py:30
  34.9 25.3 %collective-permute-start.6 = (bf16[1088,256]{1,0:T(8,128)(2,1)}, bf16[1088,256]{1,0:T(8,128)(2,1)}, u32[]{:S(2)}, u32[]{:S(2)}) collective-permute-start(bf16[1088,256]{1,0:T(8,128)(2,1)} %collective-permute-done.2.rest_3_), channel_id=1, source_target_pairs={{0,1},{1,0},{2,3},{3,2},{4,5},{5,4},{6,7},{7,6},{8,9},{9,8},{10,11... | collective-permute-start | bytes 1671176 | tf_op jit(solution)/shard_map/ppermute | solution.py:34
  35.0 25.7 %collective-permute-start.5 = (bf16[1088,256]{1,0:T(8,128)(2,1)S(1)}, bf16[1088,256]{1,0:T(8,128)(2,1)}, u32[]{:S(2)}, u32[]{:S(2)}) collective-permute-start(bf16[1088,256]{1,0:T(8,128)(2,1)S(1)} %collective-permute-done.1.rest_2_.refs_0_), channel_id=1, source_target_pairs={{0,1},{1,0},{2,3},{3,2},{4,5},{5,4},{6,7},{7,6},{8,9},{9,8},{10,11... | collective-permute-start | bytes 1671176 | tf_op jit(solution)/shard_map/ppermute | solution.py:34
  55.6 28.5 %collective-permute-start.22 = (bf16[1024,256]{1,0:T(8,128)(2,1)}, bf16[1024,256]{1,0:T(8,128)(2,1)}, u32[]{:S(2)}, u32[]{:S(2)}) collective-permute-start(bf16[1024,256]{1,0:T(8,128)(2,1)} %slice_weights.1.rest_0_), channel_id=1, source_target_pairs={{0,1},{1,0},{2,3},{3,2},{4,5},{5,4},{6,7},{7,6},{8,9},{9,8},{10,11... | collective-permute-start | bytes 1572872 | tf_op jit(solution)/shard_map/ppermute | solution.py:34
  59.3 33.2 %collective-permute-start.25 = (bf16[1024,256]{1,0:T(8,128)(2,1)}, bf16[1024,256]{1,0:T(8,128)(2,1)}, u32[]{:S(2)}, u32[]{:S(2)}) collective-permute-start(bf16[1024,256]{1,0:T(8,128)(2,1)} %collective-permute-done.21.rest_3_), channel_id=1, source_target_pairs={{0,1},{1,0},{2,3},{3,2},{4,5},{5,4},{6,7},{7,6},{8,9},{9,8},{10,11... | collective-permute-start | bytes 1572872 | tf_op jit(solution)/shard_map/ppermute | solution.py:34
  60.2 38.0 %collective-permute-start.24 = (bf16[1024,256]{1,0:T(8,128)(2,1)}, bf16[1024,256]{1,0:T(8,128)(2,1)S(1)}, u32[]{:S(2)}, u32[]{:S(2)}) collective-permute-start(bf16[1024,256]{1,0:T(8,128)(2,1)} %collective-permute-done.20.rest_2_), channel_id=1, source_target_pairs={{0,1},{1,0},{2,3},{3,2},{4,5},{5,4},{6,7},{7,6},{8,9},{9,8},{10,11... | collective-permute-start | bytes 1572872 | tf_op jit(solution)/shard_map/ppermute | solution.py:34
  60.8 40.4 %collective-permute-start.23 = (bf16[1024,256]{1,0:T(8,128)(2,1)}, bf16[1024,256]{1,0:T(8,128)(2,1)S(1)}, u32[]{:S(2)}, u32[]{:S(2)}) collective-permute-start(bf16[1024,256]{1,0:T(8,128)(2,1)} %collective-permute-done.19.rest_1_), channel_id=1, source_target_pairs={{0,1},{1,0},{2,3},{3,2},{4,5},{5,4},{6,7},{7,6},{8,9},{9,8},{10,11... | collective-permute-start | bytes 1572872 | tf_op jit(solution)/shard_map/ppermute | solution.py:34
  84.1 36.1 %collective-permute-start.13 = (bf16[4,256,256]{2,1,0:T(8,128)(2,1)S(1)}, bf16[4,256,256]{2,1,0:T(8,128)(2,1)S(1)}, u32[]{:S(2)}, u32[]{:S(2)}) collective-permute-start(bf16[4,256,256]{2,1,0:T(8,128)(2,1)S(1)} %get-tuple-element.43), channel_id=1, source_target_pairs={{0,32},{32,64},{64,96},{96,0},{1,33},{33,65},{65,97},{97,1},{2,34}... | collective-permute-start | bytes 1572872 | tf_op jit(solution)/shard_map/ppermute | solution.py:30
  89.0 31.6 %collective-permute-start.14 = (bf16[4,256,256]{2,1,0:T(8,128)(2,1)S(1)}, bf16[4,256,256]{2,1,0:T(8,128)(2,1)S(1)}, u32[]{:S(2)}, u32[]{:S(2)}) collective-permute-start(bf16[4,256,256]{2,1,0:T(8,128)(2,1)S(1)} %get-tuple-element.44), channel_id=1, source_target_pairs={{0,64},{32,96},{64,0},{96,32},{1,65},{33,97},{65,1},{97,33},{2,66}... | collective-permute-start | bytes 1572872 | tf_op jit(solution)/shard_map/ppermute | solution.py:30
  92.5 28.0 %collective-permute-start.15 = (bf16[4,256,256]{2,1,0:T(8,128)(2,1)S(1)}, bf16[4,256,256]{2,1,0:T(8,128)(2,1)S(1)}, u32[]{:S(2)}, u32[]{:S(2)}) collective-permute-start(bf16[4,256,256]{2,1,0:T(8,128)(2,1)S(1)} %get-tuple-element.45), channel_id=1, source_target_pairs={{0,96},{32,0},{64,32},{96,64},{1,97},{33,1},{65,33},{97,65},{2,98}... | collective-permute-start | bytes 1572872 | tf_op jit(solution)/shard_map/ppermute | solution.py:30
  101.1 16.5 %collective-permute-start.10 = (f32[4,8,256]{2,1,0:T(8,128)S(1)}, f32[4,8,256]{2,1,0:T(8,128)S(1)}, u32[]{:S(2)}, u32[]{:S(2)}) collective-permute-start(f32[4,8,256]{2,1,0:T(8,128)S(1)} %pad_maximum_fusion.refs_0_), channel_id=1, source_target_pairs={{0,32},{32,64},{64,96},{96,0},{1,33},{33,65},{65,97},{97,1},{2,34}... | collective-permute-start | bytes 98312 | tf_op jit(solution)/shard_map/ppermute | solution.py:30
  112.2 21.1 %collective-permute-start.26 = (bf16[4,256,256]{2,1,0:T(8,128)(2,1)S(1)}, bf16[4,256,256]{2,1,0:T(8,128)(2,1)S(1)}, u32[]{:S(2)}, u32[]{:S(2)}) collective-permute-start(bf16[4,256,256]{2,1,0:T(8,128)(2,1)S(1)} %get-tuple-element.52), channel_id=1, source_target_pairs={{0,32},{32,64},{64,96},{96,0},{1,33},{33,65},{65,97},{97,1},{2,34}... | collective-permute-start | bytes 1572872 | tf_op jit(solution)/shard_map/ppermute | solution.py:30
  117.7 15.6 %collective-permute-start.27 = (bf16[4,256,256]{2,1,0:T(8,128)(2,1)S(1)}, bf16[4,256,256]{2,1,0:T(8,128)(2,1)S(1)}, u32[]{:S(2)}, u32[]{:S(2)}) collective-permute-start(bf16[4,256,256]{2,1,0:T(8,128)(2,1)S(1)} %get-tuple-element.53), channel_id=1, source_target_pairs={{0,64},{32,96},{64,0},{96,32},{1,65},{33,97},{65,1},{97,33},{2,66}... | collective-permute-start | bytes 1572872 | tf_op jit(solution)/shard_map/ppermute | solution.py:30
  120.2 15.4 %collective-permute-start.28 = (bf16[4,256,256]{2,1,0:T(8,128)(2,1)S(1)}, bf16[4,256,256]{2,1,0:T(8,128)(2,1)S(1)}, u32[]{:S(2)}, u32[]{:S(2)}) collective-permute-start(bf16[4,256,256]{2,1,0:T(8,128)(2,1)S(1)} %get-tuple-element.54), channel_id=1, source_target_pairs={{0,96},{32,0},{64,32},{96,64},{1,97},{33,1},{65,33},{97,65},{2,98}... | collective-permute-start | bytes 1572872 | tf_op jit(solution)/shard_map/ppermute | solution.py:30
  121.9 18.0 %collective-permute-start.16 = (bf16[256,256]{1,0:T(8,128)(2,1)S(1)}, bf16[256,256]{1,0:T(8,128)(2,1)S(1)}, u32[]{:S(2)}, u32[]{:S(2)}) collective-permute-start(bf16[256,256]{1,0:T(8,128)(2,1)S(1)} %get-tuple-element.47), channel_id=1, source_target_pairs={{0,8},{8,16},{16,24},{24,0},{1,9},{9,17},{17,25},{25,1},{2,10},{10... | collective-permute-start | bytes 393224 | tf_op jit(solution)/shard_map/ppermute | solution.py:30
  122.9 18.7 %collective-permute-start.17 = (bf16[256,256]{1,0:T(8,128)(2,1)S(1)}, bf16[256,256]{1,0:T(8,128)(2,1)S(1)}, u32[]{:S(2)}, u32[]{:S(2)}) collective-permute-start(bf16[256,256]{1,0:T(8,128)(2,1)S(1)} %get-tuple-element.48), channel_id=1, source_target_pairs={{0,16},{8,24},{16,0},{24,8},{1,17},{9,25},{17,1},{25,9},{2,18},{10... | collective-permute-start | bytes 393224 | tf_op jit(solution)/shard_map/ppermute | solution.py:30
  162.1 15.2 %collective-permute-start.32 = (bf16[528,256]{1,0:T(8,128)(2,1)S(1)}, bf16[528,256]{1,0:T(8,128)(2,1)S(1)}, u32[]{:S(2)}, u32[]{:S(2)}) collective-permute-start(bf16[528,256]{1,0:T(8,128)(2,1)S(1)} %get-tuple-element.63), channel_id=1, source_target_pairs={{0,32},{32,64},{64,96},{96,0},{1,33},{33,65},{65,97},{97,1},{2,34}... | collective-permute-start | bytes 811016 | tf_op jit(solution)/shard_map/ppermute | solution.py:30
  162.7 14.7 %collective-permute-start.33 = (bf16[528,256]{1,0:T(8,128)(2,1)S(1)}, bf16[528,256]{1,0:T(8,128)(2,1)S(1)}, u32[]{:S(2)}, u32[]{:S(2)}) collective-permute-start(bf16[528,256]{1,0:T(8,128)(2,1)S(1)} %get-tuple-element.64), channel_id=1, source_target_pairs={{0,64},{32,96},{64,0},{96,32},{1,65},{33,97},{65,1},{97,33},{2,66}... | collective-permute-start | bytes 811016 | tf_op jit(solution)/shard_map/ppermute | solution.py:30
  (29 other events, 270.4 us)

commit v3 on v2

v3 whole, which is shorter than its diff:
```python
import functools

import jax
import jax.numpy as jnp
from jax import lax
from jax.experimental import pallas as pl
from jax.experimental.pallas import tpu as pltpu
from jax.sharding import Mesh
from jax.sharding import PartitionSpec as P

F32 = jnp.float32
BF16 = jnp.bfloat16
SIDE = 4
VMEM = pl.BlockSpec(memory_space=pltpu.VMEM)
SMEM = pl.BlockSpec(memory_space=pltpu.SMEM)
ANY = pl.BlockSpec(memory_space=pl.ANY)
MIB = 1024 * 1024


def params(mib=16):
    return pltpu.CompilerParams(vmem_limit_bytes=mib * MIB)


def cost(flops, moved, transcendentals=0):
    return pl.CostEstimate(flops=flops, bytes_accessed=moved, transcendentals=transcendentals)


def send(value, axis, step):
    return lax.ppermute(value, axis, [(i, (i + step) % SIDE) for i in range(SIDE)])


def swap(value):
    return lax.ppermute(value, "tc", [(0, 1), (1, 0)])


def thirds(value):
    high = value.astype(BF16).astype(F32)
    rest = value - high
    middle = rest.astype(BF16).astype(F32)
    return high, middle, rest - middle


def prepare_kernel(weights, piece):
    slots, shard_rows, _ = weights.shape
    width = piece.shape[1]
    rows = slots * shard_rows
    piece[0:rows, :] = weights[:, :, 0:width].reshape(rows, width)
    sums = jnp.sum(weights[...].astype(F32), axis=2, keepdims=True).reshape(rows, 1)
    line = jnp.broadcast_to(sums, (rows, 128)).T[0:1]
    lines = jnp.concatenate(list(thirds(line)) + [jnp.zeros((5, rows), F32)], axis=0)
    extra = jnp.concatenate([lines[:, i * 128 : (i + 1) * 128] for i in range(8)], axis=0)
    if width > 128:
        extra = jnp.concatenate([extra, jnp.zeros((64, width - 128), F32)], axis=1)
    piece[rows : rows + 64, :] = extra.astype(BF16)


def prepared(weights, width):
    slots, shard_rows, _ = weights.shape
    return pl.pallas_call(
        prepare_kernel,
        out_shape=jax.ShapeDtypeStruct((slots * shard_rows + 64, width), BF16),
        in_specs=[VMEM],
        out_specs=VMEM,
        compiler_params=params(),
        cost_estimate=cost(2 * weights.size, 3 * weights.size),
        name="prepare_weights",
    )(weights)


def slice_kernel(offset, weights, *refs):
    piece = refs[-1]
    piece[...] = weights[:, :, offset : offset + piece.shape[1]].reshape(piece.shape)


def sliced(weights, offset, width, behind):
    slots, shard_rows, _ = weights.shape
    return pl.pallas_call(
        functools.partial(slice_kernel, offset),
        out_shape=jax.ShapeDtypeStruct((slots * shard_rows, width), BF16),
        in_specs=[VMEM] + [ANY] * len(behind),
        out_specs=VMEM,
        compiler_params=params(),
        cost_estimate=cost(0, 3 * weights.size),
        name="slice_weights",
    )(weights, *behind)


def pack_kernel(number, *refs):
    out = refs[-1]
    at = 0
    for part in refs[:number]:
        out[at : at + part.shape[0], :] = part[...]
        at += part.shape[0]


def packed_pieces(parts, behind):
    depth = sum(part.shape[0] for part in parts)
    width = parts[0].shape[1]
    return pl.pallas_call(
        functools.partial(pack_kernel, len(parts)),
        out_shape=jax.ShapeDtypeStruct((depth, width), BF16),
        in_specs=[VMEM] * len(parts) + [ANY] * len(behind),
        out_specs=VMEM,
        compiler_params=params(),
        cost_estimate=cost(0, 4 * depth * width),
        name="pack_weights",
    )(*parts, *behind)


def halves_kernel(right, left, *refs):
    top, low = refs[-2:]
    top[...] = right[...]
    low[...] = left[...]


def halves(right, left, behind):
    depth, width = right.shape
    shape = (depth // 2, width)
    return pl.pallas_call(
        halves_kernel,
        grid=(1,),
        out_shape=[jax.ShapeDtypeStruct(shape, BF16)] * 2,
        in_specs=[
            pl.BlockSpec(shape, lambda i: (0, 0)),
            pl.BlockSpec(shape, lambda i: (1, 0)),
        ]
        + [ANY] * len(behind),
        out_specs=[pl.BlockSpec(shape, lambda i: (0, 0))] * 2,
        compiler_params=params(),
        cost_estimate=cost(0, 4 * depth * width),
        name="take_halves",
    )(right, left, *behind)


def product_kernel(with_stats, place, pairs, count, probs, mine, other, *rest):
    if with_stats:
        before, rest = rest[0], rest[1:]
    outs, rest = rest[:SIDE], rest[SIDE:]
    weights, total = rest[:2]
    block = weights.shape[0] * 64
    width = weights.shape[2]
    rows = probs.shape[0]
    vocab_y = place[0]
    first_block = (vocab_y * SIDE + place[1]) * (probs.shape[1] // block)
    total[...] = jnp.zeros_like(total)
    depth = weights.shape[1]
    for step in range(SIDE):
        at = lax.rem(place[2] + SIDE - step, SIDE) * 2
        weights[at + place[3]] = mine[step * depth : step * depth + depth, :]
        weights[at + 1 - place[3]] = other[step * depth : step * depth + depth, :]
    if with_stats:
        sums, line = rest[2:]
        line[...] = jnp.zeros_like(line)
        lane = lax.broadcasted_iota(jnp.int32, (64, 128), 1)
        for pair in range(SIDE):
            even = weights[2 * pair, 1024:1088, 0:128].astype(F32)
            odd = weights[2 * pair + 1, 1024:1088, 0:128].astype(F32)
            lanes = slice(pair * 128, pair * 128 + 128)
            sums[0, :, lanes] = jnp.where(lane < 64, even, pltpu.roll(odd, 64, 1))
            sums[1, :, lanes] = jnp.where(lane < 64, pltpu.roll(even, 64, 1), odd)

    def tile(slot, carry):
        teacher = pairs[slot, 0] - first_block
        owner = pairs[slot, 1] // SIDE
        columns = probs[:, pl.ds(pl.multiple_of(teacher * block, block), block)]
        matrix = weights[:, pl.ds(pl.multiple_of(slot * 64, 64), 64), :].reshape(block, width)
        total[owner] += jnp.dot(columns, matrix, preferred_element_type=F32)
        if with_stats:
            row_sums = sums[lax.rem(slot, 2), pl.ds(pl.multiple_of(slot // 2 * 8, 8), 8), :]
            line[...] += lax.dot_general(
                row_sums.astype(BF16), columns, (((1,), (1,)), ((), ())), preferred_element_type=F32
            )
        return carry

    lax.fori_loop(0, count[0], tile, 0)
    for step in range(SIDE):
        start = lax.rem(vocab_y + step, SIDE) * SIDE
        for z in range(SIDE):
            outs[step][z * rows : z * rows + rows, :] = total[start + z].astype(BF16)
    if with_stats:
        sent = line[0:1] + line[1:2] + line[2:3]
        packed = pack_rows([before[0:1], before[1:2], sent, before[3:4], before[4:5]])
        for out in outs:
            out[SIDE * rows : SIDE * rows + 16, :] = packed


def products(place, pairs, count, probs, mine, other, before=None):
    rows = probs.shape[0]
    depth, width = mine.shape[0] // SIDE, mine.shape[1]
    extra = [] if before is None else [before]
    scratch = [
        pltpu.VMEM((2 * SIDE, depth, width), BF16),
        pltpu.VMEM((SIDE * SIDE, rows, width), F32),
    ]
    if extra:
        scratch += [pltpu.VMEM((2, 64, 512), F32), pltpu.VMEM((8, rows), F32)]
    return pl.pallas_call(
        functools.partial(product_kernel, bool(extra)),
        out_shape=[jax.ShapeDtypeStruct((SIDE * rows + 16 * len(extra), width), BF16)] * SIDE,
        in_specs=[SMEM, SMEM, SMEM] + [VMEM] * (3 + len(extra)),
        out_specs=[VMEM] * SIDE,
        scratch_shapes=scratch,
        compiler_params=params(24),
        cost_estimate=cost(
            16 * 2 * rows * 512 * width, 2 * probs.size + 16 * depth * width + 32 * rows * width
        ),
        name="tile_products",
    )(place, pairs, count, probs, mine, other, *extra)


def pack_rows(lines):
    rows = [part for line in lines for part in thirds(line)]
    rows.append(jnp.zeros((16 - len(rows), rows[0].shape[1]), F32))
    return jnp.concatenate(rows, axis=0).astype(BF16)


def unpack_rows(packed, number):
    packed = packed.astype(F32)
    return [
        packed[3 * i : 3 * i + 1] + packed[3 * i + 1 : 3 * i + 2] + packed[3 * i + 2 : 3 * i + 3]
        for i in range(number)
    ]


def joined(stats):
    peak = functools.reduce(jnp.maximum, [line[0] for line in stats])
    speak = functools.reduce(jnp.maximum, [line[3] for line in stats])
    factors = [jnp.exp(line[0] - peak) for line in stats]
    mass = sum(line[1] * factor for line, factor in zip(stats, factors))
    total = sum(line[2] * factor for line, factor in zip(stats, factors))
    smass = sum(line[4] * jnp.exp(line[3] - speak) for line in stats)
    return (peak, mass, total, speak, smass), factors


def columns_of(lines):
    lines = list(lines) + [jnp.zeros((128 - len(lines), lines[0].shape[1]), F32)]
    return jnp.concatenate(lines, axis=0).T


def merge_kernel(with_stats, place, *refs):
    if with_stats:
        parts, outs, kept = refs[:SIDE], refs[SIDE : 2 * SIDE], refs[2 * SIDE]
        rows = outs[0].shape[0] - 16
        stats, factors = joined([unpack_rows(part[SIDE * rows :, :], 5) for part in parts])
        packed = pack_rows(stats)
        for out in outs:
            out[rows : rows + 16, :] = packed
        table = columns_of(factors)
        kept[...] = table
    else:
        table, parts, outs = refs[0][...], refs[1 : 1 + SIDE], refs[1 + SIDE :]
        rows = outs[0].shape[0]
    for step in range(SIDE):
        at = pl.ds(pl.multiple_of(lax.rem(place[1] + step, SIDE) * rows, rows), rows)
        value = table[:, 0:1] * parts[0][at, :].astype(F32)
        for d in range(1, SIDE):
            value += table[:, d : d + 1] * parts[d][at, :].astype(F32)
        outs[step][0:rows, :] = value.astype(BF16)


def merged(place, parts, rows, table=None):
    width = parts[0].shape[1]
    first = table is None
    outs = [jax.ShapeDtypeStruct((rows + (16 if first else 0), width), BF16)] * SIDE
    if first:
        outs = outs + [jax.ShapeDtypeStruct((rows, 128), F32)]
    return pl.pallas_call(
        functools.partial(merge_kernel, first),
        out_shape=outs,
        in_specs=[SMEM] + [VMEM] * (SIDE if first else 1 + SIDE),
        out_specs=[VMEM] * len(outs),
        compiler_params=params(),
        cost_estimate=cost(32 * rows * width, 40 * rows * width),
        name="merge_targets",
    )(place, *([] if first else [table]), *parts)


def gradient_kernel(offset, with_stats, place, logits, *refs):
    if with_stats:
        parts, grad, loss, kept = refs[:SIDE], refs[SIDE], refs[SIDE + 1], refs[SIDE + 2]
        rows = logits.shape[0]
        stats, factors = joined([unpack_rows(part[rows:, :], 5) for part in parts])
        _, mass, total, peak, smass = stats
        total = total / mass
        floored = jnp.maximum(total, 1.0)
        share = total / floored
        scales = [factor / mass / floored for factor in factors]
        table = columns_of(scales + [share / smass, peak, peak + jnp.log(smass)])
        kept[...] = table
    else:
        table, parts, grad, loss = refs[0][...], refs[1 : 1 + SIDE], refs[1 + SIDE], refs[2 + SIDE]
    rows, width = logits.shape[0], parts[0].shape[1]
    share, peak, norm = (table[:, c : c + 1] for c in range(4, 7))
    terms = jnp.zeros((rows, width), F32)
    for step in range(SIDE):
        block = lax.rem(place[1] + SIDE - step, SIDE)
        scores = logits[:, pl.ds(pl.multiple_of(block * 512 + offset, 128), width)]
        target = parts[step][0:rows, :].astype(F32) * table[:, step : step + 1]
        positive = target > 0
        entropy = jnp.where(positive, target * jnp.log(jnp.where(positive, target, 1.0)), 0.0)
        terms += entropy - target * (scores - norm)
        value = share * jnp.exp(scores - peak) - target
        grad[block] = value.T.astype(BF16)
    loss[...] = jnp.broadcast_to(jnp.sum(terms.T, axis=0, keepdims=True), loss.shape)


def gradients(offset, place, logits, parts, table=None):
    rows, width = logits.shape[0], parts[0].shape[1]
    first = table is None
    outs = [jax.ShapeDtypeStruct((SIDE, width, rows), BF16), jax.ShapeDtypeStruct((8, rows), F32)]
    if first:
        outs.append(jax.ShapeDtypeStruct((rows, 128), F32))
    return pl.pallas_call(
        functools.partial(gradient_kernel, offset, first),
        out_shape=outs,
        in_specs=[SMEM] + [VMEM] * (1 + SIDE if first else 2 + SIDE),
        out_specs=[VMEM] * len(outs),
        compiler_params=params(),
        cost_estimate=cost(60 * rows * width, 16 * rows * width + 4 * logits.size, 8 * rows * width),
        name="logit_grad",
    )(place, logits, *([] if first else [table]), *parts)


def early_kernel(*refs):
    unembed, grad, out = refs[:SIDE], refs[SIDE], refs[SIDE + 1]
    result = jnp.dot(unembed[0][...], grad[0], preferred_element_type=F32)
    for block in range(1, SIDE):
        result += jnp.dot(unembed[block][...], grad[block], preferred_element_type=F32)
    out[...] = result


def early_hidden(unembed, grad):
    depth, cols = unembed.shape
    _, width, rows = grad.shape
    per = cols // SIDE // width
    step = depth // 8
    views = [pl.BlockSpec((step, width), lambda i, at=per * b: (i, at)) for b in range(SIDE)]
    return pl.pallas_call(
        early_kernel,
        grid=(8,),
        out_shape=jax.ShapeDtypeStruct((depth, rows), F32),
        in_specs=views + [pl.BlockSpec(grad.shape, lambda i: (0, 0, 0))],
        out_specs=pl.BlockSpec((step, rows), lambda i: (i, 0)),
        compiler_params=params(48),
        cost_estimate=cost(2 * depth * SIDE * width * rows, 2 * depth * SIDE * width + 4 * depth * rows),
        name="early_hidden",
    )(*[unembed] * SIDE, grad)


def late_kernel(half, place, *refs):
    unembed, grad, early = refs[:SIDE], refs[SIDE], refs[SIDE + 1]
    if half == 0:
        losses, outs = refs[SIDE + 2 : SIDE + 4], refs[SIDE + 4 :]
    else:
        losses, outs = (), refs[SIDE + 2 :]
    index = pl.program_id(0)
    rows = grad.shape[2]
    result = early[...].reshape(512, rows)
    for block in range(SIDE):
        result += jnp.dot(
            unembed[block][...].reshape(512, -1), grad[block], preferred_element_type=F32
        )
    result = result.astype(BF16)
    for step in range(SIDE):

        @pl.when(index == step)
        def _():
            outs[step][0:512, :] = result

    if losses:

        @pl.when(index == 0)
        def _():
            packed = pack_rows([losses[0][0:1] + losses[1][0:1]])
            for out in outs:
                out[512:528, :] = packed


def late_hidden(half, place, unembed, grad, early, losses=()):
    depth, cols = unembed.shape
    _, width, rows = grad.shape
    per = cols // SIDE // width
    unembed = unembed.reshape(SIDE, SIDE, 2, 128, cols)
    early = early.reshape(SIDE, SIDE, 2, 128, rows)
    if half == 0:
        shape = lambda n: (1, SIDE, 1, 128, n)
        where = lambda i, p, at: (lax.rem(p[0] + i, SIDE), 0, 0, 0, at)
    else:
        shape = lambda n: (SIDE, 1, 1, 128, n)
        where = lambda i, p, at: (0, lax.rem(p[1] + i, SIDE), 1, 0, at)
    views = [
        pl.BlockSpec(shape(width), lambda i, p, at=per * b + per - 1: where(i, p, at))
        for b in range(SIDE)
    ]
    whole = lambda array: pl.BlockSpec(array.shape, lambda i, p: (0,) * len(array.shape))
    out = jax.ShapeDtypeStruct((512 + (16 if losses else 0), rows), BF16)
    return pl.pallas_call(
        functools.partial(late_kernel, half),
        grid_spec=pltpu.PrefetchScalarGridSpec(
            num_scalar_prefetch=1,
            grid=(SIDE,),
            in_specs=views
            + [whole(grad), pl.BlockSpec(shape(rows), lambda i, p: where(i, p, 0))]
            + [whole(v) for v in losses],
            out_specs=[whole(out)] * SIDE,
        ),
        out_shape=[out] * SIDE,
        compiler_params=params(48),
        cost_estimate=cost(depth * SIDE * width * rows, depth * SIDE * width + 3 * depth * rows),
        name="late_hidden",
    )(place, *[unembed] * SIDE, grad, early, *losses)


def packed_loss(place_index, parts, at, ordered):
    for step in range(SIDE):
        ordered[lax.rem(place_index + SIDE - step, SIDE)] = unpack_rows(parts[step][at : at + 16, :], 1)[0]
    return ((ordered[0] + ordered[1]) + ordered[2]) + ordered[3]


def middle_kernel(half, place, *refs):
    parts, outs = refs[:SIDE], refs[SIDE : 2 * SIDE]
    for step in range(SIDE):
        at = pl.ds(pl.multiple_of(lax.rem(place[1 - half] + step, SIDE) * 128, 128), 128)
        value = parts[0][at, :].astype(F32)
        for part in parts[1:]:
            value += part[at, :].astype(F32)
        outs[step][0:128, :] = value.astype(BF16)
    if half == 0:
        packed = pack_rows([packed_loss(place[0], parts, 512, refs[2 * SIDE])])
        for out in outs:
            out[128:144, :] = packed


def middle(half, place, parts):
    rows = parts[0].shape[1]
    return pl.pallas_call(
        functools.partial(middle_kernel, half),
        out_shape=[jax.ShapeDtypeStruct((128 if half else 144, rows), BF16)] * SIDE,
        in_specs=[SMEM] + [VMEM] * SIDE,
        out_specs=[VMEM] * SIDE,
        scratch_shapes=[] if half else [pltpu.VMEM((SIDE, 1, rows), F32)],
        compiler_params=params(),
        cost_estimate=cost(4 * 512 * rows, 10 * 512 * rows),
        name="merge_grads",
    )(place, *parts)


def last_kernel(place, *refs):
    first, second = refs[:SIDE], refs[SIDE : 2 * SIDE]
    grad, loss, ordered = refs[2 * SIDE :]
    loss[...] = jnp.broadcast_to(packed_loss(place[1], first, 128, ordered), loss.shape)
    top = first[0][0:128, :].astype(F32)
    low = second[0][...].astype(F32)
    for a, b in zip(first[1:], second[1:]):
        top += a[0:128, :].astype(F32)
        low += b[...].astype(F32)
    grad[:, 0:128] = top.T.astype(BF16)
    grad[:, 128:256] = low.T.astype(BF16)


def last(place, first, second):
    rows = first[0].shape[1]
    return pl.pallas_call(
        last_kernel,
        out_shape=[jax.ShapeDtypeStruct((rows, 256), BF16), jax.ShapeDtypeStruct((8, rows), F32)],
        in_specs=[SMEM] + [VMEM] * (2 * SIDE),
        out_specs=[VMEM, VMEM],
        scratch_shapes=[pltpu.VMEM((SIDE, 1, rows), F32)],
        compiler_params=params(),
        cost_estimate=cost(8 * 256 * rows, 20 * 256 * rows),
        name="last_sum",
    )(place, *first, *second)


def spread(parts, axis):
    return [parts[0]] + [send(parts[step], axis, step) for step in (1, 2, 3)]


def shards(teacher_logits, student_hidden, student_unembed, tile_weights, tile_pairs, tile_count):
    place = jnp.stack([lax.axis_index("vy"), lax.axis_index("vz"), lax.axis_index("tx"), lax.axis_index("tc")]).astype(jnp.int32)
    rows = teacher_logits.shape[0]
    teacher = teacher_logits.astype(F32)
    peak = jnp.max(teacher, axis=1)
    shifted = jnp.exp(teacher - peak[:, None])
    mass = jnp.sum(shifted, axis=1)
    probs = shifted.astype(BF16)

    logits = jnp.dot(student_hidden, student_unembed, preferred_element_type=F32)
    speak = jnp.max(logits, axis=1)
    smass = jnp.sum(jnp.exp(logits - speak[:, None]), axis=1)

    blank = jnp.zeros_like(peak)
    before = jnp.stack([peak, mass, blank, speak, smass, blank, blank, blank])

    width = tile_weights.shape[2] // 2
    piece = prepared(tile_weights, width)
    mine = packed_pieces(spread([piece] * SIDE, "tx"), [mass, smass])
    other = swap(mine)
    parts = products(place, tile_pairs, tile_count, probs, mine, other, before)

    piece = sliced(tile_weights, width, width, [mine])
    right, left = send(piece, "tx", 1), send(piece, "tx", 3)
    top, low = halves(right, left, [parts[0]])
    parts = spread(parts, "vy")
    pieces = [piece, right, send(top, "tx", 1), send(low, "tx", 3), left]
    mine = packed_pieces(pieces, [parts[1], parts[3]])
    later = products(place, tile_pairs, tile_count, probs, mine, swap(mine))

    *parts, factors = merged(place, parts, rows)
    early_grad, early_loss, table = gradients(0, place, logits, spread(parts, "vz"))
    early = early_hidden(student_unembed, early_grad)
    parts = merged(place, spread(later, "vy"), rows, factors)
    late_grad, late_loss = gradients(width, place, logits, spread(parts, "vz"), table)

    first = late_hidden(0, place, student_unembed, late_grad, early, (early_loss, late_loss))
    first = middle(0, place, spread(first, "vy"))
    second = late_hidden(1, place, student_unembed, late_grad, early)
    second = middle(1, place, spread(second, "vz"))
    grad_hidden, loss = last(place, spread(first, "vz"), spread(second, "vy"))
    return grad_hidden, loss[0]


def solution(mesh):
    grid = Mesh(mesh.devices.reshape(SIDE, SIDE, SIDE, 2), ("vy", "vz", "tx", "tc"))
    vocab, tokens = ("vy", "vz"), ("tx", "tc")
    return jax.shard_map(
        shards,
        mesh=grid,
        in_specs=(
            P(tokens, vocab),
            P(tokens, None),
            P(None, vocab),
            P(vocab, tokens, None),
            P(vocab, None),
            P(vocab),
        ),
        out_specs=(P(tokens, vocab), P(tokens)),
        check_vma=False,
    )
```

time: 194 us -> 162 us (0.84)
  the two profiles are of different devices: /device:TPU:0 before, /device:TPU:1 now
where the time goes in v3:
time: 162 us; the launch traced here: 160 us
  starting transfers between devices  59.9 us (37%)
  waiting for transfers between devices  42.9 us (26%)
  Pallas kernels  36.2 us (22%)
  matrix products  9.63 us (6%)
  other arithmetic  6.38 us (4%)
  local copies, waits for them, and re-layouts  3.71 us (2%)
    ppermute x31, starting transfers between devices, send(): lax.ppermute(value, axis, [(i, (i + step) % SIDE) for i in range(SIDE)])  57.2 us
    ppermute x31, waiting for transfers between devices, send(): lax.ppermute(value, axis, [(i, (i + step) % SIDE) for i in range(SIDE)])  41.7 us
    dot_general x1, matrix products, shards(): jnp.dot(student_hidden, student_unembed, preferred_element_type=F32)  9.63 us
    pallas_call x2, Pallas kernels, late_hidden(): pl.pallas_call(functools.partial(late_kernel, half), grid_spec=pltpu.Pref...  9.49 us
    pallas_call x1, Pallas kernels, early_hidden(): pl.pallas_call(early_kernel, grid=(8,), out_shape=jax.ShapeDtypeStruct((d...  7.32 us
    pallas_call x2, Pallas kernels, products(): pl.pallas_call(functools.partial(product_kernel, bool(extra)), out_shape=...  6.15 us
    pallas_call x2, Pallas kernels, packed_pieces(): pl.pallas_call(functools.partial(pack_kernel, len(parts)), out_shape=jax....  4.01 us
  transfers between devices with their start and end apart: 33, of which 14 were waited for; matrix products, arithmetic and copies ran while one was open for 10% of the time, Pallas kernels for 15%

profile of v3, /device:TPU:1, one launch (start us, length us, event | category | flops | bytes accessed | tf_op | source)
XLA Modules:
  0.0 160.2 jit_solution(15808853708233118081)
XLA Ops:
  4.5 2.5 %collective-permute-start.1 = (bf16[1088,256]{1,0:T(8,128)(2,1)S(1)}, bf16[1088,256]{1,0:T(8,128)(2,1)}, u32[]{:S(2)}, u32[]{:S(2)}) collective-permute-start(bf16[1088,256]{1,0:T(8,128)(2,1)S(1)} %prepare_weights.1.refs_0_), channel_id=1, source_target_pairs={{0,4},{2,6},{4,0},{6,2},{1,5},{3,7},{5,1},{7,3},{8,12},{10,14},{12... | collective-permute-start | bytes 1671176 | tf_op jit(solution)/shard_map/ppermute | solution.py:29
  8.1 9.6 %fusion.2 = (f32[256]{0:T(256)S(1)}, f32[256,2048]{1,0:T(8,128)}) fusion(bf16[256,4096]{1,0:T(8,128)(2,1)S(1)} %copy-done, bf16[4096,2048]{1,0:T(8,128)(2,1)} %refs_3_.1), kind=kOutput, calls=%fused_computation.5 | convolution fusion | flops 4295491584 | bytes 20972544 | tf_op jit(solution)/shard_map/dot_general | solution.py:488
  24.1 6.9 %collective-permute-done.1.refs_2_ = bf16[1088,256]{1,0:T(8,128)(2,1)} collective-permute-done((bf16[1088,256]{1,0:T(8,128)(2,1)S(1)}, bf16[1088,256]{1,0:T(8,128)(2,1)}, u32[]{:S(2)}, u32[]{:S(2)}) %collective-permute-start.1) | collective-permute-done | bytes 557088 | tf_op jit(solution)/shard_map/ppermute | solution.py:29
  31.0 2.8 %pack_weights.2.mine.refs_0_ = bf16[4352,256]{1,0:T(8,128)(2,1)} custom-call(bf16[1088,256]{1,0:T(8,128)(2,1)S(1)} %prepare_weights.1.refs_0_, bf16[1088,256]{1,0:T(8,128)(2,1)S(1)} %collective-permute-done.refs_1_, bf16[1088,256]{1,0:T(8,128)(2,1)} %collective-permute-done.1.refs_2_, bf16[1088,256]{1,0:T(8,128)(2,1)} %collective-permute-done.2.refs_3_, ...), custom_call_target="tpu_custom_call" | custom-call | bytes 4456448 | tf_op jit(solution)/shard_map/pack_weights/pallas_call | solution.py:99
  41.4 4.0 %tile_products.2 = (bf16[1040,256]{1,0:T(8,128)(2,1)S(1)}, bf16[1040,256]{1,0:T(8,128)(2,1)S(1)}, bf16[1040,256]{1,0:T(8,128)(2,1)S(1)}, bf16[1040,256]{1,0:T(8,128)(2,1)S(1)}) custom-call(s32[4]{0:T(128)S(1)} %pad_add_fusion.place, s32[16,2]{1,0:T(8,128)S(1)} %copy.8.pairs, s32[1]{0:T(128)S(6)} %copy.10.count, bf16[256,4096]{1,0:T(8,128)(2,1)S(1)} %copy-done.2, ...), custom_call_target="tpu_custom_call" | custom-call | flops 1073741824 | bytes 8650752 | tf_op jit(solution)/shard_map/tile_products/pallas_call | solution.py:197
  45.4 2.2 %collective-permute-start.4 = (bf16[1040,256]{1,0:T(8,128)(2,1)S(1)}, bf16[1040,256]{1,0:T(8,128)(2,1)S(1)}, u32[]{:S(2)}, u32[]{:S(2)}) collective-permute-start(bf16[1040,256]{1,0:T(8,128)(2,1)S(1)} %get-tuple-element.45), channel_id=1, source_target_pairs={{0,32},{32,64},{64,96},{96,0},{1,33},{33,65},{65,97},{97,1},{2,34}... | collective-permute-start | bytes 1597448 | tf_op jit(solution)/shard_map/ppermute | solution.py:29
  47.6 3.2 %collective-permute-start.6 = (bf16[1040,256]{1,0:T(8,128)(2,1)S(1)}, bf16[1040,256]{1,0:T(8,128)(2,1)S(1)}, u32[]{:S(2)}, u32[]{:S(2)}) collective-permute-start(bf16[1040,256]{1,0:T(8,128)(2,1)S(1)} %get-tuple-element.47), channel_id=1, source_target_pairs={{0,96},{32,0},{64,32},{96,64},{1,97},{33,1},{65,33},{97,65},{2,98}... | collective-permute-start | bytes 1597448 | tf_op jit(solution)/shard_map/ppermute | solution.py:29
  54.0 5.6 %collective-permute-done.12.refs_2_ = bf16[512,256]{1,0:T(8,128)(2,1)S(1)} collective-permute-done((bf16[512,256]{1,0:T(8,128)(2,1)S(1)}, bf16[512,256]{1,0:T(8,128)(2,1)S(1)}, u32[]{:S(2)}, u32[]{:S(2)}) %collective-permute-start.12) | collective-permute-done | bytes 262176 | tf_op jit(solution)/shard_map/ppermute | solution.py:29
  59.6 3.2 %collective-permute-done.4.refs_1_.refs_5_ = bf16[1040,256]{1,0:T(8,128)(2,1)S(1)} collective-permute-done((bf16[1040,256]{1,0:T(8,128)(2,1)S(1)}, bf16[1040,256]{1,0:T(8,128)(2,1)S(1)}, u32[]{:S(2)}, u32[]{:S(2)}) %collective-permute-start.4) | collective-permute-done | bytes 532512 | tf_op jit(solution)/shard_map/ppermute | solution.py:29
  65.1 2.7 %collective-permute-start.5 = (bf16[1040,256]{1,0:T(8,128)(2,1)S(1)}, bf16[1040,256]{1,0:T(8,128)(2,1)S(1)}, u32[]{:S(2)}, u32[]{:S(2)}) collective-permute-start(bf16[1040,256]{1,0:T(8,128)(2,1)S(1)} %get-tuple-element.46), channel_id=1, source_target_pairs={{0,64},{32,96},{64,0},{96,32},{1,65},{33,97},{65,1},{97,33},{2,66}... | collective-permute-start | bytes 1597448 | tf_op jit(solution)/shard_map/ppermute | solution.py:29
  72.7 4.4 %collective-permute-start.16 = (bf16[1024,256]{1,0:T(8,128)(2,1)S(1)}, bf16[1024,256]{1,0:T(8,128)(2,1)S(1)}, u32[]{:S(2)}, u32[]{:S(2)}) collective-permute-start(bf16[1024,256]{1,0:T(8,128)(2,1)S(1)} %get-tuple-element.58), channel_id=1, source_target_pairs={{0,64},{32,96},{64,0},{96,32},{1,65},{33,97},{65,1},{97,33},{2,66}... | collective-permute-start | bytes 1572872 | tf_op jit(solution)/shard_map/ppermute | solution.py:29
  77.1 3.2 %collective-permute-done.5.refs_2_ = bf16[1040,256]{1,0:T(8,128)(2,1)S(1)} collective-permute-done((bf16[1040,256]{1,0:T(8,128)(2,1)S(1)}, bf16[1040,256]{1,0:T(8,128)(2,1)S(1)}, u32[]{:S(2)}, u32[]{:S(2)}) %collective-permute-start.5) | collective-permute-done | bytes 532512 | tf_op jit(solution)/shard_map/ppermute | solution.py:29
  81.6 4.8 %collective-permute-start.8 = (bf16[272,256]{1,0:T(8,128)(2,1)S(1)}, bf16[272,256]{1,0:T(8,128)(2,1)S(1)}, u32[]{:S(2)}, u32[]{:S(2)}) collective-permute-start(bf16[272,256]{1,0:T(8,128)(2,1)S(1)} %get-tuple-element.50), channel_id=1, source_target_pairs={{0,16},{8,24},{16,0},{24,8},{1,17},{9,25},{17,1},{25,9},{2,18},{10... | collective-permute-start | bytes 417800 | tf_op jit(solution)/shard_map/ppermute | solution.py:29
  87.0 2.4 %collective-permute-start.9 = (bf16[272,256]{1,0:T(8,128)(2,1)S(1)}, bf16[272,256]{1,0:T(8,128)(2,1)S(1)}, u32[]{:S(2)}, u32[]{:S(2)}) collective-permute-start(bf16[272,256]{1,0:T(8,128)(2,1)S(1)} %get-tuple-element.51), channel_id=1, source_target_pairs={{0,24},{8,0},{16,8},{24,16},{1,25},{9,1},{17,9},{25,17},{2,26},{10... | collective-permute-start | bytes 417800 | tf_op jit(solution)/shard_map/ppermute | solution.py:29
  89.4 2.3 %collective-permute-done.8.refs_2_ = bf16[272,256]{1,0:T(8,128)(2,1)S(1)} collective-permute-done((bf16[272,256]{1,0:T(8,128)(2,1)S(1)}, bf16[272,256]{1,0:T(8,128)(2,1)S(1)}, u32[]{:S(2)}, u32[]{:S(2)}) %collective-permute-start.8) | collective-permute-done | bytes 139296 | tf_op jit(solution)/shard_map/ppermute | solution.py:29
  93.7 9.1 %collective-permute-done.16.refs_3_ = bf16[1024,256]{1,0:T(8,128)(2,1)S(1)} collective-permute-done((bf16[1024,256]{1,0:T(8,128)(2,1)S(1)}, bf16[1024,256]{1,0:T(8,128)(2,1)S(1)}, u32[]{:S(2)}, u32[]{:S(2)}) %collective-permute-start.16) | collective-permute-done | bytes 524320 | tf_op jit(solution)/shard_map/ppermute | solution.py:29
  104.3 4.8 %collective-permute-start.19 = (bf16[256,256]{1,0:T(8,128)(2,1)S(1)}, bf16[256,256]{1,0:T(8,128)(2,1)S(1)}, u32[]{:S(2)}, u32[]{:S(2)}) collective-permute-start(bf16[256,256]{1,0:T(8,128)(2,1)S(1)} %get-tuple-element.62), channel_id=1, source_target_pairs={{0,16},{8,24},{16,0},{24,8},{1,17},{9,25},{17,1},{25,9},{2,18},{10... | collective-permute-start | bytes 393224 | tf_op jit(solution)/shard_map/ppermute | solution.py:29
  111.1 7.3 %early_hidden.1 = f32[4096,256]{1,0:T(8,128)S(1)} custom-call(bf16[4096,2048]{1,0:T(8,128)(2,1)} %refs_3_.1, bf16[4096,2048]{1,0:T(8,128)(2,1)} %refs_3_.1, bf16[4096,2048]{1,0:T(8,128)(2,1)} %refs_3_.1, bf16[4096,2048]{1,0:T(8,128)(2,1)} %refs_3_.1, bf16[4,256,256]{2,1,0:T(8,128)(2,1)S(1)} %get-tuple-element.65.refs_4_), custom_call_target="tpu_custom_call" | custom-call | flops 2147483648 | bytes 12582912 | tf_op jit(solution)/shard_map/early_hidden/pallas_call | solution.py:338
  119.9 4.7 %late_hidden.3 = (bf16[512,256]{1,0:T(8,128)(2,1)S(1)}, bf16[512,256]{1,0:T(8,128)(2,1)S(1)}, bf16[512,256]{1,0:T(8,128)(2,1)S(1)}, bf16[512,256]{1,0:T(8,128)(2,1)S(1)}) custom-call(s32[4]{0:T(128)S(1)} %pad_add_fusion.place, bf16[4,4,2,128,2048]{4,3,2,1,0:T(8,128)(2,1)} %bitcast.17, bf16[4,4,2,128,2048]{4,3,2,1,0:T(8,128)(2,1)} %bitcast.18, ...), custom_call_target="tpu_custom_call" | custom-call | flops 1073741824 | bytes 7340032 | tf_op jit(solution)/shard_map/late_hidden/pallas_call | solution.py:397
  127.4 4.8 %late_hidden.2 = (bf16[528,256]{1,0:T(8,128)(2,1)S(1)}, bf16[528,256]{1,0:T(8,128)(2,1)S(1)}, bf16[528,256]{1,0:T(8,128)(2,1)S(1)}, bf16[528,256]{1,0:T(8,128)(2,1)S(1)}) custom-call(s32[4]{0:T(128)S(1)} %pad_add_fusion.place, bf16[4,4,2,128,2048]{4,3,2,1,0:T(8,128)(2,1)} %bitcast.21, bf16[4,4,2,128,2048]{4,3,2,1,0:T(8,128)(2,1)} %bitcast.22, ...), custom_call_target="tpu_custom_call" | custom-call | flops 1073741824 | bytes 7340032 | tf_op jit(solution)/shard_map/late_hidden/pallas_call | solution.py:397
  133.1 3.1 %collective-permute-start.22 = (bf16[528,256]{1,0:T(8,128)(2,1)S(1)}, bf16[528,256]{1,0:T(8,128)(2,1)S(1)}, u32[]{:S(2)}, u32[]{:S(2)}) collective-permute-start(bf16[528,256]{1,0:T(8,128)(2,1)S(1)} %get-tuple-element.70), channel_id=1, source_target_pairs={{0,64},{32,96},{64,0},{96,32},{1,65},{33,97},{65,1},{97,33},{2,66}... | collective-permute-start | bytes 811016 | tf_op jit(solution)/shard_map/ppermute | solution.py:29
  140.3 6.3 %collective-permute-done.22.refs_2_ = bf16[528,256]{1,0:T(8,128)(2,1)S(1)} collective-permute-done((bf16[528,256]{1,0:T(8,128)(2,1)S(1)}, bf16[528,256]{1,0:T(8,128)(2,1)S(1)}, u32[]{:S(2)}, u32[]{:S(2)}) %collective-permute-start.22) | collective-permute-done | bytes 270368 | tf_op jit(solution)/shard_map/ppermute | solution.py:29
  151.5 2.6 %collective-permute-start.31 = (bf16[128,256]{1,0:T(8,128)(2,1)S(1)}, bf16[128,256]{1,0:T(8,128)(2,1)S(1)}, u32[]{:S(2)}, u32[]{:S(2)}) collective-permute-start(bf16[128,256]{1,0:T(8,128)(2,1)S(1)} %get-tuple-element.82), channel_id=1, source_target_pairs={{0,64},{32,96},{64,0},{96,32},{1,65},{33,97},{65,1},{97,33},{2,66}... | collective-permute-start | bytes 196616 | tf_op jit(solution)/shard_map/ppermute | solution.py:29
  154.2 2.8 %collective-permute-start.32 = (bf16[128,256]{1,0:T(8,128)(2,1)S(1)}, bf16[128,256]{1,0:T(8,128)(2,1)S(1)}, u32[]{:S(2)}, u32[]{:S(2)}) collective-permute-start(bf16[128,256]{1,0:T(8,128)(2,1)S(1)} %get-tuple-element.83), channel_id=1, source_target_pairs={{0,96},{32,0},{64,32},{96,64},{1,97},{33,1},{65,33},{97,65},{2,98}... | collective-permute-start | bytes 196616 | tf_op jit(solution)/shard_map/ppermute | solution.py:29
  (86 shorter events, 53.3 us)
Async XLA Ops:
  2.4 21.7 %collective-permute-start = (bf16[1088,256]{1,0:T(8,128)(2,1)S(1)}, bf16[1088,256]{1,0:T(8,128)(2,1)S(1)}, u32[]{:S(2)}, u32[]{:S(2)}) collective-permute-start(bf16[1088,256]{1,0:T(8,128)(2,1)S(1)} %prepare_weights.1.refs_0_), channel_id=1, source_target_pairs={{0,2},{2,4},{4,6},{6,0},{1,3},{3,5},{5,7},{7,1},{8,10},{10,12},{12... | collective-permute-start | bytes 1671176 | tf_op jit(solution)/shard_map/ppermute | solution.py:29
  4.5 26.5 %collective-permute-start.1 = (bf16[1088,256]{1,0:T(8,128)(2,1)S(1)}, bf16[1088,256]{1,0:T(8,128)(2,1)}, u32[]{:S(2)}, u32[]{:S(2)}) collective-permute-start(bf16[1088,256]{1,0:T(8,128)(2,1)S(1)} %prepare_weights.1.refs_0_), channel_id=1, source_target_pairs={{0,4},{2,6},{4,0},{6,2},{1,5},{3,7},{5,1},{7,3},{8,12},{10,14},{12... | collective-permute-start | bytes 1671176 | tf_op jit(solution)/shard_map/ppermute | solution.py:29
  6.9 24.1 %collective-permute-start.2 = (bf16[1088,256]{1,0:T(8,128)(2,1)S(1)}, bf16[1088,256]{1,0:T(8,128)(2,1)}, u32[]{:S(2)}, u32[]{:S(2)}) collective-permute-start(bf16[1088,256]{1,0:T(8,128)(2,1)S(1)} %prepare_weights.1.refs_0_), channel_id=1, source_target_pairs={{0,6},{2,0},{4,2},{6,4},{1,7},{3,1},{5,3},{7,5},{8,14},{10,8},{12,... | collective-permute-start | bytes 1671176 | tf_op jit(solution)/shard_map/ppermute | solution.py:29
  36.2 15.0 %collective-permute-start.10 = (bf16[1024,256]{1,0:T(8,128)(2,1)}, bf16[1024,256]{1,0:T(8,128)(2,1)S(1)}, u32[]{:S(2)}, u32[]{:S(2)}) collective-permute-start(bf16[1024,256]{1,0:T(8,128)(2,1)} %slice_weights.1.refs_0_), channel_id=1, source_target_pairs={{0,2},{2,4},{4,6},{6,0},{1,3},{3,5},{5,7},{7,1},{8,10},{10,12},{12... | collective-permute-start | bytes 1572872 | tf_op jit(solution)/shard_map/ppermute | solution.py:29
  37.2 14.0 %collective-permute-start.11 = (bf16[1024,256]{1,0:T(8,128)(2,1)}, bf16[1024,256]{1,0:T(8,128)(2,1)S(1)}, u32[]{:S(2)}, u32[]{:S(2)}) collective-permute-start(bf16[1024,256]{1,0:T(8,128)(2,1)} %slice_weights.1.refs_0_), channel_id=1, source_target_pairs={{0,6},{2,0},{4,2},{6,4},{1,7},{3,1},{5,3},{7,5},{8,14},{10,8},{12,... | collective-permute-start | bytes 1572872 | tf_op jit(solution)/shard_map/ppermute | solution.py:29
  45.4 17.3 %collective-permute-start.4 = (bf16[1040,256]{1,0:T(8,128)(2,1)S(1)}, bf16[1040,256]{1,0:T(8,128)(2,1)S(1)}, u32[]{:S(2)}, u32[]{:S(2)}) collective-permute-start(bf16[1040,256]{1,0:T(8,128)(2,1)S(1)} %get-tuple-element.45), channel_id=1, source_target_pairs={{0,32},{32,64},{64,96},{96,0},{1,33},{33,65},{65,97},{97,1},{2,34}... | collective-permute-start | bytes 1597448 | tf_op jit(solution)/shard_map/ppermute | solution.py:29
  47.6 15.1 %collective-permute-start.6 = (bf16[1040,256]{1,0:T(8,128)(2,1)S(1)}, bf16[1040,256]{1,0:T(8,128)(2,1)S(1)}, u32[]{:S(2)}, u32[]{:S(2)}) collective-permute-start(bf16[1040,256]{1,0:T(8,128)(2,1)S(1)} %get-tuple-element.47), channel_id=1, source_target_pairs={{0,96},{32,0},{64,32},{96,64},{1,97},{33,1},{65,33},{97,65},{2,98}... | collective-permute-start | bytes 1597448 | tf_op jit(solution)/shard_map/ppermute | solution.py:29
  65.1 15.2 %collective-permute-start.5 = (bf16[1040,256]{1,0:T(8,128)(2,1)S(1)}, bf16[1040,256]{1,0:T(8,128)(2,1)S(1)}, u32[]{:S(2)}, u32[]{:S(2)}) collective-permute-start(bf16[1040,256]{1,0:T(8,128)(2,1)S(1)} %get-tuple-element.46), channel_id=1, source_target_pairs={{0,64},{32,96},{64,0},{96,32},{1,65},{33,97},{65,1},{97,33},{2,66}... | collective-permute-start | bytes 1597448 | tf_op jit(solution)/shard_map/ppermute | solution.py:29
  71.0 22.6 %collective-permute-start.15 = (bf16[1024,256]{1,0:T(8,128)(2,1)S(1)}, bf16[1024,256]{1,0:T(8,128)(2,1)S(1)}, u32[]{:S(2)}, u32[]{:S(2)}) collective-permute-start(bf16[1024,256]{1,0:T(8,128)(2,1)S(1)} %get-tuple-element.57), channel_id=1, source_target_pairs={{0,32},{32,64},{64,96},{96,0},{1,33},{33,65},{65,97},{97,1},{2,34}... | collective-permute-start | bytes 1572872 | tf_op jit(solution)/shard_map/ppermute | solution.py:29
  72.7 30.1 %collective-permute-start.16 = (bf16[1024,256]{1,0:T(8,128)(2,1)S(1)}, bf16[1024,256]{1,0:T(8,128)(2,1)S(1)}, u32[]{:S(2)}, u32[]{:S(2)}) collective-permute-start(bf16[1024,256]{1,0:T(8,128)(2,1)S(1)} %get-tuple-element.58), channel_id=1, source_target_pairs={{0,64},{32,96},{64,0},{96,32},{1,65},{33,97},{65,1},{97,33},{2,66}... | collective-permute-start | bytes 1572872 | tf_op jit(solution)/shard_map/ppermute | solution.py:29
  77.1 26.1 %collective-permute-start.17 = (bf16[1024,256]{1,0:T(8,128)(2,1)S(1)}, bf16[1024,256]{1,0:T(8,128)(2,1)S(1)}, u32[]{:S(2)}, u32[]{:S(2)}) collective-permute-start(bf16[1024,256]{1,0:T(8,128)(2,1)S(1)} %get-tuple-element.59), channel_id=1, source_target_pairs={{0,96},{32,0},{64,32},{96,64},{1,97},{33,1},{65,33},{97,65},{2,98}... | collective-permute-start | bytes 1572872 | tf_op jit(solution)/shard_map/ppermute | solution.py:29
  81.6 10.1 %collective-permute-start.8 = (bf16[272,256]{1,0:T(8,128)(2,1)S(1)}, bf16[272,256]{1,0:T(8,128)(2,1)S(1)}, u32[]{:S(2)}, u32[]{:S(2)}) collective-permute-start(bf16[272,256]{1,0:T(8,128)(2,1)S(1)} %get-tuple-element.50), channel_id=1, source_target_pairs={{0,16},{8,24},{16,0},{24,8},{1,17},{9,25},{17,1},{25,9},{2,18},{10... | collective-permute-start | bytes 417800 | tf_op jit(solution)/shard_map/ppermute | solution.py:29
  104.2 14.2 %collective-permute-start.18 = (bf16[256,256]{1,0:T(8,128)(2,1)S(1)}, bf16[256,256]{1,0:T(8,128)(2,1)S(1)}, u32[]{:S(2)}, u32[]{:S(2)}) collective-permute-start(bf16[256,256]{1,0:T(8,128)(2,1)S(1)} %get-tuple-element.61), channel_id=1, source_target_pairs={{0,8},{8,16},{16,24},{24,0},{1,9},{9,17},{17,25},{25,1},{2,10},{10... | collective-permute-start | bytes 393224 | tf_op jit(solution)/shard_map/ppermute | solution.py:29
  104.3 14.1 %collective-permute-start.19 = (bf16[256,256]{1,0:T(8,128)(2,1)S(1)}, bf16[256,256]{1,0:T(8,128)(2,1)S(1)}, u32[]{:S(2)}, u32[]{:S(2)}) collective-permute-start(bf16[256,256]{1,0:T(8,128)(2,1)S(1)} %get-tuple-element.62), channel_id=1, source_target_pairs={{0,16},{8,24},{16,0},{24,8},{1,17},{9,25},{17,1},{25,9},{2,18},{10... | collective-permute-start | bytes 393224 | tf_op jit(solution)/shard_map/ppermute | solution.py:29
  109.1 9.3 %collective-permute-start.20 = (bf16[256,256]{1,0:T(8,128)(2,1)S(1)}, bf16[256,256]{1,0:T(8,128)(2,1)S(1)}, u32[]{:S(2)}, u32[]{:S(2)}) collective-permute-start(bf16[256,256]{1,0:T(8,128)(2,1)S(1)} %get-tuple-element.63), channel_id=1, source_target_pairs={{0,24},{8,0},{16,8},{24,16},{1,25},{9,1},{17,9},{25,17},{2,26},{10... | collective-permute-start | bytes 393224 | tf_op jit(solution)/shard_map/ppermute | solution.py:29
  124.7 11.5 %collective-permute-start.27 = (bf16[512,256]{1,0:T(8,128)(2,1)S(1)}, bf16[512,256]{1,0:T(8,128)(2,1)S(1)}, u32[]{:S(2)}, u32[]{:S(2)}) collective-permute-start(bf16[512,256]{1,0:T(8,128)(2,1)S(1)} %get-tuple-element.77), channel_id=1, source_target_pairs={{0,8},{8,16},{16,24},{24,0},{1,9},{9,17},{17,25},{25,1},{2,10},{10... | collective-permute-start | bytes 786440 | tf_op jit(solution)/shard_map/ppermute | solution.py:29
  124.8 11.9 %collective-permute-start.28 = (bf16[512,256]{1,0:T(8,128)(2,1)S(1)}, bf16[512,256]{1,0:T(8,128)(2,1)S(1)}, u32[]{:S(2)}, u32[]{:S(2)}) collective-permute-start(bf16[512,256]{1,0:T(8,128)(2,1)S(1)} %get-tuple-element.78), channel_id=1, source_target_pairs={{0,16},{8,24},{16,0},{24,8},{1,17},{9,25},{17,1},{25,9},{2,18},{10... | collective-permute-start | bytes 786440 | tf_op jit(solution)/shard_map/ppermute | solution.py:29
  125.9 12.8 %collective-permute-start.29 = (bf16[512,256]{1,0:T(8,128)(2,1)S(1)}, bf16[512,256]{1,0:T(8,128)(2,1)S(1)}, u32[]{:S(2)}, u32[]{:S(2)}) collective-permute-start(bf16[512,256]{1,0:T(8,128)(2,1)S(1)} %get-tuple-element.79), channel_id=1, source_target_pairs={{0,24},{8,0},{16,8},{24,16},{1,25},{9,1},{17,9},{25,17},{2,26},{10... | collective-permute-start | bytes 786440 | tf_op jit(solution)/shard_map/ppermute | solution.py:29
  133.1 13.5 %collective-permute-start.22 = (bf16[528,256]{1,0:T(8,128)(2,1)S(1)}, bf16[528,256]{1,0:T(8,128)(2,1)S(1)}, u32[]{:S(2)}, u32[]{:S(2)}) collective-permute-start(bf16[528,256]{1,0:T(8,128)(2,1)S(1)} %get-tuple-element.70), channel_id=1, source_target_pairs={{0,64},{32,96},{64,0},{96,32},{1,65},{33,97},{65,1},{97,33},{2,66}... | collective-permute-start | bytes 811016 | tf_op jit(solution)/shard_map/ppermute | solution.py:29
  136.2 10.4 %collective-permute-start.23 = (bf16[528,256]{1,0:T(8,128)(2,1)S(1)}, bf16[528,256]{1,0:T(8,128)(2,1)S(1)}, u32[]{:S(2)}, u32[]{:S(2)}) collective-permute-start(bf16[528,256]{1,0:T(8,128)(2,1)S(1)} %get-tuple-element.71), channel_id=1, source_target_pairs={{0,96},{32,0},{64,32},{96,64},{1,97},{33,1},{65,33},{97,65},{2,98}... | collective-permute-start | bytes 811016 | tf_op jit(solution)/shard_map/ppermute | solution.py:29
  139.4 14.8 %collective-permute-start.30 = (bf16[128,256]{1,0:T(8,128)(2,1)S(1)}, bf16[128,256]{1,0:T(8,128)(2,1)S(1)}, u32[]{:S(2)}, u32[]{:S(2)}) collective-permute-start(bf16[128,256]{1,0:T(8,128)(2,1)S(1)} %get-tuple-element.81), channel_id=1, source_target_pairs={{0,32},{32,64},{64,96},{96,0},{1,33},{33,65},{65,97},{97,1},{2,34}... | collective-permute-start | bytes 196616 | tf_op jit(solution)/shard_map/ppermute | solution.py:29
  147.3 11.0 %collective-permute-start.24 = (bf16[144,256]{1,0:T(8,128)(2,1)S(1)}, bf16[144,256]{1,0:T(8,128)(2,1)S(1)}, u32[]{:S(2)}, u32[]{:S(2)}) collective-permute-start(bf16[144,256]{1,0:T(8,128)(2,1)S(1)} %get-tuple-element.73), channel_id=1, source_target_pairs={{0,8},{8,16},{16,24},{24,0},{1,9},{9,17},{17,25},{25,1},{2,10},{10... | collective-permute-start | bytes 221192 | tf_op jit(solution)/shard_map/ppermute | solution.py:29
  148.0 10.4 %collective-permute-start.25 = (bf16[144,256]{1,0:T(8,128)(2,1)S(1)}, bf16[144,256]{1,0:T(8,128)(2,1)S(1)}, u32[]{:S(2)}, u32[]{:S(2)}) collective-permute-start(bf16[144,256]{1,0:T(8,128)(2,1)S(1)} %get-tuple-element.74), channel_id=1, source_target_pairs={{0,16},{8,24},{16,0},{24,8},{1,17},{9,25},{17,1},{25,9},{2,18},{10... | collective-permute-start | bytes 221192 | tf_op jit(solution)/shard_map/ppermute | solution.py:29
  149.5 8.8 %collective-permute-start.26 = (bf16[144,256]{1,0:T(8,128)(2,1)S(1)}, bf16[144,256]{1,0:T(8,128)(2,1)S(1)}, u32[]{:S(2)}, u32[]{:S(2)}) collective-permute-start(bf16[144,256]{1,0:T(8,128)(2,1)S(1)} %get-tuple-element.75), channel_id=1, source_target_pairs={{0,24},{8,0},{16,8},{24,16},{1,25},{9,1},{17,9},{25,17},{2,26},{10... | collective-permute-start | bytes 221192 | tf_op jit(solution)/shard_map/ppermute | solution.py:29
  (17 other events, 115.1 us)

commit v4 on v3

--- a/solution.py
+++ b/solution.py
@@ -239,7 +239,7 @@
 
 def merge_kernel(with_stats, place, *refs):
     if with_stats:
-        parts, outs, kept = refs[:SIDE], refs[SIDE : 2 * SIDE], refs[2 * SIDE]
+        parts, outs, kept = refs[:SIDE], refs[-1 - SIDE : -1], refs[-1]
         rows = outs[0].shape[0] - 16
         stats, factors = joined([unpack_rows(part[SIDE * rows :, :], 5) for part in parts])
         packed = pack_rows(stats)
@@ -248,7 +248,7 @@
         table = columns_of(factors)
         kept[...] = table
     else:
-        table, parts, outs = refs[0][...], refs[1 : 1 + SIDE], refs[1 + SIDE :]
+        table, parts, outs = refs[0][...], refs[1 : 1 + SIDE], refs[-SIDE:]
         rows = outs[0].shape[0]
     for step in range(SIDE):
         at = pl.ds(pl.multiple_of(lax.rem(place[1] + step, SIDE) * rows, rows), rows)
@@ -258,7 +258,7 @@
         outs[step][0:rows, :] = value.astype(BF16)
 
 
-def merged(place, parts, rows, table=None):
+def merged(place, parts, rows, table=None, behind=()):
     width = parts[0].shape[1]
     first = table is None
     outs = [jax.ShapeDtypeStruct((rows + (16 if first else 0), width), BF16)] * SIDE
@@ -267,17 +267,17 @@
     return pl.pallas_call(
         functools.partial(merge_kernel, first),
         out_shape=outs,
-        in_specs=[SMEM] + [VMEM] * (SIDE if first else 1 + SIDE),
+        in_specs=[SMEM] + [VMEM] * (SIDE if first else 1 + SIDE) + [ANY] * len(behind),
         out_specs=[VMEM] * len(outs),
         compiler_params=params(),
-        cost_estimate=cost(32 * rows * width, 40 * rows * width),
+        cost_estimate=cost(rows * width, rows * width),
         name="merge_targets",
-    )(place, *([] if first else [table]), *parts)
+    )(place, *([] if first else [table]), *parts, *behind)
 
 
 def gradient_kernel(offset, with_stats, place, logits, *refs):
     if with_stats:
-        parts, grad, loss, kept = refs[:SIDE], refs[SIDE], refs[SIDE + 1], refs[SIDE + 2]
+        parts, (grad, loss, kept) = refs[:SIDE], refs[-3:]
         rows = logits.shape[0]
         stats, factors = joined([unpack_rows(part[rows:, :], 5) for part in parts])
         _, mass, total, peak, smass = stats
@@ -288,7 +288,7 @@
         table = columns_of(scales + [share / smass, peak, peak + jnp.log(smass)])
         kept[...] = table
     else:
-        table, parts, grad, loss = refs[0][...], refs[1 : 1 + SIDE], refs[1 + SIDE], refs[2 + SIDE]
+        table, loss, parts, grad = refs[0][...], refs[1], refs[2 : 2 + SIDE], refs[-1]
     rows, width = logits.shape[0], parts[0].shape[1]
     share, peak, norm = (table[:, c : c + 1] for c in range(4, 7))
     terms = jnp.zeros((rows, width), F32)
@@ -300,184 +300,226 @@
         entropy = jnp.where(positive, target * jnp.log(jnp.where(positive, target, 1.0)), 0.0)
         terms += entropy - target * (scores - norm)
         value = share * jnp.exp(scores - peak) - target
-        grad[block] = value.T.astype(BF16)
-    loss[...] = jnp.broadcast_to(jnp.sum(terms.T, axis=0, keepdims=True), loss.shape)
-
-
-def gradients(offset, place, logits, parts, table=None):
+        at = pl.ds(pl.multiple_of(block * width, width), width)
+        grad[at, :] = value.T.astype(BF16)
+    sum_of_terms = jnp.sum(terms.T, axis=0, keepdims=True)
+    if with_stats:
+        loss[...] = jnp.broadcast_to(sum_of_terms, loss.shape)
+    else:
+        grad[SIDE * width :, :] = pack_rows([sum_of_terms + loss[0:1]])
+
+
+def gradients(offset, place, logits, parts, before=(), behind=()):
     rows, width = logits.shape[0], parts[0].shape[1]
-    first = table is None
-    outs = [jax.ShapeDtypeStruct((SIDE, width, rows), BF16), jax.ShapeDtypeStruct((8, rows), F32)]
+    first = not before
+    outs = [jax.ShapeDtypeStruct((SIDE * width + (0 if first else 16), rows), BF16)]
     if first:
+        outs.append(jax.ShapeDtypeStruct((8, rows), F32))
         outs.append(jax.ShapeDtypeStruct((rows, 128), F32))
     return pl.pallas_call(
         functools.partial(gradient_kernel, offset, first),
         out_shape=outs,
-        in_specs=[SMEM] + [VMEM] * (1 + SIDE if first else 2 + SIDE),
+        in_specs=[SMEM] + [VMEM] * (1 + SIDE + len(before)) + [ANY] * len(behind),
         out_specs=[VMEM] * len(outs),
         compiler_params=params(),
-        cost_estimate=cost(60 * rows * width, 16 * rows * width + 4 * logits.size, 8 * rows * width),
+        cost_estimate=cost(rows * width, rows * width),
         name="logit_grad",
-    )(place, logits, *([] if first else [table]), *parts)
-
-
-def early_kernel(*refs):
-    unembed, grad, out = refs[:SIDE], refs[SIDE], refs[SIDE + 1]
-    result = jnp.dot(unembed[0][...], grad[0], preferred_element_type=F32)
-    for block in range(1, SIDE):
-        result += jnp.dot(unembed[block][...], grad[block], preferred_element_type=F32)
-    out[...] = result
-
-
-def early_hidden(unembed, grad):
+    )(place, logits, *before, *parts, *behind)
+
+
+def both_cores(core, mine, other, depth, out):
+    rows = mine.shape[1]
+    out[:, pl.ds(pl.multiple_of(core * rows, rows), rows)] = mine[0:depth, :]
+    out[:, pl.ds(pl.multiple_of((1 - core) * rows, rows), rows)] = other[0:depth, :]
+
+
+def early_kernel(place, *refs):
+    unembed = refs[:SIDE]
+    mine, other, out, stage, both = refs[SIDE:]
+    depth = both.shape[0]
+    width = depth // SIDE
+
+    @pl.when(pl.program_id(0) == 0)
+    def _():
+        both_cores(place[3], mine, other, depth, both)
+
+    for owner in range(SIDE):
+        rows = slice(owner * 128, owner * 128 + 128)
+        block = unembed[owner][...].reshape(128, 2 * depth)
+        now = [block[:, 2 * width * b : 2 * width * b + width] for b in range(SIDE)]
+        later = [block[:, 2 * width * b + width : 2 * width * (b + 1)] for b in range(SIDE)]
+        stage[rows, :] = jnp.concatenate(later, axis=1)
+        out[rows, :] = jnp.dot(jnp.concatenate(now, axis=1), both[...], preferred_element_type=F32)
+
+
+def early_hidden(place, unembed, mine, other):
     depth, cols = unembed.shape
-    _, width, rows = grad.shape
-    per = cols // SIDE // width
-    step = depth // 8
-    views = [pl.BlockSpec((step, width), lambda i, at=per * b: (i, at)) for b in range(SIDE)]
+    width, rows = mine.shape
+    unembed = unembed.reshape(SIDE, SIDE, 2, 128, cols)
+
+    def where(i, p, k):
+        first = p[3] == 0
+        return (jnp.where(first, i, k), jnp.where(first, k, i), p[3], 0, 0)
+
+    views = [
+        pl.BlockSpec((1, 1, 1, 128, cols), lambda i, p, k=k: where(i, p, k)) for k in range(SIDE)
+    ]
+    whole = pl.BlockSpec((width, rows), lambda i, p: (0, 0))
+    outs = [
+        jax.ShapeDtypeStruct((depth // 2, 2 * rows), F32),
+        jax.ShapeDtypeStruct((depth // 2, width), BF16),
+    ]
     return pl.pallas_call(
         early_kernel,
-        grid=(8,),
-        out_shape=jax.ShapeDtypeStruct((depth, rows), F32),
-        in_specs=views + [pl.BlockSpec(grad.shape, lambda i: (0, 0, 0))],
-        out_specs=pl.BlockSpec((step, rows), lambda i: (i, 0)),
-        compiler_params=params(48),
-        cost_estimate=cost(2 * depth * SIDE * width * rows, 2 * depth * SIDE * width + 4 * depth * rows),
-        name="early_hidden",
-    )(*[unembed] * SIDE, grad)
-
-
-def late_kernel(half, place, *refs):
-    unembed, grad, early = refs[:SIDE], refs[SIDE], refs[SIDE + 1]
-    if half == 0:
-        losses, outs = refs[SIDE + 2 : SIDE + 4], refs[SIDE + 4 :]
-    else:
-        losses, outs = (), refs[SIDE + 2 :]
-    index = pl.program_id(0)
-    rows = grad.shape[2]
-    result = early[...].reshape(512, rows)
-    for block in range(SIDE):
-        result += jnp.dot(
-            unembed[block][...].reshape(512, -1), grad[block], preferred_element_type=F32
-        )
-    result = result.astype(BF16)
-    for step in range(SIDE):
-
-        @pl.when(index == step)
-        def _():
-            outs[step][0:512, :] = result
-
-    if losses:
-
-        @pl.when(index == 0)
-        def _():
-            packed = pack_rows([losses[0][0:1] + losses[1][0:1]])
-            for out in outs:
-                out[512:528, :] = packed
-
-
-def late_hidden(half, place, unembed, grad, early, losses=()):
-    depth, cols = unembed.shape
-    _, width, rows = grad.shape
-    per = cols // SIDE // width
-    unembed = unembed.reshape(SIDE, SIDE, 2, 128, cols)
-    early = early.reshape(SIDE, SIDE, 2, 128, rows)
-    if half == 0:
-        shape = lambda n: (1, SIDE, 1, 128, n)
-        where = lambda i, p, at: (lax.rem(p[0] + i, SIDE), 0, 0, 0, at)
-    else:
-        shape = lambda n: (SIDE, 1, 1, 128, n)
-        where = lambda i, p, at: (0, lax.rem(p[1] + i, SIDE), 1, 0, at)
-    views = [
-        pl.BlockSpec(shape(width), lambda i, p, at=per * b + per - 1: where(i, p, at))
-        for b in range(SIDE)
-    ]
-    whole = lambda array: pl.BlockSpec(array.shape, lambda i, p: (0,) * len(array.shape))
-    out = jax.ShapeDtypeStruct((512 + (16 if losses else 0), rows), BF16)
-    return pl.pallas_call(
-        functools.partial(late_kernel, half),
         grid_spec=pltpu.PrefetchScalarGridSpec(
             num_scalar_prefetch=1,
             grid=(SIDE,),
-            in_specs=views
-            + [whole(grad), pl.BlockSpec(shape(rows), lambda i, p: where(i, p, 0))]
-            + [whole(v) for v in losses],
-            out_specs=[whole(out)] * SIDE,
+            in_specs=views + [whole, whole],
+            out_specs=[pl.BlockSpec((512, v.shape[1]), lambda i, p: (i, 0)) for v in outs],
+            scratch_shapes=[pltpu.VMEM((width, 2 * rows), BF16)],
         ),
-        out_shape=[out] * SIDE,
-        compiler_params=params(48),
-        cost_estimate=cost(depth * SIDE * width * rows, depth * SIDE * width + 3 * depth * rows),
+        out_shape=outs,
+        compiler_params=params(24),
+        cost_estimate=cost(2 * depth * width * rows, depth * cols + 6 * depth * rows),
+        name="early_hidden",
+    )(place, *[unembed] * SIDE, mine, other)
+
+
+def late_kernel(place, stage, mine, other, early, *refs):
+    outs, both = refs[:SIDE], refs[SIDE]
+    depth = both.shape[0]
+    rows = mine.shape[1]
+    both_cores(place[3], mine, other, depth, both)
+    for step in range(SIDE):
+        at = pl.ds(pl.multiple_of(lax.rem(place[4] + step, SIDE) * 512, 512), 512)
+        result = early[at, :] + jnp.dot(stage[at, :], both[...], preferred_element_type=F32)
+        outs[step][0:512, :] = result.astype(BF16)
+        for part, core in ((mine, place[3]), (other, 1 - place[3])):
+            lanes = pl.ds(pl.multiple_of(core * rows, rows), rows)
+            outs[step][512:528, lanes] = part[depth : depth + 16, :]
+
+
+def late_hidden(place, stage, mine, other, early):
+    width = stage.shape[1]
+    rows = early.shape[1]
+    return pl.pallas_call(
+        late_kernel,
+        out_shape=[jax.ShapeDtypeStruct((528, rows), BF16)] * SIDE,
+        in_specs=[SMEM] + [VMEM] * 4,
+        out_specs=[VMEM] * SIDE,
+        scratch_shapes=[pltpu.VMEM((width, rows), BF16)],
+        compiler_params=params(24),
+        cost_estimate=cost(4096 * width * rows, 4096 * width + 6 * 2048 * rows),
         name="late_hidden",
-    )(place, *[unembed] * SIDE, grad, early, *losses)
-
-
-def packed_loss(place_index, parts, at, ordered):
-    for step in range(SIDE):
-        ordered[lax.rem(place_index + SIDE - step, SIDE)] = unpack_rows(parts[step][at : at + 16, :], 1)[0]
+    )(place, stage, mine, other, early)
+
+
+def packed_loss(index, parts, at, ordered):
+    for step in range(SIDE):
+        ordered[lax.rem(index + SIDE - step, SIDE)] = unpack_rows(parts[step][at : at + 16, :], 1)[0]
     return ((ordered[0] + ordered[1]) + ordered[2]) + ordered[3]
 
 
-def middle_kernel(half, place, *refs):
-    parts, outs = refs[:SIDE], refs[SIDE : 2 * SIDE]
-    for step in range(SIDE):
-        at = pl.ds(pl.multiple_of(lax.rem(place[1 - half] + step, SIDE) * 128, 128), 128)
+def middle_kernel(place, *refs):
+    parts, outs, ordered = refs[:SIDE], refs[SIDE : 2 * SIDE], refs[2 * SIDE]
+    packed = pack_rows([packed_loss(place[4], parts, 512, ordered)])
+    for step in range(SIDE):
+        at = pl.ds(pl.multiple_of(lax.rem(place[5] + step, SIDE) * 128, 128), 128)
         value = parts[0][at, :].astype(F32)
         for part in parts[1:]:
             value += part[at, :].astype(F32)
         outs[step][0:128, :] = value.astype(BF16)
-    if half == 0:
-        packed = pack_rows([packed_loss(place[0], parts, 512, refs[2 * SIDE])])
-        for out in outs:
-            out[128:144, :] = packed
-
-
-def middle(half, place, parts):
+        outs[step][128:144, :] = packed
+
+
+def middle(place, parts):
     rows = parts[0].shape[1]
     return pl.pallas_call(
-        functools.partial(middle_kernel, half),
-        out_shape=[jax.ShapeDtypeStruct((128 if half else 144, rows), BF16)] * SIDE,
+        middle_kernel,
+        out_shape=[jax.ShapeDtypeStruct((144, rows), BF16)] * SIDE,
         in_specs=[SMEM] + [VMEM] * SIDE,
         out_specs=[VMEM] * SIDE,
-        scratch_shapes=[] if half else [pltpu.VMEM((SIDE, 1, rows), F32)],
+        scratch_shapes=[pltpu.VMEM((SIDE, 1, rows), F32)],
         compiler_params=params(),
         cost_estimate=cost(4 * 512 * rows, 10 * 512 * rows),
         name="merge_grads",
     )(place, *parts)
 
 
-def last_kernel(place, *refs):
-    first, second = refs[:SIDE], refs[SIDE : 2 * SIDE]
-    grad, loss, ordered = refs[2 * SIDE :]
-    loss[...] = jnp.broadcast_to(packed_loss(place[1], first, 128, ordered), loss.shape)
-    top = first[0][0:128, :].astype(F32)
-    low = second[0][...].astype(F32)
-    for a, b in zip(first[1:], second[1:]):
-        top += a[0:128, :].astype(F32)
-        low += b[...].astype(F32)
-    grad[:, 0:128] = top.T.astype(BF16)
-    grad[:, 128:256] = low.T.astype(BF16)
-
-
-def last(place, first, second):
-    rows = first[0].shape[1]
-    return pl.pallas_call(
-        last_kernel,
-        out_shape=[jax.ShapeDtypeStruct((rows, 256), BF16), jax.ShapeDtypeStruct((8, rows), F32)],
-        in_specs=[SMEM] + [VMEM] * (2 * SIDE),
-        out_specs=[VMEM, VMEM],
-        scratch_shapes=[pltpu.VMEM((SIDE, 1, rows), F32)],
-        compiler_params=params(),
-        cost_estimate=cost(8 * 256 * rows, 20 * 256 * rows),
-        name="last_sum",
-    )(place, *first, *second)
+def total_kernel(place, *refs):
+    parts = refs[:SIDE]
+    keep, give, loss, ordered = refs[SIDE:]
+    rows = keep.shape[1]
+    mine = pl.ds(pl.multiple_of(place[3] * rows, rows), rows)
+    other = pl.ds(pl.multiple_of((1 - place[3]) * rows, rows), rows)
+    ordered[4] = packed_loss(place[5], parts, 128, ordered)
+    loss[...] = jnp.broadcast_to(ordered[4, :, mine], loss.shape)
+    for lanes, out in ((other, give), (mine, keep)):
+        value = parts[0][0:128, lanes].astype(F32)
+        for part in parts[1:]:
+            value += part[0:128, lanes].astype(F32)
+        out[...] = value.astype(BF16)
+
+
+def totals(place, parts):
+    rows = parts[0].shape[1] // 2
+    half = jax.ShapeDtypeStruct((128, rows), BF16)
+    return pl.pallas_call(
+        total_kernel,
+        out_shape=[half, half, jax.ShapeDtypeStruct((8, rows), F32)],
+        in_specs=[SMEM] + [VMEM] * SIDE,
+        out_specs=[VMEM] * 3,
+        scratch_shapes=[pltpu.VMEM((SIDE + 1, 1, 2 * rows), F32)],
+        compiler_params=params(),
+        cost_estimate=cost(8 * 128 * rows, 20 * 128 * rows),
+        name="sum_grads",
+    )(place, *parts)
+
+
+def turn_kernel(place, keep, given, grad):
+    mine = pl.ds(pl.multiple_of(place[3] * 128, 128), 128)
+    other = pl.ds(pl.multiple_of((1 - place[3]) * 128, 128), 128)
+    grad[:, mine] = keep[...].astype(F32).T.astype(BF16)
+    grad[:, other] = given[...].astype(F32).T.astype(BF16)
+
+
+def turned(place, keep, given):
+    rows = keep.shape[1]
+    return pl.pallas_call(
+        turn_kernel,
+        out_shape=jax.ShapeDtypeStruct((rows, 256), BF16),
+        in_specs=[SMEM, VMEM, VMEM],
+        out_specs=VMEM,
+        compiler_params=params(),
+        cost_estimate=cost(0, 4 * 256 * rows),
+        name="turn_grads",
+    )(place, keep, given)
 
 
 def spread(parts, axis):
     return [parts[0]] + [send(parts[step], axis, step) for step in (1, 2, 3)]
 
 
+def crossed(parts, first):
+    def target(y, z, core, step):
+        if (core == 0) == first:
+            y = (y + step) % SIDE
+        else:
+            z = (z + step) % SIDE
+        return (y * SIDE + z) * 2 + core
+
+    places = [(y, z, core) for y in range(SIDE) for z in range(SIDE) for core in range(2)]
+    received = [parts[0]]
+    for step in (1, 2, 3):
+        pairs = [(i, target(*at, step)) for i, at in enumerate(places)]
+        received.append(lax.ppermute(parts[step], ("vy", "vz", "tc"), pairs))
+    return received
+
+
 def shards(teacher_logits, student_hidden, student_unembed, tile_weights, tile_pairs, tile_count):
-    place = jnp.stack([lax.axis_index("vy"), lax.axis_index("vz"), lax.axis_index("tx"), lax.axis_index("tc")]).astype(jnp.int32)
+    y, z, x, core = (lax.axis_index(name) for name in ("vy", "vz", "tx", "tc"))
+    crossing = [jnp.where(core == 0, y, z), jnp.where(core == 0, z, y)]
+    place = jnp.stack([y, z, x, core] + crossing).astype(jnp.int32)
     rows = teacher_logits.shape[0]
     teacher = teacher_logits.astype(F32)
     peak = jnp.max(teacher, axis=1)
@@ -506,18 +548,18 @@
     mine = packed_pieces(pieces, [parts[1], parts[3]])
     later = products(place, tile_pairs, tile_count, probs, mine, swap(mine))
 
-    *parts, factors = merged(place, parts, rows)
-    early_grad, early_loss, table = gradients(0, place, logits, spread(parts, "vz"))
-    early = early_hidden(student_unembed, early_grad)
-    parts = merged(place, spread(later, "vy"), rows, factors)
-    late_grad, late_loss = gradients(width, place, logits, spread(parts, "vz"), table)
-
-    first = late_hidden(0, place, student_unembed, late_grad, early, (early_loss, late_loss))
-    first = middle(0, place, spread(first, "vy"))
-    second = late_hidden(1, place, student_unembed, late_grad, early)
-    second = middle(1, place, spread(second, "vz"))
-    grad_hidden, loss = last(place, spread(first, "vz"), spread(second, "vy"))
-    return grad_hidden, loss[0]
+    *parts, factors = merged(place, parts, rows, None, [later[0]])
+    later = spread(later, "vy")
+    grad, *before = gradients(0, place, logits, spread(parts, "vz"), (), later[1:])
+    early, stage = early_hidden(place, student_unembed, grad, swap(grad))
+    before = [before[1], before[0]]
+    parts = merged(place, later, rows, factors)
+    (grad,) = gradients(width, place, logits, spread(parts, "vz"), before, [early])
+
+    parts = late_hidden(place, stage, grad, swap(grad), early)
+    parts = middle(place, crossed(parts, True))
+    keep, give, loss = totals(place, crossed(parts, False))
+    return turned(place, keep, swap(give)), loss[0]
 
 
 def solution(mesh):

time: 162 us -> 162 us (level)
  waiting for transfers between devices: 42.9 us -> 58.8 us
  starting transfers between devices: 59.9 us -> 44.7 us
  local copies, waits for them, and re-layouts: 3.71 us -> 9.55 us
  Pallas kernels: 36.2 us -> 30.4 us
    ppermute x31 -> x19, starting transfers between devices: 57.2 us -> 31.3 us  [send(): lax.ppermute(value, axis, [(i, (i + step) % SIDE) for i in range(SIDE)])]
    ppermute x0 -> x6, waiting for transfers between devices: none -> 16.6 us  [crossed(): received.append(lax.ppermute(parts[step], ('vy', 'vz', 'tc'), pairs))]
    pallas_call x6 -> x5, Pallas kernels: 19.6 us -> 9.51 us  [the longest x1 3.7 us: early_hidden(): pl.pallas_call(early_kernel, grid_spec=pltpu.PrefetchScalarGridSpec(num_s...]
    ppermute x0 -> x6, starting transfers between devices: none -> 7.12 us  [crossed(): received.append(lax.ppermute(parts[step], ('vy', 'vz', 'tc'), pairs))]
    unnamed x17 -> x19, local copies, waits for them, and re-layouts: 3.11 us -> 8.88 us
    ppermute x31 -> x19, waiting for transfers between devices: 41.7 us -> 37.5 us  [send(): lax.ppermute(value, axis, [(i, (i + step) % SIDE) for i in range(SIDE)])]
    pallas_call x2, Pallas kernels: 6.15 us -> 10.3 us  [products(): pl.pallas_call(functools.partial(product_kernel, bool(extra)), out_shape=...]
    ppermute x2 -> x5, starting transfers between devices: 2.73 us -> 6.29 us  [swap(): return lax.ppermute(value, 'tc', [(0, 1), (1, 0)])]
  transfers between devices with their start and end apart: 33 -> 30, of which waited for: 14 -> 18; matrix products, arithmetic and copies ran while one was open for 10% -> 10% of each run, Pallas kernels for 15% -> 11%
where the time goes in v4:
time: 162 us; the launch traced here: 161 us
  waiting for transfers between devices  58.8 us (36%)
  starting transfers between devices  44.7 us (28%)
  Pallas kernels  30.4 us (19%)
  matrix products  9.64 us (6%)
  local copies, waits for them, and re-layouts  9.55 us (6%)
  other arithmetic  6.32 us (4%)
    ppermute x19, waiting for transfers between devices, send(): lax.ppermute(value, axis, [(i, (i + step) % SIDE) for i in range(SIDE)])  37.5 us
    ppermute x19, starting transfers between devices, send(): lax.ppermute(value, axis, [(i, (i + step) % SIDE) for i in range(SIDE)])  31.3 us
    ppermute x6, waiting for transfers between devices, crossed(): received.append(lax.ppermute(parts[step], ('vy', 'vz', 'tc'), pairs))  16.6 us
    pallas_call x2, Pallas kernels, products(): pl.pallas_call(functools.partial(product_kernel, bool(extra)), out_shape=...  10.3 us
    dot_general x1, matrix products, shards(): jnp.dot(student_hidden, student_unembed, preferred_element_type=F32)  9.64 us
    unnamed x19, local copies, waits for them, and re-layouts  8.88 us
    ppermute x6, starting transfers between devices, crossed(): received.append(lax.ppermute(parts[step], ('vy', 'vz', 'tc'), pairs))  7.12 us
    ppermute x5, starting transfers between devices, swap(): return lax.ppermute(value, 'tc', [(0, 1), (1, 0)])  6.29 us
  transfers between devices with their start and end apart: 30, of which 18 were waited for; matrix products, arithmetic and copies ran while one was open for 10% of the time, Pallas kernels for 11%

profile of v4, /device:TPU:1, one launch (start us, length us, event | category | flops | bytes accessed | tf_op | source)
XLA Modules:
  0.0 160.9 jit_solution(12510686329082562298)
XLA Ops:
  2.4 3.4 %collective-permute-start.2 = (bf16[1088,256]{1,0:T(8,128)(2,1)S(1)}, bf16[1088,256]{1,0:T(8,128)(2,1)S(1)}, u32[]{:S(2)}, u32[]{:S(2)}) collective-permute-start(bf16[1088,256]{1,0:T(8,128)(2,1)S(1)} %prepare_weights.1.refs_0_), channel_id=1, source_target_pairs={{0,6},{2,0},{4,2},{6,4},{1,7},{3,1},{5,3},{7,5},{8,14},{10,8},{12,... | collective-permute-start | bytes 1671176 | tf_op jit(solution)/shard_map/ppermute | solution.py:29
  6.9 9.6 %fusion.2 = (f32[256]{0:T(256)S(1)}, f32[256,2048]{1,0:T(8,128)}) fusion(bf16[256,4096]{1,0:T(8,128)(2,1)S(1)} %copy-done, bf16[4096,2048]{1,0:T(8,128)(2,1)} %param.8), kind=kOutput, calls=%fused_computation.4 | convolution fusion | flops 4295491584 | bytes 20972544 | tf_op jit(solution)/shard_map/dot_general | solution.py:530
  20.7 2.2 %fusion = (f32[256]{0:T(256)S(1)}, bf16[256,4096]{1,0:T(8,128)(2,1)}) fusion(bf16[256,4096]{1,0:T(8,128)(2,1)S(1)} %copy-done.7, f32[256]{0:T(256)S(1)} %reduce_max.28), kind=kLoop, calls=%fused_computation.1 | loop fusion | flops 4194048 | bytes 4196352 | tf_op jit(solution)/shard_map/reduce_sum | solution.py:527
  22.9 10.9 %collective-permute-done.refs_1_ = bf16[1088,256]{1,0:T(8,128)(2,1)} collective-permute-done((bf16[1088,256]{1,0:T(8,128)(2,1)S(1)}, bf16[1088,256]{1,0:T(8,128)(2,1)}, u32[]{:S(2)}, u32[]{:S(2)}) %collective-permute-start) | collective-permute-done | bytes 557088 | tf_op jit(solution)/shard_map/ppermute | solution.py:29
  33.8 2.8 %pack_weights.2.mine.refs_0_ = bf16[4352,256]{1,0:T(8,128)(2,1)} custom-call(bf16[1088,256]{1,0:T(8,128)(2,1)S(1)} %prepare_weights.1.refs_0_, bf16[1088,256]{1,0:T(8,128)(2,1)} %collective-permute-done.refs_1_, bf16[1088,256]{1,0:T(8,128)(2,1)} %collective-permute-done.1.refs_2_, bf16[1088,256]{1,0:T(8,128)(2,1)S(1)} %collective-permute-done.2.refs_3_, ...), custom_call_target="tpu_custom_call" | custom-call | bytes 4456448 | tf_op jit(solution)/shard_map/pack_weights/pallas_call | solution.py:99
  43.1 6.3 %tile_products.2 = (bf16[1040,256]{1,0:T(8,128)(2,1)S(1)}, bf16[1040,256]{1,0:T(8,128)(2,1)S(1)}, bf16[1040,256]{1,0:T(8,128)(2,1)S(1)}, bf16[1040,256]{1,0:T(8,128)(2,1)S(1)}) custom-call(s32[6]{0:T(128)S(1)} %stack.43.place, s32[16,2]{1,0:T(8,128)S(1)} %copy.8.pairs, s32[1]{0:T(128)S(6)} %copy.10.count, bf16[256,4096]{1,0:T(8,128)(2,1)S(1)} %copy-done.3, ...), custom_call_target="tpu_custom_call" | custom-call | flops 1073741824 | bytes 8650752 | tf_op jit(solution)/shard_map/tile_products/pallas_call | solution.py:197
  53.1 2.7 %collective-permute-start.10 = (bf16[512,256]{1,0:T(8,128)(2,1)S(1)}, bf16[512,256]{1,0:T(8,128)(2,1)S(1)}, u32[]{:S(2)}, u32[]{:S(2)}) collective-permute-start(bf16[512,256]{1,0:T(8,128)(2,1)S(1)} %get-tuple-element.42), channel_id=1, source_target_pairs={{0,6},{2,0},{4,2},{6,4},{1,7},{3,1},{5,3},{7,5},{8,14},{10,8},{12,... | collective-permute-start | bytes 786440 | tf_op jit(solution)/shard_map/ppermute | solution.py:29
  55.8 5.2 %collective-permute-done.9.refs_2_ = bf16[512,256]{1,0:T(8,128)(2,1)S(1)} collective-permute-done((bf16[512,256]{1,0:T(8,128)(2,1)S(1)}, bf16[512,256]{1,0:T(8,128)(2,1)S(1)}, u32[]{:S(2)}, u32[]{:S(2)}) %collective-permute-start.9) | collective-permute-done | bytes 262176 | tf_op jit(solution)/shard_map/ppermute | solution.py:29
  61.0 3.0 %collective-permute-done.4.refs_5_.refs_1_ = bf16[1040,256]{1,0:T(8,128)(2,1)S(1)} collective-permute-done((bf16[1040,256]{1,0:T(8,128)(2,1)S(1)}, bf16[1040,256]{1,0:T(8,128)(2,1)S(1)}, u32[]{:S(2)}, u32[]{:S(2)}) %collective-permute-start.4) | collective-permute-done | bytes 532512 | tf_op jit(solution)/shard_map/ppermute | solution.py:29
  70.3 3.9 %tile_products.3 = (bf16[1024,256]{1,0:T(8,128)(2,1)S(1)}, bf16[1024,256]{1,0:T(8,128)(2,1)S(1)}, bf16[1024,256]{1,0:T(8,128)(2,1)S(1)}, bf16[1024,256]{1,0:T(8,128)(2,1)S(1)}) custom-call(s32[6]{0:T(128)S(1)} %stack.43.place, s32[16,2]{1,0:T(8,128)S(1)} %copy.8.pairs, s32[1]{0:T(128)S(6)} %copy.10.count, bf16[256,4096]{1,0:T(8,128)(2,1)S(1)} %copy-done.4, ...), custom_call_target="tpu_custom_call" | custom-call | flops 1073741824 | bytes 8388608 | tf_op jit(solution)/shard_map/tile_products/pallas_call | solution.py:197
  74.3 3.4 %collective-permute-start.16 = (bf16[1024,256]{1,0:T(8,128)(2,1)S(1)}, bf16[1024,256]{1,0:T(8,128)(2,1)S(1)}, u32[]{:S(2)}, u32[]{:S(2)}) collective-permute-start(bf16[1024,256]{1,0:T(8,128)(2,1)S(1)} %get-tuple-element.49), channel_id=1, source_target_pairs={{0,64},{32,96},{64,0},{96,32},{1,65},{33,97},{65,1},{97,33},{2,66}... | collective-permute-start | bytes 1572872 | tf_op jit(solution)/shard_map/ppermute | solution.py:29
  77.7 4.0 %collective-permute-done.5.refs_2_ = bf16[1040,256]{1,0:T(8,128)(2,1)S(1)} collective-permute-done((bf16[1040,256]{1,0:T(8,128)(2,1)S(1)}, bf16[1040,256]{1,0:T(8,128)(2,1)S(1)}, u32[]{:S(2)}, u32[]{:S(2)}) %collective-permute-start.5) | collective-permute-done | bytes 532512 | tf_op jit(solution)/shard_map/ppermute | solution.py:29
  84.1 5.3 %collective-permute-start.13 = (bf16[272,256]{1,0:T(8,128)(2,1)S(1)}, bf16[272,256]{1,0:T(8,128)(2,1)S(1)}, u32[]{:S(2)}, u32[]{:S(2)}) collective-permute-start(bf16[272,256]{1,0:T(8,128)(2,1)S(1)} %get-tuple-element.46), channel_id=1, source_target_pairs={{0,16},{8,24},{16,0},{24,8},{1,17},{9,25},{17,1},{25,9},{2,18},{10... | collective-permute-start | bytes 417800 | tf_op jit(solution)/shard_map/ppermute | solution.py:29
  92.4 2.3 %collective-permute-done.13.refs_2_ = bf16[272,256]{1,0:T(8,128)(2,1)S(1)} collective-permute-done((bf16[272,256]{1,0:T(8,128)(2,1)S(1)}, bf16[272,256]{1,0:T(8,128)(2,1)S(1)}, u32[]{:S(2)}, u32[]{:S(2)}) %collective-permute-start.13) | collective-permute-done | bytes 139296 | tf_op jit(solution)/shard_map/ppermute | solution.py:29
  95.2 9.0 %collective-permute-done.16.refs_5_.refs_3_ = bf16[1024,256]{1,0:T(8,128)(2,1)S(1)} collective-permute-done((bf16[1024,256]{1,0:T(8,128)(2,1)S(1)}, bf16[1024,256]{1,0:T(8,128)(2,1)S(1)}, u32[]{:S(2)}, u32[]{:S(2)}) %collective-permute-start.16) | collective-permute-done | bytes 524320 | tf_op jit(solution)/shard_map/ppermute | solution.py:29
  109.0 5.3 %collective-permute-start.20 = (bf16[256,256]{1,0:T(8,128)(2,1)S(1)}, bf16[256,256]{1,0:T(8,128)(2,1)S(1)}, u32[]{:S(2)}, u32[]{:S(2)}) collective-permute-start(bf16[256,256]{1,0:T(8,128)(2,1)S(1)} %get-tuple-element.58), channel_id=1, source_target_pairs={{0,16},{8,24},{16,0},{24,8},{1,17},{9,25},{17,1},{25,9},{2,18},{10... | collective-permute-start | bytes 393224 | tf_op jit(solution)/shard_map/ppermute | solution.py:29
  114.3 5.8 %copy-done.1 = bf16[4096,2048]{1,0:T(8,128)(2,1)S(1)} copy-done((bf16[4096,2048]{1,0:T(8,128)(2,1)S(1)}, bf16[4096,2048]{1,0:T(8,128)(2,1)}, u32[]{:S(2)}) %copy-start.1) | copy-done | bytes 16777240
  120.1 3.7 %early_hidden.1 = (f32[2048,512]{1,0:T(8,128)S(1)}, bf16[2048,1024]{1,0:T(8,128)(2,1)S(1)}) custom-call(s32[6]{0:T(128)S(1)} %stack.43.place, bf16[4,4,2,128,2048]{4,3,2,1,0:T(8,128)(2,1)S(1)} %bitcast.14, bf16[4,4,2,128,2048]{4,3,2,1,0:T(8,128)(2,1)S(1)} %bitcast.15, bf16[4,4,2,128,2048]{4,3,2,1,0:T(8,128)(2,1)S(1)} %bitcast.16, ...), custom_call_target="tpu_custom_call" | custom-call | flops 2147483648 | bytes 14680064 | tf_op jit(solution)/shard_map/early_hidden/pallas_call | solution.py:372
  127.5 3.0 %late_hidden.1 = (bf16[528,512]{1,0:T(8,128)(2,1)S(1)}, bf16[528,512]{1,0:T(8,128)(2,1)S(1)}, bf16[528,512]{1,0:T(8,128)(2,1)S(1)}, bf16[528,512]{1,0:T(8,128)(2,1)S(1)}) custom-call(s32[6]{0:T(128)S(1)} %stack.43.place, bf16[2048,1024]{1,0:T(8,128)(2,1)S(1)} %get-tuple-element.52.stage, bf16[1040,256]{1,0:T(8,128)(2,1)S(1)} %logit_grad.3.mine, ...), custom_call_target="tpu_custom_call" | custom-call | flops 2147483648 | bytes 10485760 | tf_op jit(solution)/shard_map/late_hidden/pallas_call | solution.py:405
  132.3 2.5 %collective-permute-start.25 = (bf16[528,512]{1,0:T(8,128)(2,1)S(1)}, bf16[528,512]{1,0:T(8,128)(2,1)S(1)}, u32[]{:S(2)}, u32[]{:S(2)}) collective-permute-start(bf16[528,512]{1,0:T(8,128)(2,1)S(1)} %get-tuple-element.64), channel_id=1, source_target_pairs={{0,96},{1,25},{8,104},{9,1},{16,112},{17,9},{24,120},{25,17},{32,0... | collective-permute-start | bytes 1622024 | tf_op jit(solution)/shard_map/ppermute | solution.py:515
  134.8 11.3 %collective-permute-done.23.refs_1_ = bf16[528,512]{1,0:T(8,128)(2,1)S(1)} collective-permute-done((bf16[528,512]{1,0:T(8,128)(2,1)S(1)}, bf16[528,512]{1,0:T(8,128)(2,1)S(1)}, u32[]{:S(2)}, u32[]{:S(2)}) %collective-permute-start.23) | collective-permute-done | bytes 540704 | tf_op jit(solution)/shard_map/ppermute | solution.py:515
  147.7 2.3 %collective-permute-start.27 = (bf16[144,512]{1,0:T(8,128)(2,1)S(1)}, bf16[144,512]{1,0:T(8,128)(2,1)S(1)}, u32[]{:S(2)}, u32[]{:S(2)}) collective-permute-start(bf16[144,512]{1,0:T(8,128)(2,1)S(1)} %get-tuple-element.67), channel_id=1, source_target_pairs={{0,16},{1,65},{8,24},{9,73},{16,0},{17,81},{24,8},{25,89},{32,48},... | collective-permute-start | bytes 442376 | tf_op jit(solution)/shard_map/ppermute | solution.py:515
  150.4 4.3 %collective-permute-done.26.refs_1_ = bf16[144,512]{1,0:T(8,128)(2,1)S(1)} collective-permute-done((bf16[144,512]{1,0:T(8,128)(2,1)S(1)}, bf16[144,512]{1,0:T(8,128)(2,1)S(1)}, u32[]{:S(2)}, u32[]{:S(2)}) %collective-permute-start.26) | collective-permute-done | bytes 147488 | tf_op jit(solution)/shard_map/ppermute | solution.py:515
  155.8 2.9 %collective-permute-start.29 = (bf16[128,256]{1,0:T(8,128)(2,1)S(1)}, bf16[128,256]{1,0:T(8,128)(2,1)S(1)}, u32[]{:S(2)}, u32[]{:S(2)}) collective-permute-start(bf16[128,256]{1,0:T(8,128)(2,1)S(1)} %get-tuple-element.70), channel_id=1, source_target_pairs={{0,1},{1,0},{2,3},{3,2},{4,5},{5,4},{6,7},{7,6},{8,9},{9,8},{10,11... | collective-permute-start | bytes 196616 | tf_op jit(solution)/shard_map/ppermute | solution.py:33
  (81 shorter events, 44.3 us)
Async XLA Ops:
  2.4 20.5 %collective-permute-start.2 = (bf16[1088,256]{1,0:T(8,128)(2,1)S(1)}, bf16[1088,256]{1,0:T(8,128)(2,1)S(1)}, u32[]{:S(2)}, u32[]{:S(2)}) collective-permute-start(bf16[1088,256]{1,0:T(8,128)(2,1)S(1)} %prepare_weights.1.refs_0_), channel_id=1, source_target_pairs={{0,6},{2,0},{4,2},{6,4},{1,7},{3,1},{5,3},{7,5},{8,14},{10,8},{12,... | collective-permute-start | bytes 1671176 | tf_op jit(solution)/shard_map/ppermute | solution.py:29
  5.7 17.2 %collective-permute-start.1 = (bf16[1088,256]{1,0:T(8,128)(2,1)S(1)}, bf16[1088,256]{1,0:T(8,128)(2,1)}, u32[]{:S(2)}, u32[]{:S(2)}) collective-permute-start(bf16[1088,256]{1,0:T(8,128)(2,1)S(1)} %prepare_weights.1.refs_0_), channel_id=1, source_target_pairs={{0,4},{2,6},{4,0},{6,2},{1,5},{3,7},{5,1},{7,3},{8,12},{10,14},{12... | collective-permute-start | bytes 1671176 | tf_op jit(solution)/shard_map/ppermute | solution.py:29
  6.3 27.6 %collective-permute-start = (bf16[1088,256]{1,0:T(8,128)(2,1)S(1)}, bf16[1088,256]{1,0:T(8,128)(2,1)}, u32[]{:S(2)}, u32[]{:S(2)}) collective-permute-start(bf16[1088,256]{1,0:T(8,128)(2,1)S(1)} %prepare_weights.1.refs_0_), channel_id=1, source_target_pairs={{0,2},{2,4},{4,6},{6,0},{1,3},{3,5},{5,7},{7,1},{8,10},{10,12},{12... | collective-permute-start | bytes 1671176 | tf_op jit(solution)/shard_map/ppermute | solution.py:29
  38.0 14.2 %collective-permute-start.8 = (bf16[1024,256]{1,0:T(8,128)(2,1)}, bf16[1024,256]{1,0:T(8,128)(2,1)S(1)}, u32[]{:S(2)}, u32[]{:S(2)}) collective-permute-start(bf16[1024,256]{1,0:T(8,128)(2,1)} %slice_weights.1.refs_0_), channel_id=1, source_target_pairs={{0,6},{2,0},{4,2},{6,4},{1,7},{3,1},{5,3},{7,5},{8,14},{10,8},{12,... | collective-permute-start | bytes 1572872 | tf_op jit(solution)/shard_map/ppermute | solution.py:29
  38.3 14.7 %collective-permute-start.7 = (bf16[1024,256]{1,0:T(8,128)(2,1)}, bf16[1024,256]{1,0:T(8,128)(2,1)S(1)}, u32[]{:S(2)}, u32[]{:S(2)}) collective-permute-start(bf16[1024,256]{1,0:T(8,128)(2,1)} %slice_weights.1.refs_0_), channel_id=1, source_target_pairs={{0,2},{2,4},{4,6},{6,0},{1,3},{3,5},{5,7},{7,1},{8,10},{10,12},{12... | collective-permute-start | bytes 1572872 | tf_op jit(solution)/shard_map/ppermute | solution.py:29
  49.4 14.6 %collective-permute-start.4 = (bf16[1040,256]{1,0:T(8,128)(2,1)S(1)}, bf16[1040,256]{1,0:T(8,128)(2,1)S(1)}, u32[]{:S(2)}, u32[]{:S(2)}) collective-permute-start(bf16[1040,256]{1,0:T(8,128)(2,1)S(1)} %get-tuple-element.38), channel_id=1, source_target_pairs={{0,32},{32,64},{64,96},{96,0},{1,33},{33,65},{65,97},{97,1},{2,34}... | collective-permute-start | bytes 1597448 | tf_op jit(solution)/shard_map/ppermute | solution.py:29
  50.2 13.8 %collective-permute-start.6 = (bf16[1040,256]{1,0:T(8,128)(2,1)S(1)}, bf16[1040,256]{1,0:T(8,128)(2,1)S(1)}, u32[]{:S(2)}, u32[]{:S(2)}) collective-permute-start(bf16[1040,256]{1,0:T(8,128)(2,1)S(1)} %get-tuple-element.40), channel_id=1, source_target_pairs={{0,96},{32,0},{64,32},{96,64},{1,97},{33,1},{65,33},{97,65},{2,98}... | collective-permute-start | bytes 1597448 | tf_op jit(solution)/shard_map/ppermute | solution.py:29
  53.0 8.0 %collective-permute-start.9 = (bf16[512,256]{1,0:T(8,128)(2,1)S(1)}, bf16[512,256]{1,0:T(8,128)(2,1)S(1)}, u32[]{:S(2)}, u32[]{:S(2)}) collective-permute-start(bf16[512,256]{1,0:T(8,128)(2,1)S(1)} %get-tuple-element.41), channel_id=1, source_target_pairs={{0,2},{2,4},{4,6},{6,0},{1,3},{3,5},{5,7},{7,1},{8,10},{10,12},{12... | collective-permute-start | bytes 786440 | tf_op jit(solution)/shard_map/ppermute | solution.py:29
  53.1 7.9 %collective-permute-start.10 = (bf16[512,256]{1,0:T(8,128)(2,1)S(1)}, bf16[512,256]{1,0:T(8,128)(2,1)S(1)}, u32[]{:S(2)}, u32[]{:S(2)}) collective-permute-start(bf16[512,256]{1,0:T(8,128)(2,1)S(1)} %get-tuple-element.42), channel_id=1, source_target_pairs={{0,6},{2,0},{4,2},{6,4},{1,7},{3,1},{5,3},{7,5},{8,14},{10,8},{12,... | collective-permute-start | bytes 786440 | tf_op jit(solution)/shard_map/ppermute | solution.py:29
  66.5 15.2 %collective-permute-start.5 = (bf16[1040,256]{1,0:T(8,128)(2,1)S(1)}, bf16[1040,256]{1,0:T(8,128)(2,1)S(1)}, u32[]{:S(2)}, u32[]{:S(2)}) collective-permute-start(bf16[1040,256]{1,0:T(8,128)(2,1)S(1)} %get-tuple-element.39), channel_id=1, source_target_pairs={{0,64},{32,96},{64,0},{96,32},{1,65},{33,97},{65,1},{97,33},{2,66}... | collective-permute-start | bytes 1597448 | tf_op jit(solution)/shard_map/ppermute | solution.py:29
  74.2 20.9 %collective-permute-start.15 = (bf16[1024,256]{1,0:T(8,128)(2,1)S(1)}, bf16[1024,256]{1,0:T(8,128)(2,1)S(1)}, u32[]{:S(2)}, u32[]{:S(2)}) collective-permute-start(bf16[1024,256]{1,0:T(8,128)(2,1)S(1)} %get-tuple-element.48), channel_id=1, source_target_pairs={{0,32},{32,64},{64,96},{96,0},{1,33},{33,65},{65,97},{97,1},{2,34}... | collective-permute-start | bytes 1572872 | tf_op jit(solution)/shard_map/ppermute | solution.py:29
  74.3 29.8 %collective-permute-start.16 = (bf16[1024,256]{1,0:T(8,128)(2,1)S(1)}, bf16[1024,256]{1,0:T(8,128)(2,1)S(1)}, u32[]{:S(2)}, u32[]{:S(2)}) collective-permute-start(bf16[1024,256]{1,0:T(8,128)(2,1)S(1)} %get-tuple-element.49), channel_id=1, source_target_pairs={{0,64},{32,96},{64,0},{96,32},{1,65},{33,97},{65,1},{97,33},{2,66}... | collective-permute-start | bytes 1572872 | tf_op jit(solution)/shard_map/ppermute | solution.py:29
  77.7 26.7 %collective-permute-start.17 = (bf16[1024,256]{1,0:T(8,128)(2,1)S(1)}, bf16[1024,256]{1,0:T(8,128)(2,1)S(1)}, u32[]{:S(2)}, u32[]{:S(2)}) collective-permute-start(bf16[1024,256]{1,0:T(8,128)(2,1)S(1)} %get-tuple-element.50), channel_id=1, source_target_pairs={{0,96},{32,0},{64,32},{96,64},{1,97},{33,1},{65,33},{97,65},{2,98}... | collective-permute-start | bytes 1572872 | tf_op jit(solution)/shard_map/ppermute | solution.py:29
  82.9 8.1 %collective-permute-start.12 = (bf16[272,256]{1,0:T(8,128)(2,1)S(1)}, bf16[272,256]{1,0:T(8,128)(2,1)S(1)}, u32[]{:S(2)}, u32[]{:S(2)}) collective-permute-start(bf16[272,256]{1,0:T(8,128)(2,1)S(1)} %get-tuple-element.45), channel_id=1, source_target_pairs={{0,8},{8,16},{16,24},{24,0},{1,9},{9,17},{17,25},{25,1},{2,10},{10... | collective-permute-start | bytes 417800 | tf_op jit(solution)/shard_map/ppermute | solution.py:29
  84.1 10.6 %collective-permute-start.13 = (bf16[272,256]{1,0:T(8,128)(2,1)S(1)}, bf16[272,256]{1,0:T(8,128)(2,1)S(1)}, u32[]{:S(2)}, u32[]{:S(2)}) collective-permute-start(bf16[272,256]{1,0:T(8,128)(2,1)S(1)} %get-tuple-element.46), channel_id=1, source_target_pairs={{0,16},{8,24},{16,0},{24,8},{1,17},{9,25},{17,1},{25,9},{2,18},{10... | collective-permute-start | bytes 417800 | tf_op jit(solution)/shard_map/ppermute | solution.py:29
  106.1 8.3 %collective-permute-start.18 = (bf16[1024,256]{1,0:T(8,128)(2,1)S(1)}, bf16[1024,256]{1,0:T(8,128)(2,1)S(1)}, u32[]{:S(2)}, u32[]{:S(2)}) collective-permute-start(bf16[1024,256]{1,0:T(8,128)(2,1)S(1)} %get-tuple-element.51.refs_4_), channel_id=1, source_target_pairs={{0,1},{1,0},{2,3},{3,2},{4,5},{5,4},{6,7},{7,6},{8,9},{9,8},{10,11... | collective-permute-start | bytes 1572872 | tf_op jit(solution)/shard_map/ppermute | solution.py:33
  108.1 15.8 %collective-permute-start.19 = (bf16[256,256]{1,0:T(8,128)(2,1)S(1)}, bf16[256,256]{1,0:T(8,128)(2,1)S(1)}, u32[]{:S(2)}, u32[]{:S(2)}) collective-permute-start(bf16[256,256]{1,0:T(8,128)(2,1)S(1)} %get-tuple-element.57), channel_id=1, source_target_pairs={{0,8},{8,16},{16,24},{24,0},{1,9},{9,17},{17,25},{25,1},{2,10},{10... | collective-permute-start | bytes 393224 | tf_op jit(solution)/shard_map/ppermute | solution.py:29
  109.0 14.8 %collective-permute-start.20 = (bf16[256,256]{1,0:T(8,128)(2,1)S(1)}, bf16[256,256]{1,0:T(8,128)(2,1)S(1)}, u32[]{:S(2)}, u32[]{:S(2)}) collective-permute-start(bf16[256,256]{1,0:T(8,128)(2,1)S(1)} %get-tuple-element.58), channel_id=1, source_target_pairs={{0,16},{8,24},{16,0},{24,8},{1,17},{9,25},{17,1},{25,9},{2,18},{10... | collective-permute-start | bytes 393224 | tf_op jit(solution)/shard_map/ppermute | solution.py:29
  114.3 9.5 %collective-permute-start.21 = (bf16[256,256]{1,0:T(8,128)(2,1)S(1)}, bf16[256,256]{1,0:T(8,128)(2,1)S(1)}, u32[]{:S(2)}, u32[]{:S(2)}) collective-permute-start(bf16[256,256]{1,0:T(8,128)(2,1)S(1)} %get-tuple-element.59), channel_id=1, source_target_pairs={{0,24},{8,0},{16,8},{24,16},{1,25},{9,1},{17,9},{25,17},{2,26},{10... | collective-permute-start | bytes 393224 | tf_op jit(solution)/shard_map/ppermute | solution.py:29
  130.5 15.6 %collective-permute-start.23 = (bf16[528,512]{1,0:T(8,128)(2,1)S(1)}, bf16[528,512]{1,0:T(8,128)(2,1)S(1)}, u32[]{:S(2)}, u32[]{:S(2)}) collective-permute-start(bf16[528,512]{1,0:T(8,128)(2,1)S(1)} %get-tuple-element.62), channel_id=1, source_target_pairs={{0,32},{1,9},{8,40},{9,17},{16,48},{17,25},{24,56},{25,1},{32,64},... | collective-permute-start | bytes 1622024 | tf_op jit(solution)/shard_map/ppermute | solution.py:515
  132.3 13.8 %collective-permute-start.24 = (bf16[528,512]{1,0:T(8,128)(2,1)S(1)}, bf16[528,512]{1,0:T(8,128)(2,1)S(1)}, u32[]{:S(2)}, u32[]{:S(2)}) collective-permute-start(bf16[528,512]{1,0:T(8,128)(2,1)S(1)} %get-tuple-element.63), channel_id=1, source_target_pairs={{0,64},{1,17},{8,72},{9,25},{16,80},{17,1},{24,88},{25,9},{32,96},... | collective-permute-start | bytes 1622024 | tf_op jit(solution)/shard_map/ppermute | solution.py:515
  132.3 14.4 %collective-permute-start.25 = (bf16[528,512]{1,0:T(8,128)(2,1)S(1)}, bf16[528,512]{1,0:T(8,128)(2,1)S(1)}, u32[]{:S(2)}, u32[]{:S(2)}) collective-permute-start(bf16[528,512]{1,0:T(8,128)(2,1)S(1)} %get-tuple-element.64), channel_id=1, source_target_pairs={{0,96},{1,25},{8,104},{9,1},{16,112},{17,9},{24,120},{25,17},{32,0... | collective-permute-start | bytes 1622024 | tf_op jit(solution)/shard_map/ppermute | solution.py:515
  147.6 7.1 %collective-permute-start.26 = (bf16[144,512]{1,0:T(8,128)(2,1)S(1)}, bf16[144,512]{1,0:T(8,128)(2,1)S(1)}, u32[]{:S(2)}, u32[]{:S(2)}) collective-permute-start(bf16[144,512]{1,0:T(8,128)(2,1)S(1)} %get-tuple-element.66), channel_id=1, source_target_pairs={{0,8},{1,33},{8,16},{9,41},{16,24},{17,49},{24,0},{25,57},{32,40},... | collective-permute-start | bytes 442376 | tf_op jit(solution)/shard_map/ppermute | solution.py:515
  147.7 7.0 %collective-permute-start.27 = (bf16[144,512]{1,0:T(8,128)(2,1)S(1)}, bf16[144,512]{1,0:T(8,128)(2,1)S(1)}, u32[]{:S(2)}, u32[]{:S(2)}) collective-permute-start(bf16[144,512]{1,0:T(8,128)(2,1)S(1)} %get-tuple-element.67), channel_id=1, source_target_pairs={{0,16},{1,65},{8,24},{9,73},{16,0},{17,81},{24,8},{25,89},{32,48},... | collective-permute-start | bytes 442376 | tf_op jit(solution)/shard_map/ppermute | solution.py:515
  (15 other events, 96.6 us)

commit v5 on v4

--- a/solution.py
+++ b/solution.py
@@ -85,6 +85,23 @@
     )(weights, *behind)
 
 
+def gate_kernel(*refs):
+    pass
+
+
+def gated(parts, behind):
+    return pl.pallas_call(
+        gate_kernel,
+        out_shape=[jax.ShapeDtypeStruct(part.shape, part.dtype) for part in parts],
+        in_specs=[ANY] * (len(parts) + len(behind)),
+        out_specs=[ANY] * len(parts),
+        input_output_aliases={i: i for i in range(len(parts))},
+        compiler_params=params(),
+        cost_estimate=cost(0, 0),
+        name="gate",
+    )(*parts, *behind)
+
+
 def pack_kernel(number, *refs):
     out = refs[-1]
     at = 0
@@ -132,7 +149,8 @@
     )(right, left, *behind)
 
 
-def product_kernel(with_stats, place, pairs, count, probs, mine, other, *rest):
+def product_kernel(number, with_stats, place, pairs, count, probs, *rest):
+    mine, other, rest = rest[:number], rest[number : 2 * number], rest[2 * number :]
     if with_stats:
         before, rest = rest[0], rest[1:]
     outs, rest = rest[:SIDE], rest[SIDE:]
@@ -146,8 +164,11 @@
     depth = weights.shape[1]
     for step in range(SIDE):
         at = lax.rem(place[2] + SIDE - step, SIDE) * 2
-        weights[at + place[3]] = mine[step * depth : step * depth + depth, :]
-        weights[at + 1 - place[3]] = other[step * depth : step * depth + depth, :]
+        for parts, core in ((mine, place[3]), (other, 1 - place[3])):
+            if number == 1:
+                weights[at + core] = parts[0][step * depth : step * depth + depth, :]
+            else:
+                weights[at + core] = parts[step][...]
     if with_stats:
         sums, line = rest[2:]
         line[...] = jnp.zeros_like(line)
@@ -186,7 +207,7 @@
 
 def products(place, pairs, count, probs, mine, other, before=None):
     rows = probs.shape[0]
-    depth, width = mine.shape[0] // SIDE, mine.shape[1]
+    depth, width = sum(part.shape[0] for part in mine) // SIDE, mine[0].shape[1]
     extra = [] if before is None else [before]
     scratch = [
         pltpu.VMEM((2 * SIDE, depth, width), BF16),
@@ -195,9 +216,9 @@
     if extra:
         scratch += [pltpu.VMEM((2, 64, 512), F32), pltpu.VMEM((8, rows), F32)]
     return pl.pallas_call(
-        functools.partial(product_kernel, bool(extra)),
+        functools.partial(product_kernel, len(mine), bool(extra)),
         out_shape=[jax.ShapeDtypeStruct((SIDE * rows + 16 * len(extra), width), BF16)] * SIDE,
-        in_specs=[SMEM, SMEM, SMEM] + [VMEM] * (3 + len(extra)),
+        in_specs=[SMEM, SMEM, SMEM] + [VMEM] * (1 + 2 * len(mine) + len(extra)),
         out_specs=[VMEM] * SIDE,
         scratch_shapes=scratch,
         compiler_params=params(24),
@@ -205,7 +226,7 @@
             16 * 2 * rows * 512 * width, 2 * probs.size + 16 * depth * width + 32 * rows * width
         ),
         name="tile_products",
-    )(place, pairs, count, probs, mine, other, *extra)
+    )(place, pairs, count, probs, *mine, *other, *extra)
 
 
 def pack_rows(lines):
@@ -333,28 +354,21 @@
     out[:, pl.ds(pl.multiple_of((1 - core) * rows, rows), rows)] = other[0:depth, :]
 
 
-def early_kernel(place, *refs):
-    unembed = refs[:SIDE]
-    mine, other, out, stage, both = refs[SIDE:]
-    depth = both.shape[0]
-    width = depth // SIDE
-
-    @pl.when(pl.program_id(0) == 0)
-    def _():
-        both_cores(place[3], mine, other, depth, both)
-
+def stage_kernel(place, *refs):
+    unembed, stage = refs[:SIDE], refs[-1]
+    half = stage.shape[1] // 2
+    width = half // SIDE
     for owner in range(SIDE):
         rows = slice(owner * 128, owner * 128 + 128)
-        block = unembed[owner][...].reshape(128, 2 * depth)
-        now = [block[:, 2 * width * b : 2 * width * b + width] for b in range(SIDE)]
-        later = [block[:, 2 * width * b + width : 2 * width * (b + 1)] for b in range(SIDE)]
-        stage[rows, :] = jnp.concatenate(later, axis=1)
-        out[rows, :] = jnp.dot(jnp.concatenate(now, axis=1), both[...], preferred_element_type=F32)
-
-
-def early_hidden(place, unembed, mine, other):
+        block = unembed[owner][...].reshape(128, 2 * half)
+        for b in range(SIDE):
+            for c in range(2):
+                part = block[:, (2 * b + c) * width : (2 * b + c + 1) * width]
+                stage[rows, c * half + b * width : c * half + (b + 1) * width] = part
+
+
+def staged(place, unembed, behind):
     depth, cols = unembed.shape
-    width, rows = mine.shape
     unembed = unembed.reshape(SIDE, SIDE, 2, 128, cols)
 
     def where(i, p, k):
@@ -364,25 +378,42 @@
     views = [
         pl.BlockSpec((1, 1, 1, 128, cols), lambda i, p, k=k: where(i, p, k)) for k in range(SIDE)
     ]
-    whole = pl.BlockSpec((width, rows), lambda i, p: (0, 0))
-    outs = [
-        jax.ShapeDtypeStruct((depth // 2, 2 * rows), F32),
-        jax.ShapeDtypeStruct((depth // 2, width), BF16),
-    ]
-    return pl.pallas_call(
-        early_kernel,
+    return pl.pallas_call(
+        stage_kernel,
         grid_spec=pltpu.PrefetchScalarGridSpec(
             num_scalar_prefetch=1,
             grid=(SIDE,),
-            in_specs=views + [whole, whole],
-            out_specs=[pl.BlockSpec((512, v.shape[1]), lambda i, p: (i, 0)) for v in outs],
-            scratch_shapes=[pltpu.VMEM((width, 2 * rows), BF16)],
+            in_specs=views + [ANY] * len(behind),
+            out_specs=pl.BlockSpec((512, cols), lambda i, p: (i, 0)),
         ),
-        out_shape=outs,
-        compiler_params=params(24),
-        cost_estimate=cost(2 * depth * width * rows, depth * cols + 6 * depth * rows),
+        out_shape=jax.ShapeDtypeStruct((depth // 2, cols), BF16),
+        compiler_params=params(48),
+        cost_estimate=cost(0, 2 * depth * cols),
+        name="stage_unembed",
+    )(place, *[unembed] * SIDE, *behind)
+
+
+def early_kernel(place, stage, mine, other, out, both):
+    depth = both.shape[0]
+    both_cores(place[3], mine, other, depth, both)
+    for step in range(SIDE):
+        rows = slice(step * 512, step * 512 + 512)
+        out[rows, :] = jnp.dot(stage[rows, 0:depth], both[...], preferred_element_type=F32)
+
+
+def early_hidden(place, stage, mine, other):
+    depth = stage.shape[0]
+    width, rows = mine.shape
+    return pl.pallas_call(
+        early_kernel,
+        out_shape=jax.ShapeDtypeStruct((depth, 2 * rows), F32),
+        in_specs=[SMEM] + [VMEM] * 3,
+        out_specs=VMEM,
+        scratch_shapes=[pltpu.VMEM((width, 2 * rows), BF16)],
+        compiler_params=params(),
+        cost_estimate=cost(4 * depth * width * rows, 4 * depth * width + 8 * depth * rows),
         name="early_hidden",
-    )(place, *[unembed] * SIDE, mine, other)
+    )(place, stage, mine, other)
 
 
 def late_kernel(place, stage, mine, other, early, *refs):
@@ -392,24 +423,24 @@
     both_cores(place[3], mine, other, depth, both)
     for step in range(SIDE):
         at = pl.ds(pl.multiple_of(lax.rem(place[4] + step, SIDE) * 512, 512), 512)
-        result = early[at, :] + jnp.dot(stage[at, :], both[...], preferred_element_type=F32)
-        outs[step][0:512, :] = result.astype(BF16)
+        result = jnp.dot(stage[at, depth : 2 * depth], both[...], preferred_element_type=F32)
+        outs[step][0:512, :] = (early[at, :] + result).astype(BF16)
         for part, core in ((mine, place[3]), (other, 1 - place[3])):
             lanes = pl.ds(pl.multiple_of(core * rows, rows), rows)
             outs[step][512:528, lanes] = part[depth : depth + 16, :]
 
 
 def late_hidden(place, stage, mine, other, early):
-    width = stage.shape[1]
-    rows = early.shape[1]
+    depth, width = stage.shape
+    width, rows = width // 2, early.shape[1]
     return pl.pallas_call(
         late_kernel,
         out_shape=[jax.ShapeDtypeStruct((528, rows), BF16)] * SIDE,
         in_specs=[SMEM] + [VMEM] * 4,
         out_specs=[VMEM] * SIDE,
         scratch_shapes=[pltpu.VMEM((width, rows), BF16)],
-        compiler_params=params(24),
-        cost_estimate=cost(4096 * width * rows, 4096 * width + 6 * 2048 * rows),
+        compiler_params=params(),
+        cost_estimate=cost(2 * depth * width * rows, 2 * depth * width + 6 * depth * rows),
         name="late_hidden",
     )(place, stage, mine, other, early)
 
@@ -536,22 +567,23 @@
 
     width = tile_weights.shape[2] // 2
     piece = prepared(tile_weights, width)
-    mine = packed_pieces(spread([piece] * SIDE, "tx"), [mass, smass])
-    other = swap(mine)
+    mine = [piece, *gated(spread([piece] * SIDE, "tx")[1:], [mass, smass])]
+    other = [swap(piece) for piece in mine]
     parts = products(place, tile_pairs, tile_count, probs, mine, other, before)
 
-    piece = sliced(tile_weights, width, width, [mine])
+    piece = sliced(tile_weights, width, width, [mine[1]])
     right, left = send(piece, "tx", 1), send(piece, "tx", 3)
     top, low = halves(right, left, [parts[0]])
     parts = spread(parts, "vy")
     pieces = [piece, right, send(top, "tx", 1), send(low, "tx", 3), left]
     mine = packed_pieces(pieces, [parts[1], parts[3]])
-    later = products(place, tile_pairs, tile_count, probs, mine, swap(mine))
+    later = products(place, tile_pairs, tile_count, probs, [mine], [swap(mine)])
 
     *parts, factors = merged(place, parts, rows, None, [later[0]])
     later = spread(later, "vy")
-    grad, *before = gradients(0, place, logits, spread(parts, "vz"), (), later[1:])
-    early, stage = early_hidden(place, student_unembed, grad, swap(grad))
+    stage = staged(place, student_unembed, [parts[0]])
+    grad, *before = gradients(0, place, logits, spread(parts, "vz"), (), later[1:] + [stage])
+    early = early_hidden(place, stage, grad, swap(grad))
     before = [before[1], before[0]]
     parts = merged(place, later, rows, factors)
     (grad,) = gradients(width, place, logits, spread(parts, "vz"), before, [early])

time: 162 us -> 159 us (0.981)
  waiting for transfers between devices: 58.8 us -> 51.9 us
  starting transfers between devices: 44.7 us -> 50.5 us
  local copies, waits for them, and re-layouts: 9.55 us -> 7.13 us
    ppermute x19, waiting for transfers between devices: 37.5 us -> 32.9 us  [send(): lax.ppermute(value, axis, [(i, (i + step) % SIDE) for i in range(SIDE)])]
    pallas_call x2 -> x1, Pallas kernels: 4.01 us -> 1.49 us  [packed_pieces(): pl.pallas_call(functools.partial(pack_kernel, len(parts)), out_shape=jax....]
    unnamed x19 -> x21, local copies, waits for them, and re-layouts: 8.88 us -> 6.45 us
    ppermute x5 -> x8, starting transfers between devices: 6.29 us -> 8.4 us  [swap(): return lax.ppermute(value, 'tc', [(0, 1), (1, 0)])]
    pallas_call x3 -> x5, Pallas kernels: 14 us -> 16 us  [the longest x1 7.82 us: staged(): pl.pallas_call(stage_kernel, grid_spec=pltpu.PrefetchScalarGridSpec(num_s...]
    ppermute x19, starting transfers between devices: 31.3 us -> 33.3 us  [send(): lax.ppermute(value, axis, [(i, (i + step) % SIDE) for i in range(SIDE)])]
    reduce_sum x1, other arithmetic: 2.16 us -> 0.43 us  [shards(): smass = jnp.sum(jnp.exp(logits - speak[:, None]), axis=1)]
    reduce_sum x1, other arithmetic: 2.19 us -> 3.91 us  [shards(): mass = jnp.sum(shifted, axis=1)]
  transfers between devices with their start and end apart: 30 -> 33, of which waited for: 18 -> 18; matrix products, arithmetic and copies ran while one was open for 10% -> 11% of each run, Pallas kernels for 11% -> 13%
where the time goes in v5:
time: 159 us
  waiting for transfers between devices  51.9 us (33%)
  starting transfers between devices  50.5 us (32%)
  Pallas kernels  31.9 us (20%)
  matrix products  9.63 us (6%)
  local copies, waits for them, and re-layouts  7.13 us (4%)
  other arithmetic  6.3 us (4%)
    ppermute x19, starting transfers between devices, send(): lax.ppermute(value, axis, [(i, (i + step) % SIDE) for i in range(SIDE)])  33.3 us
    ppermute x19, waiting for transfers between devices, send(): lax.ppermute(value, axis, [(i, (i + step) % SIDE) for i in range(SIDE)])  32.9 us
    ppermute x6, waiting for transfers between devices, crossed(): received.append(lax.ppermute(parts[step], ('vy', 'vz', 'tc'), pairs))  15.4 us
    dot_general x1, matrix products, shards(): jnp.dot(student_hidden, student_unembed, preferred_element_type=F32)  9.63 us
    ppermute x6, starting transfers between devices, crossed(): received.append(lax.ppermute(parts[step], ('vy', 'vz', 'tc'), pairs))  8.81 us
    ppermute x8, starting transfers between devices, swap(): return lax.ppermute(value, 'tc', [(0, 1), (1, 0)])  8.4 us
    pallas_call x1, Pallas kernels, staged(): pl.pallas_call(stage_kernel, grid_spec=pltpu.PrefetchScalarGridSpec(num_s...  7.82 us
    unnamed x21, local copies, waits for them, and re-layouts  6.45 us
  transfers between devices with their start and end apart: 33, of which 18 were waited for; matrix products, arithmetic and copies ran while one was open for 11% of the time, Pallas kernels for 13%

profile of v5, /device:TPU:1, one launch (start us, length us, event | category | flops | bytes accessed | tf_op | source)
XLA Modules:
  0.0 158.9 jit_solution(5323775739215779219)
XLA Ops:
  4.6 2.6 %collective-permute-start.2 = (bf16[1088,256]{1,0:T(8,128)(2,1)}, bf16[1088,256]{1,0:T(8,128)(2,1)S(1)}, u32[]{:S(2)}, u32[]{:S(2)}) collective-permute-start(bf16[1088,256]{1,0:T(8,128)(2,1)} %prepare_weights.1.rest_0_), channel_id=1, source_target_pairs={{0,6},{2,0},{4,2},{6,4},{1,7},{3,1},{5,3},{7,5},{8,14},{10,8},{12,... | collective-permute-start | bytes 1671176 | tf_op jit(solution)/shard_map/ppermute | solution.py:29
  8.3 9.6 %fusion.2 = (f32[256]{0:T(256)S(1)}, f32[256,2048]{1,0:T(8,128)}) fusion(bf16[256,4096]{1,0:T(8,128)(2,1)S(1)} %copy-done, bf16[4096,2048]{1,0:T(8,128)(2,1)} %param.8), kind=kOutput, calls=%fused_computation.4 | convolution fusion | flops 4295491584 | bytes 20972544 | tf_op jit(solution)/shard_map/dot_general | solution.py:561
  19.9 3.9 %fusion = (f32[256]{0:T(256)S(1)}, bf16[256,4096]{1,0:T(8,128)(2,1)}) fusion(bf16[256,4096]{1,0:T(8,128)(2,1)} %param.6, f32[256]{0:T(256)S(1)} %reduce_max.28), kind=kLoop, calls=%fused_computation.1 | loop fusion | flops 4194048 | bytes 4196352 | tf_op jit(solution)/shard_map/reduce_sum | solution.py:558
  24.3 7.1 %collective-permute-done.2.refs_2_ = bf16[1088,256]{1,0:T(8,128)(2,1)S(1)} collective-permute-done((bf16[1088,256]{1,0:T(8,128)(2,1)}, bf16[1088,256]{1,0:T(8,128)(2,1)S(1)}, u32[]{:S(2)}, u32[]{:S(2)}) %collective-permute-start.2) | collective-permute-done | bytes 557088 | tf_op jit(solution)/shard_map/ppermute | solution.py:29
  31.3 4.0 %collective-permute-done.refs_0_ = bf16[1088,256]{1,0:T(8,128)(2,1)S(1)} collective-permute-done((bf16[1088,256]{1,0:T(8,128)(2,1)}, bf16[1088,256]{1,0:T(8,128)(2,1)S(1)}, u32[]{:S(2)}, u32[]{:S(2)}) %collective-permute-start) | collective-permute-done | bytes 557088 | tf_op jit(solution)/shard_map/ppermute | solution.py:29
  41.2 3.3 %tile_products.2 = (bf16[1040,256]{1,0:T(8,128)(2,1)S(1)}, bf16[1040,256]{1,0:T(8,128)(2,1)S(1)}, bf16[1040,256]{1,0:T(8,128)(2,1)S(1)}, bf16[1040,256]{1,0:T(8,128)(2,1)S(1)}) custom-call(s32[6]{0:T(128)S(1)} %stack.43.place, s32[16,2]{1,0:T(8,128)S(1)} %copy.11.pairs, s32[1]{0:T(128)S(6)} %copy.16.count, bf16[256,4096]{1,0:T(8,128)(2,1)S(1)} %copy-done.5, ...), custom_call_target="tpu_custom_call" | custom-call | flops 1073741824 | bytes 8650752 | tf_op jit(solution)/shard_map/tile_products/pallas_call | solution.py:218
  44.5 5.1 %collective-permute-start.7 = (bf16[1040,256]{1,0:T(8,128)(2,1)S(1)}, bf16[1040,256]{1,0:T(8,128)(2,1)S(1)}, u32[]{:S(2)}, u32[]{:S(2)}) collective-permute-start(bf16[1040,256]{1,0:T(8,128)(2,1)S(1)} %get-tuple-element.42), channel_id=1, source_target_pairs={{0,32},{32,64},{64,96},{96,0},{1,33},{33,65},{65,97},{97,1},{2,34}... | collective-permute-start | bytes 1597448 | tf_op jit(solution)/shard_map/ppermute | solution.py:29
  53.5 2.7 %collective-permute-start.13 = (bf16[512,256]{1,0:T(8,128)(2,1)S(1)}, bf16[512,256]{1,0:T(8,128)(2,1)S(1)}, u32[]{:S(2)}, u32[]{:S(2)}) collective-permute-start(bf16[512,256]{1,0:T(8,128)(2,1)S(1)} %get-tuple-element.46), channel_id=1, source_target_pairs={{0,6},{2,0},{4,2},{6,4},{1,7},{3,1},{5,3},{7,5},{8,14},{10,8},{12,... | collective-permute-start | bytes 786440 | tf_op jit(solution)/shard_map/ppermute | solution.py:29
  56.1 5.2 %collective-permute-done.12.refs_2_ = bf16[512,256]{1,0:T(8,128)(2,1)S(1)} collective-permute-done((bf16[512,256]{1,0:T(8,128)(2,1)S(1)}, bf16[512,256]{1,0:T(8,128)(2,1)S(1)}, u32[]{:S(2)}, u32[]{:S(2)}) %collective-permute-start.12) | collective-permute-done | bytes 262176 | tf_op jit(solution)/shard_map/ppermute | solution.py:29
  71.5 4.5 %collective-permute-start.18 = (bf16[1024,256]{1,0:T(8,128)(2,1)S(1)}, bf16[1024,256]{1,0:T(8,128)(2,1)S(1)}, u32[]{:S(2)}, u32[]{:S(2)}) collective-permute-start(bf16[1024,256]{1,0:T(8,128)(2,1)S(1)} %get-tuple-element.52), channel_id=1, source_target_pairs={{0,32},{32,64},{64,96},{96,0},{1,33},{33,65},{65,97},{97,1},{2,34}... | collective-permute-start | bytes 1572872 | tf_op jit(solution)/shard_map/ppermute | solution.py:29
  78.9 2.1 %collective-permute-done.8.refs_2_ = bf16[1040,256]{1,0:T(8,128)(2,1)S(1)} collective-permute-done((bf16[1040,256]{1,0:T(8,128)(2,1)S(1)}, bf16[1040,256]{1,0:T(8,128)(2,1)S(1)}, u32[]{:S(2)}, u32[]{:S(2)}) %collective-permute-start.8) | collective-permute-done | bytes 532512 | tf_op jit(solution)/shard_map/ppermute | solution.py:29
  83.1 3.3 %collective-permute-start.16 = (bf16[272,256]{1,0:T(8,128)(2,1)S(1)}, bf16[272,256]{1,0:T(8,128)(2,1)S(1)}, u32[]{:S(2)}, u32[]{:S(2)}) collective-permute-start(bf16[272,256]{1,0:T(8,128)(2,1)S(1)} %get-tuple-element.50), channel_id=1, source_target_pairs={{0,16},{8,24},{16,0},{24,8},{1,17},{9,25},{17,1},{25,9},{2,18},{10... | collective-permute-start | bytes 417800 | tf_op jit(solution)/shard_map/ppermute | solution.py:29
  89.4 7.8 %stage_unembed.1.refs_7_.stage = bf16[2048,2048]{1,0:T(8,128)(2,1)} custom-call(s32[6]{0:T(128)S(1)} %stack.43.place, bf16[4,4,2,128,2048]{4,3,2,1,0:T(8,128)(2,1)} %bitcast.16, bf16[4,4,2,128,2048]{4,3,2,1,0:T(8,128)(2,1)} %bitcast.17, bf16[4,4,2,128,2048]{4,3,2,1,0:T(8,128)(2,1)} %bitcast.18, bf16[4,4,2,128,2048]{4,3,2,1,0:T(8,128)(2,1)} %bitcast.19, ...), custom_call_target="tpu_custom_call" | custom-call | bytes 16777216 | tf_op jit(solution)/shard_map/stage_unembed/pallas_call | solution.py:381
  97.3 6.2 %collective-permute-done.19.refs_5_.refs_3_ = bf16[1024,256]{1,0:T(8,128)(2,1)S(1)} collective-permute-done((bf16[1024,256]{1,0:T(8,128)(2,1)S(1)}, bf16[1024,256]{1,0:T(8,128)(2,1)S(1)}, u32[]{:S(2)}, u32[]{:S(2)}) %collective-permute-start.19) | collective-permute-done | bytes 524320 | tf_op jit(solution)/shard_map/ppermute | solution.py:29
  103.5 3.4 %copy-done.1 = bf16[2048,2048]{1,0:T(8,128)(2,1)S(1)} copy-done((bf16[2048,2048]{1,0:T(8,128)(2,1)S(1)}, bf16[2048,2048]{1,0:T(8,128)(2,1)}, u32[]{:S(2)}) %copy-start.1) | copy-done | bytes 8388632
  111.8 3.3 %collective-permute-start.22 = (bf16[256,256]{1,0:T(8,128)(2,1)S(1)}, bf16[256,256]{1,0:T(8,128)(2,1)S(1)}, u32[]{:S(2)}, u32[]{:S(2)}) collective-permute-start(bf16[256,256]{1,0:T(8,128)(2,1)S(1)} %get-tuple-element.60), channel_id=1, source_target_pairs={{0,16},{8,24},{16,0},{24,8},{1,17},{9,25},{17,1},{25,9},{2,18},{10... | collective-permute-start | bytes 393224 | tf_op jit(solution)/shard_map/ppermute | solution.py:29
  115.8 3.0 %early_hidden.1.refs_6_.early = f32[2048,512]{1,0:T(8,128)S(1)} custom-call(s32[6]{0:T(128)S(1)} %stack.43.place, bf16[2048,2048]{1,0:T(8,128)(2,1)S(1)} %copy-done.2, bf16[1024,256]{1,0:T(8,128)(2,1)S(1)} %get-tuple-element.62.mine, bf16[1024,256]{1,0:T(8,128)(2,1)S(1)} %collective-permute-done.24.other), custom_call_target="tpu_custom_call" | custom-call | flops 2147483648 | bytes 12582912 | tf_op jit(solution)/shard_map/early_hidden/pallas_call | solution.py:407
  118.8 2.7 %collective-permute-done.22.refs_4_ = bf16[256,256]{1,0:T(8,128)(2,1)S(1)} collective-permute-done((bf16[256,256]{1,0:T(8,128)(2,1)S(1)}, bf16[256,256]{1,0:T(8,128)(2,1)S(1)}, u32[]{:S(2)}, u32[]{:S(2)}) %collective-permute-start.22) | collective-permute-done | bytes 131104 | tf_op jit(solution)/shard_map/ppermute | solution.py:29
  125.5 3.0 %late_hidden.1 = (bf16[528,512]{1,0:T(8,128)(2,1)S(1)}, bf16[528,512]{1,0:T(8,128)(2,1)S(1)}, bf16[528,512]{1,0:T(8,128)(2,1)S(1)}, bf16[528,512]{1,0:T(8,128)(2,1)S(1)}) custom-call(s32[6]{0:T(128)S(1)} %stack.43.place, bf16[2048,2048]{1,0:T(8,128)(2,1)S(1)} %copy-done.2, bf16[1040,256]{1,0:T(8,128)(2,1)S(1)} %logit_grad.3.mine, ...), custom_call_target="tpu_custom_call" | custom-call | flops 2147483648 | bytes 10485760 | tf_op jit(solution)/shard_map/late_hidden/pallas_call | solution.py:436
  132.6 5.7 %collective-permute-done.26.refs_1_ = bf16[528,512]{1,0:T(8,128)(2,1)S(1)} collective-permute-done((bf16[528,512]{1,0:T(8,128)(2,1)S(1)}, bf16[528,512]{1,0:T(8,128)(2,1)S(1)}, u32[]{:S(2)}, u32[]{:S(2)}) %collective-permute-start.26) | collective-permute-done | bytes 540704 | tf_op jit(solution)/shard_map/ppermute | solution.py:546
  138.3 6.2 %collective-permute-done.27.refs_2_ = bf16[528,512]{1,0:T(8,128)(2,1)S(1)} collective-permute-done((bf16[528,512]{1,0:T(8,128)(2,1)S(1)}, bf16[528,512]{1,0:T(8,128)(2,1)S(1)}, u32[]{:S(2)}, u32[]{:S(2)}) %collective-permute-start.27) | collective-permute-done | bytes 540704 | tf_op jit(solution)/shard_map/ppermute | solution.py:546
  146.6 2.6 %collective-permute-start.30 = (bf16[144,512]{1,0:T(8,128)(2,1)S(1)}, bf16[144,512]{1,0:T(8,128)(2,1)S(1)}, u32[]{:S(2)}, u32[]{:S(2)}) collective-permute-start(bf16[144,512]{1,0:T(8,128)(2,1)S(1)} %get-tuple-element.69), channel_id=1, source_target_pairs={{0,16},{1,65},{8,24},{9,73},{16,0},{17,81},{24,8},{25,89},{32,48},... | collective-permute-start | bytes 442376 | tf_op jit(solution)/shard_map/ppermute | solution.py:546
  150.9 2.7 %collective-permute-done.30.refs_2_ = bf16[144,512]{1,0:T(8,128)(2,1)S(1)} collective-permute-done((bf16[144,512]{1,0:T(8,128)(2,1)S(1)}, bf16[144,512]{1,0:T(8,128)(2,1)S(1)}, u32[]{:S(2)}, u32[]{:S(2)}) %collective-permute-start.30) | collective-permute-done | bytes 147488 | tf_op jit(solution)/shard_map/ppermute | solution.py:546
  154.3 2.4 %collective-permute-start.32 = (bf16[128,256]{1,0:T(8,128)(2,1)S(1)}, bf16[128,256]{1,0:T(8,128)(2,1)S(1)}, u32[]{:S(2)}, u32[]{:S(2)}) collective-permute-start(bf16[128,256]{1,0:T(8,128)(2,1)S(1)} %get-tuple-element.72), channel_id=1, source_target_pairs={{0,1},{1,0},{2,3},{3,2},{4,5},{5,4},{6,7},{7,6},{8,9},{9,8},{10,11... | collective-permute-start | bytes 196616 | tf_op jit(solution)/shard_map/ppermute | solution.py:33
  (90 shorter events, 54.8 us)
Async XLA Ops:
  3.2 34.4 %collective-permute-start.3 = (bf16[1088,256]{1,0:T(8,128)(2,1)}, bf16[1088,256]{1,0:T(8,128)(2,1)}, u32[]{:S(2)}, u32[]{:S(2)}) collective-permute-start(bf16[1088,256]{1,0:T(8,128)(2,1)} %prepare_weights.1.rest_0_), channel_id=1, source_target_pairs={{0,1},{1,0},{2,3},{3,2},{4,5},{5,4},{6,7},{7,6},{8,9},{9,8},{10,11... | collective-permute-start | bytes 1671176 | tf_op jit(solution)/shard_map/ppermute | solution.py:33
  4.6 26.7 %collective-permute-start.2 = (bf16[1088,256]{1,0:T(8,128)(2,1)}, bf16[1088,256]{1,0:T(8,128)(2,1)S(1)}, u32[]{:S(2)}, u32[]{:S(2)}) collective-permute-start(bf16[1088,256]{1,0:T(8,128)(2,1)} %prepare_weights.1.rest_0_), channel_id=1, source_target_pairs={{0,6},{2,0},{4,2},{6,4},{1,7},{3,1},{5,3},{7,5},{8,14},{10,8},{12,... | collective-permute-start | bytes 1671176 | tf_op jit(solution)/shard_map/ppermute | solution.py:29
  7.2 24.2 %collective-permute-start.1 = (bf16[1088,256]{1,0:T(8,128)(2,1)}, bf16[1088,256]{1,0:T(8,128)(2,1)}, u32[]{:S(2)}, u32[]{:S(2)}) collective-permute-start(bf16[1088,256]{1,0:T(8,128)(2,1)} %prepare_weights.1.rest_0_), channel_id=1, source_target_pairs={{0,4},{2,6},{4,0},{6,2},{1,5},{3,7},{5,1},{7,3},{8,12},{10,14},{12... | collective-permute-start | bytes 1671176 | tf_op jit(solution)/shard_map/ppermute | solution.py:29
  7.7 27.7 %collective-permute-start = (bf16[1088,256]{1,0:T(8,128)(2,1)}, bf16[1088,256]{1,0:T(8,128)(2,1)S(1)}, u32[]{:S(2)}, u32[]{:S(2)}) collective-permute-start(bf16[1088,256]{1,0:T(8,128)(2,1)} %prepare_weights.1.rest_0_), channel_id=1, source_target_pairs={{0,2},{2,4},{4,6},{6,0},{1,3},{3,5},{5,7},{7,1},{8,10},{10,12},{12... | collective-permute-start | bytes 1671176 | tf_op jit(solution)/shard_map/ppermute | solution.py:29
  37.2 13.9 %collective-permute-start.11 = (bf16[1024,256]{1,0:T(8,128)(2,1)}, bf16[1024,256]{1,0:T(8,128)(2,1)}, u32[]{:S(2)}, u32[]{:S(2)}) collective-permute-start(bf16[1024,256]{1,0:T(8,128)(2,1)} %slice_weights.1.refs_0_), channel_id=1, source_target_pairs={{0,6},{2,0},{4,2},{6,4},{1,7},{3,1},{5,3},{7,5},{8,14},{10,8},{12,... | collective-permute-start | bytes 1572872 | tf_op jit(solution)/shard_map/ppermute | solution.py:29
  37.6 14.8 %collective-permute-start.10 = (bf16[1024,256]{1,0:T(8,128)(2,1)}, bf16[1024,256]{1,0:T(8,128)(2,1)}, u32[]{:S(2)}, u32[]{:S(2)}) collective-permute-start(bf16[1024,256]{1,0:T(8,128)(2,1)} %slice_weights.1.refs_0_), channel_id=1, source_target_pairs={{0,2},{2,4},{4,6},{6,0},{1,3},{3,5},{5,7},{7,1},{8,10},{10,12},{12... | collective-permute-start | bytes 1572872 | tf_op jit(solution)/shard_map/ppermute | solution.py:29
  44.5 16.8 %collective-permute-start.7 = (bf16[1040,256]{1,0:T(8,128)(2,1)S(1)}, bf16[1040,256]{1,0:T(8,128)(2,1)S(1)}, u32[]{:S(2)}, u32[]{:S(2)}) collective-permute-start(bf16[1040,256]{1,0:T(8,128)(2,1)S(1)} %get-tuple-element.42), channel_id=1, source_target_pairs={{0,32},{32,64},{64,96},{96,0},{1,33},{33,65},{65,97},{97,1},{2,34}... | collective-permute-start | bytes 1597448 | tf_op jit(solution)/shard_map/ppermute | solution.py:29
  49.6 13.0 %collective-permute-start.9 = (bf16[1040,256]{1,0:T(8,128)(2,1)S(1)}, bf16[1040,256]{1,0:T(8,128)(2,1)S(1)}, u32[]{:S(2)}, u32[]{:S(2)}) collective-permute-start(bf16[1040,256]{1,0:T(8,128)(2,1)S(1)} %get-tuple-element.44), channel_id=1, source_target_pairs={{0,96},{32,0},{64,32},{96,64},{1,97},{33,1},{65,33},{97,65},{2,98}... | collective-permute-start | bytes 1597448 | tf_op jit(solution)/shard_map/ppermute | solution.py:29
  53.4 8.0 %collective-permute-start.12 = (bf16[512,256]{1,0:T(8,128)(2,1)S(1)}, bf16[512,256]{1,0:T(8,128)(2,1)S(1)}, u32[]{:S(2)}, u32[]{:S(2)}) collective-permute-start(bf16[512,256]{1,0:T(8,128)(2,1)S(1)} %get-tuple-element.45), channel_id=1, source_target_pairs={{0,2},{2,4},{4,6},{6,0},{1,3},{3,5},{5,7},{7,1},{8,10},{10,12},{12... | collective-permute-start | bytes 786440 | tf_op jit(solution)/shard_map/ppermute | solution.py:29
  53.5 7.9 %collective-permute-start.13 = (bf16[512,256]{1,0:T(8,128)(2,1)S(1)}, bf16[512,256]{1,0:T(8,128)(2,1)S(1)}, u32[]{:S(2)}, u32[]{:S(2)}) collective-permute-start(bf16[512,256]{1,0:T(8,128)(2,1)S(1)} %get-tuple-element.46), channel_id=1, source_target_pairs={{0,6},{2,0},{4,2},{6,4},{1,7},{3,1},{5,3},{7,5},{8,14},{10,8},{12,... | collective-permute-start | bytes 786440 | tf_op jit(solution)/shard_map/ppermute | solution.py:29
  65.8 15.2 %collective-permute-start.8 = (bf16[1040,256]{1,0:T(8,128)(2,1)S(1)}, bf16[1040,256]{1,0:T(8,128)(2,1)S(1)}, u32[]{:S(2)}, u32[]{:S(2)}) collective-permute-start(bf16[1040,256]{1,0:T(8,128)(2,1)S(1)} %get-tuple-element.43), channel_id=1, source_target_pairs={{0,64},{32,96},{64,0},{96,32},{1,65},{33,97},{65,1},{97,33},{2,66}... | collective-permute-start | bytes 1597448 | tf_op jit(solution)/shard_map/ppermute | solution.py:29
  71.5 25.7 %collective-permute-start.18 = (bf16[1024,256]{1,0:T(8,128)(2,1)S(1)}, bf16[1024,256]{1,0:T(8,128)(2,1)S(1)}, u32[]{:S(2)}, u32[]{:S(2)}) collective-permute-start(bf16[1024,256]{1,0:T(8,128)(2,1)S(1)} %get-tuple-element.52), channel_id=1, source_target_pairs={{0,32},{32,64},{64,96},{96,0},{1,33},{33,65},{65,97},{97,1},{2,34}... | collective-permute-start | bytes 1572872 | tf_op jit(solution)/shard_map/ppermute | solution.py:29
  76.0 27.5 %collective-permute-start.19 = (bf16[1024,256]{1,0:T(8,128)(2,1)S(1)}, bf16[1024,256]{1,0:T(8,128)(2,1)S(1)}, u32[]{:S(2)}, u32[]{:S(2)}) collective-permute-start(bf16[1024,256]{1,0:T(8,128)(2,1)S(1)} %get-tuple-element.53), channel_id=1, source_target_pairs={{0,64},{32,96},{64,0},{96,32},{1,65},{33,97},{65,1},{97,33},{2,66}... | collective-permute-start | bytes 1572872 | tf_op jit(solution)/shard_map/ppermute | solution.py:29
  76.9 26.6 %collective-permute-start.20 = (bf16[1024,256]{1,0:T(8,128)(2,1)S(1)}, bf16[1024,256]{1,0:T(8,128)(2,1)S(1)}, u32[]{:S(2)}, u32[]{:S(2)}) collective-permute-start(bf16[1024,256]{1,0:T(8,128)(2,1)S(1)} %get-tuple-element.54), channel_id=1, source_target_pairs={{0,96},{32,0},{64,32},{96,64},{1,97},{33,1},{65,33},{97,65},{2,98}... | collective-permute-start | bytes 1572872 | tf_op jit(solution)/shard_map/ppermute | solution.py:29
  83.1 14.1 %collective-permute-start.16 = (bf16[272,256]{1,0:T(8,128)(2,1)S(1)}, bf16[272,256]{1,0:T(8,128)(2,1)S(1)}, u32[]{:S(2)}, u32[]{:S(2)}) collective-permute-start(bf16[272,256]{1,0:T(8,128)(2,1)S(1)} %get-tuple-element.50), channel_id=1, source_target_pairs={{0,16},{8,24},{16,0},{24,8},{1,17},{9,25},{17,1},{25,9},{2,18},{10... | collective-permute-start | bytes 417800 | tf_op jit(solution)/shard_map/ppermute | solution.py:29
  88.0 9.3 %collective-permute-start.17 = (bf16[272,256]{1,0:T(8,128)(2,1)S(1)}, bf16[272,256]{1,0:T(8,128)(2,1)S(1)}, u32[]{:S(2)}, u32[]{:S(2)}) collective-permute-start(bf16[272,256]{1,0:T(8,128)(2,1)S(1)} %get-tuple-element.51), channel_id=1, source_target_pairs={{0,24},{8,0},{16,8},{24,16},{1,25},{9,1},{17,9},{25,17},{2,26},{10... | collective-permute-start | bytes 417800 | tf_op jit(solution)/shard_map/ppermute | solution.py:29
  108.5 7.3 %collective-permute-start.24 = (bf16[1024,256]{1,0:T(8,128)(2,1)S(1)}, bf16[1024,256]{1,0:T(8,128)(2,1)S(1)}, u32[]{:S(2)}, u32[]{:S(2)}) collective-permute-start(bf16[1024,256]{1,0:T(8,128)(2,1)S(1)} %get-tuple-element.62.mine), channel_id=1, source_target_pairs={{0,1},{1,0},{2,3},{3,2},{4,5},{5,4},{6,7},{7,6},{8,9},{9,8},{10,11... | collective-permute-start | bytes 1572872 | tf_op jit(solution)/shard_map/ppermute | solution.py:33
  110.6 8.2 %collective-permute-start.21 = (bf16[256,256]{1,0:T(8,128)(2,1)S(1)}, bf16[256,256]{1,0:T(8,128)(2,1)S(1)}, u32[]{:S(2)}, u32[]{:S(2)}) collective-permute-start(bf16[256,256]{1,0:T(8,128)(2,1)S(1)} %get-tuple-element.59), channel_id=1, source_target_pairs={{0,8},{8,16},{16,24},{24,0},{1,9},{9,17},{17,25},{25,1},{2,10},{10... | collective-permute-start | bytes 393224 | tf_op jit(solution)/shard_map/ppermute | solution.py:29
  111.8 9.8 %collective-permute-start.22 = (bf16[256,256]{1,0:T(8,128)(2,1)S(1)}, bf16[256,256]{1,0:T(8,128)(2,1)S(1)}, u32[]{:S(2)}, u32[]{:S(2)}) collective-permute-start(bf16[256,256]{1,0:T(8,128)(2,1)S(1)} %get-tuple-element.60), channel_id=1, source_target_pairs={{0,16},{8,24},{16,0},{24,8},{1,17},{9,25},{17,1},{25,9},{2,18},{10... | collective-permute-start | bytes 393224 | tf_op jit(solution)/shard_map/ppermute | solution.py:29
  115.1 6.5 %collective-permute-start.23 = (bf16[256,256]{1,0:T(8,128)(2,1)S(1)}, bf16[256,256]{1,0:T(8,128)(2,1)S(1)}, u32[]{:S(2)}, u32[]{:S(2)}) collective-permute-start(bf16[256,256]{1,0:T(8,128)(2,1)S(1)} %get-tuple-element.61), channel_id=1, source_target_pairs={{0,24},{8,0},{16,8},{24,16},{1,25},{9,1},{17,9},{25,17},{2,26},{10... | collective-permute-start | bytes 393224 | tf_op jit(solution)/shard_map/ppermute | solution.py:29
  128.5 9.8 %collective-permute-start.26 = (bf16[528,512]{1,0:T(8,128)(2,1)S(1)}, bf16[528,512]{1,0:T(8,128)(2,1)S(1)}, u32[]{:S(2)}, u32[]{:S(2)}) collective-permute-start(bf16[528,512]{1,0:T(8,128)(2,1)S(1)} %get-tuple-element.64), channel_id=1, source_target_pairs={{0,32},{1,9},{8,40},{9,17},{16,48},{17,25},{24,56},{25,1},{32,64},... | collective-permute-start | bytes 1622024 | tf_op jit(solution)/shard_map/ppermute | solution.py:546
  129.5 14.9 %collective-permute-start.27 = (bf16[528,512]{1,0:T(8,128)(2,1)S(1)}, bf16[528,512]{1,0:T(8,128)(2,1)S(1)}, u32[]{:S(2)}, u32[]{:S(2)}) collective-permute-start(bf16[528,512]{1,0:T(8,128)(2,1)S(1)} %get-tuple-element.65), channel_id=1, source_target_pairs={{0,64},{1,17},{8,72},{9,25},{16,80},{17,1},{24,88},{25,9},{32,96},... | collective-permute-start | bytes 1622024 | tf_op jit(solution)/shard_map/ppermute | solution.py:546
  131.6 13.1 %collective-permute-start.28 = (bf16[528,512]{1,0:T(8,128)(2,1)S(1)}, bf16[528,512]{1,0:T(8,128)(2,1)S(1)}, u32[]{:S(2)}, u32[]{:S(2)}) collective-permute-start(bf16[528,512]{1,0:T(8,128)(2,1)S(1)} %get-tuple-element.66), channel_id=1, source_target_pairs={{0,96},{1,25},{8,104},{9,1},{16,112},{17,9},{24,120},{25,17},{32,0... | collective-permute-start | bytes 1622024 | tf_op jit(solution)/shard_map/ppermute | solution.py:546
  146.6 7.0 %collective-permute-start.30 = (bf16[144,512]{1,0:T(8,128)(2,1)S(1)}, bf16[144,512]{1,0:T(8,128)(2,1)S(1)}, u32[]{:S(2)}, u32[]{:S(2)}) collective-permute-start(bf16[144,512]{1,0:T(8,128)(2,1)S(1)} %get-tuple-element.69), channel_id=1, source_target_pairs={{0,16},{1,65},{8,24},{9,73},{16,0},{17,81},{24,8},{25,89},{32,48},... | collective-permute-start | bytes 442376 | tf_op jit(solution)/shard_map/ppermute | solution.py:546
  (19 other events, 123.0 us)

commit v6 on v5

--- a/solution.py
+++ b/solution.py
@@ -153,7 +153,8 @@
     mine, other, rest = rest[:number], rest[number : 2 * number], rest[2 * number :]
     if with_stats:
         before, rest = rest[0], rest[1:]
-    outs, rest = rest[:SIDE], rest[SIDE:]
+    first = len(rest) - (SIDE + 5 if with_stats else SIDE + 3)
+    outs, rest = rest[first : first + SIDE + 1], rest[first + SIDE + 1 :]
     weights, total = rest[:2]
     block = weights.shape[0] * 64
     width = weights.shape[2]
@@ -194,18 +195,24 @@
         return carry
 
     lax.fori_loop(0, count[0], tile, 0)
+    half = rows // 2
     for step in range(SIDE):
         start = lax.rem(vocab_y + step, SIDE) * SIDE
         for z in range(SIDE):
-            outs[step][z * rows : z * rows + rows, :] = total[start + z].astype(BF16)
+            value = total[start + z].astype(BF16)
+            if step == 2:
+                outs[3][z * half : z * half + half, :] = value[:half]
+                outs[4][z * half : z * half + half, :] = value[half:]
+            else:
+                outs[step - step // 3][z * rows : z * rows + rows, :] = value
     if with_stats:
         sent = line[0:1] + line[1:2] + line[2:3]
         packed = pack_rows([before[0:1], before[1:2], sent, before[3:4], before[4:5]])
-        for out in outs:
-            out[SIDE * rows : SIDE * rows + 16, :] = packed
-
-
-def products(place, pairs, count, probs, mine, other, before=None):
+        for out in outs[3:]:
+            out[SIDE * half : SIDE * half + 16, :] = packed
+
+
+def products(place, pairs, count, probs, mine, other, before=None, behind=()):
     rows = probs.shape[0]
     depth, width = sum(part.shape[0] for part in mine) // SIDE, mine[0].shape[1]
     extra = [] if before is None else [before]
@@ -217,16 +224,17 @@
         scratch += [pltpu.VMEM((2, 64, 512), F32), pltpu.VMEM((8, rows), F32)]
     return pl.pallas_call(
         functools.partial(product_kernel, len(mine), bool(extra)),
-        out_shape=[jax.ShapeDtypeStruct((SIDE * rows + 16 * len(extra), width), BF16)] * SIDE,
-        in_specs=[SMEM, SMEM, SMEM] + [VMEM] * (1 + 2 * len(mine) + len(extra)),
-        out_specs=[VMEM] * SIDE,
+        out_shape=[jax.ShapeDtypeStruct((SIDE * rows, width), BF16)] * 3
+        + [jax.ShapeDtypeStruct((SIDE * rows // 2 + 16 * len(extra), width), BF16)] * 2,
+        in_specs=[SMEM, SMEM, SMEM] + [VMEM] * (1 + 2 * len(mine) + len(extra)) + [ANY] * len(behind),
+        out_specs=[VMEM] * (SIDE + 1),
         scratch_shapes=scratch,
         compiler_params=params(24),
         cost_estimate=cost(
             16 * 2 * rows * 512 * width, 2 * probs.size + 16 * depth * width + 32 * rows * width
         ),
         name="tile_products",
-    )(place, pairs, count, probs, *mine, *other, *extra)
+    )(place, pairs, count, probs, *mine, *other, *extra, *behind)
 
 
 def pack_rows(lines):
@@ -258,42 +266,103 @@
     return jnp.concatenate(lines, axis=0).T
 
 
-def merge_kernel(with_stats, place, *refs):
+def relay_kernel(with_stats, *refs):
     if with_stats:
-        parts, outs, kept = refs[:SIDE], refs[-1 - SIDE : -1], refs[-1]
+        near, far, from_left, from_right, mine = refs[:5]
+        near_out, far_out, kept, table_out = refs[-4:]
+        depth = from_left.shape[0] - 16
+        rows = 2 * depth // SIDE
+        stats = [unpack_rows(part[depth:, :], 5) for part in (mine, from_left, from_right)]
+        kept[...] = jnp.concatenate(stats[0] + stats[1] + stats[2] + [jnp.zeros((1, rows), F32)], axis=0)
+        own, left, right = (line[0] for line in stats)
+        lane = lax.broadcasted_iota(jnp.int32, own.shape, 1)
+        other = jnp.where(lane < rows // 2, left, right)
+        peak = jnp.maximum(own, other)
+        table = columns_of([jnp.exp(own - peak), jnp.exp(other - peak)])
+        table_out[...] = table
+        near_out[SIDE * rows : SIDE * rows + 16, :] = from_left[depth : depth + 16, :]
+    else:
+        near, far, from_left, from_right, table = refs[:5]
+        near_out, far_out = refs[-2:]
+        table = table[...]
+        depth = from_left.shape[0]
+        rows = 2 * depth // SIDE
+    half = rows // 2
+    for z in range(SIDE):
+        low, high = slice(z * rows, z * rows + half), slice(z * rows + half, (z + 1) * rows)
+        part = slice(z * half, (z + 1) * half)
+        value = table[:half, 0:1] * near[low, :].astype(F32) + table[:half, 1:2] * from_left[part, :].astype(F32)
+        near_out[low, :] = value.astype(BF16)
+        near_out[high, :] = near[high, :]
+        value = table[half:, 0:1] * far[high, :].astype(F32) + table[half:, 1:2] * from_right[part, :].astype(F32)
+        far_out[high, :] = value.astype(BF16)
+        far_out[low, :] = far[low, :]
+
+
+def relayed(near, far, from_left, from_right, last, first, behind=()):
+    depth, width = near.shape
+    rows = depth // SIDE
+    outs = [
+        jax.ShapeDtypeStruct((depth + (16 if first else 0), width), BF16),
+        jax.ShapeDtypeStruct((depth, width), BF16),
+    ]
+    if first:
+        outs.append(jax.ShapeDtypeStruct((16, rows), F32))
+        outs.append(jax.ShapeDtypeStruct((rows, 128), F32))
+    return pl.pallas_call(
+        functools.partial(relay_kernel, first),
+        out_shape=outs,
+        in_specs=[VMEM] * 5 + [ANY] * len(behind),
+        out_specs=[VMEM] * len(outs),
+        compiler_params=params(),
+        cost_estimate=cost(depth * width, depth * width),
+        name="relay_targets",
+    )(near, far, from_left, from_right, last, *behind)
+
+
+def merge_kernel(with_stats, place, given, *refs):
+    parts = refs[:3]
+    if with_stats:
+        outs, kept = refs[-1 - SIDE : -1], refs[-1]
         rows = outs[0].shape[0] - 16
-        stats, factors = joined([unpack_rows(part[SIDE * rows :, :], 5) for part in parts])
+        lines = [[given[5 * i + j : 5 * i + j + 1] for j in range(5)] for i in range(3)]
+        lines.append(unpack_rows(parts[1][SIDE * rows :, :], 5))
+        stats, _ = joined(lines)
         packed = pack_rows(stats)
         for out in outs:
             out[rows : rows + 16, :] = packed
-        table = columns_of(factors)
+        own, left, right, across = (line[0] for line in lines)
+        lane = lax.broadcasted_iota(jnp.int32, own.shape, 1)
+        low = lane < rows // 2
+        left = jnp.where(low, jnp.maximum(left, across), left)
+        right = jnp.where(low, right, jnp.maximum(right, across))
+        table = columns_of([jnp.exp(base - stats[0]) for base in (own, left, right)])
         kept[...] = table
     else:
-        table, parts, outs = refs[0][...], refs[1 : 1 + SIDE], refs[-SIDE:]
+        table, outs = given[...], refs[-SIDE:]
         rows = outs[0].shape[0]
     for step in range(SIDE):
         at = pl.ds(pl.multiple_of(lax.rem(place[1] + step, SIDE) * rows, rows), rows)
         value = table[:, 0:1] * parts[0][at, :].astype(F32)
-        for d in range(1, SIDE):
+        for d in range(1, 3):
             value += table[:, d : d + 1] * parts[d][at, :].astype(F32)
         outs[step][0:rows, :] = value.astype(BF16)
 
 
-def merged(place, parts, rows, table=None, behind=()):
+def merged(place, given, parts, rows, first, behind=()):
     width = parts[0].shape[1]
-    first = table is None
     outs = [jax.ShapeDtypeStruct((rows + (16 if first else 0), width), BF16)] * SIDE
     if first:
         outs = outs + [jax.ShapeDtypeStruct((rows, 128), F32)]
     return pl.pallas_call(
         functools.partial(merge_kernel, first),
         out_shape=outs,
-        in_specs=[SMEM] + [VMEM] * (SIDE if first else 1 + SIDE) + [ANY] * len(behind),
+        in_specs=[SMEM] + [VMEM] * 4 + [ANY] * len(behind),
         out_specs=[VMEM] * len(outs),
         compiler_params=params(),
         cost_estimate=cost(rows * width, rows * width),
         name="merge_targets",
-    )(place, *([] if first else [table]), *parts, *behind)
+    )(place, given, *parts, *behind)
 
 
 def gradient_kernel(offset, with_stats, place, logits, *refs):
@@ -354,43 +423,45 @@
     out[:, pl.ds(pl.multiple_of((1 - core) * rows, rows), rows)] = other[0:depth, :]
 
 
-def stage_kernel(place, *refs):
-    unembed, stage = refs[:SIDE], refs[-1]
-    half = stage.shape[1] // 2
-    width = half // SIDE
-    for owner in range(SIDE):
-        rows = slice(owner * 128, owner * 128 + 128)
-        block = unembed[owner][...].reshape(128, 2 * half)
-        for b in range(SIDE):
-            for c in range(2):
-                part = block[:, (2 * b + c) * width : (2 * b + c + 1) * width]
-                stage[rows, c * half + b * width : c * half + (b + 1) * width] = part
+def stage_kernel(place, unembed, *refs):
+    stage, sems = refs[-2:]
+    first = place[3] == 0
+    copies = []
+    for major in range(SIDE):
+        for minor in range(SIDE):
+            index = major * SIDE + minor
+            owner = jnp.where(first, index, minor * SIDE + major)
+            start = pl.multiple_of(owner * 256 + place[3] * 128, 128)
+            copies.append(
+                pltpu.make_async_copy(
+                    unembed.at[pl.ds(start, 128), :],
+                    stage.at[pl.ds(index * 128, 128), :],
+                    sems.at[index],
+                )
+            )
+    for copy in copies:
+        copy.start()
+    for copy in copies:
+        copy.wait()
 
 
 def staged(place, unembed, behind):
     depth, cols = unembed.shape
-    unembed = unembed.reshape(SIDE, SIDE, 2, 128, cols)
-
-    def where(i, p, k):
-        first = p[3] == 0
-        return (jnp.where(first, i, k), jnp.where(first, k, i), p[3], 0, 0)
-
-    views = [
-        pl.BlockSpec((1, 1, 1, 128, cols), lambda i, p, k=k: where(i, p, k)) for k in range(SIDE)
-    ]
     return pl.pallas_call(
         stage_kernel,
-        grid_spec=pltpu.PrefetchScalarGridSpec(
-            num_scalar_prefetch=1,
-            grid=(SIDE,),
-            in_specs=views + [ANY] * len(behind),
-            out_specs=pl.BlockSpec((512, cols), lambda i, p: (i, 0)),
-        ),
         out_shape=jax.ShapeDtypeStruct((depth // 2, cols), BF16),
-        compiler_params=params(48),
-        cost_estimate=cost(0, 2 * depth * cols),
+        in_specs=[SMEM, pl.BlockSpec(memory_space=pltpu.HBM)] + [ANY] * len(behind),
+        out_specs=VMEM,
+        scratch_shapes=[pltpu.SemaphoreType.DMA((SIDE * SIDE,))],
+        compiler_params=params(42),
+        cost_estimate=cost(0, depth * cols),
         name="stage_unembed",
-    )(place, *[unembed] * SIDE, *behind)
+    )(place, unembed, *behind)
+
+
+def columns_at(stage, rows, chunk, width):
+    parts = [stage[rows, (2 * b + chunk) * width : (2 * b + chunk + 1) * width] for b in range(SIDE)]
+    return jnp.concatenate(parts, axis=1)
 
 
 def early_kernel(place, stage, mine, other, out, both):
@@ -398,7 +469,9 @@
     both_cores(place[3], mine, other, depth, both)
     for step in range(SIDE):
         rows = slice(step * 512, step * 512 + 512)
-        out[rows, :] = jnp.dot(stage[rows, 0:depth], both[...], preferred_element_type=F32)
+        out[rows, :] = jnp.dot(
+            columns_at(stage, rows, 0, depth // SIDE), both[...], preferred_element_type=F32
+        )
 
 
 def early_hidden(place, stage, mine, other):
@@ -423,7 +496,9 @@
     both_cores(place[3], mine, other, depth, both)
     for step in range(SIDE):
         at = pl.ds(pl.multiple_of(lax.rem(place[4] + step, SIDE) * 512, 512), 512)
-        result = jnp.dot(stage[at, depth : 2 * depth], both[...], preferred_element_type=F32)
+        result = jnp.dot(
+            columns_at(stage, at, 1, depth // SIDE), both[...], preferred_element_type=F32
+        )
         outs[step][0:512, :] = (early[at, :] + result).astype(BF16)
         for part, core in ((mine, place[3]), (other, 1 - place[3])):
             lanes = pl.ds(pl.multiple_of(core * rows, rows), rows)
@@ -569,23 +644,29 @@
     piece = prepared(tile_weights, width)
     mine = [piece, *gated(spread([piece] * SIDE, "tx")[1:], [mass, smass])]
     other = [swap(piece) for piece in mine]
-    parts = products(place, tile_pairs, tile_count, probs, mine, other, before)
 
     piece = sliced(tile_weights, width, width, [mine[1]])
     right, left = send(piece, "tx", 1), send(piece, "tx", 3)
+    parts = products(place, tile_pairs, tile_count, probs, mine, other, before, [piece])
     top, low = halves(right, left, [parts[0]])
-    parts = spread(parts, "vy")
+    own, near, far, to_right, to_left = parts
+    left_part, right_part = send(to_right, "vy", 1), send(to_left, "vy", 3)
+    near, far, given, factors = relayed(near, far, left_part, right_part, to_right, True, [right, left])
     pieces = [piece, right, send(top, "tx", 1), send(low, "tx", 3), left]
-    mine = packed_pieces(pieces, [parts[1], parts[3]])
+    near, far = send(near, "vy", 1), send(far, "vy", 3)
+    mine = packed_pieces(pieces, [near, far])
     later = products(place, tile_pairs, tile_count, probs, [mine], [swap(mine)])
 
-    *parts, factors = merged(place, parts, rows, None, [later[0]])
-    later = spread(later, "vy")
+    *parts, scales = merged(place, given, [own, near, far], rows, True, [later[0]])
+    own, near, far, to_right, to_left = later
+    left_part, right_part = send(to_right, "vy", 1), send(to_left, "vy", 3)
+    near, far = relayed(near, far, left_part, right_part, factors, False)
+    later = [own, send(near, "vy", 1), send(far, "vy", 3)]
     stage = staged(place, student_unembed, [parts[0]])
     grad, *before = gradients(0, place, logits, spread(parts, "vz"), (), later[1:] + [stage])
     early = early_hidden(place, stage, grad, swap(grad))
     before = [before[1], before[0]]
-    parts = merged(place, later, rows, factors)
+    parts = merged(place, scales, later, rows, False)
     (grad,) = gradients(width, place, logits, spread(parts, "vz"), before, [early])
 
     parts = late_hidden(place, stage, grad, swap(grad), early)

time: 159 us -> 160 us (level); the launches traced: 159 us -> 158 us
  local copies, waits for them, and re-layouts: 7.13 us -> 3.74 us
  waiting for transfers between devices: 51.9 us -> 54.5 us
  starting transfers between devices: 50.5 us -> 53 us
  Pallas kernels: 31.9 us -> 29.6 us
    ppermute x8, starting transfers between devices: 8.4 us -> 12.1 us  [swap(): return lax.ppermute(value, 'tc', [(0, 1), (1, 0)])]
    unnamed x21 -> x17, local copies, waits for them, and re-layouts: 6.45 us -> 3.07 us
    pallas_call x1 -> x3, Pallas kernels: 7.82 us -> 4.76 us  [the longest x1 4.06 us: staged(): pl.pallas_call(stage_kernel, out_shape=jax.ShapeDtypeStruct((depth // 2,...]
    ppermute x8, waiting for transfers between devices: 3.61 us -> 5.69 us  [swap(): return lax.ppermute(value, 'tc', [(0, 1), (1, 0)])]
    ppermute x19 -> x21, starting transfers between devices: 33.3 us -> 32.1 us  [send(): lax.ppermute(value, axis, [(i, (i + step) % SIDE) for i in range(SIDE)])]
    ppermute x19 -> x21, waiting for transfers between devices: 32.9 us -> 33.7 us  [send(): lax.ppermute(value, axis, [(i, (i + step) % SIDE) for i in range(SIDE)])]
  transfers between devices with their start and end apart: 33 -> 35, of which waited for: 18 -> 18; matrix products, arithmetic and copies ran while one was open for 11% -> 11% of each run, Pallas kernels for 13% -> 9%
where the time goes in v6:
time: 160 us; the launch traced here: 158 us
  waiting for transfers between devices  54.5 us (34%)
  starting transfers between devices  53 us (33%)
  Pallas kernels  29.6 us (18%)
  matrix products  9.63 us (6%)
  other arithmetic  6.29 us (4%)
  local copies, waits for them, and re-layouts  3.74 us (2%)
    ppermute x21, waiting for transfers between devices, send(): lax.ppermute(value, axis, [(i, (i + step) % SIDE) for i in range(SIDE)])  33.7 us
    ppermute x21, starting transfers between devices, send(): lax.ppermute(value, axis, [(i, (i + step) % SIDE) for i in range(SIDE)])  32.1 us
    ppermute x6, waiting for transfers between devices, crossed(): received.append(lax.ppermute(parts[step], ('vy', 'vz', 'tc'), pairs))  15.2 us
    ppermute x8, starting transfers between devices, swap(): return lax.ppermute(value, 'tc', [(0, 1), (1, 0)])  12.1 us
    dot_general x1, matrix products, shards(): jnp.dot(student_hidden, student_unembed, preferred_element_type=F32)  9.63 us
    ppermute x6, starting transfers between devices, crossed(): received.append(lax.ppermute(parts[step], ('vy', 'vz', 'tc'), pairs))  8.76 us
    pallas_call x2, Pallas kernels, products(): pl.pallas_call(functools.partial(product_kernel, len(mine), bool(extra)),...  6.6 us
    ppermute x8, waiting for transfers between devices, swap(): return lax.ppermute(value, 'tc', [(0, 1), (1, 0)])  5.69 us
  transfers between devices with their start and end apart: 35, of which 18 were waited for; matrix products, arithmetic and copies ran while one was open for 11% of the time, Pallas kernels for 9%

profile of v6, /device:TPU:1, one launch (start us, length us, event | category | flops | bytes accessed | tf_op | source)
XLA Modules:
  0.0 158.3 jit_solution(17744680979259978994)
XLA Ops:
  8.3 9.6 %fusion.2 = (f32[256]{0:T(256)S(1)}, f32[256,2048]{1,0:T(8,128)}) fusion(bf16[256,4096]{1,0:T(8,128)(2,1)S(1)} %copy-done, bf16[4096,2048]{1,0:T(8,128)(2,1)} %unembed.1), kind=kOutput, calls=%fused_computation.4 | convolution fusion | flops 4295491584 | bytes 20972544 | tf_op jit(solution)/shard_map/dot_general | solution.py:636
  19.9 3.9 %fusion = (f32[256]{0:T(256)S(1)}, bf16[256,4096]{1,0:T(8,128)(2,1)}) fusion(bf16[256,4096]{1,0:T(8,128)(2,1)} %param.6, f32[256]{0:T(256)S(1)} %reduce_max.28), kind=kLoop, calls=%fused_computation.1 | loop fusion | flops 4194048 | bytes 4196352 | tf_op jit(solution)/shard_map/reduce_sum | solution.py:633
  24.2 7.1 %collective-permute-done.2.refs_2_ = bf16[1088,256]{1,0:T(8,128)(2,1)} collective-permute-done((bf16[1088,256]{1,0:T(8,128)(2,1)}, bf16[1088,256]{1,0:T(8,128)(2,1)}, u32[]{:S(2)}, u32[]{:S(2)}) %collective-permute-start.2) | collective-permute-done | bytes 557088 | tf_op jit(solution)/shard_map/ppermute | solution.py:29
  31.3 4.0 %collective-permute-done.refs_0_ = bf16[1088,256]{1,0:T(8,128)(2,1)S(1)} collective-permute-done((bf16[1088,256]{1,0:T(8,128)(2,1)}, bf16[1088,256]{1,0:T(8,128)(2,1)S(1)}, u32[]{:S(2)}, u32[]{:S(2)}) %collective-permute-start) | collective-permute-done | bytes 557088 | tf_op jit(solution)/shard_map/ppermute | solution.py:29
  41.2 4.1 %tile_products.2 = (bf16[1024,256]{1,0:T(8,128)(2,1)S(1)}, bf16[1024,256]{1,0:T(8,128)(2,1)S(1)}, bf16[1024,256]{1,0:T(8,128)(2,1)S(1)}, bf16[528,256]{1,0:T(8,128)(2,1)S(1)}, bf16[528,256]{1,0:T(8,128)(2,1)S(1)}) custom-call(s32[6]{0:T(128)S(1)} %stack.43.place, s32[16,2]{1,0:T(8,128)S(1)} %copy.11.pairs, s32[1]{0:T(128)S(6)} %copy.16.count, ...), custom_call_target="tpu_custom_call" | custom-call | flops 1073741824 | bytes 8650752 | tf_op jit(solution)/shard_map/tile_products/pallas_call | solution.py:225
  45.2 2.8 %collective-permute-start.8 = (bf16[528,256]{1,0:T(8,128)(2,1)S(1)}, bf16[528,256]{1,0:T(8,128)(2,1)S(1)}, u32[]{:S(2)}, u32[]{:S(2)}) collective-permute-start(bf16[528,256]{1,0:T(8,128)(2,1)S(1)} %get-tuple-element.52), channel_id=1, source_target_pairs={{0,96},{32,0},{64,32},{96,64},{1,97},{33,1},{65,33},{97,65},{2,98}... | collective-permute-start | bytes 811016 | tf_op jit(solution)/shard_map/ppermute | solution.py:29
  48.1 3.0 %collective-permute-done.10.refs_6_.left.refs_4_ = bf16[1024,256]{1,0:T(8,128)(2,1)S(1)} collective-permute-done((bf16[1024,256]{1,0:T(8,128)(2,1)}, bf16[1024,256]{1,0:T(8,128)(2,1)S(1)}, u32[]{:S(2)}, u32[]{:S(2)}) %collective-permute-start.10) | collective-permute-done | bytes 524320 | tf_op jit(solution)/shard_map/ppermute | solution.py:29
  53.3 3.1 %collective-permute-done.7.refs_2_ = bf16[528,256]{1,0:T(8,128)(2,1)S(1)} collective-permute-done((bf16[528,256]{1,0:T(8,128)(2,1)S(1)}, bf16[528,256]{1,0:T(8,128)(2,1)S(1)}, u32[]{:S(2)}, u32[]{:S(2)}) %collective-permute-start.7) | collective-permute-done | bytes 270368 | tf_op jit(solution)/shard_map/ppermute | solution.py:29
  56.9 2.7 %collective-permute-start.12 = (bf16[1024,256]{1,0:T(8,128)(2,1)S(1)}, bf16[1024,256]{1,0:T(8,128)(2,1)S(1)}, u32[]{:S(2)}, u32[]{:S(2)}) collective-permute-start(bf16[1024,256]{1,0:T(8,128)(2,1)S(1)} %get-tuple-element.56), channel_id=1, source_target_pairs={{0,96},{32,0},{64,32},{96,64},{1,97},{33,1},{65,33},{97,65},{2,98}... | collective-permute-start | bytes 1572872 | tf_op jit(solution)/shard_map/ppermute | solution.py:29
  63.3 4.0 %collective-permute-done.13.refs_2_ = bf16[512,256]{1,0:T(8,128)(2,1)S(1)} collective-permute-done((bf16[512,256]{1,0:T(8,128)(2,1)S(1)}, bf16[512,256]{1,0:T(8,128)(2,1)S(1)}, u32[]{:S(2)}, u32[]{:S(2)}) %collective-permute-start.13) | collective-permute-done | bytes 262176 | tf_op jit(solution)/shard_map/ppermute | solution.py:29
  71.3 2.8 %collective-permute-start.15 = (bf16[4096,256]{1,0:T(8,128)(2,1)S(1)}, bf16[4096,256]{1,0:T(8,128)(2,1)S(1)}, u32[]{:S(2)}, u32[]{:S(2)}) collective-permute-start(bf16[4096,256]{1,0:T(8,128)(2,1)S(1)} %pack_weights.1.rest_0_), channel_id=1, source_target_pairs={{0,1},{1,0},{2,3},{3,2},{4,5},{5,4},{6,7},{7,6},{8,9},{9,8},{10,11... | collective-permute-start | bytes 6291464 | tf_op jit(solution)/shard_map/ppermute | solution.py:33
  74.0 3.8 %collective-permute-done.15.rest_1_ = bf16[4096,256]{1,0:T(8,128)(2,1)S(1)} collective-permute-done((bf16[4096,256]{1,0:T(8,128)(2,1)S(1)}, bf16[4096,256]{1,0:T(8,128)(2,1)S(1)}, u32[]{:S(2)}, u32[]{:S(2)}) %collective-permute-start.15) | collective-permute-done | bytes 2097184 | tf_op jit(solution)/shard_map/ppermute | solution.py:33
  80.4 2.7 %collective-permute-start.20 = (bf16[512,256]{1,0:T(8,128)(2,1)S(1)}, bf16[512,256]{1,0:T(8,128)(2,1)S(1)}, u32[]{:S(2)}, u32[]{:S(2)}) collective-permute-start(bf16[512,256]{1,0:T(8,128)(2,1)S(1)} %get-tuple-element.67), channel_id=1, source_target_pairs={{0,96},{32,0},{64,32},{96,64},{1,97},{33,1},{65,33},{97,65},{2,98}... | collective-permute-start | bytes 786440 | tf_op jit(solution)/shard_map/ppermute | solution.py:29
  83.1 6.1 %collective-permute-done.19.refs_2_ = bf16[512,256]{1,0:T(8,128)(2,1)S(1)} collective-permute-done((bf16[512,256]{1,0:T(8,128)(2,1)S(1)}, bf16[512,256]{1,0:T(8,128)(2,1)S(1)}, u32[]{:S(2)}, u32[]{:S(2)}) %collective-permute-start.19) | collective-permute-done | bytes 262176 | tf_op jit(solution)/shard_map/ppermute | solution.py:29
  93.6 5.7 %collective-permute-start.17 = (bf16[272,256]{1,0:T(8,128)(2,1)S(1)}, bf16[272,256]{1,0:T(8,128)(2,1)S(1)}, u32[]{:S(2)}, u32[]{:S(2)}) collective-permute-start(bf16[272,256]{1,0:T(8,128)(2,1)S(1)} %get-tuple-element.62), channel_id=1, source_target_pairs={{0,16},{8,24},{16,0},{24,8},{1,17},{9,25},{17,1},{25,9},{2,18},{10... | collective-permute-start | bytes 417800 | tf_op jit(solution)/shard_map/ppermute | solution.py:29
  101.3 4.1 %stage_unembed.1.refs_6_.stage = bf16[2048,2048]{1,0:T(8,128)(2,1)S(1)} custom-call(s32[6]{0:T(128)S(1)} %stack.43.place, bf16[4096,2048]{1,0:T(8,128)(2,1)} %unembed.1, bf16[272,256]{1,0:T(8,128)(2,1)S(1)} %get-tuple-element.60.refs_0_), custom_call_target="tpu_custom_call" | custom-call | bytes 8388608 | tf_op jit(solution)/shard_map/stage_unembed/pallas_call | solution.py:450
  107.1 2.7 %collective-permute-start.26 = (bf16[1024,256]{1,0:T(8,128)(2,1)S(1)}, bf16[1024,256]{1,0:T(8,128)(2,1)S(1)}, u32[]{:S(2)}, u32[]{:S(2)}) collective-permute-start(bf16[1024,256]{1,0:T(8,128)(2,1)S(1)} %get-tuple-element.78.mine), channel_id=1, source_target_pairs={{0,1},{1,0},{2,3},{3,2},{4,5},{5,4},{6,7},{7,6},{8,9},{9,8},{10,11... | collective-permute-start | bytes 1572872 | tf_op jit(solution)/shard_map/ppermute | solution.py:33
  110.8 3.0 %collective-permute-start.24 = (bf16[256,256]{1,0:T(8,128)(2,1)S(1)}, bf16[256,256]{1,0:T(8,128)(2,1)S(1)}, u32[]{:S(2)}, u32[]{:S(2)}) collective-permute-start(bf16[256,256]{1,0:T(8,128)(2,1)S(1)} %get-tuple-element.76), channel_id=1, source_target_pairs={{0,16},{8,24},{16,0},{24,8},{1,17},{9,25},{17,1},{25,9},{2,18},{10... | collective-permute-start | bytes 393224 | tf_op jit(solution)/shard_map/ppermute | solution.py:29
  115.8 3.0 %early_hidden.1.refs_6_.early = f32[2048,512]{1,0:T(8,128)S(1)} custom-call(s32[6]{0:T(128)S(1)} %stack.43.place, bf16[2048,2048]{1,0:T(8,128)(2,1)S(1)} %stage_unembed.1.refs_6_.stage, bf16[1024,256]{1,0:T(8,128)(2,1)S(1)} %get-tuple-element.78.mine, bf16[1024,256]{1,0:T(8,128)(2,1)S(1)} %collective-permute-done.26.other), custom_call_target="tpu_custom_call" | custom-call | flops 2147483648 | bytes 12582912 | tf_op jit(solution)/shard_map/early_hidden/pallas_call | solution.py:480
  124.4 3.0 %late_hidden.1 = (bf16[528,512]{1,0:T(8,128)(2,1)S(1)}, bf16[528,512]{1,0:T(8,128)(2,1)S(1)}, bf16[528,512]{1,0:T(8,128)(2,1)S(1)}, bf16[528,512]{1,0:T(8,128)(2,1)S(1)}) custom-call(s32[6]{0:T(128)S(1)} %stack.43.place, bf16[2048,2048]{1,0:T(8,128)(2,1)S(1)} %stage_unembed.1.refs_6_.stage, bf16[1040,256]{1,0:T(8,128)(2,1)S(1)} %logit_grad.3.mine, ...), custom_call_target="tpu_custom_call" | custom-call | flops 2147483648 | bytes 10485760 | tf_op jit(solution)/shard_map/late_hidden/pallas_call | solution.py:511
  132.5 4.7 %collective-permute-done.28.refs_1_ = bf16[528,512]{1,0:T(8,128)(2,1)S(1)} collective-permute-done((bf16[528,512]{1,0:T(8,128)(2,1)S(1)}, bf16[528,512]{1,0:T(8,128)(2,1)S(1)}, u32[]{:S(2)}, u32[]{:S(2)}) %collective-permute-start.28) | collective-permute-done | bytes 540704 | tf_op jit(solution)/shard_map/ppermute | solution.py:621
  137.1 6.7 %collective-permute-done.29.refs_2_ = bf16[528,512]{1,0:T(8,128)(2,1)S(1)} collective-permute-done((bf16[528,512]{1,0:T(8,128)(2,1)S(1)}, bf16[528,512]{1,0:T(8,128)(2,1)S(1)}, u32[]{:S(2)}, u32[]{:S(2)}) %collective-permute-start.29) | collective-permute-done | bytes 540704 | tf_op jit(solution)/shard_map/ppermute | solution.py:621
  144.9 3.3 %collective-permute-start.32 = (bf16[144,512]{1,0:T(8,128)(2,1)S(1)}, bf16[144,512]{1,0:T(8,128)(2,1)S(1)}, u32[]{:S(2)}, u32[]{:S(2)}) collective-permute-start(bf16[144,512]{1,0:T(8,128)(2,1)S(1)} %get-tuple-element.85), channel_id=1, source_target_pairs={{0,16},{1,65},{8,24},{9,73},{16,0},{17,81},{24,8},{25,89},{32,48},... | collective-permute-start | bytes 442376 | tf_op jit(solution)/shard_map/ppermute | solution.py:621
  152.9 3.2 %collective-permute-start.34 = (bf16[128,256]{1,0:T(8,128)(2,1)S(1)}, bf16[128,256]{1,0:T(8,128)(2,1)S(1)}, u32[]{:S(2)}, u32[]{:S(2)}) collective-permute-start(bf16[128,256]{1,0:T(8,128)(2,1)S(1)} %get-tuple-element.88), channel_id=1, source_target_pairs={{0,1},{1,0},{2,3},{3,2},{4,5},{5,4},{6,7},{7,6},{8,9},{9,8},{10,11... | collective-permute-start | bytes 196616 | tf_op jit(solution)/shard_map/ppermute | solution.py:33
  (92 shorter events, 57.9 us)
Async XLA Ops:
  3.2 34.4 %collective-permute-start.3 = (bf16[1088,256]{1,0:T(8,128)(2,1)}, bf16[1088,256]{1,0:T(8,128)(2,1)}, u32[]{:S(2)}, u32[]{:S(2)}) collective-permute-start(bf16[1088,256]{1,0:T(8,128)(2,1)} %prepare_weights.1.rest_0_), channel_id=1, source_target_pairs={{0,1},{1,0},{2,3},{3,2},{4,5},{5,4},{6,7},{7,6},{8,9},{9,8},{10,11... | collective-permute-start | bytes 1671176 | tf_op jit(solution)/shard_map/ppermute | solution.py:33
  4.6 26.7 %collective-permute-start.2 = (bf16[1088,256]{1,0:T(8,128)(2,1)}, bf16[1088,256]{1,0:T(8,128)(2,1)}, u32[]{:S(2)}, u32[]{:S(2)}) collective-permute-start(bf16[1088,256]{1,0:T(8,128)(2,1)} %prepare_weights.1.rest_0_), channel_id=1, source_target_pairs={{0,6},{2,0},{4,2},{6,4},{1,7},{3,1},{5,3},{7,5},{8,14},{10,8},{12,... | collective-permute-start | bytes 1671176 | tf_op jit(solution)/shard_map/ppermute | solution.py:29
  7.2 24.2 %collective-permute-start.1 = (bf16[1088,256]{1,0:T(8,128)(2,1)}, bf16[1088,256]{1,0:T(8,128)(2,1)}, u32[]{:S(2)}, u32[]{:S(2)}) collective-permute-start(bf16[1088,256]{1,0:T(8,128)(2,1)} %prepare_weights.1.rest_0_), channel_id=1, source_target_pairs={{0,4},{2,6},{4,0},{6,2},{1,5},{3,7},{5,1},{7,3},{8,12},{10,14},{12... | collective-permute-start | bytes 1671176 | tf_op jit(solution)/shard_map/ppermute | solution.py:29
  7.7 27.7 %collective-permute-start = (bf16[1088,256]{1,0:T(8,128)(2,1)}, bf16[1088,256]{1,0:T(8,128)(2,1)S(1)}, u32[]{:S(2)}, u32[]{:S(2)}) collective-permute-start(bf16[1088,256]{1,0:T(8,128)(2,1)} %prepare_weights.1.rest_0_), channel_id=1, source_target_pairs={{0,2},{2,4},{4,6},{6,0},{1,3},{3,5},{5,7},{7,1},{8,10},{10,12},{12... | collective-permute-start | bytes 1671176 | tf_op jit(solution)/shard_map/ppermute | solution.py:29
  37.2 13.9 %collective-permute-start.10 = (bf16[1024,256]{1,0:T(8,128)(2,1)}, bf16[1024,256]{1,0:T(8,128)(2,1)S(1)}, u32[]{:S(2)}, u32[]{:S(2)}) collective-permute-start(bf16[1024,256]{1,0:T(8,128)(2,1)} %slice_weights.1.rest_9_.refs_0_), channel_id=1, source_target_pairs={{0,6},{2,0},{4,2},{6,4},{1,7},{3,1},{5,3},{7,5},{8,14},{10,8},{12,... | collective-permute-start | bytes 1572872 | tf_op jit(solution)/shard_map/ppermute | solution.py:29
  37.5 14.8 %collective-permute-start.9 = (bf16[1024,256]{1,0:T(8,128)(2,1)}, bf16[1024,256]{1,0:T(8,128)(2,1)}, u32[]{:S(2)}, u32[]{:S(2)}) collective-permute-start(bf16[1024,256]{1,0:T(8,128)(2,1)} %slice_weights.1.rest_9_.refs_0_), channel_id=1, source_target_pairs={{0,2},{2,4},{4,6},{6,0},{1,3},{3,5},{5,7},{7,1},{8,10},{10,12},{12... | collective-permute-start | bytes 1572872 | tf_op jit(solution)/shard_map/ppermute | solution.py:29
  45.2 8.1 %collective-permute-start.8 = (bf16[528,256]{1,0:T(8,128)(2,1)S(1)}, bf16[528,256]{1,0:T(8,128)(2,1)S(1)}, u32[]{:S(2)}, u32[]{:S(2)}) collective-permute-start(bf16[528,256]{1,0:T(8,128)(2,1)S(1)} %get-tuple-element.52), channel_id=1, source_target_pairs={{0,96},{32,0},{64,32},{96,64},{1,97},{33,1},{65,33},{97,65},{2,98}... | collective-permute-start | bytes 811016 | tf_op jit(solution)/shard_map/ppermute | solution.py:29
  48.1 8.3 %collective-permute-start.7 = (bf16[528,256]{1,0:T(8,128)(2,1)S(1)}, bf16[528,256]{1,0:T(8,128)(2,1)S(1)}, u32[]{:S(2)}, u32[]{:S(2)}) collective-permute-start(bf16[528,256]{1,0:T(8,128)(2,1)S(1)} %get-tuple-element.51.refs_4_), channel_id=1, source_target_pairs={{0,32},{32,64},{64,96},{96,0},{1,33},{33,65},{65,97},{97,1},{2,34}... | collective-permute-start | bytes 811016 | tf_op jit(solution)/shard_map/ppermute | solution.py:29
  56.8 13.1 %collective-permute-start.11 = (bf16[1040,256]{1,0:T(8,128)(2,1)S(1)}, bf16[1040,256]{1,0:T(8,128)(2,1)S(1)}, u32[]{:S(2)}, u32[]{:S(2)}) collective-permute-start(bf16[1040,256]{1,0:T(8,128)(2,1)S(1)} %get-tuple-element.55), channel_id=1, source_target_pairs={{0,32},{32,64},{64,96},{96,0},{1,33},{33,65},{65,97},{97,1},{2,34}... | collective-permute-start | bytes 1597448 | tf_op jit(solution)/shard_map/ppermute | solution.py:29
  56.9 11.8 %collective-permute-start.12 = (bf16[1024,256]{1,0:T(8,128)(2,1)S(1)}, bf16[1024,256]{1,0:T(8,128)(2,1)S(1)}, u32[]{:S(2)}, u32[]{:S(2)}) collective-permute-start(bf16[1024,256]{1,0:T(8,128)(2,1)S(1)} %get-tuple-element.56), channel_id=1, source_target_pairs={{0,96},{32,0},{64,32},{96,64},{1,97},{33,1},{65,33},{97,65},{2,98}... | collective-permute-start | bytes 1572872 | tf_op jit(solution)/shard_map/ppermute | solution.py:29
  60.6 6.8 %collective-permute-start.13 = (bf16[512,256]{1,0:T(8,128)(2,1)S(1)}, bf16[512,256]{1,0:T(8,128)(2,1)S(1)}, u32[]{:S(2)}, u32[]{:S(2)}) collective-permute-start(bf16[512,256]{1,0:T(8,128)(2,1)S(1)} %get-tuple-element.57), channel_id=1, source_target_pairs={{0,2},{2,4},{4,6},{6,0},{1,3},{3,5},{5,7},{7,1},{8,10},{10,12},{12... | collective-permute-start | bytes 786440 | tf_op jit(solution)/shard_map/ppermute | solution.py:29
  80.4 8.8 %collective-permute-start.19 = (bf16[512,256]{1,0:T(8,128)(2,1)S(1)}, bf16[512,256]{1,0:T(8,128)(2,1)S(1)}, u32[]{:S(2)}, u32[]{:S(2)}) collective-permute-start(bf16[512,256]{1,0:T(8,128)(2,1)S(1)} %get-tuple-element.66), channel_id=1, source_target_pairs={{0,32},{32,64},{64,96},{96,0},{1,33},{33,65},{65,97},{97,1},{2,34}... | collective-permute-start | bytes 786440 | tf_op jit(solution)/shard_map/ppermute | solution.py:29
  80.4 8.7 %collective-permute-start.20 = (bf16[512,256]{1,0:T(8,128)(2,1)S(1)}, bf16[512,256]{1,0:T(8,128)(2,1)S(1)}, u32[]{:S(2)}, u32[]{:S(2)}) collective-permute-start(bf16[512,256]{1,0:T(8,128)(2,1)S(1)} %get-tuple-element.67), channel_id=1, source_target_pairs={{0,96},{32,0},{64,32},{96,64},{1,97},{33,1},{65,33},{97,65},{2,98}... | collective-permute-start | bytes 786440 | tf_op jit(solution)/shard_map/ppermute | solution.py:29
  89.5 16.0 %collective-permute-start.21 = (bf16[1024,256]{1,0:T(8,128)(2,1)S(1)}, bf16[1024,256]{1,0:T(8,128)(2,1)S(1)}, u32[]{:S(2)}, u32[]{:S(2)}) collective-permute-start(bf16[1024,256]{1,0:T(8,128)(2,1)S(1)} %get-tuple-element.69), channel_id=1, source_target_pairs={{0,32},{32,64},{64,96},{96,0},{1,33},{33,65},{65,97},{97,1},{2,34}... | collective-permute-start | bytes 1572872 | tf_op jit(solution)/shard_map/ppermute | solution.py:29
  90.2 15.3 %collective-permute-start.22 = (bf16[1024,256]{1,0:T(8,128)(2,1)S(1)}, bf16[1024,256]{1,0:T(8,128)(2,1)S(1)}, u32[]{:S(2)}, u32[]{:S(2)}) collective-permute-start(bf16[1024,256]{1,0:T(8,128)(2,1)S(1)} %get-tuple-element.70), channel_id=1, source_target_pairs={{0,96},{32,0},{64,32},{96,64},{1,97},{33,1},{65,33},{97,65},{2,98}... | collective-permute-start | bytes 1572872 | tf_op jit(solution)/shard_map/ppermute | solution.py:29
  93.3 12.1 %collective-permute-start.16 = (bf16[272,256]{1,0:T(8,128)(2,1)S(1)}, bf16[272,256]{1,0:T(8,128)(2,1)S(1)}, u32[]{:S(2)}, u32[]{:S(2)}) collective-permute-start(bf16[272,256]{1,0:T(8,128)(2,1)S(1)} %get-tuple-element.61), channel_id=1, source_target_pairs={{0,8},{8,16},{16,24},{24,0},{1,9},{9,17},{17,25},{25,1},{2,10},{10... | collective-permute-start | bytes 417800 | tf_op jit(solution)/shard_map/ppermute | solution.py:29
  93.6 11.8 %collective-permute-start.17 = (bf16[272,256]{1,0:T(8,128)(2,1)S(1)}, bf16[272,256]{1,0:T(8,128)(2,1)S(1)}, u32[]{:S(2)}, u32[]{:S(2)}) collective-permute-start(bf16[272,256]{1,0:T(8,128)(2,1)S(1)} %get-tuple-element.62), channel_id=1, source_target_pairs={{0,16},{8,24},{16,0},{24,8},{1,17},{9,25},{17,1},{25,9},{2,18},{10... | collective-permute-start | bytes 417800 | tf_op jit(solution)/shard_map/ppermute | solution.py:29
  107.1 8.7 %collective-permute-start.26 = (bf16[1024,256]{1,0:T(8,128)(2,1)S(1)}, bf16[1024,256]{1,0:T(8,128)(2,1)S(1)}, u32[]{:S(2)}, u32[]{:S(2)}) collective-permute-start(bf16[1024,256]{1,0:T(8,128)(2,1)S(1)} %get-tuple-element.78.mine), channel_id=1, source_target_pairs={{0,1},{1,0},{2,3},{3,2},{4,5},{5,4},{6,7},{7,6},{8,9},{9,8},{10,11... | collective-permute-start | bytes 1572872 | tf_op jit(solution)/shard_map/ppermute | solution.py:33
  110.7 8.0 %collective-permute-start.23 = (bf16[256,256]{1,0:T(8,128)(2,1)S(1)}, bf16[256,256]{1,0:T(8,128)(2,1)S(1)}, u32[]{:S(2)}, u32[]{:S(2)}) collective-permute-start(bf16[256,256]{1,0:T(8,128)(2,1)S(1)} %get-tuple-element.75), channel_id=1, source_target_pairs={{0,8},{8,16},{16,24},{24,0},{1,9},{9,17},{17,25},{25,1},{2,10},{10... | collective-permute-start | bytes 393224 | tf_op jit(solution)/shard_map/ppermute | solution.py:29
  110.8 9.5 %collective-permute-start.24 = (bf16[256,256]{1,0:T(8,128)(2,1)S(1)}, bf16[256,256]{1,0:T(8,128)(2,1)S(1)}, u32[]{:S(2)}, u32[]{:S(2)}) collective-permute-start(bf16[256,256]{1,0:T(8,128)(2,1)S(1)} %get-tuple-element.76), channel_id=1, source_target_pairs={{0,16},{8,24},{16,0},{24,8},{1,17},{9,25},{17,1},{25,9},{2,18},{10... | collective-permute-start | bytes 393224 | tf_op jit(solution)/shard_map/ppermute | solution.py:29
  127.4 9.8 %collective-permute-start.28 = (bf16[528,512]{1,0:T(8,128)(2,1)S(1)}, bf16[528,512]{1,0:T(8,128)(2,1)S(1)}, u32[]{:S(2)}, u32[]{:S(2)}) collective-permute-start(bf16[528,512]{1,0:T(8,128)(2,1)S(1)} %get-tuple-element.80), channel_id=1, source_target_pairs={{0,32},{1,9},{8,40},{9,17},{16,48},{17,25},{24,56},{25,1},{32,64},... | collective-permute-start | bytes 1622024 | tf_op jit(solution)/shard_map/ppermute | solution.py:621
  128.9 14.9 %collective-permute-start.29 = (bf16[528,512]{1,0:T(8,128)(2,1)S(1)}, bf16[528,512]{1,0:T(8,128)(2,1)S(1)}, u32[]{:S(2)}, u32[]{:S(2)}) collective-permute-start(bf16[528,512]{1,0:T(8,128)(2,1)S(1)} %get-tuple-element.81), channel_id=1, source_target_pairs={{0,64},{1,17},{8,72},{9,25},{16,80},{17,1},{24,88},{25,9},{32,96},... | collective-permute-start | bytes 1622024 | tf_op jit(solution)/shard_map/ppermute | solution.py:621
  131.0 12.8 %collective-permute-start.30 = (bf16[528,512]{1,0:T(8,128)(2,1)S(1)}, bf16[528,512]{1,0:T(8,128)(2,1)S(1)}, u32[]{:S(2)}, u32[]{:S(2)}) collective-permute-start(bf16[528,512]{1,0:T(8,128)(2,1)S(1)} %get-tuple-element.82), channel_id=1, source_target_pairs={{0,96},{1,25},{8,104},{9,1},{16,112},{17,9},{24,120},{25,17},{32,0... | collective-permute-start | bytes 1622024 | tf_op jit(solution)/shard_map/ppermute | solution.py:621
  144.9 7.4 %collective-permute-start.32 = (bf16[144,512]{1,0:T(8,128)(2,1)S(1)}, bf16[144,512]{1,0:T(8,128)(2,1)S(1)}, u32[]{:S(2)}, u32[]{:S(2)}) collective-permute-start(bf16[144,512]{1,0:T(8,128)(2,1)S(1)} %get-tuple-element.85), channel_id=1, source_target_pairs={{0,16},{1,65},{8,24},{9,73},{16,0},{17,81},{24,8},{25,89},{32,48},... | collective-permute-start | bytes 442376 | tf_op jit(solution)/shard_map/ppermute | solution.py:621
  (19 other events, 146.2 us)

commit v7 on v6

--- a/solution.py
+++ b/solution.py
@@ -149,7 +149,10 @@
     )(right, left, *behind)
 
 
-def product_kernel(number, with_stats, place, pairs, count, probs, *rest):
+def product_kernel(number, with_stats, place, pairs, count, source, *rest):
+    probs, sem, rest = rest[-2], rest[-1], rest[:-2]
+    copy = pltpu.make_async_copy(source, probs, sem)
+    copy.start()
     mine, other, rest = rest[:number], rest[number : 2 * number], rest[2 * number :]
     if with_stats:
         before, rest = rest[0], rest[1:]
@@ -194,6 +197,7 @@
             )
         return carry
 
+    copy.wait()
     lax.fori_loop(0, count[0], tile, 0)
     half = rows // 2
     for step in range(SIDE):
@@ -226,9 +230,11 @@
         functools.partial(product_kernel, len(mine), bool(extra)),
         out_shape=[jax.ShapeDtypeStruct((SIDE * rows, width), BF16)] * 3
         + [jax.ShapeDtypeStruct((SIDE * rows // 2 + 16 * len(extra), width), BF16)] * 2,
-        in_specs=[SMEM, SMEM, SMEM] + [VMEM] * (1 + 2 * len(mine) + len(extra)) + [ANY] * len(behind),
+        in_specs=[SMEM, SMEM, SMEM, ANY]
+        + [VMEM] * (2 * len(mine) + len(extra))
+        + [ANY] * len(behind),
         out_specs=[VMEM] * (SIDE + 1),
-        scratch_shapes=scratch,
+        scratch_shapes=scratch + [pltpu.VMEM(probs.shape, BF16), pltpu.SemaphoreType.DMA(())],
         compiler_params=params(24),
         cost_estimate=cost(
             16 * 2 * rows * 512 * width, 2 * probs.size + 16 * depth * width + 32 * rows * width
@@ -378,7 +384,8 @@
         table = columns_of(scales + [share / smass, peak, peak + jnp.log(smass)])
         kept[...] = table
     else:
-        table, loss, parts, grad = refs[0][...], refs[1], refs[2 : 2 + SIDE], refs[-1]
+        table, loss, earlier = refs[0][...], refs[1], refs[2]
+        parts, grad = refs[3 : 3 + SIDE], refs[-1]
     rows, width = logits.shape[0], parts[0].shape[1]
     share, peak, norm = (table[:, c : c + 1] for c in range(4, 7))
     terms = jnp.zeros((rows, width), F32)
@@ -390,19 +397,24 @@
         entropy = jnp.where(positive, target * jnp.log(jnp.where(positive, target, 1.0)), 0.0)
         terms += entropy - target * (scores - norm)
         value = share * jnp.exp(scores - peak) - target
-        at = pl.ds(pl.multiple_of(block * width, width), width)
+        if with_stats:
+            at = pl.ds(pl.multiple_of(block * width, width), width)
+        else:
+            at = pl.ds(pl.multiple_of(block * 512 + offset, width), width)
         grad[at, :] = value.T.astype(BF16)
     sum_of_terms = jnp.sum(terms.T, axis=0, keepdims=True)
     if with_stats:
         loss[...] = jnp.broadcast_to(sum_of_terms, loss.shape)
     else:
-        grad[SIDE * width :, :] = pack_rows([sum_of_terms + loss[0:1]])
+        grad[SIDE * 512 :, :] = pack_rows([sum_of_terms + loss[0:1]])
+        for block in range(SIDE):
+            grad[block * 512 : block * 512 + offset, :] = earlier[block * offset : (block + 1) * offset, :]
 
 
 def gradients(offset, place, logits, parts, before=(), behind=()):
     rows, width = logits.shape[0], parts[0].shape[1]
     first = not before
-    outs = [jax.ShapeDtypeStruct((SIDE * width + (0 if first else 16), rows), BF16)]
+    outs = [jax.ShapeDtypeStruct((SIDE * width if first else SIDE * 512 + 16, rows), BF16)]
     if first:
         outs.append(jax.ShapeDtypeStruct((8, rows), F32))
         outs.append(jax.ShapeDtypeStruct((rows, 128), F32))
@@ -415,12 +427,6 @@
         cost_estimate=cost(rows * width, rows * width),
         name="logit_grad",
     )(place, logits, *before, *parts, *behind)
-
-
-def both_cores(core, mine, other, depth, out):
-    rows = mine.shape[1]
-    out[:, pl.ds(pl.multiple_of(core * rows, rows), rows)] = mine[0:depth, :]
-    out[:, pl.ds(pl.multiple_of((1 - core) * rows, rows), rows)] = other[0:depth, :]
 
 
 def stage_kernel(place, unembed, *refs):
@@ -459,65 +465,53 @@
     )(place, unembed, *behind)
 
 
-def columns_at(stage, rows, chunk, width):
-    parts = [stage[rows, (2 * b + chunk) * width : (2 * b + chunk + 1) * width] for b in range(SIDE)]
-    return jnp.concatenate(parts, axis=1)
-
-
-def early_kernel(place, stage, mine, other, out, both):
-    depth = both.shape[0]
-    both_cores(place[3], mine, other, depth, both)
+def own_kernel(stage, mine, out):
+    depth = stage.shape[1]
     for step in range(SIDE):
         rows = slice(step * 512, step * 512 + 512)
-        out[rows, :] = jnp.dot(
-            columns_at(stage, rows, 0, depth // SIDE), both[...], preferred_element_type=F32
-        )
-
-
-def early_hidden(place, stage, mine, other):
-    depth = stage.shape[0]
-    width, rows = mine.shape
-    return pl.pallas_call(
-        early_kernel,
-        out_shape=jax.ShapeDtypeStruct((depth, 2 * rows), F32),
-        in_specs=[SMEM] + [VMEM] * 3,
+        result = jnp.dot(stage[rows, :], mine[0:depth, :], preferred_element_type=F32)
+        out[rows, :] = result.astype(BF16)
+
+
+def own_hidden(stage, mine):
+    depth, rows = stage.shape[0], mine.shape[1]
+    return pl.pallas_call(
+        own_kernel,
+        out_shape=jax.ShapeDtypeStruct((depth, rows), BF16),
+        in_specs=[VMEM, VMEM],
         out_specs=VMEM,
-        scratch_shapes=[pltpu.VMEM((width, 2 * rows), BF16)],
-        compiler_params=params(),
-        cost_estimate=cost(4 * depth * width * rows, 4 * depth * width + 8 * depth * rows),
-        name="early_hidden",
-    )(place, stage, mine, other)
-
-
-def late_kernel(place, stage, mine, other, early, *refs):
-    outs, both = refs[:SIDE], refs[SIDE]
-    depth = both.shape[0]
+        compiler_params=params(),
+        cost_estimate=cost(2 * stage.size * rows, 2 * stage.size),
+        name="own_hidden",
+    )(stage, mine)
+
+
+def other_kernel(steps, place, stage, mine, other, own, *refs):
+    outs = refs[-len(steps) :]
+    depth = stage.shape[1]
     rows = mine.shape[1]
-    both_cores(place[3], mine, other, depth, both)
-    for step in range(SIDE):
+    lanes = pl.ds(pl.multiple_of(place[3] * rows, rows), rows)
+    other_lanes = pl.ds(pl.multiple_of((1 - place[3]) * rows, rows), rows)
+    for out, step in zip(outs, steps):
         at = pl.ds(pl.multiple_of(lax.rem(place[4] + step, SIDE) * 512, 512), 512)
-        result = jnp.dot(
-            columns_at(stage, at, 1, depth // SIDE), both[...], preferred_element_type=F32
-        )
-        outs[step][0:512, :] = (early[at, :] + result).astype(BF16)
-        for part, core in ((mine, place[3]), (other, 1 - place[3])):
-            lanes = pl.ds(pl.multiple_of(core * rows, rows), rows)
-            outs[step][512:528, lanes] = part[depth : depth + 16, :]
-
-
-def late_hidden(place, stage, mine, other, early):
-    depth, width = stage.shape
-    width, rows = width // 2, early.shape[1]
-    return pl.pallas_call(
-        late_kernel,
-        out_shape=[jax.ShapeDtypeStruct((528, rows), BF16)] * SIDE,
-        in_specs=[SMEM] + [VMEM] * 4,
-        out_specs=[VMEM] * SIDE,
-        scratch_shapes=[pltpu.VMEM((width, rows), BF16)],
-        compiler_params=params(),
-        cost_estimate=cost(2 * depth * width * rows, 2 * depth * width + 6 * depth * rows),
-        name="late_hidden",
-    )(place, stage, mine, other, early)
+        result = jnp.dot(stage[at, :], other[0:depth, :], preferred_element_type=F32)
+        out[0:512, other_lanes] = result.astype(BF16)
+        out[0:512, lanes] = own[at, :]
+        out[512:528, lanes] = mine[depth : depth + 16, :]
+        out[512:528, other_lanes] = other[depth : depth + 16, :]
+
+
+def other_hidden(steps, place, stage, mine, other, own, behind=()):
+    rows = mine.shape[1]
+    return pl.pallas_call(
+        functools.partial(other_kernel, steps),
+        out_shape=[jax.ShapeDtypeStruct((528, 2 * rows), BF16)] * len(steps),
+        in_specs=[SMEM] + [VMEM] * 4 + [ANY] * len(behind),
+        out_specs=[VMEM] * len(steps),
+        compiler_params=params(),
+        cost_estimate=cost(len(steps) * stage.size * rows // 2, 2 * stage.size),
+        name="other_hidden",
+    )(place, stage, mine, other, own, *behind)
 
 
 def packed_loss(index, parts, at, ordered):
@@ -660,16 +654,17 @@
     *parts, scales = merged(place, given, [own, near, far], rows, True, [later[0]])
     own, near, far, to_right, to_left = later
     left_part, right_part = send(to_right, "vy", 1), send(to_left, "vy", 3)
-    near, far = relayed(near, far, left_part, right_part, factors, False)
+    stage = staged(place, student_unembed, [own])
+    near, far = relayed(near, far, left_part, right_part, factors, False, [stage])
     later = [own, send(near, "vy", 1), send(far, "vy", 3)]
-    stage = staged(place, student_unembed, [parts[0]])
-    grad, *before = gradients(0, place, logits, spread(parts, "vz"), (), later[1:] + [stage])
-    early = early_hidden(place, stage, grad, swap(grad))
-    before = [before[1], before[0]]
+    grad, *before = gradients(0, place, logits, spread(parts, "vz"), (), later[1:])
+    before = [before[1], before[0], grad]
     parts = merged(place, scales, later, rows, False)
-    (grad,) = gradients(width, place, logits, spread(parts, "vz"), before, [early])
-
-    parts = late_hidden(place, stage, grad, swap(grad), early)
+    (mine,) = gradients(width, place, logits, spread(parts, "vz"), before)
+
+    own = own_hidden(stage, mine)
+    other = swap(mine)
+    parts = other_hidden(range(SIDE), place, stage, mine, other, own)
     parts = middle(place, crossed(parts, True))
     keep, give, loss = totals(place, crossed(parts, False))
     return turned(place, keep, swap(give)), loss[0]

time: 160 us -> 157 us (0.981)
  Pallas kernels: 29.6 us -> 27.9 us
    ppermute x8 -> x7, starting transfers between devices: 12.1 us -> 10.5 us  [swap(): return lax.ppermute(value, 'tc', [(0, 1), (1, 0)])]
    ppermute x8 -> x7, waiting for transfers between devices: 5.69 us -> 4.14 us  [swap(): return lax.ppermute(value, 'tc', [(0, 1), (1, 0)])]
  transfers between devices with their start and end apart: 35 -> 34, of which waited for: 18 -> 18; matrix products, arithmetic and copies ran while one was open for 11% -> 11% of each run, Pallas kernels for 9% -> 10%
where the time goes in v7:
time: 157 us; the launch traced here: 155 us
  waiting for transfers between devices  54.2 us (35%)
  starting transfers between devices  51.8 us (33%)
  Pallas kernels  27.9 us (18%)
  matrix products  9.64 us (6%)
  other arithmetic  6.26 us (4%)
  local copies, waits for them, and re-layouts  3.74 us (2%)
    ppermute x21, waiting for transfers between devices, send(): lax.ppermute(value, axis, [(i, (i + step) % SIDE) for i in range(SIDE)])  34.5 us
    ppermute x21, starting transfers between devices, send(): lax.ppermute(value, axis, [(i, (i + step) % SIDE) for i in range(SIDE)])  32.7 us
    ppermute x6, waiting for transfers between devices, crossed(): received.append(lax.ppermute(parts[step], ('vy', 'vz', 'tc'), pairs))  15.5 us
    ppermute x7, starting transfers between devices, swap(): return lax.ppermute(value, 'tc', [(0, 1), (1, 0)])  10.5 us
    dot_general x1, matrix products, shards(): jnp.dot(student_hidden, student_unembed, preferred_element_type=F32)  9.64 us
    ppermute x6, starting transfers between devices, crossed(): received.append(lax.ppermute(parts[step], ('vy', 'vz', 'tc'), pairs))  8.69 us
    pallas_call x2, Pallas kernels, products(): pl.pallas_call(functools.partial(product_kernel, len(mine), bool(extra)),...  5.36 us
    ppermute x7, waiting for transfers between devices, swap(): return lax.ppermute(value, 'tc', [(0, 1), (1, 0)])  4.14 us
  transfers between devices with their start and end apart: 34, of which 18 were waited for; matrix products, arithmetic and copies ran while one was open for 11% of the time, Pallas kernels for 10%

profile of v7, /device:TPU:1, one launch (start us, length us, event | category | flops | bytes accessed | tf_op | source)
XLA Modules:
  0.0 155.0 jit_solution(4141233536692014837)
XLA Ops:
  4.6 2.6 %collective-permute-start.2 = (bf16[1088,256]{1,0:T(8,128)(2,1)}, bf16[1088,256]{1,0:T(8,128)(2,1)}, u32[]{:S(2)}, u32[]{:S(2)}) collective-permute-start(bf16[1088,256]{1,0:T(8,128)(2,1)} %prepare_weights.1.rest_0_), channel_id=1, source_target_pairs={{0,6},{2,0},{4,2},{6,4},{1,7},{3,1},{5,3},{7,5},{8,14},{10,8},{12,... | collective-permute-start | bytes 1671176 | tf_op jit(solution)/shard_map/ppermute | solution.py:29
  8.3 9.6 %fusion.2 = (f32[256]{0:T(256)S(1)}, f32[256,2048]{1,0:T(8,128)}) fusion(bf16[256,4096]{1,0:T(8,128)(2,1)S(1)} %copy-done, bf16[4096,2048]{1,0:T(8,128)(2,1)} %unembed.1), kind=kOutput, calls=%fused_computation.4 | convolution fusion | flops 4295491584 | bytes 20972544 | tf_op jit(solution)/shard_map/dot_general | solution.py:630
  19.9 3.9 %fusion = (f32[256]{0:T(256)S(1)}, bf16[256,4096]{1,0:T(8,128)(2,1)}) fusion(bf16[256,4096]{1,0:T(8,128)(2,1)} %param.6, f32[256]{0:T(256)S(1)} %reduce_max.28), kind=kLoop, calls=%fused_computation.1 | loop fusion | flops 4194048 | bytes 4196352 | tf_op jit(solution)/shard_map/reduce_sum | solution.py:627
  24.2 7.1 %collective-permute-done.2.refs_2_ = bf16[1088,256]{1,0:T(8,128)(2,1)} collective-permute-done((bf16[1088,256]{1,0:T(8,128)(2,1)}, bf16[1088,256]{1,0:T(8,128)(2,1)}, u32[]{:S(2)}, u32[]{:S(2)}) %collective-permute-start.2) | collective-permute-done | bytes 557088 | tf_op jit(solution)/shard_map/ppermute | solution.py:29
  31.3 4.0 %collective-permute-done.refs_0_ = bf16[1088,256]{1,0:T(8,128)(2,1)S(1)} collective-permute-done((bf16[1088,256]{1,0:T(8,128)(2,1)}, bf16[1088,256]{1,0:T(8,128)(2,1)S(1)}, u32[]{:S(2)}, u32[]{:S(2)}) %collective-permute-start) | collective-permute-done | bytes 557088 | tf_op jit(solution)/shard_map/ppermute | solution.py:29
  41.2 3.4 %tile_products.2 = (bf16[1024,256]{1,0:T(8,128)(2,1)S(1)}, bf16[1024,256]{1,0:T(8,128)(2,1)S(1)}, bf16[1024,256]{1,0:T(8,128)(2,1)S(1)}, bf16[528,256]{1,0:T(8,128)(2,1)S(1)}, bf16[528,256]{1,0:T(8,128)(2,1)S(1)}) custom-call(s32[6]{0:T(128)S(1)} %stack.43.place, s32[16,2]{1,0:T(8,128)S(1)} %copy.12.pairs, s32[1]{0:T(128)S(6)} %copy.16.count, ...), custom_call_target="tpu_custom_call" | custom-call | flops 1073741824 | bytes 8650752 | tf_op jit(solution)/shard_map/tile_products/pallas_call | solution.py:229
  44.6 3.7 %collective-permute-start.12 = (bf16[528,256]{1,0:T(8,128)(2,1)S(1)}, bf16[528,256]{1,0:T(8,128)(2,1)S(1)}, u32[]{:S(2)}, u32[]{:S(2)}) collective-permute-start(bf16[528,256]{1,0:T(8,128)(2,1)S(1)} %get-tuple-element.55), channel_id=1, source_target_pairs={{0,96},{32,0},{64,32},{96,64},{1,97},{33,1},{65,33},{97,65},{2,98}... | collective-permute-start | bytes 811016 | tf_op jit(solution)/shard_map/ppermute | solution.py:29
  48.3 2.9 %collective-permute-done.4.left.refs_6_.refs_4_ = bf16[1024,256]{1,0:T(8,128)(2,1)S(1)} collective-permute-done((bf16[1024,256]{1,0:T(8,128)(2,1)}, bf16[1024,256]{1,0:T(8,128)(2,1)S(1)}, u32[]{:S(2)}, u32[]{:S(2)}) %collective-permute-start.4) | collective-permute-done | bytes 524320 | tf_op jit(solution)/shard_map/ppermute | solution.py:29
  54.0 2.6 %collective-permute-done.11.refs_2_ = bf16[528,256]{1,0:T(8,128)(2,1)S(1)} collective-permute-done((bf16[528,256]{1,0:T(8,128)(2,1)S(1)}, bf16[528,256]{1,0:T(8,128)(2,1)S(1)}, u32[]{:S(2)}, u32[]{:S(2)}) %collective-permute-start.11) | collective-permute-done | bytes 270368 | tf_op jit(solution)/shard_map/ppermute | solution.py:29
  57.1 2.7 %collective-permute-start.14 = (bf16[1024,256]{1,0:T(8,128)(2,1)S(1)}, bf16[1024,256]{1,0:T(8,128)(2,1)S(1)}, u32[]{:S(2)}, u32[]{:S(2)}) collective-permute-start(bf16[1024,256]{1,0:T(8,128)(2,1)S(1)} %get-tuple-element.57), channel_id=1, source_target_pairs={{0,96},{32,0},{64,32},{96,64},{1,97},{33,1},{65,33},{97,65},{2,98}... | collective-permute-start | bytes 1572872 | tf_op jit(solution)/shard_map/ppermute | solution.py:29
  63.5 4.0 %collective-permute-done.9.refs_2_ = bf16[512,256]{1,0:T(8,128)(2,1)S(1)} collective-permute-done((bf16[512,256]{1,0:T(8,128)(2,1)S(1)}, bf16[512,256]{1,0:T(8,128)(2,1)S(1)}, u32[]{:S(2)}, u32[]{:S(2)}) %collective-permute-start.9) | collective-permute-done | bytes 262176 | tf_op jit(solution)/shard_map/ppermute | solution.py:29
  71.5 2.8 %collective-permute-start.15 = (bf16[4096,256]{1,0:T(8,128)(2,1)S(1)}, bf16[4096,256]{1,0:T(8,128)(2,1)S(1)}, u32[]{:S(2)}, u32[]{:S(2)}) collective-permute-start(bf16[4096,256]{1,0:T(8,128)(2,1)S(1)} %pack_weights.1.rest_0_), channel_id=1, source_target_pairs={{0,1},{1,0},{2,3},{3,2},{4,5},{5,4},{6,7},{7,6},{8,9},{9,8},{10,11... | collective-permute-start | bytes 6291464 | tf_op jit(solution)/shard_map/ppermute | solution.py:33
  74.3 3.8 %collective-permute-done.15.rest_1_ = bf16[4096,256]{1,0:T(8,128)(2,1)S(1)} collective-permute-done((bf16[4096,256]{1,0:T(8,128)(2,1)S(1)}, bf16[4096,256]{1,0:T(8,128)(2,1)S(1)}, u32[]{:S(2)}, u32[]{:S(2)}) %collective-permute-start.15) | collective-permute-done | bytes 2097184 | tf_op jit(solution)/shard_map/ppermute | solution.py:33
  80.3 3.1 %collective-permute-start.20 = (bf16[512,256]{1,0:T(8,128)(2,1)S(1)}, bf16[512,256]{1,0:T(8,128)(2,1)S(1)}, u32[]{:S(2)}, u32[]{:S(2)}) collective-permute-start(bf16[512,256]{1,0:T(8,128)(2,1)S(1)} %get-tuple-element.67), channel_id=1, source_target_pairs={{0,96},{32,0},{64,32},{96,64},{1,97},{33,1},{65,33},{97,65},{2,98}... | collective-permute-start | bytes 786440 | tf_op jit(solution)/shard_map/ppermute | solution.py:29
  83.4 4.1 %stage_unembed.1.refs_5_.stage = bf16[2048,2048]{1,0:T(8,128)(2,1)S(1)} custom-call(s32[6]{0:T(128)S(1)} %stack.43.place, bf16[4096,2048]{1,0:T(8,128)(2,1)} %unembed.1, bf16[1024,256]{1,0:T(8,128)(2,1)S(1)} %get-tuple-element.58.refs_0_.refs_3_), custom_call_target="tpu_custom_call" | custom-call | bytes 8388608 | tf_op jit(solution)/shard_map/stage_unembed/pallas_call | solution.py:456
  93.8 3.8 %collective-permute-start.16 = (bf16[272,256]{1,0:T(8,128)(2,1)S(1)}, bf16[272,256]{1,0:T(8,128)(2,1)S(1)}, u32[]{:S(2)}, u32[]{:S(2)}) collective-permute-start(bf16[272,256]{1,0:T(8,128)(2,1)S(1)} %get-tuple-element.61), channel_id=1, source_target_pairs={{0,8},{8,16},{16,24},{24,0},{1,9},{9,17},{17,25},{25,1},{2,10},{10... | collective-permute-start | bytes 417800 | tf_op jit(solution)/shard_map/ppermute | solution.py:29
  100.1 3.7 %collective-permute-done.21.refs_4_.refs_1_ = bf16[1024,256]{1,0:T(8,128)(2,1)S(1)} collective-permute-done((bf16[1024,256]{1,0:T(8,128)(2,1)S(1)}, bf16[1024,256]{1,0:T(8,128)(2,1)S(1)}, u32[]{:S(2)}, u32[]{:S(2)}) %collective-permute-start.21) | collective-permute-done | bytes 524320 | tf_op jit(solution)/shard_map/ppermute | solution.py:29
  104.8 3.5 %collective-permute-start.23 = (bf16[256,256]{1,0:T(8,128)(2,1)S(1)}, bf16[256,256]{1,0:T(8,128)(2,1)S(1)}, u32[]{:S(2)}, u32[]{:S(2)}) collective-permute-start(bf16[256,256]{1,0:T(8,128)(2,1)S(1)} %get-tuple-element.76), channel_id=1, source_target_pairs={{0,8},{8,16},{16,24},{24,0},{1,9},{9,17},{17,25},{25,1},{2,10},{10... | collective-permute-start | bytes 393224 | tf_op jit(solution)/shard_map/ppermute | solution.py:29
  121.1 3.0 %other_hidden.1 = (bf16[528,512]{1,0:T(8,128)(2,1)S(1)}, bf16[528,512]{1,0:T(8,128)(2,1)S(1)}, bf16[528,512]{1,0:T(8,128)(2,1)S(1)}, bf16[528,512]{1,0:T(8,128)(2,1)S(1)}) custom-call(s32[6]{0:T(128)S(1)} %stack.43.place, bf16[2048,2048]{1,0:T(8,128)(2,1)S(1)} %stage_unembed.1.refs_5_.stage, bf16[2064,256]{1,0:T(8,128)(2,1)S(1)} %logit_grad.3.mine, ...), custom_call_target="tpu_custom_call" | custom-call | flops 2147483648 | bytes 8388608 | tf_op jit(solution)/shard_map/other_hidden/pallas_call | solution.py:506
  128.4 5.5 %collective-permute-done.27.refs_1_ = bf16[528,512]{1,0:T(8,128)(2,1)S(1)} collective-permute-done((bf16[528,512]{1,0:T(8,128)(2,1)S(1)}, bf16[528,512]{1,0:T(8,128)(2,1)S(1)}, u32[]{:S(2)}, u32[]{:S(2)}) %collective-permute-start.27) | collective-permute-done | bytes 540704 | tf_op jit(solution)/shard_map/ppermute | solution.py:615
  133.9 6.5 %collective-permute-done.28.refs_2_ = bf16[528,512]{1,0:T(8,128)(2,1)S(1)} collective-permute-done((bf16[528,512]{1,0:T(8,128)(2,1)S(1)}, bf16[528,512]{1,0:T(8,128)(2,1)S(1)}, u32[]{:S(2)}, u32[]{:S(2)}) %collective-permute-start.28) | collective-permute-done | bytes 540704 | tf_op jit(solution)/shard_map/ppermute | solution.py:615
  141.9 3.2 %collective-permute-start.31 = (bf16[144,512]{1,0:T(8,128)(2,1)S(1)}, bf16[144,512]{1,0:T(8,128)(2,1)S(1)}, u32[]{:S(2)}, u32[]{:S(2)}) collective-permute-start(bf16[144,512]{1,0:T(8,128)(2,1)S(1)} %get-tuple-element.85), channel_id=1, source_target_pairs={{0,16},{1,65},{8,24},{9,73},{16,0},{17,81},{24,8},{25,89},{32,48},... | collective-permute-start | bytes 442376 | tf_op jit(solution)/shard_map/ppermute | solution.py:615
  146.6 2.7 %collective-permute-done.31.refs_2_ = bf16[144,512]{1,0:T(8,128)(2,1)S(1)} collective-permute-done((bf16[144,512]{1,0:T(8,128)(2,1)S(1)}, bf16[144,512]{1,0:T(8,128)(2,1)S(1)}, u32[]{:S(2)}, u32[]{:S(2)}) %collective-permute-start.31) | collective-permute-done | bytes 147488 | tf_op jit(solution)/shard_map/ppermute | solution.py:615
  149.9 2.9 %collective-permute-start.33 = (bf16[128,256]{1,0:T(8,128)(2,1)S(1)}, bf16[128,256]{1,0:T(8,128)(2,1)S(1)}, u32[]{:S(2)}, u32[]{:S(2)}) collective-permute-start(bf16[128,256]{1,0:T(8,128)(2,1)S(1)} %get-tuple-element.88), channel_id=1, source_target_pairs={{0,1},{1,0},{2,3},{3,2},{4,5},{5,4},{6,7},{7,6},{8,9},{9,8},{10,11... | collective-permute-start | bytes 196616 | tf_op jit(solution)/shard_map/ppermute | solution.py:33
  (90 shorter events, 58.5 us)
Async XLA Ops:
  3.2 34.4 %collective-permute-start.5 = (bf16[1088,256]{1,0:T(8,128)(2,1)}, bf16[1088,256]{1,0:T(8,128)(2,1)}, u32[]{:S(2)}, u32[]{:S(2)}) collective-permute-start(bf16[1088,256]{1,0:T(8,128)(2,1)} %prepare_weights.1.rest_0_), channel_id=1, source_target_pairs={{0,1},{1,0},{2,3},{3,2},{4,5},{5,4},{6,7},{7,6},{8,9},{9,8},{10,11... | collective-permute-start | bytes 1671176 | tf_op jit(solution)/shard_map/ppermute | solution.py:33
  4.6 26.7 %collective-permute-start.2 = (bf16[1088,256]{1,0:T(8,128)(2,1)}, bf16[1088,256]{1,0:T(8,128)(2,1)}, u32[]{:S(2)}, u32[]{:S(2)}) collective-permute-start(bf16[1088,256]{1,0:T(8,128)(2,1)} %prepare_weights.1.rest_0_), channel_id=1, source_target_pairs={{0,6},{2,0},{4,2},{6,4},{1,7},{3,1},{5,3},{7,5},{8,14},{10,8},{12,... | collective-permute-start | bytes 1671176 | tf_op jit(solution)/shard_map/ppermute | solution.py:29
  7.2 24.2 %collective-permute-start.1 = (bf16[1088,256]{1,0:T(8,128)(2,1)}, bf16[1088,256]{1,0:T(8,128)(2,1)}, u32[]{:S(2)}, u32[]{:S(2)}) collective-permute-start(bf16[1088,256]{1,0:T(8,128)(2,1)} %prepare_weights.1.rest_0_), channel_id=1, source_target_pairs={{0,4},{2,6},{4,0},{6,2},{1,5},{3,7},{5,1},{7,3},{8,12},{10,14},{12... | collective-permute-start | bytes 1671176 | tf_op jit(solution)/shard_map/ppermute | solution.py:29
  7.7 27.7 %collective-permute-start = (bf16[1088,256]{1,0:T(8,128)(2,1)}, bf16[1088,256]{1,0:T(8,128)(2,1)S(1)}, u32[]{:S(2)}, u32[]{:S(2)}) collective-permute-start(bf16[1088,256]{1,0:T(8,128)(2,1)} %prepare_weights.1.rest_0_), channel_id=1, source_target_pairs={{0,2},{2,4},{4,6},{6,0},{1,3},{3,5},{5,7},{7,1},{8,10},{10,12},{12... | collective-permute-start | bytes 1671176 | tf_op jit(solution)/shard_map/ppermute | solution.py:29
  37.3 13.9 %collective-permute-start.4 = (bf16[1024,256]{1,0:T(8,128)(2,1)}, bf16[1024,256]{1,0:T(8,128)(2,1)S(1)}, u32[]{:S(2)}, u32[]{:S(2)}) collective-permute-start(bf16[1024,256]{1,0:T(8,128)(2,1)} %slice_weights.1.rest_9_.refs_0_), channel_id=1, source_target_pairs={{0,6},{2,0},{4,2},{6,4},{1,7},{3,1},{5,3},{7,5},{8,14},{10,8},{12,... | collective-permute-start | bytes 1572872 | tf_op jit(solution)/shard_map/ppermute | solution.py:29
  37.6 14.8 %collective-permute-start.3 = (bf16[1024,256]{1,0:T(8,128)(2,1)}, bf16[1024,256]{1,0:T(8,128)(2,1)}, u32[]{:S(2)}, u32[]{:S(2)}) collective-permute-start(bf16[1024,256]{1,0:T(8,128)(2,1)} %slice_weights.1.rest_9_.refs_0_), channel_id=1, source_target_pairs={{0,2},{2,4},{4,6},{6,0},{1,3},{3,5},{5,7},{7,1},{8,10},{10,12},{12... | collective-permute-start | bytes 1572872 | tf_op jit(solution)/shard_map/ppermute | solution.py:29
  44.6 9.4 %collective-permute-start.12 = (bf16[528,256]{1,0:T(8,128)(2,1)S(1)}, bf16[528,256]{1,0:T(8,128)(2,1)S(1)}, u32[]{:S(2)}, u32[]{:S(2)}) collective-permute-start(bf16[528,256]{1,0:T(8,128)(2,1)S(1)} %get-tuple-element.55), channel_id=1, source_target_pairs={{0,96},{32,0},{64,32},{96,64},{1,97},{33,1},{65,33},{97,65},{2,98}... | collective-permute-start | bytes 811016 | tf_op jit(solution)/shard_map/ppermute | solution.py:29
  48.3 8.4 %collective-permute-start.11 = (bf16[528,256]{1,0:T(8,128)(2,1)S(1)}, bf16[528,256]{1,0:T(8,128)(2,1)S(1)}, u32[]{:S(2)}, u32[]{:S(2)}) collective-permute-start(bf16[528,256]{1,0:T(8,128)(2,1)S(1)} %get-tuple-element.54.refs_4_), channel_id=1, source_target_pairs={{0,32},{32,64},{64,96},{96,0},{1,33},{33,65},{65,97},{97,1},{2,34}... | collective-permute-start | bytes 811016 | tf_op jit(solution)/shard_map/ppermute | solution.py:29
  57.0 13.1 %collective-permute-start.13 = (bf16[1040,256]{1,0:T(8,128)(2,1)S(1)}, bf16[1040,256]{1,0:T(8,128)(2,1)S(1)}, u32[]{:S(2)}, u32[]{:S(2)}) collective-permute-start(bf16[1040,256]{1,0:T(8,128)(2,1)S(1)} %get-tuple-element.56), channel_id=1, source_target_pairs={{0,32},{32,64},{64,96},{96,0},{1,33},{33,65},{65,97},{97,1},{2,34}... | collective-permute-start | bytes 1597448 | tf_op jit(solution)/shard_map/ppermute | solution.py:29
  57.1 11.8 %collective-permute-start.14 = (bf16[1024,256]{1,0:T(8,128)(2,1)S(1)}, bf16[1024,256]{1,0:T(8,128)(2,1)S(1)}, u32[]{:S(2)}, u32[]{:S(2)}) collective-permute-start(bf16[1024,256]{1,0:T(8,128)(2,1)S(1)} %get-tuple-element.57), channel_id=1, source_target_pairs={{0,96},{32,0},{64,32},{96,64},{1,97},{33,1},{65,33},{97,65},{2,98}... | collective-permute-start | bytes 1572872 | tf_op jit(solution)/shard_map/ppermute | solution.py:29
  60.8 6.8 %collective-permute-start.9 = (bf16[512,256]{1,0:T(8,128)(2,1)S(1)}, bf16[512,256]{1,0:T(8,128)(2,1)S(1)}, u32[]{:S(2)}, u32[]{:S(2)}) collective-permute-start(bf16[512,256]{1,0:T(8,128)(2,1)S(1)} %get-tuple-element.50), channel_id=1, source_target_pairs={{0,2},{2,4},{4,6},{6,0},{1,3},{3,5},{5,7},{7,1},{8,10},{10,12},{12... | collective-permute-start | bytes 786440 | tf_op jit(solution)/shard_map/ppermute | solution.py:29
  80.0 9.6 %collective-permute-start.19 = (bf16[512,256]{1,0:T(8,128)(2,1)S(1)}, bf16[512,256]{1,0:T(8,128)(2,1)S(1)}, u32[]{:S(2)}, u32[]{:S(2)}) collective-permute-start(bf16[512,256]{1,0:T(8,128)(2,1)S(1)} %get-tuple-element.66), channel_id=1, source_target_pairs={{0,32},{32,64},{64,96},{96,0},{1,33},{33,65},{65,97},{97,1},{2,34}... | collective-permute-start | bytes 786440 | tf_op jit(solution)/shard_map/ppermute | solution.py:29
  80.3 9.4 %collective-permute-start.20 = (bf16[512,256]{1,0:T(8,128)(2,1)S(1)}, bf16[512,256]{1,0:T(8,128)(2,1)S(1)}, u32[]{:S(2)}, u32[]{:S(2)}) collective-permute-start(bf16[512,256]{1,0:T(8,128)(2,1)S(1)} %get-tuple-element.67), channel_id=1, source_target_pairs={{0,96},{32,0},{64,32},{96,64},{1,97},{33,1},{65,33},{97,65},{2,98}... | collective-permute-start | bytes 786440 | tf_op jit(solution)/shard_map/ppermute | solution.py:29
  90.0 13.8 %collective-permute-start.21 = (bf16[1024,256]{1,0:T(8,128)(2,1)S(1)}, bf16[1024,256]{1,0:T(8,128)(2,1)S(1)}, u32[]{:S(2)}, u32[]{:S(2)}) collective-permute-start(bf16[1024,256]{1,0:T(8,128)(2,1)S(1)} %get-tuple-element.69), channel_id=1, source_target_pairs={{0,32},{32,64},{64,96},{96,0},{1,33},{33,65},{65,97},{97,1},{2,34}... | collective-permute-start | bytes 1572872 | tf_op jit(solution)/shard_map/ppermute | solution.py:29
  90.6 13.2 %collective-permute-start.22 = (bf16[1024,256]{1,0:T(8,128)(2,1)S(1)}, bf16[1024,256]{1,0:T(8,128)(2,1)S(1)}, u32[]{:S(2)}, u32[]{:S(2)}) collective-permute-start(bf16[1024,256]{1,0:T(8,128)(2,1)S(1)} %get-tuple-element.70), channel_id=1, source_target_pairs={{0,96},{32,0},{64,32},{96,64},{1,97},{33,1},{65,33},{97,65},{2,98}... | collective-permute-start | bytes 1572872 | tf_op jit(solution)/shard_map/ppermute | solution.py:29
  93.8 15.0 %collective-permute-start.16 = (bf16[272,256]{1,0:T(8,128)(2,1)S(1)}, bf16[272,256]{1,0:T(8,128)(2,1)S(1)}, u32[]{:S(2)}, u32[]{:S(2)}) collective-permute-start(bf16[272,256]{1,0:T(8,128)(2,1)S(1)} %get-tuple-element.61), channel_id=1, source_target_pairs={{0,8},{8,16},{16,24},{24,0},{1,9},{9,17},{17,25},{25,1},{2,10},{10... | collective-permute-start | bytes 417800 | tf_op jit(solution)/shard_map/ppermute | solution.py:29
  97.6 13.1 %collective-permute-start.17 = (bf16[272,256]{1,0:T(8,128)(2,1)S(1)}, bf16[272,256]{1,0:T(8,128)(2,1)S(1)}, u32[]{:S(2)}, u32[]{:S(2)}) collective-permute-start(bf16[272,256]{1,0:T(8,128)(2,1)S(1)} %get-tuple-element.62), channel_id=1, source_target_pairs={{0,16},{8,24},{16,0},{24,8},{1,17},{9,25},{17,1},{25,9},{2,18},{10... | collective-permute-start | bytes 417800 | tf_op jit(solution)/shard_map/ppermute | solution.py:29
  98.1 12.6 %collective-permute-start.18 = (bf16[272,256]{1,0:T(8,128)(2,1)S(1)}, bf16[272,256]{1,0:T(8,128)(2,1)S(1)}, u32[]{:S(2)}, u32[]{:S(2)}) collective-permute-start(bf16[272,256]{1,0:T(8,128)(2,1)S(1)} %get-tuple-element.63), channel_id=1, source_target_pairs={{0,24},{8,0},{16,8},{24,16},{1,25},{9,1},{17,9},{25,17},{2,26},{10... | collective-permute-start | bytes 417800 | tf_op jit(solution)/shard_map/ppermute | solution.py:29
  104.8 7.6 %collective-permute-start.23 = (bf16[256,256]{1,0:T(8,128)(2,1)S(1)}, bf16[256,256]{1,0:T(8,128)(2,1)S(1)}, u32[]{:S(2)}, u32[]{:S(2)}) collective-permute-start(bf16[256,256]{1,0:T(8,128)(2,1)S(1)} %get-tuple-element.76), channel_id=1, source_target_pairs={{0,8},{8,16},{16,24},{24,0},{1,9},{9,17},{17,25},{25,1},{2,10},{10... | collective-permute-start | bytes 393224 | tf_op jit(solution)/shard_map/ppermute | solution.py:29
  108.3 6.6 %collective-permute-start.24 = (bf16[256,256]{1,0:T(8,128)(2,1)S(1)}, bf16[256,256]{1,0:T(8,128)(2,1)S(1)}, u32[]{:S(2)}, u32[]{:S(2)}) collective-permute-start(bf16[256,256]{1,0:T(8,128)(2,1)S(1)} %get-tuple-element.77), channel_id=1, source_target_pairs={{0,16},{8,24},{16,0},{24,8},{1,17},{9,25},{17,1},{25,9},{2,18},{10... | collective-permute-start | bytes 393224 | tf_op jit(solution)/shard_map/ppermute | solution.py:29
  124.1 9.8 %collective-permute-start.27 = (bf16[528,512]{1,0:T(8,128)(2,1)S(1)}, bf16[528,512]{1,0:T(8,128)(2,1)S(1)}, u32[]{:S(2)}, u32[]{:S(2)}) collective-permute-start(bf16[528,512]{1,0:T(8,128)(2,1)S(1)} %get-tuple-element.80), channel_id=1, source_target_pairs={{0,32},{1,9},{8,40},{9,17},{16,48},{17,25},{24,56},{25,1},{32,64},... | collective-permute-start | bytes 1622024 | tf_op jit(solution)/shard_map/ppermute | solution.py:615
  125.3 15.1 %collective-permute-start.28 = (bf16[528,512]{1,0:T(8,128)(2,1)S(1)}, bf16[528,512]{1,0:T(8,128)(2,1)S(1)}, u32[]{:S(2)}, u32[]{:S(2)}) collective-permute-start(bf16[528,512]{1,0:T(8,128)(2,1)S(1)} %get-tuple-element.81), channel_id=1, source_target_pairs={{0,64},{1,17},{8,72},{9,25},{16,80},{17,1},{24,88},{25,9},{32,96},... | collective-permute-start | bytes 1622024 | tf_op jit(solution)/shard_map/ppermute | solution.py:615
  127.6 12.8 %collective-permute-start.29 = (bf16[528,512]{1,0:T(8,128)(2,1)S(1)}, bf16[528,512]{1,0:T(8,128)(2,1)S(1)}, u32[]{:S(2)}, u32[]{:S(2)}) collective-permute-start(bf16[528,512]{1,0:T(8,128)(2,1)S(1)} %get-tuple-element.82), channel_id=1, source_target_pairs={{0,96},{1,25},{8,104},{9,1},{16,112},{17,9},{24,120},{25,17},{32,0... | collective-permute-start | bytes 1622024 | tf_op jit(solution)/shard_map/ppermute | solution.py:615
  141.9 7.4 %collective-permute-start.31 = (bf16[144,512]{1,0:T(8,128)(2,1)S(1)}, bf16[144,512]{1,0:T(8,128)(2,1)S(1)}, u32[]{:S(2)}, u32[]{:S(2)}) collective-permute-start(bf16[144,512]{1,0:T(8,128)(2,1)S(1)} %get-tuple-element.85), channel_id=1, source_target_pairs={{0,16},{1,65},{8,24},{9,73},{16,0},{17,81},{24,8},{25,89},{32,48},... | collective-permute-start | bytes 442376 | tf_op jit(solution)/shard_map/ppermute | solution.py:615
  (18 other events, 128.7 us)

commit v8 on v7

v8 whole, which is shorter than its diff:
```python
import functools

import jax
import jax.numpy as jnp
from jax import lax
from jax.experimental import pallas as pl
from jax.experimental.pallas import tpu as pltpu
from jax.sharding import Mesh
from jax.sharding import PartitionSpec as P

F32 = jnp.float32
BF16 = jnp.bfloat16
SIDE = 4
VMEM = pl.BlockSpec(memory_space=pltpu.VMEM)
SMEM = pl.BlockSpec(memory_space=pltpu.SMEM)
ANY = pl.BlockSpec(memory_space=pl.ANY)
MIB = 1024 * 1024


def params(mib=16):
    return pltpu.CompilerParams(vmem_limit_bytes=mib * MIB)


def cost(flops, moved, transcendentals=0):
    return pl.CostEstimate(flops=flops, bytes_accessed=moved, transcendentals=transcendentals)


def send(value, axis, step):
    return lax.ppermute(value, axis, [(i, (i + step) % SIDE) for i in range(SIDE)])


def swap(value):
    return lax.ppermute(value, "tc", [(0, 1), (1, 0)])


def thirds(value):
    high = value.astype(BF16).astype(F32)
    rest = value - high
    middle = rest.astype(BF16).astype(F32)
    return high, middle, rest - middle


def prepare_kernel(weights, piece):
    slots, shard_rows, _ = weights.shape
    width = piece.shape[1]
    rows = slots * shard_rows
    piece[0:rows, :] = weights[:, :, 0:width].reshape(rows, width)
    sums = jnp.sum(weights[...].astype(F32), axis=2, keepdims=True).reshape(rows, 1)
    line = jnp.broadcast_to(sums, (rows, 128)).T[0:1]
    lines = jnp.concatenate(list(thirds(line)) + [jnp.zeros((5, rows), F32)], axis=0)
    extra = jnp.concatenate([lines[:, i * 128 : (i + 1) * 128] for i in range(8)], axis=0)
    if width > 128:
        extra = jnp.concatenate([extra, jnp.zeros((64, width - 128), F32)], axis=1)
    piece[rows : rows + 64, :] = extra.astype(BF16)


def prepared(weights):
    slots, shard_rows, width = weights.shape
    return pl.pallas_call(
        prepare_kernel,
        out_shape=jax.ShapeDtypeStruct((slots * shard_rows + 64, width), BF16),
        in_specs=[VMEM],
        out_specs=VMEM,
        compiler_params=params(),
        cost_estimate=cost(2 * weights.size, 3 * weights.size),
        name="prepare_weights",
    )(weights)


def halves_kernel(right, left, *refs):
    top, low = refs[-2:]
    top[...] = right[0 : top.shape[0], :]
    low[...] = left[top.shape[0] :, :]


def halves(right, left, behind):
    depth, width = right.shape
    outs = [jax.ShapeDtypeStruct((rows, width), BF16) for rows in (512, depth - 512)]
    return pl.pallas_call(
        halves_kernel,
        out_shape=outs,
        in_specs=[VMEM, VMEM] + [ANY] * len(behind),
        out_specs=[VMEM, VMEM],
        compiler_params=params(),
        cost_estimate=cost(0, 4 * depth * width),
        name="take_halves",
    )(right, left, *behind)


def product_kernel(place, pairs, count, probs, before, *rest):
    pieces, outs = rest[:10], rest[10:15]
    across, total, sums, line, seen = rest[15:]
    mine = [pieces[0], pieces[1], across.at[0], pieces[2]]
    other = [pieces[5], pieces[6], across.at[1], pieces[7]]
    for core in range(2):
        across[core, 0:512] = pieces[5 * core + 3][...]
        across[core, 512:] = pieces[5 * core + 4][...]
    block = 512
    rows = probs.shape[0]
    half = rows // 2
    vocab_y = place[0]
    first_block = (vocab_y * SIDE + place[1]) * (probs.shape[1] // block)
    core_0 = place[3] == 0

    def in_order(step, at):
        one, two = mine[step][at, :], other[step][at, :]
        return jnp.where(core_0, one, two), jnp.where(core_0, two, one)

    line[...] = jnp.zeros_like(line)
    lane = lax.broadcasted_iota(jnp.int32, (64, 128), 1)
    for step in range(SIDE):
        even, odd = in_order(step, slice(1024, 1088))
        even, odd = even[:, 0:128].astype(F32), odd[:, 0:128].astype(F32)
        x = lax.rem(place[2] + SIDE - step, SIDE)
        lanes = pl.ds(pl.multiple_of(x * 128, 128), 128)
        sums[0, :, lanes] = jnp.where(lane < 64, even, pltpu.roll(odd, 64, 1))
        sums[1, :, lanes] = jnp.where(lane < 64, pltpu.roll(even, 64, 1), odd)
    for owner in range(SIDE * SIDE):
        seen[owner] = 0

    def tile(slot, carry):
        teacher = pairs[slot, 0] - first_block
        owner = pairs[slot, 1] // SIDE
        at = pl.ds(pl.multiple_of(slot * 64, 64), 64)
        matrix, columns = [], []
        for step in range(SIDE):
            matrix.extend(in_order(step, at))
            x = lax.rem(place[2] + SIDE - step, SIDE)
            columns.append(probs[:, pl.ds(pl.multiple_of(teacher * block + x * 128, 128), 128)])
        product = jnp.dot(
            jnp.concatenate(columns, axis=1), jnp.concatenate(matrix, axis=0), preferred_element_type=F32
        )
        row_sums = sums[lax.rem(slot, 2), pl.ds(pl.multiple_of(slot // 2 * 8, 8), 8), :]
        line[...] += lax.dot_general(
            row_sums.astype(BF16),
            probs[:, pl.ds(pl.multiple_of(teacher * block, block), block)],
            (((1,), (1,)), ((), ())),
            preferred_element_type=F32,
        )
        fresh = seen[owner] == 0

        @pl.when(fresh)
        def _():
            total[owner] = product

        @pl.when(jnp.logical_not(fresh))
        def _():
            total[owner] += product

        seen[owner] = 1
        return carry

    lax.fori_loop(0, count[0], tile, 0)
    for step in range(SIDE):
        start = lax.rem(vocab_y + step, SIDE) * SIDE
        for z in range(SIDE):
            used = seen[start + z] == 1

            def put(value):
                if step == 2:
                    outs[3][z * half : z * half + half, :] = value[:half]
                    outs[4][z * half : z * half + half, :] = value[half:]
                else:
                    outs[step - step // 3][z * rows : z * rows + rows, :] = value

            @pl.when(used)
            def _():
                put(total[start + z].astype(BF16))

            @pl.when(jnp.logical_not(used))
            def _():
                put(jnp.zeros(total.shape[1:], BF16))

    sent = line[0:1] + line[1:2] + line[2:3]
    packed = pack_rows([before[0:1], before[1:2], sent, before[3:4], before[4:5]])
    for out in outs[3:]:
        put_rows(out, SIDE * half, packed)


def put_rows(out, at, packed):
    wide = jnp.zeros((16, out.shape[1] - packed.shape[1]), BF16)
    out[at : at + 16, :] = jnp.concatenate([packed, wide], axis=1)


def products(place, pairs, count, probs, before, pieces):
    rows = probs.shape[0]
    depth, width = pieces[0].shape
    return pl.pallas_call(
        product_kernel,
        out_shape=[jax.ShapeDtypeStruct((SIDE * rows, width), BF16)] * 3
        + [jax.ShapeDtypeStruct((SIDE * rows // 2 + 16, width), BF16)] * 2,
        in_specs=[SMEM, SMEM, SMEM] + [VMEM] * (2 + len(pieces)),
        out_specs=[VMEM] * (SIDE + 1),
        scratch_shapes=[
            pltpu.VMEM((2, depth, width), BF16),
            pltpu.VMEM((SIDE * SIDE, rows, width), F32),
            pltpu.VMEM((2, 64, 512), F32),
            pltpu.VMEM((8, rows), F32),
            pltpu.SMEM((SIDE * SIDE,), jnp.int32),
        ],
        compiler_params=params(20),
        cost_estimate=cost(
            16 * 2 * rows * 512 * width, 2 * probs.size + 16 * depth * width + 32 * rows * width
        ),
        name="tile_products",
    )(place, pairs, count, probs, before, *pieces)


def pack_rows(lines):
    rows = [part for line in lines for part in thirds(line)]
    rows.append(jnp.zeros((16 - len(rows), rows[0].shape[1]), F32))
    return jnp.concatenate(rows, axis=0).astype(BF16)


def unpack_rows(packed, number):
    packed = packed.astype(F32)
    return [
        packed[3 * i : 3 * i + 1] + packed[3 * i + 1 : 3 * i + 2] + packed[3 * i + 2 : 3 * i + 3]
        for i in range(number)
    ]


def joined(stats):
    peak = functools.reduce(jnp.maximum, [line[0] for line in stats])
    speak = functools.reduce(jnp.maximum, [line[3] for line in stats])
    factors = [jnp.exp(line[0] - peak) for line in stats]
    mass = sum(line[1] * factor for line, factor in zip(stats, factors))
    total = sum(line[2] * factor for line, factor in zip(stats, factors))
    smass = sum(line[4] * jnp.exp(line[3] - speak) for line in stats)
    return (peak, mass, total, speak, smass), factors


def columns_of(lines):
    lines = list(lines) + [jnp.zeros((128 - len(lines), lines[0].shape[1]), F32)]
    return jnp.concatenate(lines, axis=0).T


def relay_kernel(near, far, from_left, from_right, mine, *refs):
    near_out, far_out, kept = refs[-3:]
    depth = from_left.shape[0] - 16
    half = depth // SIDE
    rows = 2 * half
    stats = [unpack_rows(part[depth:, 0:rows], 5) for part in (mine, from_left, from_right)]
    kept[...] = jnp.concatenate(stats[0] + stats[1] + stats[2] + [jnp.zeros((1, rows), F32)], axis=0)
    own, left, right = (line[0] for line in stats)
    lane = lax.broadcasted_iota(jnp.int32, own.shape, 1)
    other = jnp.where(lane < half, left, right)
    peak = jnp.maximum(own, other)
    table = columns_of([jnp.exp(own - peak), jnp.exp(other - peak)])
    near_out[SIDE * rows : SIDE * rows + 16, :] = from_left[depth : depth + 16, :]
    for z in range(SIDE):
        low, high = slice(z * rows, z * rows + half), slice(z * rows + half, (z + 1) * rows)
        part = slice(z * half, (z + 1) * half)
        value = table[:half, 0:1] * near[low, :].astype(F32) + table[:half, 1:2] * from_left[part, :].astype(F32)
        near_out[low, :] = value.astype(BF16)
        near_out[high, :] = near[high, :]
        value = table[half:, 0:1] * far[high, :].astype(F32) + table[half:, 1:2] * from_right[part, :].astype(F32)
        far_out[high, :] = value.astype(BF16)
        far_out[low, :] = far[low, :]


def relayed(near, far, from_left, from_right, last, behind):
    depth, width = near.shape
    rows = depth // SIDE
    return pl.pallas_call(
        relay_kernel,
        out_shape=[
            jax.ShapeDtypeStruct((depth + 16, width), BF16),
            jax.ShapeDtypeStruct((depth, width), BF16),
            jax.ShapeDtypeStruct((16, rows), F32),
        ],
        in_specs=[VMEM] * 5 + [ANY] * len(behind),
        out_specs=[VMEM] * 3,
        compiler_params=params(),
        cost_estimate=cost(depth * width, 8 * depth * width),
        name="relay_targets",
    )(near, far, from_left, from_right, last, *behind)


def merge_kernel(place, given, *refs):
    parts, outs = refs[:3], refs[3:]
    rows = outs[0].shape[0] - 16
    lines = [[given[5 * i + j : 5 * i + j + 1] for j in range(5)] for i in range(3)]
    lines.append(unpack_rows(parts[1][SIDE * rows :, 0:rows], 5))
    stats, _ = joined(lines)
    packed = pack_rows(stats)
    own, left, right, across = (line[0] for line in lines)
    lane = lax.broadcasted_iota(jnp.int32, own.shape, 1)
    low = lane < rows // 2
    left = jnp.where(low, jnp.maximum(left, across), left)
    right = jnp.where(low, right, jnp.maximum(right, across))
    table = columns_of([jnp.exp(base - stats[0]) for base in (own, left, right)])
    for step in range(SIDE):
        at = pl.ds(pl.multiple_of(lax.rem(place[1] + step, SIDE) * rows, rows), rows)
        value = table[:, 0:1] * parts[0][at, :].astype(F32)
        for d in range(1, 3):
            value += table[:, d : d + 1] * parts[d][at, :].astype(F32)
        outs[step][0:rows, :] = value.astype(BF16)
        put_rows(outs[step], rows, packed)


def merged(place, given, parts, rows):
    width = parts[0].shape[1]
    return pl.pallas_call(
        merge_kernel,
        out_shape=[jax.ShapeDtypeStruct((rows + 16, width), BF16)] * SIDE,
        in_specs=[SMEM] + [VMEM] * 4,
        out_specs=[VMEM] * SIDE,
        compiler_params=params(),
        cost_estimate=cost(32 * rows * width, 40 * rows * width),
        name="merge_targets",
    )(place, given, *parts)


def gradient_kernel(place, logits, *refs):
    parts, grad = refs[:SIDE], refs[SIDE]
    rows, width = logits.shape[0], parts[0].shape[1]
    stats, factors = joined([unpack_rows(part[rows:, 0:rows], 5) for part in parts])
    _, mass, total, peak, smass = stats
    total = total / mass
    floored = jnp.maximum(total, 1.0)
    scales = [factor / mass / floored for factor in factors]
    table = columns_of(scales + [total / floored / smass, peak, peak + jnp.log(smass)])
    share, peak, norm = (table[:, c : c + 1] for c in range(4, 7))
    terms = jnp.zeros((rows, width), F32)
    for step in range(SIDE):
        block = lax.rem(place[1] + SIDE - step, SIDE)
        at = pl.ds(pl.multiple_of(block * width, width), width)
        scores = logits[:, at]
        target = parts[step][0:rows, :].astype(F32) * table[:, step : step + 1]
        positive = target > 0
        entropy = jnp.where(positive, target * jnp.log(jnp.where(positive, target, 1.0)), 0.0)
        terms += entropy - target * (scores - norm)
        value = share * jnp.exp(scores - peak) - target
        grad[at, :] = value.T.astype(BF16)
    grad[SIDE * width :, :] = pack_rows([jnp.sum(terms.T, axis=0, keepdims=True)])


def gradients(place, logits, parts):
    rows, cols = logits.shape
    return pl.pallas_call(
        gradient_kernel,
        out_shape=jax.ShapeDtypeStruct((cols + 16, rows), BF16),
        in_specs=[SMEM] + [VMEM] * (1 + SIDE),
        out_specs=VMEM,
        compiler_params=params(),
        cost_estimate=cost(60 * rows * cols, 8 * rows * cols, 2 * rows * cols),
        name="logit_grad",
    )(place, logits, *parts)


def stage_kernel(place, unembed, *refs):
    stage, sems = refs[-2:]
    first = place[3] == 0
    copies = []
    for major in range(SIDE):
        for minor in range(SIDE):
            index = major * SIDE + minor
            owner = jnp.where(first, index, minor * SIDE + major)
            start = pl.multiple_of(owner * 256 + place[3] * 128, 128)
            copies.append(
                pltpu.make_async_copy(
                    unembed.at[pl.ds(start, 128), :],
                    stage.at[pl.ds(index * 128, 128), :],
                    sems.at[index],
                )
            )
    for copy in copies:
        copy.start()
    for copy in copies:
        copy.wait()


def staged(place, unembed, behind):
    depth, cols = unembed.shape
    return pl.pallas_call(
        stage_kernel,
        out_shape=jax.ShapeDtypeStruct((depth // 2, cols), BF16),
        in_specs=[SMEM, pl.BlockSpec(memory_space=pltpu.HBM)] + [ANY] * len(behind),
        out_specs=VMEM,
        scratch_shapes=[pltpu.SemaphoreType.DMA((SIDE * SIDE,))],
        compiler_params=params(42),
        cost_estimate=cost(0, depth * cols),
        name="stage_unembed",
    )(place, unembed, *behind)


def own_kernel(stage, mine, out):
    depth = stage.shape[1]
    for step in range(SIDE):
        rows = slice(step * 512, step * 512 + 512)
        result = jnp.dot(stage[rows, :], mine[0:depth, :], preferred_element_type=F32)
        out[rows, :] = result.astype(BF16)


def own_hidden(stage, mine):
    depth, rows = stage.shape[0], mine.shape[1]
    return pl.pallas_call(
        own_kernel,
        out_shape=jax.ShapeDtypeStruct((depth, rows), BF16),
        in_specs=[VMEM, VMEM],
        out_specs=VMEM,
        compiler_params=params(),
        cost_estimate=cost(2 * stage.size * rows, 2 * stage.size),
        name="own_hidden",
    )(stage, mine)


def other_kernel(steps, place, stage, mine, other, own, *refs):
    outs = refs[-len(steps) :]
    depth = stage.shape[1]
    rows = mine.shape[1]
    lanes = pl.ds(pl.multiple_of(place[3] * rows, rows), rows)
    other_lanes = pl.ds(pl.multiple_of((1 - place[3]) * rows, rows), rows)
    for out, step in zip(outs, steps):
        at = pl.ds(pl.multiple_of(lax.rem(place[4] + step, SIDE) * 512, 512), 512)
        result = jnp.dot(stage[at, :], other[0:depth, :], preferred_element_type=F32)
        out[0:512, other_lanes] = result.astype(BF16)
        out[0:512, lanes] = own[at, :]
        out[512:528, lanes] = mine[depth : depth + 16, :]
        out[512:528, other_lanes] = other[depth : depth + 16, :]


def other_hidden(steps, place, stage, mine, other, own, behind=()):
    rows = mine.shape[1]
    return pl.pallas_call(
        functools.partial(other_kernel, steps),
        out_shape=[jax.ShapeDtypeStruct((528, 2 * rows), BF16)] * len(steps),
        in_specs=[SMEM] + [VMEM] * 4 + [ANY] * len(behind),
        out_specs=[VMEM] * len(steps),
        compiler_params=params(),
        cost_estimate=cost(len(steps) * stage.size * rows // 2, 2 * stage.size),
        name="other_hidden",
    )(place, stage, mine, other, own, *behind)


def packed_loss(index, parts, at, ordered):
    for step in range(SIDE):
        ordered[lax.rem(index + SIDE - step, SIDE)] = unpack_rows(parts[step][at : at + 16, :], 1)[0]
    return ((ordered[0] + ordered[1]) + ordered[2]) + ordered[3]


def middle_kernel(place, *refs):
    parts, outs, ordered = refs[:SIDE], refs[SIDE : 2 * SIDE], refs[2 * SIDE]
    packed = pack_rows([packed_loss(place[4], parts, 512, ordered)])
    for step in range(SIDE):
        at = pl.ds(pl.multiple_of(lax.rem(place[5] + step, SIDE) * 128, 128), 128)
        value = parts[0][at, :].astype(F32)
        for part in parts[1:]:
            value += part[at, :].astype(F32)
        outs[step][0:128, :] = value.astype(BF16)
        outs[step][128:144, :] = packed


def middle(place, parts):
    rows = parts[0].shape[1]
    return pl.pallas_call(
        middle_kernel,
        out_shape=[jax.ShapeDtypeStruct((144, rows), BF16)] * SIDE,
        in_specs=[SMEM] + [VMEM] * SIDE,
        out_specs=[VMEM] * SIDE,
        scratch_shapes=[pltpu.VMEM((SIDE, 1, rows), F32)],
        compiler_params=params(),
        cost_estimate=cost(4 * 512 * rows, 10 * 512 * rows),
        name="merge_grads",
    )(place, *parts)


def total_kernel(place, *refs):
    parts = refs[:SIDE]
    keep, give, loss, ordered = refs[SIDE:]
    rows = keep.shape[1]
    mine = pl.ds(pl.multiple_of(place[3] * rows, rows), rows)
    other = pl.ds(pl.multiple_of((1 - place[3]) * rows, rows), rows)
    ordered[4] = packed_loss(place[5], parts, 128, ordered)
    loss[...] = jnp.broadcast_to(ordered[4, :, mine], loss.shape)
    for lanes, out in ((other, give), (mine, keep)):
        value = parts[0][0:128, lanes].astype(F32)
        for part in parts[1:]:
            value += part[0:128, lanes].astype(F32)
        out[...] = value.astype(BF16)


def totals(place, parts):
    rows = parts[0].shape[1] // 2
    half = jax.ShapeDtypeStruct((128, rows), BF16)
    return pl.pallas_call(
        total_kernel,
        out_shape=[half, half, jax.ShapeDtypeStruct((8, rows), F32)],
        in_specs=[SMEM] + [VMEM] * SIDE,
        out_specs=[VMEM] * 3,
        scratch_shapes=[pltpu.VMEM((SIDE + 1, 1, 2 * rows), F32)],
        compiler_params=params(),
        cost_estimate=cost(8 * 128 * rows, 20 * 128 * rows),
        name="sum_grads",
    )(place, *parts)


def turn_kernel(place, keep, given, grad):
    mine = pl.ds(pl.multiple_of(place[3] * 128, 128), 128)
    other = pl.ds(pl.multiple_of((1 - place[3]) * 128, 128), 128)
    grad[:, mine] = keep[...].astype(F32).T.astype(BF16)
    grad[:, other] = given[...].astype(F32).T.astype(BF16)


def turned(place, keep, given):
    rows = keep.shape[1]
    return pl.pallas_call(
        turn_kernel,
        out_shape=jax.ShapeDtypeStruct((rows, 256), BF16),
        in_specs=[SMEM, VMEM, VMEM],
        out_specs=VMEM,
        compiler_params=params(),
        cost_estimate=cost(0, 4 * 256 * rows),
        name="turn_grads",
    )(place, keep, given)


def spread(parts, axis):
    return [parts[0]] + [send(parts[step], axis, step) for step in (1, 2, 3)]


def crossed(parts, first):
    def target(y, z, core, step):
        if (core == 0) == first:
            y = (y + step) % SIDE
        else:
            z = (z + step) % SIDE
        return (y * SIDE + z) * 2 + core

    places = [(y, z, core) for y in range(SIDE) for z in range(SIDE) for core in range(2)]
    received = [parts[0]]
    for step in (1, 2, 3):
        pairs = [(i, target(*at, step)) for i, at in enumerate(places)]
        received.append(lax.ppermute(parts[step], ("vy", "vz", "tc"), pairs))
    return received


def shards(teacher_logits, student_hidden, student_unembed, tile_weights, tile_pairs, tile_count):
    y, z, x, core = (lax.axis_index(name) for name in ("vy", "vz", "tx", "tc"))
    crossing = [jnp.where(core == 0, y, z), jnp.where(core == 0, z, y)]
    place = jnp.stack([y, z, x, core] + crossing).astype(jnp.int32)
    rows = teacher_logits.shape[0]
    teacher = teacher_logits.astype(F32)
    peak = jnp.max(teacher, axis=1)
    shifted = jnp.exp(teacher - peak[:, None])
    mass = jnp.sum(shifted, axis=1)
    probs = shifted.astype(BF16)

    logits = jnp.dot(student_hidden, student_unembed, preferred_element_type=F32)
    speak = jnp.max(logits, axis=1)
    smass = jnp.sum(jnp.exp(logits - speak[:, None]), axis=1)

    blank = jnp.zeros_like(peak)
    before = jnp.stack([peak, mass, blank, speak, smass, blank, blank, blank])

    piece = prepared(tile_weights)
    right, left = send(piece, "tx", 1), send(piece, "tx", 3)
    top, low = halves(right, left, [mass, smass])
    pieces = [piece, right, left, send(top, "tx", 1), send(low, "tx", 3)]
    pieces = pieces + [swap(piece) for piece in pieces]

    own, near, far, to_right, to_left = products(
        place, tile_pairs, tile_count, probs, before, pieces
    )
    stage = staged(place, student_unembed, [own])
    left_part, right_part = send(to_right, "vy", 1), send(to_left, "vy", 3)
    near, far, given = relayed(near, far, left_part, right_part, to_right, [stage])
    parts = merged(place, given, [own, send(near, "vy", 1), send(far, "vy", 3)], rows)
    mine = gradients(place, logits, spread(parts, "vz"))

    own = own_hidden(stage, mine)
    other = swap(mine)
    parts = other_hidden(range(SIDE), place, stage, mine, other, own)
    parts = middle(place, crossed(parts, True))
    keep, give, loss = totals(place, crossed(parts, False))
    return turned(place, keep, swap(give)), loss[0]


def solution(mesh):
    grid = Mesh(mesh.devices.reshape(SIDE, SIDE, SIDE, 2), ("vy", "vz", "tx", "tc"))
    vocab, tokens = ("vy", "vz"), ("tx", "tc")
    return jax.shard_map(
        shards,
        mesh=grid,
        in_specs=(
            P(tokens, vocab),
            P(tokens, None),
            P(None, vocab),
            P(vocab, tokens, None),
            P(vocab, None),
            P(vocab),
        ),
        out_specs=(P(tokens, vocab), P(tokens)),
        check_vma=False,
    )
```

time: 157 us -> 165 us (1.051)
  waiting for transfers between devices: 54.2 us -> 82.5 us
  starting transfers between devices: 51.8 us -> 34.8 us
  Pallas kernels: 27.9 us -> 25.7 us
    ppermute x21 -> x11, waiting for transfers between devices: 34.5 us -> 63.9 us  [send(): lax.ppermute(value, axis, [(i, (i + step) % SIDE) for i in range(SIDE)])]
    ppermute x21 -> x11, starting transfers between devices: 32.7 us -> 17.5 us  [send(): lax.ppermute(value, axis, [(i, (i + step) % SIDE) for i in range(SIDE)])]
    ppermute x7, waiting for transfers between devices: 4.14 us -> 1.36 us  [swap(): return lax.ppermute(value, 'tc', [(0, 1), (1, 0)])]
    pallas_call x12 -> x5, Pallas kernels: 14.5 us -> 12.1 us  [the longest x1 6.41 us: products(): pl.pallas_call(product_kernel, out_shape=[jax.ShapeDtypeStruct((SIDE * ro...]
    ppermute x6, starting transfers between devices: 8.69 us -> 6.39 us  [crossed(): received.append(lax.ppermute(parts[step], ('vy', 'vz', 'tc'), pairs))]
    reduce_sum x1, other arithmetic: 3.87 us -> 2.11 us  [shards(): mass = jnp.sum(shifted, axis=1)]
    ppermute x6, waiting for transfers between devices: 15.5 us -> 17.3 us  [crossed(): received.append(lax.ppermute(parts[step], ('vy', 'vz', 'tc'), pairs))]
    reduce_sum x1, other arithmetic: 0.43 us -> 2.16 us  [shards(): smass = jnp.sum(jnp.exp(logits - speak[:, None]), axis=1)]
  transfers between devices with their start and end apart: 34 -> 24, of which waited for: 18 -> 19; matrix products, arithmetic and copies ran while one was open for 11% -> 10% of each run, Pallas kernels for 10% -> 4%
where the time goes in v8:
time: 165 us; the launch traced here: 164 us
  waiting for transfers between devices  82.5 us (50%)
  starting transfers between devices  34.8 us (21%)
  Pallas kernels  25.7 us (16%)
  matrix products  9.61 us (6%)
  other arithmetic  6.23 us (4%)
  local copies, waits for them, and re-layouts  3.77 us (2%)
    ppermute x11, waiting for transfers between devices, send(): lax.ppermute(value, axis, [(i, (i + step) % SIDE) for i in range(SIDE)])  63.9 us
    ppermute x11, starting transfers between devices, send(): lax.ppermute(value, axis, [(i, (i + step) % SIDE) for i in range(SIDE)])  17.5 us
    ppermute x6, waiting for transfers between devices, crossed(): received.append(lax.ppermute(parts[step], ('vy', 'vz', 'tc'), pairs))  17.3 us
    ppermute x7, starting transfers between devices, swap(): return lax.ppermute(value, 'tc', [(0, 1), (1, 0)])  10.9 us
    dot_general x1, matrix products, shards(): jnp.dot(student_hidden, student_unembed, preferred_element_type=F32)  9.61 us
    pallas_call x1, Pallas kernels, products(): pl.pallas_call(product_kernel, out_shape=[jax.ShapeDtypeStruct((SIDE * ro...  6.41 us
    ppermute x6, starting transfers between devices, crossed(): received.append(lax.ppermute(parts[step], ('vy', 'vz', 'tc'), pairs))  6.39 us
    pallas_call x1, Pallas kernels, staged(): pl.pallas_call(stage_kernel, out_shape=jax.ShapeDtypeStruct((depth // 2,...  4.06 us
  transfers between devices with their start and end apart: 24, of which 19 were waited for; matrix products, arithmetic and copies ran while one was open for 10% of the time, Pallas kernels for 4%

profile of v8, /device:TPU:1, one launch (start us, length us, event | category | flops | bytes accessed | tf_op | source)
XLA Modules:
  0.0 164.1 jit_solution(9290268412316373143)
XLA Ops:
  3.4 3.3 %collective-permute-start.1 = (bf16[1088,512]{1,0:T(8,128)(2,1)}, bf16[1088,512]{1,0:T(8,128)(2,1)S(1)}, u32[]{:S(2)}, u32[]{:S(2)}) collective-permute-start(bf16[1088,512]{1,0:T(8,128)(2,1)} %prepare_weights.1.rest_0_), channel_id=1, source_target_pairs={{0,6},{2,0},{4,2},{6,4},{1,7},{3,1},{5,3},{7,5},{8,14},{10,8},{12,... | collective-permute-start | bytes 3342344 | tf_op jit(solution)/shard_map/ppermute | solution.py:29
  6.7 9.6 %fusion.2 = (f32[256]{0:T(256)S(1)}, f32[256,2048]{1,0:T(8,128)}) fusion(bf16[256,4096]{1,0:T(8,128)(2,1)S(1)} %copy-done, bf16[4096,2048]{1,0:T(8,128)(2,1)} %unembed.1), kind=kOutput, calls=%fused_computation.4 | convolution fusion | flops 4295491584 | bytes 20972544 | tf_op jit(solution)/shard_map/dot_general | solution.py:550
  18.3 2.2 %exponential_reduce_fusion.refs_1_ = f32[256]{0:T(256)S(1)} fusion(f32[256,2048]{1,0:T(8,128)} %get-tuple-element.55.logits, f32[256]{0:T(256)S(1)} %get-tuple-element.54), kind=kLoop, calls=%fused_computation.3 | loop fusion | flops 1048320 | bytes 2099200 | tf_op jit(solution)/shard_map/reduce_sum | solution.py:552
  22.6 7.6 %collective-permute-done.1.left.rest_2_ = bf16[1088,512]{1,0:T(8,128)(2,1)S(1)} collective-permute-done((bf16[1088,512]{1,0:T(8,128)(2,1)}, bf16[1088,512]{1,0:T(8,128)(2,1)S(1)}, u32[]{:S(2)}, u32[]{:S(2)}) %collective-permute-start.1) | collective-permute-done | bytes 1114144 | tf_op jit(solution)/shard_map/ppermute | solution.py:29
  30.3 3.1 %collective-permute-done.right.rest_1_ = bf16[1088,512]{1,0:T(8,128)(2,1)} collective-permute-done((bf16[1088,512]{1,0:T(8,128)(2,1)}, bf16[1088,512]{1,0:T(8,128)(2,1)}, u32[]{:S(2)}, u32[]{:S(2)}) %collective-permute-start) | collective-permute-done | bytes 1114144 | tf_op jit(solution)/shard_map/ppermute | solution.py:29
  38.9 8.9 %collective-permute-done.3.rest_4_ = bf16[576,512]{1,0:T(8,128)(2,1)} collective-permute-done((bf16[576,512]{1,0:T(8,128)(2,1)S(1)}, bf16[576,512]{1,0:T(8,128)(2,1)}, u32[]{:S(2)}, u32[]{:S(2)}) %collective-permute-start.3) | collective-permute-done | bytes 589856 | tf_op jit(solution)/shard_map/ppermute | solution.py:29
  47.8 2.8 %collective-permute-start.8 = (bf16[576,512]{1,0:T(8,128)(2,1)}, bf16[576,512]{1,0:T(8,128)(2,1)}, u32[]{:S(2)}, u32[]{:S(2)}) collective-permute-start(bf16[576,512]{1,0:T(8,128)(2,1)} %collective-permute-done.3.rest_4_), channel_id=1, source_target_pairs={{0,1},{1,0},{2,3},{3,2},{4,5},{5,4},{6,7},{7,6},{8,9},{9,8},{10,11... | collective-permute-start | bytes 1769480 | tf_op jit(solution)/shard_map/ppermute | solution.py:33
  56.4 6.4 %tile_products.1 = (bf16[1024,512]{1,0:T(8,128)(2,1)S(1)}, bf16[1024,512]{1,0:T(8,128)(2,1)S(1)}, bf16[1024,512]{1,0:T(8,128)(2,1)S(1)}, bf16[528,512]{1,0:T(8,128)(2,1)S(1)}, bf16[528,512]{1,0:T(8,128)(2,1)S(1)}) custom-call(s32[6]{0:T(128)S(1)} %stack.43.place, s32[16,2]{1,0:T(8,128)S(1)} %copy.8.pairs, s32[1]{0:T(128)S(6)} %copy.9.count, ...), custom_call_target="tpu_custom_call" | custom-call | flops 2147483648 | bytes 15204352 | tf_op jit(solution)/shard_map/tile_products/pallas_call | solution.py:188
  64.7 4.1 %stage_unembed.1.refs_0_.stage = bf16[2048,2048]{1,0:T(8,128)(2,1)S(1)} custom-call(s32[6]{0:T(128)S(1)} %stack.43.place, bf16[4096,2048]{1,0:T(8,128)(2,1)} %unembed.1, bf16[1024,512]{1,0:T(8,128)(2,1)S(1)} %get-tuple-element.29.refs_0_), custom_call_target="tpu_custom_call" | custom-call | bytes 8388608 | tf_op jit(solution)/shard_map/stage_unembed/pallas_call | solution.py:376
  68.8 8.1 %collective-permute-done.10.from_right = bf16[528,512]{1,0:T(8,128)(2,1)S(1)} collective-permute-done((bf16[528,512]{1,0:T(8,128)(2,1)S(1)}, bf16[528,512]{1,0:T(8,128)(2,1)S(1)}, u32[]{:S(2)}, u32[]{:S(2)}) %collective-permute-start.10) | collective-permute-done | bytes 540704 | tf_op jit(solution)/shard_map/ppermute | solution.py:29
  78.9 2.4 %collective-permute-start.12 = (bf16[1024,512]{1,0:T(8,128)(2,1)S(1)}, bf16[1024,512]{1,0:T(8,128)(2,1)S(1)}, u32[]{:S(2)}, u32[]{:S(2)}) collective-permute-start(bf16[1024,512]{1,0:T(8,128)(2,1)S(1)} %get-tuple-element.36), channel_id=1, source_target_pairs={{0,96},{32,0},{64,32},{96,64},{1,97},{33,1},{65,33},{97,65},{2,98}... | collective-permute-start | bytes 3145736 | tf_op jit(solution)/shard_map/ppermute | solution.py:29
  81.2 20.8 %collective-permute-done.12.refs_2_ = bf16[1024,512]{1,0:T(8,128)(2,1)S(1)} collective-permute-done((bf16[1024,512]{1,0:T(8,128)(2,1)S(1)}, bf16[1024,512]{1,0:T(8,128)(2,1)S(1)}, u32[]{:S(2)}, u32[]{:S(2)}) %collective-permute-start.12) | collective-permute-done | bytes 1048608 | tf_op jit(solution)/shard_map/ppermute | solution.py:29
  104.6 3.2 %collective-permute-start.13 = (bf16[272,512]{1,0:T(8,128)(2,1)S(1)}, bf16[272,512]{1,0:T(8,128)(2,1)S(1)}, u32[]{:S(2)}, u32[]{:S(2)}) collective-permute-start(bf16[272,512]{1,0:T(8,128)(2,1)S(1)} %get-tuple-element.38), channel_id=1, source_target_pairs={{0,8},{8,16},{16,24},{24,0},{1,9},{9,17},{17,25},{25,1},{2,10},{10... | collective-permute-start | bytes 835592 | tf_op jit(solution)/shard_map/ppermute | solution.py:29
  107.8 4.6 %collective-permute-start.14 = (bf16[272,512]{1,0:T(8,128)(2,1)S(1)}, bf16[272,512]{1,0:T(8,128)(2,1)S(1)}, u32[]{:S(2)}, u32[]{:S(2)}) collective-permute-start(bf16[272,512]{1,0:T(8,128)(2,1)S(1)} %get-tuple-element.39), channel_id=1, source_target_pairs={{0,16},{8,24},{16,0},{24,8},{1,17},{9,25},{17,1},{25,9},{2,18},{10... | collective-permute-start | bytes 835592 | tf_op jit(solution)/shard_map/ppermute | solution.py:29
  112.4 4.0 %collective-permute-done.13.refs_1_ = bf16[272,512]{1,0:T(8,128)(2,1)S(1)} collective-permute-done((bf16[272,512]{1,0:T(8,128)(2,1)S(1)}, bf16[272,512]{1,0:T(8,128)(2,1)S(1)}, u32[]{:S(2)}, u32[]{:S(2)}) %collective-permute-start.13) | collective-permute-done | bytes 278560 | tf_op jit(solution)/shard_map/ppermute | solution.py:29
  116.3 6.9 %collective-permute-done.14.refs_2_ = bf16[272,512]{1,0:T(8,128)(2,1)S(1)} collective-permute-done((bf16[272,512]{1,0:T(8,128)(2,1)S(1)}, bf16[272,512]{1,0:T(8,128)(2,1)S(1)}, u32[]{:S(2)}, u32[]{:S(2)}) %collective-permute-start.14) | collective-permute-done | bytes 278560 | tf_op jit(solution)/shard_map/ppermute | solution.py:29
  123.9 2.3 %logit_grad.1.mine = bf16[2064,256]{1,0:T(8,128)(2,1)S(1)} custom-call(s32[6]{0:T(128)S(1)} %stack.43.place, f32[256,2048]{1,0:T(8,128)S(1)} %copy-done.1, bf16[272,512]{1,0:T(8,128)(2,1)S(1)} %get-tuple-element.37.refs_0_, bf16[272,512]{1,0:T(8,128)(2,1)S(1)} %collective-permute-done.13.refs_1_, bf16[272,512]{1,0:T(8,128)(2,1)S(1)} %collective-permute-done.14.refs_2_, ...), custom_call_target="tpu_custom_call" | custom-call | flops 31457280 | bytes 4194304 | tf_op jit(solution)/shard_map/logit_grad/pallas_call | solution.py:341
  128.4 2.3 %own_hidden.1.own = bf16[2048,256]{1,0:T(8,128)(2,1)S(1)} custom-call(bf16[2048,2048]{1,0:T(8,128)(2,1)S(1)} %stage_unembed.1.refs_0_.stage, bf16[2064,256]{1,0:T(8,128)(2,1)S(1)} %logit_grad.1.mine), custom_call_target="tpu_custom_call" | custom-call | flops 2147483648 | bytes 8388608 | tf_op jit(solution)/shard_map/own_hidden/pallas_call | solution.py:398
  130.7 3.0 %other_hidden.1 = (bf16[528,512]{1,0:T(8,128)(2,1)S(1)}, bf16[528,512]{1,0:T(8,128)(2,1)S(1)}, bf16[528,512]{1,0:T(8,128)(2,1)S(1)}, bf16[528,512]{1,0:T(8,128)(2,1)S(1)}) custom-call(s32[6]{0:T(128)S(1)} %stack.43.place, bf16[2048,2048]{1,0:T(8,128)(2,1)S(1)} %stage_unembed.1.refs_0_.stage, bf16[2064,256]{1,0:T(8,128)(2,1)S(1)} %logit_grad.1.mine, ...), custom_call_target="tpu_custom_call" | custom-call | flops 2147483648 | bytes 8388608 | tf_op jit(solution)/shard_map/other_hidden/pallas_call | solution.py:426
  133.8 3.0 %collective-permute-start.18 = (bf16[528,512]{1,0:T(8,128)(2,1)S(1)}, bf16[528,512]{1,0:T(8,128)(2,1)S(1)}, u32[]{:S(2)}, u32[]{:S(2)}) collective-permute-start(bf16[528,512]{1,0:T(8,128)(2,1)S(1)} %get-tuple-element.43), channel_id=1, source_target_pairs={{0,64},{1,17},{8,72},{9,25},{16,80},{17,1},{24,88},{25,9},{32,96},... | collective-permute-start | bytes 1622024 | tf_op jit(solution)/shard_map/ppermute | solution.py:535
  136.9 6.7 %collective-permute-done.17.refs_1_ = bf16[528,512]{1,0:T(8,128)(2,1)S(1)} collective-permute-done((bf16[528,512]{1,0:T(8,128)(2,1)S(1)}, bf16[528,512]{1,0:T(8,128)(2,1)S(1)}, u32[]{:S(2)}, u32[]{:S(2)}) %collective-permute-start.17) | collective-permute-done | bytes 540704 | tf_op jit(solution)/shard_map/ppermute | solution.py:535
  143.5 6.2 %collective-permute-done.18.refs_2_ = bf16[528,512]{1,0:T(8,128)(2,1)S(1)} collective-permute-done((bf16[528,512]{1,0:T(8,128)(2,1)S(1)}, bf16[528,512]{1,0:T(8,128)(2,1)S(1)}, u32[]{:S(2)}, u32[]{:S(2)}) %collective-permute-start.18) | collective-permute-done | bytes 540704 | tf_op jit(solution)/shard_map/ppermute | solution.py:535
  150.9 3.2 %collective-permute-start.21 = (bf16[144,512]{1,0:T(8,128)(2,1)S(1)}, bf16[144,512]{1,0:T(8,128)(2,1)S(1)}, u32[]{:S(2)}, u32[]{:S(2)}) collective-permute-start(bf16[144,512]{1,0:T(8,128)(2,1)S(1)} %get-tuple-element.47), channel_id=1, source_target_pairs={{0,16},{1,65},{8,24},{9,73},{16,0},{17,81},{24,8},{25,89},{32,48},... | collective-permute-start | bytes 442376 | tf_op jit(solution)/shard_map/ppermute | solution.py:535
  159.0 2.9 %collective-permute-start.23 = (bf16[128,256]{1,0:T(8,128)(2,1)S(1)}, bf16[128,256]{1,0:T(8,128)(2,1)S(1)}, u32[]{:S(2)}, u32[]{:S(2)}) collective-permute-start(bf16[128,256]{1,0:T(8,128)(2,1)S(1)} %get-tuple-element.50), channel_id=1, source_target_pairs={{0,1},{1,0},{2,3},{3,2},{4,5},{5,4},{6,7},{7,6},{8,9},{9,8},{10,11... | collective-permute-start | bytes 196616 | tf_op jit(solution)/shard_map/ppermute | solution.py:33
  (59 shorter events, 35.1 us)
Async XLA Ops:
  3.4 26.9 %collective-permute-start.1 = (bf16[1088,512]{1,0:T(8,128)(2,1)}, bf16[1088,512]{1,0:T(8,128)(2,1)S(1)}, u32[]{:S(2)}, u32[]{:S(2)}) collective-permute-start(bf16[1088,512]{1,0:T(8,128)(2,1)} %prepare_weights.1.rest_0_), channel_id=1, source_target_pairs={{0,6},{2,0},{4,2},{6,4},{1,7},{3,1},{5,3},{7,5},{8,14},{10,8},{12,... | collective-permute-start | bytes 3342344 | tf_op jit(solution)/shard_map/ppermute | solution.py:29
  6.7 26.6 %collective-permute-start = (bf16[1088,512]{1,0:T(8,128)(2,1)}, bf16[1088,512]{1,0:T(8,128)(2,1)}, u32[]{:S(2)}, u32[]{:S(2)}) collective-permute-start(bf16[1088,512]{1,0:T(8,128)(2,1)} %prepare_weights.1.rest_0_), channel_id=1, source_target_pairs={{0,2},{2,4},{4,6},{6,0},{1,3},{3,5},{5,7},{7,1},{8,10},{10,12},{12... | collective-permute-start | bytes 3342344 | tf_op jit(solution)/shard_map/ppermute | solution.py:29
  34.7 13.1 %collective-permute-start.3 = (bf16[576,512]{1,0:T(8,128)(2,1)S(1)}, bf16[576,512]{1,0:T(8,128)(2,1)}, u32[]{:S(2)}, u32[]{:S(2)}) collective-permute-start(bf16[576,512]{1,0:T(8,128)(2,1)S(1)} %get-tuple-element.28), channel_id=1, source_target_pairs={{0,6},{2,0},{4,2},{6,4},{1,7},{3,1},{5,3},{7,5},{8,14},{10,8},{12,... | collective-permute-start | bytes 1769480 | tf_op jit(solution)/shard_map/ppermute | solution.py:29
  35.0 18.9 %collective-permute-start.4 = (bf16[1088,512]{1,0:T(8,128)(2,1)}, bf16[1088,512]{1,0:T(8,128)(2,1)}, u32[]{:S(2)}, u32[]{:S(2)}) collective-permute-start(bf16[1088,512]{1,0:T(8,128)(2,1)} %prepare_weights.1.rest_0_), channel_id=1, source_target_pairs={{0,1},{1,0},{2,3},{3,2},{4,5},{5,4},{6,7},{7,6},{8,9},{9,8},{10,11... | collective-permute-start | bytes 3342344 | tf_op jit(solution)/shard_map/ppermute | solution.py:33
  36.8 18.0 %collective-permute-start.6 = (bf16[1088,512]{1,0:T(8,128)(2,1)S(1)}, bf16[1088,512]{1,0:T(8,128)(2,1)}, u32[]{:S(2)}, u32[]{:S(2)}) collective-permute-start(bf16[1088,512]{1,0:T(8,128)(2,1)S(1)} %collective-permute-done.1.left.rest_2_), channel_id=1, source_target_pairs={{0,1},{1,0},{2,3},{3,2},{4,5},{5,4},{6,7},{7,6},{8,9},{9,8},{10,11... | collective-permute-start | bytes 3342344 | tf_op jit(solution)/shard_map/ppermute | solution.py:33
  36.8 18.0 %collective-permute-start.5 = (bf16[1088,512]{1,0:T(8,128)(2,1)}, bf16[1088,512]{1,0:T(8,128)(2,1)}, u32[]{:S(2)}, u32[]{:S(2)}) collective-permute-start(bf16[1088,512]{1,0:T(8,128)(2,1)} %collective-permute-done.right.rest_1_), channel_id=1, source_target_pairs={{0,1},{1,0},{2,3},{3,2},{4,5},{5,4},{6,7},{7,6},{8,9},{9,8},{10,11... | collective-permute-start | bytes 3342344 | tf_op jit(solution)/shard_map/ppermute | solution.py:33
  37.3 14.9 %collective-permute-start.2 = (bf16[512,512]{1,0:T(8,128)(2,1)S(1)}, bf16[512,512]{1,0:T(8,128)(2,1)}, u32[]{:S(2)}, u32[]{:S(2)}) collective-permute-start(bf16[512,512]{1,0:T(8,128)(2,1)S(1)} %get-tuple-element.27), channel_id=1, source_target_pairs={{0,2},{2,4},{4,6},{6,0},{1,3},{3,5},{5,7},{7,1},{8,10},{10,12},{12... | collective-permute-start | bytes 1572872 | tf_op jit(solution)/shard_map/ppermute | solution.py:29
  47.8 7.0 %collective-permute-start.8 = (bf16[576,512]{1,0:T(8,128)(2,1)}, bf16[576,512]{1,0:T(8,128)(2,1)}, u32[]{:S(2)}, u32[]{:S(2)}) collective-permute-start(bf16[576,512]{1,0:T(8,128)(2,1)} %collective-permute-done.3.rest_4_), channel_id=1, source_target_pairs={{0,1},{1,0},{2,3},{3,2},{4,5},{5,4},{6,7},{7,6},{8,9},{9,8},{10,11... | collective-permute-start | bytes 1769480 | tf_op jit(solution)/shard_map/ppermute | solution.py:33
  52.2 2.7 %collective-permute-start.7 = (bf16[512,512]{1,0:T(8,128)(2,1)}, bf16[512,512]{1,0:T(8,128)(2,1)}, u32[]{:S(2)}, u32[]{:S(2)}) collective-permute-start(bf16[512,512]{1,0:T(8,128)(2,1)} %collective-permute-done.2.rest_3_), channel_id=1, source_target_pairs={{0,1},{1,0},{2,3},{3,2},{4,5},{5,4},{6,7},{7,6},{8,9},{9,8},{10,11... | collective-permute-start | bytes 1572872 | tf_op jit(solution)/shard_map/ppermute | solution.py:33
  62.9 14.0 %collective-permute-start.10 = (bf16[528,512]{1,0:T(8,128)(2,1)S(1)}, bf16[528,512]{1,0:T(8,128)(2,1)S(1)}, u32[]{:S(2)}, u32[]{:S(2)}) collective-permute-start(bf16[528,512]{1,0:T(8,128)(2,1)S(1)} %get-tuple-element.33), channel_id=1, source_target_pairs={{0,96},{32,0},{64,32},{96,64},{1,97},{33,1},{65,33},{97,65},{2,98}... | collective-permute-start | bytes 1622024 | tf_op jit(solution)/shard_map/ppermute | solution.py:29
  63.5 14.4 %collective-permute-start.9 = (bf16[528,512]{1,0:T(8,128)(2,1)S(1)}, bf16[528,512]{1,0:T(8,128)(2,1)S(1)}, u32[]{:S(2)}, u32[]{:S(2)}) collective-permute-start(bf16[528,512]{1,0:T(8,128)(2,1)S(1)} %get-tuple-element.32.mine), channel_id=1, source_target_pairs={{0,32},{32,64},{64,96},{96,0},{1,33},{33,65},{65,97},{97,1},{2,34}... | collective-permute-start | bytes 1622024 | tf_op jit(solution)/shard_map/ppermute | solution.py:29
  78.5 24.8 %collective-permute-start.11 = (bf16[1040,512]{1,0:T(8,128)(2,1)S(1)}, bf16[1040,512]{1,0:T(8,128)(2,1)S(1)}, u32[]{:S(2)}, u32[]{:S(2)}) collective-permute-start(bf16[1040,512]{1,0:T(8,128)(2,1)S(1)} %get-tuple-element.35), channel_id=1, source_target_pairs={{0,32},{32,64},{64,96},{96,0},{1,33},{33,65},{65,97},{97,1},{2,34}... | collective-permute-start | bytes 3194888 | tf_op jit(solution)/shard_map/ppermute | solution.py:29
  78.9 23.1 %collective-permute-start.12 = (bf16[1024,512]{1,0:T(8,128)(2,1)S(1)}, bf16[1024,512]{1,0:T(8,128)(2,1)S(1)}, u32[]{:S(2)}, u32[]{:S(2)}) collective-permute-start(bf16[1024,512]{1,0:T(8,128)(2,1)S(1)} %get-tuple-element.36), channel_id=1, source_target_pairs={{0,96},{32,0},{64,32},{96,64},{1,97},{33,1},{65,33},{97,65},{2,98}... | collective-permute-start | bytes 3145736 | tf_op jit(solution)/shard_map/ppermute | solution.py:29
  104.6 11.7 %collective-permute-start.13 = (bf16[272,512]{1,0:T(8,128)(2,1)S(1)}, bf16[272,512]{1,0:T(8,128)(2,1)S(1)}, u32[]{:S(2)}, u32[]{:S(2)}) collective-permute-start(bf16[272,512]{1,0:T(8,128)(2,1)S(1)} %get-tuple-element.38), channel_id=1, source_target_pairs={{0,8},{8,16},{16,24},{24,0},{1,9},{9,17},{17,25},{25,1},{2,10},{10... | collective-permute-start | bytes 835592 | tf_op jit(solution)/shard_map/ppermute | solution.py:29
  107.8 15.4 %collective-permute-start.14 = (bf16[272,512]{1,0:T(8,128)(2,1)S(1)}, bf16[272,512]{1,0:T(8,128)(2,1)S(1)}, u32[]{:S(2)}, u32[]{:S(2)}) collective-permute-start(bf16[272,512]{1,0:T(8,128)(2,1)S(1)} %get-tuple-element.39), channel_id=1, source_target_pairs={{0,16},{8,24},{16,0},{24,8},{1,17},{9,25},{17,1},{25,9},{2,18},{10... | collective-permute-start | bytes 835592 | tf_op jit(solution)/shard_map/ppermute | solution.py:29
  112.4 11.6 %collective-permute-start.15 = (bf16[272,512]{1,0:T(8,128)(2,1)S(1)}, bf16[272,512]{1,0:T(8,128)(2,1)S(1)}, u32[]{:S(2)}, u32[]{:S(2)}) collective-permute-start(bf16[272,512]{1,0:T(8,128)(2,1)S(1)} %get-tuple-element.40), channel_id=1, source_target_pairs={{0,24},{8,0},{16,8},{24,16},{1,25},{9,1},{17,9},{25,17},{2,26},{10... | collective-permute-start | bytes 835592 | tf_op jit(solution)/shard_map/ppermute | solution.py:29
  126.2 4.4 %collective-permute-start.16 = (bf16[2064,256]{1,0:T(8,128)(2,1)S(1)}, bf16[2064,256]{1,0:T(8,128)(2,1)S(1)}, u32[]{:S(2)}, u32[]{:S(2)}) collective-permute-start(bf16[2064,256]{1,0:T(8,128)(2,1)S(1)} %logit_grad.1.mine), channel_id=1, source_target_pairs={{0,1},{1,0},{2,3},{3,2},{4,5},{5,4},{6,7},{7,6},{8,9},{9,8},{10,11... | collective-permute-start | bytes 3170312 | tf_op jit(solution)/shard_map/ppermute | solution.py:33
  133.7 9.8 %collective-permute-start.17 = (bf16[528,512]{1,0:T(8,128)(2,1)S(1)}, bf16[528,512]{1,0:T(8,128)(2,1)S(1)}, u32[]{:S(2)}, u32[]{:S(2)}) collective-permute-start(bf16[528,512]{1,0:T(8,128)(2,1)S(1)} %get-tuple-element.42), channel_id=1, source_target_pairs={{0,32},{1,9},{8,40},{9,17},{16,48},{17,25},{24,56},{25,1},{32,64},... | collective-permute-start | bytes 1622024 | tf_op jit(solution)/shard_map/ppermute | solution.py:535
  133.8 15.9 %collective-permute-start.18 = (bf16[528,512]{1,0:T(8,128)(2,1)S(1)}, bf16[528,512]{1,0:T(8,128)(2,1)S(1)}, u32[]{:S(2)}, u32[]{:S(2)}) collective-permute-start(bf16[528,512]{1,0:T(8,128)(2,1)S(1)} %get-tuple-element.43), channel_id=1, source_target_pairs={{0,64},{1,17},{8,72},{9,25},{16,80},{17,1},{24,88},{25,9},{32,96},... | collective-permute-start | bytes 1622024 | tf_op jit(solution)/shard_map/ppermute | solution.py:535
  136.8 13.1 %collective-permute-start.19 = (bf16[528,512]{1,0:T(8,128)(2,1)S(1)}, bf16[528,512]{1,0:T(8,128)(2,1)S(1)}, u32[]{:S(2)}, u32[]{:S(2)}) collective-permute-start(bf16[528,512]{1,0:T(8,128)(2,1)S(1)} %get-tuple-element.44), channel_id=1, source_target_pairs={{0,96},{1,25},{8,104},{9,1},{16,112},{17,9},{24,120},{25,17},{32,0... | collective-permute-start | bytes 1622024 | tf_op jit(solution)/shard_map/ppermute | solution.py:535
  150.8 5.3 %collective-permute-start.20 = (bf16[144,512]{1,0:T(8,128)(2,1)S(1)}, bf16[144,512]{1,0:T(8,128)(2,1)S(1)}, u32[]{:S(2)}, u32[]{:S(2)}) collective-permute-start(bf16[144,512]{1,0:T(8,128)(2,1)S(1)} %get-tuple-element.46), channel_id=1, source_target_pairs={{0,8},{1,33},{8,16},{9,41},{16,24},{17,49},{24,0},{25,57},{32,40},... | collective-permute-start | bytes 442376 | tf_op jit(solution)/shard_map/ppermute | solution.py:535
  150.9 7.3 %collective-permute-start.21 = (bf16[144,512]{1,0:T(8,128)(2,1)S(1)}, bf16[144,512]{1,0:T(8,128)(2,1)S(1)}, u32[]{:S(2)}, u32[]{:S(2)}) collective-permute-start(bf16[144,512]{1,0:T(8,128)(2,1)S(1)} %get-tuple-element.47), channel_id=1, source_target_pairs={{0,16},{1,65},{8,24},{9,73},{16,0},{17,81},{24,8},{25,89},{32,48},... | collective-permute-start | bytes 442376 | tf_op jit(solution)/shard_map/ppermute | solution.py:535
  154.1 4.2 %collective-permute-start.22 = (bf16[144,512]{1,0:T(8,128)(2,1)S(1)}, bf16[144,512]{1,0:T(8,128)(2,1)S(1)}, u32[]{:S(2)}, u32[]{:S(2)}) collective-permute-start(bf16[144,512]{1,0:T(8,128)(2,1)S(1)} %get-tuple-element.48), channel_id=1, source_target_pairs={{0,24},{1,97},{8,0},{9,105},{16,8},{17,113},{24,16},{25,121},{32,5... | collective-permute-start | bytes 442376 | tf_op jit(solution)/shard_map/ppermute | solution.py:535
  159.0 3.8 %collective-permute-start.23 = (bf16[128,256]{1,0:T(8,128)(2,1)S(1)}, bf16[128,256]{1,0:T(8,128)(2,1)S(1)}, u32[]{:S(2)}, u32[]{:S(2)}) collective-permute-start(bf16[128,256]{1,0:T(8,128)(2,1)S(1)} %get-tuple-element.50), channel_id=1, source_target_pairs={{0,1},{1,0},{2,3},{3,2},{4,5},{5,4},{6,7},{7,6},{8,9},{9,8},{10,11... | collective-permute-start | bytes 196616 | tf_op jit(solution)/shard_map/ppermute | solution.py:33
  (6 other events, 87.7 us)

commit v9 on v8

--- a/solution.py
+++ b/solution.py
@@ -40,81 +40,107 @@
     return high, middle, rest - middle
 
 
-def prepare_kernel(weights, piece):
-    slots, shard_rows, _ = weights.shape
-    width = piece.shape[1]
-    rows = slots * shard_rows
-    piece[0:rows, :] = weights[:, :, 0:width].reshape(rows, width)
-    sums = jnp.sum(weights[...].astype(F32), axis=2, keepdims=True).reshape(rows, 1)
-    line = jnp.broadcast_to(sums, (rows, 128)).T[0:1]
-    lines = jnp.concatenate(list(thirds(line)) + [jnp.zeros((5, rows), F32)], axis=0)
-    extra = jnp.concatenate([lines[:, i * 128 : (i + 1) * 128] for i in range(8)], axis=0)
-    if width > 128:
-        extra = jnp.concatenate([extra, jnp.zeros((64, width - 128), F32)], axis=1)
-    piece[rows : rows + 64, :] = extra.astype(BF16)
-
-
-def prepared(weights):
-    slots, shard_rows, width = weights.shape
-    return pl.pallas_call(
-        prepare_kernel,
-        out_shape=jax.ShapeDtypeStruct((slots * shard_rows + 64, width), BF16),
-        in_specs=[VMEM],
+def slice_kernel(weights, *refs):
+    piece = refs[-1]
+    piece[...] = weights[...].reshape(piece.shape)
+
+
+def sliced(weights, index, behind=()):
+    slots, shard_rows, cols = weights.shape
+    width = cols // 2
+    return pl.pallas_call(
+        slice_kernel,
+        grid=(1,),
+        out_shape=jax.ShapeDtypeStruct((slots * shard_rows, width), BF16),
+        in_specs=[pl.BlockSpec((slots, shard_rows, width), lambda i: (0, 0, index))]
+        + [ANY] * len(behind),
+        out_specs=pl.BlockSpec((slots * shard_rows, width), lambda i: (0, 0)),
+        compiler_params=params(),
+        cost_estimate=cost(0, 2 * weights.size),
+        name="slice_weights",
+    )(weights, *behind)
+
+
+def gate_kernel(*refs):
+    pass
+
+
+def gated(parts, behind):
+    return pl.pallas_call(
+        gate_kernel,
+        out_shape=[jax.ShapeDtypeStruct(part.shape, part.dtype) for part in parts],
+        in_specs=[ANY] * (len(parts) + len(behind)),
+        out_specs=[ANY] * len(parts),
+        input_output_aliases={i: i for i in range(len(parts))},
+        compiler_params=params(),
+        cost_estimate=cost(0, 0),
+        name="gate",
+    )(*parts, *behind)
+
+
+def pack_kernel(number, *refs):
+    out = refs[-1]
+    at = 0
+    for part in refs[:number]:
+        out[at : at + part.shape[0], :] = part[...]
+        at += part.shape[0]
+
+
+def packed_pieces(parts, behind):
+    depth = sum(part.shape[0] for part in parts)
+    width = parts[0].shape[1]
+    return pl.pallas_call(
+        functools.partial(pack_kernel, len(parts)),
+        out_shape=jax.ShapeDtypeStruct((depth, width), BF16),
+        in_specs=[VMEM] * len(parts) + [ANY] * len(behind),
         out_specs=VMEM,
         compiler_params=params(),
-        cost_estimate=cost(2 * weights.size, 3 * weights.size),
-        name="prepare_weights",
-    )(weights)
+        cost_estimate=cost(0, 4 * depth * width),
+        name="pack_weights",
+    )(*parts, *behind)
 
 
 def halves_kernel(right, left, *refs):
     top, low = refs[-2:]
-    top[...] = right[0 : top.shape[0], :]
-    low[...] = left[top.shape[0] :, :]
+    top[...] = right[...]
+    low[...] = left[...]
 
 
 def halves(right, left, behind):
     depth, width = right.shape
-    outs = [jax.ShapeDtypeStruct((rows, width), BF16) for rows in (512, depth - 512)]
+    shape = (depth // 2, width)
     return pl.pallas_call(
         halves_kernel,
-        out_shape=outs,
-        in_specs=[VMEM, VMEM] + [ANY] * len(behind),
-        out_specs=[VMEM, VMEM],
+        grid=(1,),
+        out_shape=[jax.ShapeDtypeStruct(shape, BF16)] * 2,
+        in_specs=[
+            pl.BlockSpec(shape, lambda i: (0, 0)),
+            pl.BlockSpec(shape, lambda i: (1, 0)),
+        ]
+        + [ANY] * len(behind),
+        out_specs=[pl.BlockSpec(shape, lambda i: (0, 0))] * 2,
         compiler_params=params(),
         cost_estimate=cost(0, 4 * depth * width),
         name="take_halves",
     )(right, left, *behind)
 
 
-def product_kernel(place, pairs, count, probs, before, *rest):
-    pieces, outs = rest[:10], rest[10:15]
-    across, total, sums, line, seen = rest[15:]
-    mine = [pieces[0], pieces[1], across.at[0], pieces[2]]
-    other = [pieces[5], pieces[6], across.at[1], pieces[7]]
-    for core in range(2):
-        across[core, 0:512] = pieces[5 * core + 3][...]
-        across[core, 512:] = pieces[5 * core + 4][...]
+def product_kernel(number, later, place, pairs, count, probs, before, *rest):
+    pieces, (across, total, seen) = rest[:number], rest[-3:]
+    outs = rest[-9:-4] if not later else rest[-8:-3]
+    half_number = number // 2
+    mine, other = list(pieces[:half_number]), list(pieces[half_number:])
+    if half_number == 5:
+        for core, parts in enumerate((mine, other)):
+            across[core, 0:512] = parts[3][...]
+            across[core, 512:1024] = parts[4][...]
+            parts[2:] = [across.at[core], parts[2]]
     block = 512
-    rows = probs.shape[0]
+    rows, width = probs.shape[0], total.shape[2]
     half = rows // 2
     vocab_y = place[0]
     first_block = (vocab_y * SIDE + place[1]) * (probs.shape[1] // block)
     core_0 = place[3] == 0
-
-    def in_order(step, at):
-        one, two = mine[step][at, :], other[step][at, :]
-        return jnp.where(core_0, one, two), jnp.where(core_0, two, one)
-
-    line[...] = jnp.zeros_like(line)
-    lane = lax.broadcasted_iota(jnp.int32, (64, 128), 1)
-    for step in range(SIDE):
-        even, odd = in_order(step, slice(1024, 1088))
-        even, odd = even[:, 0:128].astype(F32), odd[:, 0:128].astype(F32)
-        x = lax.rem(place[2] + SIDE - step, SIDE)
-        lanes = pl.ds(pl.multiple_of(x * 128, 128), 128)
-        sums[0, :, lanes] = jnp.where(lane < 64, even, pltpu.roll(odd, 64, 1))
-        sums[1, :, lanes] = jnp.where(lane < 64, pltpu.roll(even, 64, 1), odd)
     for owner in range(SIDE * SIDE):
         seen[owner] = 0
 
@@ -124,19 +150,13 @@
         at = pl.ds(pl.multiple_of(slot * 64, 64), 64)
         matrix, columns = [], []
         for step in range(SIDE):
-            matrix.extend(in_order(step, at))
+            one, two = mine[step][at, :], other[step][at, :]
+            matrix += [jnp.where(core_0, one, two), jnp.where(core_0, two, one)]
             x = lax.rem(place[2] + SIDE - step, SIDE)
             columns.append(probs[:, pl.ds(pl.multiple_of(teacher * block + x * 128, 128), 128)])
         product = jnp.dot(
             jnp.concatenate(columns, axis=1), jnp.concatenate(matrix, axis=0), preferred_element_type=F32
         )
-        row_sums = sums[lax.rem(slot, 2), pl.ds(pl.multiple_of(slot // 2 * 8, 8), 8), :]
-        line[...] += lax.dot_general(
-            row_sums.astype(BF16),
-            probs[:, pl.ds(pl.multiple_of(teacher * block, block), block)],
-            (((1,), (1,)), ((), ())),
-            preferred_element_type=F32,
-        )
         fresh = seen[owner] == 0
 
         @pl.when(fresh)
@@ -151,6 +171,8 @@
         return carry
 
     lax.fori_loop(0, count[0], tile, 0)
+    summed = total.at[SIDE * SIDE]
+    summed[...] = jnp.zeros(summed.shape, F32)
     for step in range(SIDE):
         start = lax.rem(vocab_y + step, SIDE) * SIDE
         for z in range(SIDE):
@@ -165,45 +187,48 @@
 
             @pl.when(used)
             def _():
-                put(total[start + z].astype(BF16))
+                value = total[start + z]
+                summed[...] += value
+                put(value.astype(BF16))
 
             @pl.when(jnp.logical_not(used))
             def _():
-                put(jnp.zeros(total.shape[1:], BF16))
-
-    sent = line[0:1] + line[1:2] + line[2:3]
-    packed = pack_rows([before[0:1], before[1:2], sent, before[3:4], before[4:5]])
+                put(jnp.zeros((rows, width), BF16))
+
+    line = jnp.sum(summed[...].T, axis=0, keepdims=True)
+    if later:
+        packed = pack_rows([line + before[0:1]])
+    else:
+        rest[-4][...] = jnp.broadcast_to(line, rest[-4].shape)
+        packed = pack_rows([before[i : i + 1] for i in range(4)])
     for out in outs[3:]:
-        put_rows(out, SIDE * half, packed)
-
-
-def put_rows(out, at, packed):
-    wide = jnp.zeros((16, out.shape[1] - packed.shape[1]), BF16)
-    out[at : at + 16, :] = jnp.concatenate([packed, wide], axis=1)
-
-
-def products(place, pairs, count, probs, before, pieces):
+        out[SIDE * half : SIDE * half + 16, :] = packed
+
+
+def products(place, pairs, count, probs, before, mine, other, later, behind=()):
     rows = probs.shape[0]
-    depth, width = pieces[0].shape
-    return pl.pallas_call(
-        product_kernel,
-        out_shape=[jax.ShapeDtypeStruct((SIDE * rows, width), BF16)] * 3
-        + [jax.ShapeDtypeStruct((SIDE * rows // 2 + 16, width), BF16)] * 2,
-        in_specs=[SMEM, SMEM, SMEM] + [VMEM] * (2 + len(pieces)),
-        out_specs=[VMEM] * (SIDE + 1),
+    depth, width = mine[0].shape
+    pieces = [*mine, *other]
+    outs = [jax.ShapeDtypeStruct((SIDE * rows, width), BF16)] * 3
+    outs += [jax.ShapeDtypeStruct((SIDE * rows // 2 + 16, width), BF16)] * 2
+    if not later:
+        outs.append(jax.ShapeDtypeStruct((8, rows), F32))
+    return pl.pallas_call(
+        functools.partial(product_kernel, len(pieces), later),
+        out_shape=outs,
+        in_specs=[SMEM, SMEM, SMEM] + [VMEM] * (2 + len(pieces)) + [ANY] * len(behind),
+        out_specs=[VMEM] * len(outs),
         scratch_shapes=[
-            pltpu.VMEM((2, depth, width), BF16),
-            pltpu.VMEM((SIDE * SIDE, rows, width), F32),
-            pltpu.VMEM((2, 64, 512), F32),
-            pltpu.VMEM((8, rows), F32),
+            pltpu.VMEM((2, depth if later else 16, width), BF16),
+            pltpu.VMEM((SIDE * SIDE + 1, rows, width), F32),
             pltpu.SMEM((SIDE * SIDE,), jnp.int32),
         ],
-        compiler_params=params(20),
+        compiler_params=params(12),
         cost_estimate=cost(
             16 * 2 * rows * 512 * width, 2 * probs.size + 16 * depth * width + 32 * rows * width
         ),
         name="tile_products",
-    )(place, pairs, count, probs, before, *pieces)
+    )(place, pairs, count, probs, before, *pieces, *behind)
 
 
 def pack_rows(lines):
@@ -222,12 +247,11 @@
 
 def joined(stats):
     peak = functools.reduce(jnp.maximum, [line[0] for line in stats])
-    speak = functools.reduce(jnp.maximum, [line[3] for line in stats])
+    speak = functools.reduce(jnp.maximum, [line[2] for line in stats])
     factors = [jnp.exp(line[0] - peak) for line in stats]
     mass = sum(line[1] * factor for line, factor in zip(stats, factors))
-    total = sum(line[2] * factor for line, factor in zip(stats, factors))
-    smass = sum(line[4] * jnp.exp(line[3] - speak) for line in stats)
-    return (peak, mass, total, speak, smass), factors
+    smass = sum(line[3] * jnp.exp(line[2] - speak) for line in stats)
+    return (peak, mass, speak, smass), factors
 
 
 def columns_of(lines):
@@ -235,18 +259,26 @@
     return jnp.concatenate(lines, axis=0).T
 
 
-def relay_kernel(near, far, from_left, from_right, mine, *refs):
-    near_out, far_out, kept = refs[-3:]
+def relay_kernel(later, near, far, from_left, from_right, mine, *refs):
     depth = from_left.shape[0] - 16
     half = depth // SIDE
     rows = 2 * half
-    stats = [unpack_rows(part[depth:, 0:rows], 5) for part in (mine, from_left, from_right)]
-    kept[...] = jnp.concatenate(stats[0] + stats[1] + stats[2] + [jnp.zeros((1, rows), F32)], axis=0)
-    own, left, right = (line[0] for line in stats)
-    lane = lax.broadcasted_iota(jnp.int32, own.shape, 1)
-    other = jnp.where(lane < half, left, right)
-    peak = jnp.maximum(own, other)
-    table = columns_of([jnp.exp(own - peak), jnp.exp(other - peak)])
+    number = 1 if later else 4
+    stats = [unpack_rows(part[depth:, :], number) for part in (mine, from_left, from_right)]
+    lines = stats[0] + stats[1] + stats[2]
+    lines.append(jnp.zeros((16 - len(lines), rows), F32))
+    if later:
+        table = refs[0][...]
+        near_out, far_out, kept = refs[-3:]
+    else:
+        near_out, far_out, kept, table_out = refs[-4:]
+        own, left, right = (line[0] for line in stats)
+        lane = lax.broadcasted_iota(jnp.int32, own.shape, 1)
+        other = jnp.where(lane < half, left, right)
+        peak = jnp.maximum(own, other)
+        table = columns_of([jnp.exp(own - peak), jnp.exp(other - peak)])
+        table_out[...] = table
+    kept[...] = jnp.concatenate(lines, axis=0)
     near_out[SIDE * rows : SIDE * rows + 16, :] = from_left[depth : depth + 16, :]
     for z in range(SIDE):
         low, high = slice(z * rows, z * rows + half), slice(z * rows + half, (z + 1) * rows)
@@ -259,64 +291,84 @@
         far_out[low, :] = far[low, :]
 
 
-def relayed(near, far, from_left, from_right, last, behind):
+def relayed(near, far, from_left, from_right, mine, tables, behind=()):
     depth, width = near.shape
     rows = depth // SIDE
-    return pl.pallas_call(
-        relay_kernel,
-        out_shape=[
-            jax.ShapeDtypeStruct((depth + 16, width), BF16),
-            jax.ShapeDtypeStruct((depth, width), BF16),
-            jax.ShapeDtypeStruct((16, rows), F32),
-        ],
-        in_specs=[VMEM] * 5 + [ANY] * len(behind),
-        out_specs=[VMEM] * 3,
-        compiler_params=params(),
-        cost_estimate=cost(depth * width, 8 * depth * width),
+    outs = [
+        jax.ShapeDtypeStruct((depth + 16, width), BF16),
+        jax.ShapeDtypeStruct((depth, width), BF16),
+        jax.ShapeDtypeStruct((16, rows), F32),
+    ]
+    if not tables:
+        outs.append(jax.ShapeDtypeStruct((rows, 128), F32))
+    return pl.pallas_call(
+        functools.partial(relay_kernel, bool(tables)),
+        out_shape=outs,
+        in_specs=[VMEM] * (5 + len(tables)) + [ANY] * len(behind),
+        out_specs=[VMEM] * len(outs),
+        compiler_params=params(),
+        cost_estimate=cost(depth * width, depth * width),
         name="relay_targets",
-    )(near, far, from_left, from_right, last, *behind)
-
-
-def merge_kernel(place, given, *refs):
-    parts, outs = refs[:3], refs[3:]
-    rows = outs[0].shape[0] - 16
-    lines = [[given[5 * i + j : 5 * i + j + 1] for j in range(5)] for i in range(3)]
-    lines.append(unpack_rows(parts[1][SIDE * rows :, 0:rows], 5))
-    stats, _ = joined(lines)
-    packed = pack_rows(stats)
-    own, left, right, across = (line[0] for line in lines)
-    lane = lax.broadcasted_iota(jnp.int32, own.shape, 1)
-    low = lane < rows // 2
-    left = jnp.where(low, jnp.maximum(left, across), left)
-    right = jnp.where(low, right, jnp.maximum(right, across))
-    table = columns_of([jnp.exp(base - stats[0]) for base in (own, left, right)])
+    )(near, far, from_left, from_right, mine, *tables, *behind)
+
+
+def merge_kernel(later, place, given, *refs):
+    parts = refs[:3]
+    width = parts[0].shape[1]
+    rows = parts[0].shape[0] // SIDE
+    sent = parts[1][SIDE * rows :, :]
+    if later:
+        table, factors, outs = refs[3][...], refs[4], refs[-SIDE:]
+        lines = [given[i : i + 1] for i in range(3)] + unpack_rows(sent, 1)
+        packed = pack_rows([sum(line * factors[i : i + 1] for i, line in enumerate(lines))])
+    else:
+        outs = refs[-2 - SIDE : -2]
+        lines = [[given[4 * i + j : 4 * i + j + 1] for j in range(4)] for i in range(3)]
+        lines.append(unpack_rows(sent, 4))
+        stats, factors = joined(lines)
+        packed = pack_rows(stats)
+        own, left, right, across = (line[0] for line in lines)
+        lane = lax.broadcasted_iota(jnp.int32, own.shape, 1)
+        low = lane < rows // 2
+        left = jnp.where(low, jnp.maximum(left, across), left)
+        right = jnp.where(low, right, jnp.maximum(right, across))
+        table = columns_of([jnp.exp(base - stats[0]) for base in (own, left, right)])
+        refs[-2][...] = table
+        refs[-1][...] = jnp.concatenate(factors + [jnp.zeros((4, rows), F32)], axis=0)
     for step in range(SIDE):
         at = pl.ds(pl.multiple_of(lax.rem(place[1] + step, SIDE) * rows, rows), rows)
         value = table[:, 0:1] * parts[0][at, :].astype(F32)
         for d in range(1, 3):
             value += table[:, d : d + 1] * parts[d][at, :].astype(F32)
         outs[step][0:rows, :] = value.astype(BF16)
-        put_rows(outs[step], rows, packed)
-
-
-def merged(place, given, parts, rows):
+        outs[step][rows : rows + 16, :] = packed
+
+
+def merged(place, given, parts, tables, behind=()):
     width = parts[0].shape[1]
-    return pl.pallas_call(
-        merge_kernel,
-        out_shape=[jax.ShapeDtypeStruct((rows + 16, width), BF16)] * SIDE,
-        in_specs=[SMEM] + [VMEM] * 4,
-        out_specs=[VMEM] * SIDE,
-        compiler_params=params(),
-        cost_estimate=cost(32 * rows * width, 40 * rows * width),
+    rows = parts[0].shape[0] // SIDE
+    outs = [jax.ShapeDtypeStruct((rows + 16, width), BF16)] * SIDE
+    if not tables:
+        outs += [jax.ShapeDtypeStruct((rows, 128), F32), jax.ShapeDtypeStruct((8, rows), F32)]
+    return pl.pallas_call(
+        functools.partial(merge_kernel, bool(tables)),
+        out_shape=outs,
+        in_specs=[SMEM] + [VMEM] * (4 + len(tables)) + [ANY] * len(behind),
+        out_specs=[VMEM] * len(outs),
+        compiler_params=params(),
+        cost_estimate=cost(rows * width, rows * width),
         name="merge_targets",
-    )(place, given, *parts)
+    )(place, given, *parts, *tables, *behind)
 
 
 def gradient_kernel(place, logits, *refs):
-    parts, grad = refs[:SIDE], refs[SIDE]
-    rows, width = logits.shape[0], parts[0].shape[1]
-    stats, factors = joined([unpack_rows(part[rows:, 0:rows], 5) for part in parts])
-    _, mass, total, peak, smass = stats
+    chunks, grad = (refs[:SIDE], refs[SIDE : 2 * SIDE]), refs[2 * SIDE]
+    rows, width = logits.shape[0], refs[0].shape[1]
+    stats, factors = joined([unpack_rows(part[rows:, :], 4) for part in chunks[0]])
+    _, mass, peak, smass = stats
+    total = sum(
+        unpack_rows(part[rows:, :], 1)[0] * factor for part, factor in zip(chunks[1], factors)
+    )
     total = total / mass
     floored = jnp.maximum(total, 1.0)
     scales = [factor / mass / floored for factor in factors]
@@ -325,15 +377,16 @@
     terms = jnp.zeros((rows, width), F32)
     for step in range(SIDE):
         block = lax.rem(place[1] + SIDE - step, SIDE)
-        at = pl.ds(pl.multiple_of(block * width, width), width)
-        scores = logits[:, at]
-        target = parts[step][0:rows, :].astype(F32) * table[:, step : step + 1]
-        positive = target > 0
-        entropy = jnp.where(positive, target * jnp.log(jnp.where(positive, target, 1.0)), 0.0)
-        terms += entropy - target * (scores - norm)
-        value = share * jnp.exp(scores - peak) - target
-        grad[at, :] = value.T.astype(BF16)
-    grad[SIDE * width :, :] = pack_rows([jnp.sum(terms.T, axis=0, keepdims=True)])
+        for chunk, parts in enumerate(chunks):
+            at = pl.ds(pl.multiple_of(block * 512 + chunk * width, width), width)
+            scores = logits[:, at]
+            target = parts[step][0:rows, :].astype(F32) * table[:, step : step + 1]
+            positive = target > 0
+            entropy = jnp.where(positive, target * jnp.log(jnp.where(positive, target, 1.0)), 0.0)
+            terms += entropy - target * (scores - norm)
+            value = share * jnp.exp(scores - peak) - target
+            grad[at, :] = value.T.astype(BF16)
+    grad[SIDE * 512 :, :] = pack_rows([jnp.sum(terms.T, axis=0, keepdims=True)])
 
 
 def gradients(place, logits, parts):
@@ -341,7 +394,7 @@
     return pl.pallas_call(
         gradient_kernel,
         out_shape=jax.ShapeDtypeStruct((cols + 16, rows), BF16),
-        in_specs=[SMEM] + [VMEM] * (1 + SIDE),
+        in_specs=[SMEM] + [VMEM] * (1 + 2 * SIDE),
         out_specs=VMEM,
         compiler_params=params(),
         cost_estimate=cost(60 * rows * cols, 8 * rows * cols, 2 * rows * cols),
@@ -551,23 +604,37 @@
     speak = jnp.max(logits, axis=1)
     smass = jnp.sum(jnp.exp(logits - speak[:, None]), axis=1)
 
-    blank = jnp.zeros_like(peak)
-    before = jnp.stack([peak, mass, blank, speak, smass, blank, blank, blank])
-
-    piece = prepared(tile_weights)
+    before = jnp.stack([peak, mass, speak, smass] * 2)
+
+    piece = sliced(tile_weights, 0)
+    mine = [piece, *gated(spread([piece] * SIDE, "tx")[1:], [mass, smass])]
+    other = [swap(piece) for piece in mine]
+
+    piece = sliced(tile_weights, 1, [mine[1]])
     right, left = send(piece, "tx", 1), send(piece, "tx", 3)
-    top, low = halves(right, left, [mass, smass])
-    pieces = [piece, right, left, send(top, "tx", 1), send(low, "tx", 3)]
-    pieces = pieces + [swap(piece) for piece in pieces]
-
-    own, near, far, to_right, to_left = products(
-        place, tile_pairs, tile_count, probs, before, pieces
+    *parts, total = products(
+        place, tile_pairs, tile_count, probs, before, mine, other, False, [piece]
     )
+    top, low = halves(right, left, [parts[0]])
+    own, near, far, to_right, to_left = parts
+    left_part, right_part = send(to_right, "vy", 1), send(to_left, "vy", 3)
+    near, far, given, table = relayed(near, far, left_part, right_part, to_right, [], [right, left])
+    near, far = send(near, "vy", 1), send(far, "vy", 3)
+    top, low = gated([send(top, "tx", 1), send(low, "tx", 3)], [near, far])
+    mine = [piece, right, left, top, low]
+    later = products(
+        place, tile_pairs, tile_count, probs, total, mine, [swap(piece) for piece in mine], True
+    )
+
+    *first, scales, factors = merged(place, given, [own, near, far], [], [later[0]])
+    own, near, far, to_right, to_left = later
+    left_part, right_part = send(to_right, "vy", 1), send(to_left, "vy", 3)
     stage = staged(place, student_unembed, [own])
-    left_part, right_part = send(to_right, "vy", 1), send(to_left, "vy", 3)
-    near, far, given = relayed(near, far, left_part, right_part, to_right, [stage])
-    parts = merged(place, given, [own, send(near, "vy", 1), send(far, "vy", 3)], rows)
-    mine = gradients(place, logits, spread(parts, "vz"))
+    near, far, given = relayed(near, far, left_part, right_part, to_right, [table], [stage])
+    parts = [own, send(near, "vy", 1), send(far, "vy", 3)]
+    first = spread(first, "vz")
+    second = merged(place, given, parts, [scales, factors])
+    mine = gradients(place, logits, first + spread(second, "vz"))
 
     own = own_hidden(stage, mine)
     other = swap(mine)

time: 165 us -> 158 us (0.958)
  waiting for transfers between devices: 82.5 us -> 50.7 us
  starting transfers between devices: 34.8 us -> 56.7 us
  Pallas kernels: 25.7 us -> 31 us
  other arithmetic: 6.23 us -> 4.54 us
    ppermute x11 -> x21, waiting for transfers between devices: 63.9 us -> 32.1 us  [send(): lax.ppermute(value, axis, [(i, (i + step) % SIDE) for i in range(SIDE)])]
    ppermute x11 -> x21, starting transfers between devices: 17.5 us -> 31.8 us  [send(): lax.ppermute(value, axis, [(i, (i + step) % SIDE) for i in range(SIDE)])]
    pallas_call x5 -> x11, Pallas kernels: 11.1 us -> 16.5 us  [the longest x2 11.6 us: products(): pl.pallas_call(functools.partial(product_kernel, len(pieces), later), out...]
    ppermute x7 -> x11, starting transfers between devices: 10.9 us -> 15.9 us  [swap(): return lax.ppermute(value, 'tc', [(0, 1), (1, 0)])]
    ppermute x6, starting transfers between devices: 6.39 us -> 9.03 us  [crossed(): received.append(lax.ppermute(parts[step], ('vy', 'vz', 'tc'), pairs))]
    reduce_sum x1, other arithmetic: 2.16 us -> 0.43 us  [shards(): smass = jnp.sum(jnp.exp(logits - speak[:, None]), axis=1)]
  transfers between devices with their start and end apart: 24 -> 38, of which waited for: 19 -> 22; matrix products, arithmetic and copies ran while one was open for 10% -> 9% of each run, Pallas kernels for 4% -> 10%
where the time goes in v9:
time: 158 us; the launch traced here: 157 us
  starting transfers between devices  56.7 us (36%)
  waiting for transfers between devices  50.7 us (32%)
  Pallas kernels  31 us (20%)
  matrix products  8.37 us (5%)
  other arithmetic  4.54 us (3%)
  local copies, waits for them, and re-layouts  3.76 us (2%)
    ppermute x21, waiting for transfers between devices, send(): lax.ppermute(value, axis, [(i, (i + step) % SIDE) for i in range(SIDE)])  32.1 us
    ppermute x21, starting transfers between devices, send(): lax.ppermute(value, axis, [(i, (i + step) % SIDE) for i in range(SIDE)])  31.8 us
    ppermute x6, waiting for transfers between devices, crossed(): received.append(lax.ppermute(parts[step], ('vy', 'vz', 'tc'), pairs))  16.2 us
    ppermute x11, starting transfers between devices, swap(): return lax.ppermute(value, 'tc', [(0, 1), (1, 0)])  15.9 us
    pallas_call x2, Pallas kernels, products(): pl.pallas_call(functools.partial(product_kernel, len(pieces), later), out...  11.6 us
    ppermute x6, starting transfers between devices, crossed(): received.append(lax.ppermute(parts[step], ('vy', 'vz', 'tc'), pairs))  9.03 us
    dot_general x1, matrix products, shards(): jnp.dot(student_hidden, student_unembed, preferred_element_type=F32)  8.37 us
    pallas_call x1, Pallas kernels, staged(): pl.pallas_call(stage_kernel, out_shape=jax.ShapeDtypeStruct((depth // 2,...  4.06 us
  transfers between devices with their start and end apart: 38, of which 22 were waited for; matrix products, arithmetic and copies ran while one was open for 9% of the time, Pallas kernels for 10%

profile of v9, /device:TPU:1, one launch (start us, length us, event | category | flops | bytes accessed | tf_op | source)
XLA Modules:
  0.0 156.6 jit_solution(5991948787049692922)
XLA Ops:
  4.3 2.6 %collective-permute-start.2 = (bf16[1024,256]{1,0:T(8,128)(2,1)}, bf16[1024,256]{1,0:T(8,128)(2,1)}, u32[]{:S(2)}, u32[]{:S(2)}) collective-permute-start(bf16[1024,256]{1,0:T(8,128)(2,1)} %slice_weights.2.rest_0_), channel_id=1, source_target_pairs={{0,6},{2,0},{4,2},{6,4},{1,7},{3,1},{5,3},{7,5},{8,14},{10,8},{12,... | collective-permute-start | bytes 1572872 | tf_op jit(solution)/shard_map/ppermute | solution.py:29
  10.0 8.4 %fusion.2 = (f32[256]{0:T(256)S(1)}, f32[256,2048]{1,0:T(8,128)S(1)}) fusion(bf16[256,4096]{1,0:T(8,128)(2,1)S(1)} %copy-done, bf16[4096,2048]{1,0:T(8,128)(2,1)} %unembed.1), kind=kOutput, calls=%fused_computation.4 | convolution fusion | flops 4295491584 | bytes 20972544 | tf_op jit(solution)/shard_map/dot_general | solution.py:603
  20.9 8.7 %collective-permute-done.2.refs_2_ = bf16[1024,256]{1,0:T(8,128)(2,1)} collective-permute-done((bf16[1024,256]{1,0:T(8,128)(2,1)}, bf16[1024,256]{1,0:T(8,128)(2,1)}, u32[]{:S(2)}, u32[]{:S(2)}) %collective-permute-start.2) | collective-permute-done | bytes 524320 | tf_op jit(solution)/shard_map/ppermute | solution.py:29
  29.6 4.0 %collective-permute-done.refs_0_ = bf16[1024,256]{1,0:T(8,128)(2,1)S(1)} collective-permute-done((bf16[1024,256]{1,0:T(8,128)(2,1)}, bf16[1024,256]{1,0:T(8,128)(2,1)S(1)}, u32[]{:S(2)}, u32[]{:S(2)}) %collective-permute-start) | collective-permute-done | bytes 524320 | tf_op jit(solution)/shard_map/ppermute | solution.py:29
  39.1 6.2 %tile_products.2 = (bf16[1024,256]{1,0:T(8,128)(2,1)S(1)}, bf16[1024,256]{1,0:T(8,128)(2,1)S(1)}, bf16[1024,256]{1,0:T(8,128)(2,1)S(1)}, bf16[528,256]{1,0:T(8,1...) custom-call(s32[6]{0:T(128)S(1)} %stack.44.place, s32[16,2]{1,0:T(8,128)S(1)} %copy.14.pairs, ...), custom_call_target="tpu_custom_call" | custom-call | flops 1073741824 | bytes 8388608 | tf_op jit(solution)/shard_map/tile_products/pallas_call | solution.py:216
  49.6 3.4 %collective-permute-done.12.from_right = bf16[528,256]{1,0:T(8,128)(2,1)S(1)} collective-permute-done((bf16[528,256]{1,0:T(8,128)(2,1)S(1)}, bf16[528,256]{1,0:T(8,128)(2,1)S(1)}, u32[]{:S(2)}, u32[]{:S(2)}) %collective-permute-start.12) | collective-permute-done | bytes 270368 | tf_op jit(solution)/shard_map/ppermute | solution.py:29
  56.6 2.6 %collective-permute-start.14 = (bf16[1024,256]{1,0:T(8,128)(2,1)S(1)}, bf16[1024,256]{1,0:T(8,128)(2,1)S(1)}, u32[]{:S(2)}, u32[]{:S(2)}) collective-permute-start(bf16[1024,256]{1,0:T(8,128)(2,1)S(1)} %get-tuple-element.60), channel_id=1, source_target_pairs={{0,96},{32,0},{64,32},{96,64},{1,97},{33,1},{65,33},{97,65},{2,98}... | collective-permute-start | bytes 1572872 | tf_op jit(solution)/shard_map/ppermute | solution.py:29
  59.2 2.7 %collective-permute-start.10 = (bf16[512,256]{1,0:T(8,128)(2,1)S(1)}, bf16[512,256]{1,0:T(8,128)(2,1)S(1)}, u32[]{:S(2)}, u32[]{:S(2)}) collective-permute-start(bf16[512,256]{1,0:T(8,128)(2,1)S(1)} %get-tuple-element.54), channel_id=1, source_target_pairs={{0,6},{2,0},{4,2},{6,4},{1,7},{3,1},{5,3},{7,5},{8,14},{10,8},{12,... | collective-permute-start | bytes 786440 | tf_op jit(solution)/shard_map/ppermute | solution.py:29
  61.9 2.7 %collective-permute-start.15 = (bf16[1024,256]{1,0:T(8,128)(2,1)S(1)}, bf16[1024,256]{1,0:T(8,128)(2,1)S(1)}, u32[]{:S(2)}, u32[]{:S(2)}) collective-permute-start(bf16[1024,256]{1,0:T(8,128)(2,1)S(1)} %slice_weights.3.rest_8_.rest_0_), channel_id=1, source_target_pairs={{0,1},{1,0},{2,3},{3,2},{4,5},{5,4},{6,7},{7,6},{8,9},{9,8},{10,11... | collective-permute-start | bytes 1572872 | tf_op jit(solution)/shard_map/ppermute | solution.py:33
  66.1 3.0 %collective-permute-start.17 = (bf16[1024,256]{1,0:T(8,128)(2,1)}, bf16[1024,256]{1,0:T(8,128)(2,1)S(1)}, u32[]{:S(2)}, u32[]{:S(2)}) collective-permute-start(bf16[1024,256]{1,0:T(8,128)(2,1)} %collective-permute-done.8.left.refs_1_.rest_2_), channel_id=1, source_target_pairs={{0,1},{1,0},{2,3},{3,2},{4,5},{5,4},{6,7},{7,6},{8,9},{9,8},{10,11... | collective-permute-start | bytes 1572872 | tf_op jit(solution)/shard_map/ppermute | solution.py:33
  72.9 5.4 %tile_products.3 = (bf16[1024,256]{1,0:T(8,128)(2,1)S(1)}, bf16[1024,256]{1,0:T(8,128)(2,1)S(1)}, bf16[1024,256]{1,0:T(8,128)(2,1)S(1)}, bf16[528,256]{1,0:T(8,128)(2,1)S(1)}, bf16[528,256]{1,0:T(8,128)(2,1)S(1)}) custom-call(s32[6]{0:T(128)S(1)} %stack.44.place, s32[16,2]{1,0:T(8,128)S(1)} %copy.14.pairs, s32[1]{0:T(128)S(6)} %copy.20.count, ...), custom_call_target="tpu_custom_call" | custom-call | flops 1073741824 | bytes 8388608 | tf_op jit(solution)/shard_map/tile_products/pallas_call | solution.py:216
  79.9 4.1 %stage_unembed.1.refs_1_.stage = bf16[2048,2048]{1,0:T(8,128)(2,1)S(1)} custom-call(s32[6]{0:T(128)S(1)} %stack.44.place, bf16[4096,2048]{1,0:T(8,128)(2,1)} %unembed.1, bf16[1024,256]{1,0:T(8,128)(2,1)S(1)} %get-tuple-element.63.refs_0_.refs_3_), custom_call_target="tpu_custom_call" | custom-call | bytes 8388608 | tf_op jit(solution)/shard_map/stage_unembed/pallas_call | solution.py:429
  86.0 2.5 %collective-permute-done.23.from_left = bf16[528,256]{1,0:T(8,128)(2,1)S(1)} collective-permute-done((bf16[528,256]{1,0:T(8,128)(2,1)S(1)}, bf16[528,256]{1,0:T(8,128)(2,1)S(1)}, u32[]{:S(2)}, u32[]{:S(2)}) %collective-permute-start.23) | collective-permute-done | bytes 270368 | tf_op jit(solution)/shard_map/ppermute | solution.py:29
  88.9 2.7 %collective-permute-start.26 = (bf16[1024,256]{1,0:T(8,128)(2,1)S(1)}, bf16[1024,256]{1,0:T(8,128)(2,1)S(1)}, u32[]{:S(2)}, u32[]{:S(2)}) collective-permute-start(bf16[1024,256]{1,0:T(8,128)(2,1)S(1)} %get-tuple-element.76), channel_id=1, source_target_pairs={{0,96},{32,0},{64,32},{96,64},{1,97},{33,1},{65,33},{97,65},{2,98}... | collective-permute-start | bytes 1572872 | tf_op jit(solution)/shard_map/ppermute | solution.py:29
  92.8 5.6 %collective-permute-start.21 = (bf16[272,256]{1,0:T(8,128)(2,1)S(1)}, bf16[272,256]{1,0:T(8,128)(2,1)S(1)}, u32[]{:S(2)}, u32[]{:S(2)}) collective-permute-start(bf16[272,256]{1,0:T(8,128)(2,1)S(1)} %get-tuple-element.67), channel_id=1, source_target_pairs={{0,16},{8,24},{16,0},{24,8},{1,17},{9,25},{17,1},{25,9},{2,18},{10... | collective-permute-start | bytes 417800 | tf_op jit(solution)/shard_map/ppermute | solution.py:29
  103.2 5.6 %collective-permute-start.28 = (bf16[272,256]{1,0:T(8,128)(2,1)S(1)}, bf16[272,256]{1,0:T(8,128)(2,1)S(1)}, u32[]{:S(2)}, u32[]{:S(2)}) collective-permute-start(bf16[272,256]{1,0:T(8,128)(2,1)S(1)} %get-tuple-element.81), channel_id=1, source_target_pairs={{0,16},{8,24},{16,0},{24,8},{1,17},{9,25},{17,1},{25,9},{2,18},{10... | collective-permute-start | bytes 417800 | tf_op jit(solution)/shard_map/ppermute | solution.py:29
  116.6 2.5 %collective-permute-start.30 = (bf16[2064,256]{1,0:T(8,128)(2,1)S(1)}, bf16[2064,256]{1,0:T(8,128)(2,1)S(1)}, u32[]{:S(2)}, u32[]{:S(2)}) collective-permute-start(bf16[2064,256]{1,0:T(8,128)(2,1)S(1)} %logit_grad.1.mine), channel_id=1, source_target_pairs={{0,1},{1,0},{2,3},{3,2},{4,5},{5,4},{6,7},{7,6},{8,9},{9,8},{10,11... | collective-permute-start | bytes 3170312 | tf_op jit(solution)/shard_map/ppermute | solution.py:33
  119.1 2.3 %own_hidden.1.own = bf16[2048,256]{1,0:T(8,128)(2,1)S(1)} custom-call(bf16[2048,2048]{1,0:T(8,128)(2,1)S(1)} %stage_unembed.1.refs_1_.stage, bf16[2064,256]{1,0:T(8,128)(2,1)S(1)} %logit_grad.1.mine), custom_call_target="tpu_custom_call" | custom-call | flops 2147483648 | bytes 8388608 | tf_op jit(solution)/shard_map/own_hidden/pallas_call | solution.py:451
  121.4 3.0 %other_hidden.1 = (bf16[528,512]{1,0:T(8,128)(2,1)S(1)}, bf16[528,512]{1,0:T(8,128)(2,1)S(1)}, bf16[528,512]{1,0:T(8,128)(2,1)S(1)}, bf16[528,512]{1,0:T(8,128)(2,1)S(1)}) custom-call(s32[6]{0:T(128)S(1)} %stack.44.place, bf16[2048,2048]{1,0:T(8,128)(2,1)S(1)} %stage_unembed.1.refs_1_.stage, bf16[2064,256]{1,0:T(8,128)(2,1)S(1)} %logit_grad.1.mine, ...), custom_call_target="tpu_custom_call" | custom-call | flops 2147483648 | bytes 8388608 | tf_op jit(solution)/shard_map/other_hidden/pallas_call | solution.py:479
  125.7 3.6 %collective-permute-start.32 = (bf16[528,512]{1,0:T(8,128)(2,1)S(1)}, bf16[528,512]{1,0:T(8,128)(2,1)S(1)}, u32[]{:S(2)}, u32[]{:S(2)}) collective-permute-start(bf16[528,512]{1,0:T(8,128)(2,1)S(1)} %get-tuple-element.85), channel_id=1, source_target_pairs={{0,64},{1,17},{8,72},{9,25},{16,80},{17,1},{24,88},{25,9},{32,96},... | collective-permute-start | bytes 1622024 | tf_op jit(solution)/shard_map/ppermute | solution.py:588
  129.9 5.3 %collective-permute-done.31.refs_1_ = bf16[528,512]{1,0:T(8,128)(2,1)S(1)} collective-permute-done((bf16[528,512]{1,0:T(8,128)(2,1)S(1)}, bf16[528,512]{1,0:T(8,128)(2,1)S(1)}, u32[]{:S(2)}, u32[]{:S(2)}) %collective-permute-start.31) | collective-permute-done | bytes 540704 | tf_op jit(solution)/shard_map/ppermute | solution.py:588
  135.2 6.8 %collective-permute-done.32.refs_2_ = bf16[528,512]{1,0:T(8,128)(2,1)S(1)} collective-permute-done((bf16[528,512]{1,0:T(8,128)(2,1)S(1)}, bf16[528,512]{1,0:T(8,128)(2,1)S(1)}, u32[]{:S(2)}, u32[]{:S(2)}) %collective-permute-start.32) | collective-permute-done | bytes 540704 | tf_op jit(solution)/shard_map/ppermute | solution.py:588
  143.0 3.5 %collective-permute-start.35 = (bf16[144,512]{1,0:T(8,128)(2,1)S(1)}, bf16[144,512]{1,0:T(8,128)(2,1)S(1)}, u32[]{:S(2)}, u32[]{:S(2)}) collective-permute-start(bf16[144,512]{1,0:T(8,128)(2,1)S(1)} %get-tuple-element.89), channel_id=1, source_target_pairs={{0,16},{1,65},{8,24},{9,73},{16,0},{17,81},{24,8},{25,89},{32,48},... | collective-permute-start | bytes 442376 | tf_op jit(solution)/shard_map/ppermute | solution.py:588
  151.3 3.1 %collective-permute-start.37 = (bf16[128,256]{1,0:T(8,128)(2,1)S(1)}, bf16[128,256]{1,0:T(8,128)(2,1)S(1)}, u32[]{:S(2)}, u32[]{:S(2)}) collective-permute-start(bf16[128,256]{1,0:T(8,128)(2,1)S(1)} %get-tuple-element.92), channel_id=1, source_target_pairs={{0,1},{1,0},{2,3},{3,2},{4,5},{5,4},{6,7},{7,6},{8,9},{9,8},{10,11... | collective-permute-start | bytes 196616 | tf_op jit(solution)/shard_map/ppermute | solution.py:33
  (97 shorter events, 54.9 us)
Async XLA Ops:
  2.9 32.2 %collective-permute-start.3 = (bf16[1024,256]{1,0:T(8,128)(2,1)}, bf16[1024,256]{1,0:T(8,128)(2,1)}, u32[]{:S(2)}, u32[]{:S(2)}) collective-permute-start(bf16[1024,256]{1,0:T(8,128)(2,1)} %slice_weights.2.rest_0_), channel_id=1, source_target_pairs={{0,1},{1,0},{2,3},{3,2},{4,5},{5,4},{6,7},{7,6},{8,9},{9,8},{10,11... | collective-permute-start | bytes 1572872 | tf_op jit(solution)/shard_map/ppermute | solution.py:33
  4.3 25.3 %collective-permute-start.2 = (bf16[1024,256]{1,0:T(8,128)(2,1)}, bf16[1024,256]{1,0:T(8,128)(2,1)}, u32[]{:S(2)}, u32[]{:S(2)}) collective-permute-start(bf16[1024,256]{1,0:T(8,128)(2,1)} %slice_weights.2.rest_0_), channel_id=1, source_target_pairs={{0,6},{2,0},{4,2},{6,4},{1,7},{3,1},{5,3},{7,5},{8,14},{10,8},{12,... | collective-permute-start | bytes 1572872 | tf_op jit(solution)/shard_map/ppermute | solution.py:29
  6.8 22.8 %collective-permute-start.1 = (bf16[1024,256]{1,0:T(8,128)(2,1)}, bf16[1024,256]{1,0:T(8,128)(2,1)}, u32[]{:S(2)}, u32[]{:S(2)}) collective-permute-start(bf16[1024,256]{1,0:T(8,128)(2,1)} %slice_weights.2.rest_0_), channel_id=1, source_target_pairs={{0,4},{2,6},{4,0},{6,2},{1,5},{3,7},{5,1},{7,3},{8,12},{10,14},{12... | collective-permute-start | bytes 1572872 | tf_op jit(solution)/shard_map/ppermute | solution.py:29
  7.4 26.3 %collective-permute-start = (bf16[1024,256]{1,0:T(8,128)(2,1)}, bf16[1024,256]{1,0:T(8,128)(2,1)S(1)}, u32[]{:S(2)}, u32[]{:S(2)}) collective-permute-start(bf16[1024,256]{1,0:T(8,128)(2,1)} %slice_weights.2.rest_0_), channel_id=1, source_target_pairs={{0,2},{2,4},{4,6},{6,0},{1,3},{3,5},{5,7},{7,1},{8,10},{10,12},{12... | collective-permute-start | bytes 1572872 | tf_op jit(solution)/shard_map/ppermute | solution.py:29
  34.7 13.7 %collective-permute-start.8 = (bf16[1024,256]{1,0:T(8,128)(2,1)S(1)}, bf16[1024,256]{1,0:T(8,128)(2,1)}, u32[]{:S(2)}, u32[]{:S(2)}) collective-permute-start(bf16[1024,256]{1,0:T(8,128)(2,1)S(1)} %slice_weights.3.rest_8_.rest_0_), channel_id=1, source_target_pairs={{0,6},{2,0},{4,2},{6,4},{1,7},{3,1},{5,3},{7,5},{8,14},{10,8},{12,... | collective-permute-start | bytes 1572872 | tf_op jit(solution)/shard_map/ppermute | solution.py:29
  35.1 14.6 %collective-permute-start.7 = (bf16[1024,256]{1,0:T(8,128)(2,1)S(1)}, bf16[1024,256]{1,0:T(8,128)(2,1)}, u32[]{:S(2)}, u32[]{:S(2)}) collective-permute-start(bf16[1024,256]{1,0:T(8,128)(2,1)S(1)} %slice_weights.3.rest_8_.rest_0_), channel_id=1, source_target_pairs={{0,2},{2,4},{4,6},{6,0},{1,3},{3,5},{5,7},{7,1},{8,10},{10,12},{12... | collective-permute-start | bytes 1572872 | tf_op jit(solution)/shard_map/ppermute | solution.py:29
  45.3 7.8 %collective-permute-start.12 = (bf16[528,256]{1,0:T(8,128)(2,1)S(1)}, bf16[528,256]{1,0:T(8,128)(2,1)S(1)}, u32[]{:S(2)}, u32[]{:S(2)}) collective-permute-start(bf16[528,256]{1,0:T(8,128)(2,1)S(1)} %get-tuple-element.58), channel_id=1, source_target_pairs={{0,96},{32,0},{64,32},{96,64},{1,97},{33,1},{65,33},{97,65},{2,98}... | collective-permute-start | bytes 811016 | tf_op jit(solution)/shard_map/ppermute | solution.py:29
  46.3 8.6 %collective-permute-start.11 = (bf16[528,256]{1,0:T(8,128)(2,1)S(1)}, bf16[528,256]{1,0:T(8,128)(2,1)S(1)}, u32[]{:S(2)}, u32[]{:S(2)}) collective-permute-start(bf16[528,256]{1,0:T(8,128)(2,1)S(1)} %get-tuple-element.57.mine), channel_id=1, source_target_pairs={{0,32},{32,64},{64,96},{96,0},{1,33},{33,65},{65,97},{97,1},{2,34}... | collective-permute-start | bytes 811016 | tf_op jit(solution)/shard_map/ppermute | solution.py:29
  55.3 13.8 %collective-permute-start.13 = (bf16[1040,256]{1,0:T(8,128)(2,1)S(1)}, bf16[1040,256]{1,0:T(8,128)(2,1)S(1)}, u32[]{:S(2)}, u32[]{:S(2)}) collective-permute-start(bf16[1040,256]{1,0:T(8,128)(2,1)S(1)} %get-tuple-element.59), channel_id=1, source_target_pairs={{0,32},{32,64},{64,96},{96,0},{1,33},{33,65},{65,97},{97,1},{2,34}... | collective-permute-start | bytes 1597448 | tf_op jit(solution)/shard_map/ppermute | solution.py:29
  56.6 12.5 %collective-permute-start.14 = (bf16[1024,256]{1,0:T(8,128)(2,1)S(1)}, bf16[1024,256]{1,0:T(8,128)(2,1)S(1)}, u32[]{:S(2)}, u32[]{:S(2)}) collective-permute-start(bf16[1024,256]{1,0:T(8,128)(2,1)S(1)} %get-tuple-element.60), channel_id=1, source_target_pairs={{0,96},{32,0},{64,32},{96,64},{1,97},{33,1},{65,33},{97,65},{2,98}... | collective-permute-start | bytes 1572872 | tf_op jit(solution)/shard_map/ppermute | solution.py:29
  59.2 9.9 %collective-permute-start.10 = (bf16[512,256]{1,0:T(8,128)(2,1)S(1)}, bf16[512,256]{1,0:T(8,128)(2,1)S(1)}, u32[]{:S(2)}, u32[]{:S(2)}) collective-permute-start(bf16[512,256]{1,0:T(8,128)(2,1)S(1)} %get-tuple-element.54), channel_id=1, source_target_pairs={{0,6},{2,0},{4,2},{6,4},{1,7},{3,1},{5,3},{7,5},{8,14},{10,8},{12,... | collective-permute-start | bytes 786440 | tf_op jit(solution)/shard_map/ppermute | solution.py:29
  61.9 9.5 %collective-permute-start.15 = (bf16[1024,256]{1,0:T(8,128)(2,1)S(1)}, bf16[1024,256]{1,0:T(8,128)(2,1)S(1)}, u32[]{:S(2)}, u32[]{:S(2)}) collective-permute-start(bf16[1024,256]{1,0:T(8,128)(2,1)S(1)} %slice_weights.3.rest_8_.rest_0_), channel_id=1, source_target_pairs={{0,1},{1,0},{2,3},{3,2},{4,5},{5,4},{6,7},{7,6},{8,9},{9,8},{10,11... | collective-permute-start | bytes 1572872 | tf_op jit(solution)/shard_map/ppermute | solution.py:33
  78.3 7.8 %collective-permute-start.24 = (bf16[528,256]{1,0:T(8,128)(2,1)S(1)}, bf16[528,256]{1,0:T(8,128)(2,1)S(1)}, u32[]{:S(2)}, u32[]{:S(2)}) collective-permute-start(bf16[528,256]{1,0:T(8,128)(2,1)S(1)} %get-tuple-element.72), channel_id=1, source_target_pairs={{0,96},{32,0},{64,32},{96,64},{1,97},{33,1},{65,33},{97,65},{2,98}... | collective-permute-start | bytes 811016 | tf_op jit(solution)/shard_map/ppermute | solution.py:29
  79.9 8.6 %collective-permute-start.23 = (bf16[528,256]{1,0:T(8,128)(2,1)S(1)}, bf16[528,256]{1,0:T(8,128)(2,1)S(1)}, u32[]{:S(2)}, u32[]{:S(2)}) collective-permute-start(bf16[528,256]{1,0:T(8,128)(2,1)S(1)} %get-tuple-element.71.mine), channel_id=1, source_target_pairs={{0,32},{32,64},{64,96},{96,0},{1,33},{33,65},{65,97},{97,1},{2,34}... | collective-permute-start | bytes 811016 | tf_op jit(solution)/shard_map/ppermute | solution.py:29
  88.8 13.3 %collective-permute-start.25 = (bf16[1040,256]{1,0:T(8,128)(2,1)S(1)}, bf16[1040,256]{1,0:T(8,128)(2,1)S(1)}, u32[]{:S(2)}, u32[]{:S(2)}) collective-permute-start(bf16[1040,256]{1,0:T(8,128)(2,1)S(1)} %get-tuple-element.75), channel_id=1, source_target_pairs={{0,32},{32,64},{64,96},{96,0},{1,33},{33,65},{65,97},{97,1},{2,34}... | collective-permute-start | bytes 1597448 | tf_op jit(solution)/shard_map/ppermute | solution.py:29
  88.9 12.1 %collective-permute-start.26 = (bf16[1024,256]{1,0:T(8,128)(2,1)S(1)}, bf16[1024,256]{1,0:T(8,128)(2,1)S(1)}, u32[]{:S(2)}, u32[]{:S(2)}) collective-permute-start(bf16[1024,256]{1,0:T(8,128)(2,1)S(1)} %get-tuple-element.76), channel_id=1, source_target_pairs={{0,96},{32,0},{64,32},{96,64},{1,97},{33,1},{65,33},{97,65},{2,98}... | collective-permute-start | bytes 1572872 | tf_op jit(solution)/shard_map/ppermute | solution.py:29
  92.7 16.2 %collective-permute-start.20 = (bf16[272,256]{1,0:T(8,128)(2,1)S(1)}, bf16[272,256]{1,0:T(8,128)(2,1)S(1)}, u32[]{:S(2)}, u32[]{:S(2)}) collective-permute-start(bf16[272,256]{1,0:T(8,128)(2,1)S(1)} %get-tuple-element.66), channel_id=1, source_target_pairs={{0,8},{8,16},{16,24},{24,0},{1,9},{9,17},{17,25},{25,1},{2,10},{10... | collective-permute-start | bytes 417800 | tf_op jit(solution)/shard_map/ppermute | solution.py:29
  92.8 18.1 %collective-permute-start.21 = (bf16[272,256]{1,0:T(8,128)(2,1)S(1)}, bf16[272,256]{1,0:T(8,128)(2,1)S(1)}, u32[]{:S(2)}, u32[]{:S(2)}) collective-permute-start(bf16[272,256]{1,0:T(8,128)(2,1)S(1)} %get-tuple-element.67), channel_id=1, source_target_pairs={{0,16},{8,24},{16,0},{24,8},{1,17},{9,25},{17,1},{25,9},{2,18},{10... | collective-permute-start | bytes 417800 | tf_op jit(solution)/shard_map/ppermute | solution.py:29
  98.4 12.5 %collective-permute-start.22 = (bf16[272,256]{1,0:T(8,128)(2,1)S(1)}, bf16[272,256]{1,0:T(8,128)(2,1)S(1)}, u32[]{:S(2)}, u32[]{:S(2)}) collective-permute-start(bf16[272,256]{1,0:T(8,128)(2,1)S(1)} %get-tuple-element.68), channel_id=1, source_target_pairs={{0,24},{8,0},{16,8},{24,16},{1,25},{9,1},{17,9},{25,17},{2,26},{10... | collective-permute-start | bytes 417800 | tf_op jit(solution)/shard_map/ppermute | solution.py:29
  103.2 7.7 %collective-permute-start.27 = (bf16[272,256]{1,0:T(8,128)(2,1)S(1)}, bf16[272,256]{1,0:T(8,128)(2,1)S(1)}, u32[]{:S(2)}, u32[]{:S(2)}) collective-permute-start(bf16[272,256]{1,0:T(8,128)(2,1)S(1)} %get-tuple-element.80), channel_id=1, source_target_pairs={{0,8},{8,16},{16,24},{24,0},{1,9},{9,17},{17,25},{25,1},{2,10},{10... | collective-permute-start | bytes 417800 | tf_op jit(solution)/shard_map/ppermute | solution.py:29
  103.2 9.7 %collective-permute-start.28 = (bf16[272,256]{1,0:T(8,128)(2,1)S(1)}, bf16[272,256]{1,0:T(8,128)(2,1)S(1)}, u32[]{:S(2)}, u32[]{:S(2)}) collective-permute-start(bf16[272,256]{1,0:T(8,128)(2,1)S(1)} %get-tuple-element.81), channel_id=1, source_target_pairs={{0,16},{8,24},{16,0},{24,8},{1,17},{9,25},{17,1},{25,9},{2,18},{10... | collective-permute-start | bytes 417800 | tf_op jit(solution)/shard_map/ppermute | solution.py:29
  124.4 10.7 %collective-permute-start.31 = (bf16[528,512]{1,0:T(8,128)(2,1)S(1)}, bf16[528,512]{1,0:T(8,128)(2,1)S(1)}, u32[]{:S(2)}, u32[]{:S(2)}) collective-permute-start(bf16[528,512]{1,0:T(8,128)(2,1)S(1)} %get-tuple-element.84), channel_id=1, source_target_pairs={{0,32},{1,9},{8,40},{9,17},{16,48},{17,25},{24,56},{25,1},{32,64},... | collective-permute-start | bytes 1622024 | tf_op jit(solution)/shard_map/ppermute | solution.py:588
  125.7 16.3 %collective-permute-start.32 = (bf16[528,512]{1,0:T(8,128)(2,1)S(1)}, bf16[528,512]{1,0:T(8,128)(2,1)S(1)}, u32[]{:S(2)}, u32[]{:S(2)}) collective-permute-start(bf16[528,512]{1,0:T(8,128)(2,1)S(1)} %get-tuple-element.85), channel_id=1, source_target_pairs={{0,64},{1,17},{8,72},{9,25},{16,80},{17,1},{24,88},{25,9},{32,96},... | collective-permute-start | bytes 1622024 | tf_op jit(solution)/shard_map/ppermute | solution.py:588
  129.3 12.7 %collective-permute-start.33 = (bf16[528,512]{1,0:T(8,128)(2,1)S(1)}, bf16[528,512]{1,0:T(8,128)(2,1)S(1)}, u32[]{:S(2)}, u32[]{:S(2)}) collective-permute-start(bf16[528,512]{1,0:T(8,128)(2,1)S(1)} %get-tuple-element.86), channel_id=1, source_target_pairs={{0,96},{1,25},{8,104},{9,1},{16,112},{17,9},{24,120},{25,17},{32,0... | collective-permute-start | bytes 1622024 | tf_op jit(solution)/shard_map/ppermute | solution.py:588
  (23 other events, 157.3 us)

commit v10 on v9

--- a/solution.py
+++ b/solution.py
@@ -78,26 +78,20 @@
     )(*parts, *behind)
 
 
-def pack_kernel(number, *refs):
-    out = refs[-1]
-    at = 0
-    for part in refs[:number]:
-        out[at : at + part.shape[0], :] = part[...]
-        at += part.shape[0]
-
-
-def packed_pieces(parts, behind):
-    depth = sum(part.shape[0] for part in parts)
-    width = parts[0].shape[1]
-    return pl.pallas_call(
-        functools.partial(pack_kernel, len(parts)),
-        out_shape=jax.ShapeDtypeStruct((depth, width), BF16),
-        in_specs=[VMEM] * len(parts) + [ANY] * len(behind),
+def hold_kernel(source, out):
+    out[...] = source[...]
+
+
+def held(value):
+    return pl.pallas_call(
+        hold_kernel,
+        out_shape=jax.ShapeDtypeStruct(value.shape, value.dtype),
+        in_specs=[VMEM],
         out_specs=VMEM,
         compiler_params=params(),
-        cost_estimate=cost(0, 4 * depth * width),
-        name="pack_weights",
-    )(*parts, *behind)
+        cost_estimate=cost(0, 4 * value.size),
+        name="hold_probs",
+    )(value)
 
 
 def halves_kernel(right, left, *refs):
@@ -126,80 +120,52 @@
 
 
 def product_kernel(number, later, place, pairs, count, probs, before, *rest):
-    pieces, (across, total, seen) = rest[:number], rest[-3:]
-    outs = rest[-9:-4] if not later else rest[-8:-3]
-    half_number = number // 2
-    mine, other = list(pieces[:half_number]), list(pieces[half_number:])
-    if half_number == 5:
-        for core, parts in enumerate((mine, other)):
-            across[core, 0:512] = parts[3][...]
-            across[core, 512:1024] = parts[4][...]
-            parts[2:] = [across.at[core], parts[2]]
+    pieces, (weights, total) = rest[:number], rest[-2:]
+    outs = rest[-7:-2] if later else rest[-9:-4]
     block = 512
     rows, width = probs.shape[0], total.shape[2]
     half = rows // 2
     vocab_y = place[0]
     first_block = (vocab_y * SIDE + place[1]) * (probs.shape[1] // block)
-    core_0 = place[3] == 0
-    for owner in range(SIDE * SIDE):
-        seen[owner] = 0
-
-    def tile(slot, carry):
-        teacher = pairs[slot, 0] - first_block
-        owner = pairs[slot, 1] // SIDE
-        at = pl.ds(pl.multiple_of(slot * 64, 64), 64)
-        matrix, columns = [], []
-        for step in range(SIDE):
-            one, two = mine[step][at, :], other[step][at, :]
-            matrix += [jnp.where(core_0, one, two), jnp.where(core_0, two, one)]
+    total[...] = jnp.zeros_like(total)
+    starts = ((0, 0), (1, 0), (3, 0), (2, 0), (2, 512)) if number == 10 else ((0, 0), (1, 0), (2, 0), (3, 0))
+    for core, parts in ((place[3], pieces[: number // 2]), (1 - place[3], pieces[number // 2 :])):
+        for part, (step, start) in zip(parts, starts):
             x = lax.rem(place[2] + SIDE - step, SIDE)
-            columns.append(probs[:, pl.ds(pl.multiple_of(teacher * block + x * 128, 128), 128)])
-        product = jnp.dot(
-            jnp.concatenate(columns, axis=1), jnp.concatenate(matrix, axis=0), preferred_element_type=F32
-        )
-        fresh = seen[owner] == 0
-
-        @pl.when(fresh)
-        def _():
-            total[owner] = product
-
-        @pl.when(jnp.logical_not(fresh))
-        def _():
+            weights[x * 2 + core, start : start + part.shape[0]] = part[...]
+
+    def tiles(group, carry):
+        for member in range(4):
+            slot = group * 4 + member
+            teacher = pairs[slot, 0] - first_block
+            owner = pairs[slot, 1] // SIDE
+            columns = probs[:, pl.ds(pl.multiple_of(teacher * block, block), block)]
+            matrix = weights[:, pl.ds(pl.multiple_of(slot * 64, 64), 64), :].reshape(block, width)
+            product = jnp.dot(columns, matrix, preferred_element_type=F32)
+            if member:
+                product = jnp.where(slot < count[0], product, 0.0)
             total[owner] += product
-
-        seen[owner] = 1
         return carry
 
-    lax.fori_loop(0, count[0], tile, 0)
-    summed = total.at[SIDE * SIDE]
-    summed[...] = jnp.zeros(summed.shape, F32)
+    lax.fori_loop(0, (count[0] + 3) // 4, tiles, 0)
+    summed = jnp.zeros((rows, width), F32)
     for step in range(SIDE):
         start = lax.rem(vocab_y + step, SIDE) * SIDE
         for z in range(SIDE):
-            used = seen[start + z] == 1
-
-            def put(value):
-                if step == 2:
-                    outs[3][z * half : z * half + half, :] = value[:half]
-                    outs[4][z * half : z * half + half, :] = value[half:]
-                else:
-                    outs[step - step // 3][z * rows : z * rows + rows, :] = value
-
-            @pl.when(used)
-            def _():
-                value = total[start + z]
-                summed[...] += value
-                put(value.astype(BF16))
-
-            @pl.when(jnp.logical_not(used))
-            def _():
-                put(jnp.zeros((rows, width), BF16))
-
-    line = jnp.sum(summed[...].T, axis=0, keepdims=True)
+            value = total[start + z]
+            summed += value
+            value = value.astype(BF16)
+            if step == 2:
+                outs[3][z * half : z * half + half, :] = value[:half]
+                outs[4][z * half : z * half + half, :] = value[half:]
+            else:
+                outs[step - step // 3][z * rows : z * rows + rows, :] = value
+    line = jnp.sum(summed.T, axis=0, keepdims=True)
     if later:
         packed = pack_rows([line + before[0:1]])
     else:
         rest[-4][...] = jnp.broadcast_to(line, rest[-4].shape)
+        rest[-3][...] = probs[...]
         packed = pack_rows([before[i : i + 1] for i in range(4)])
     for out in outs[3:]:
         out[SIDE * half : SIDE * half + 16, :] = packed
@@ -212,18 +178,17 @@
     outs = [jax.ShapeDtypeStruct((SIDE * rows, width), BF16)] * 3
     outs += [jax.ShapeDtypeStruct((SIDE * rows // 2 + 16, width), BF16)] * 2
     if not later:
-        outs.append(jax.ShapeDtypeStruct((8, rows), F32))
+        outs += [jax.ShapeDtypeStruct((8, rows), F32), jax.ShapeDtypeStruct(probs.shape, BF16)]
     return pl.pallas_call(
         functools.partial(product_kernel, len(pieces), later),
         out_shape=outs,
         in_specs=[SMEM, SMEM, SMEM] + [VMEM] * (2 + len(pieces)) + [ANY] * len(behind),
         out_specs=[VMEM] * len(outs),
         scratch_shapes=[
-            pltpu.VMEM((2, depth if later else 16, width), BF16),
-            pltpu.VMEM((SIDE * SIDE + 1, rows, width), F32),
-            pltpu.SMEM((SIDE * SIDE,), jnp.int32),
+            pltpu.VMEM((2 * SIDE, depth, width), BF16),
+            pltpu.VMEM((SIDE * SIDE, rows, width), F32),
         ],
-        compiler_params=params(12),
+        compiler_params=params(14),
         cost_estimate=cost(
             16 * 2 * rows * 512 * width, 2 * probs.size + 16 * depth * width + 32 * rows * width
         ),
@@ -607,12 +572,13 @@
     before = jnp.stack([peak, mass, speak, smass] * 2)
 
     piece = sliced(tile_weights, 0)
-    mine = [piece, *gated(spread([piece] * SIDE, "tx")[1:], [mass, smass])]
+    probs = held(probs)
+    mine = [piece, *gated(spread([piece] * SIDE, "tx")[1:], [mass, smass, probs])]
     other = [swap(piece) for piece in mine]
 
     piece = sliced(tile_weights, 1, [mine[1]])
     right, left = send(piece, "tx", 1), send(piece, "tx", 3)
-    *parts, total = products(
+    *parts, total, probs = products(
         place, tile_pairs, tile_count, probs, before, mine, other, False, [piece]
     )
     top, low = halves(right, left, [parts[0]])

time: 158 us -> 147 us (0.930)
  waiting for transfers between devices: 50.7 us -> 43 us
  starting transfers between devices: 56.7 us -> 62.7 us
  Pallas kernels: 31 us -> 25.6 us
    ppermute x21, waiting for transfers between devices: 32.1 us -> 25.5 us  [send(): lax.ppermute(value, axis, [(i, (i + step) % SIDE) for i in range(SIDE)])]
    pallas_call x2, Pallas kernels: 11.6 us -> 6.26 us  [products(): pl.pallas_call(functools.partial(product_kernel, len(pieces), later), out...]
    ppermute x21, starting transfers between devices: 31.8 us -> 36.6 us  [send(): lax.ppermute(value, axis, [(i, (i + step) % SIDE) for i in range(SIDE)])]
    ppermute x11, starting transfers between devices: 15.9 us -> 17.6 us  [swap(): return lax.ppermute(value, 'tc', [(0, 1), (1, 0)])]
  transfers between devices with their start and end apart: 38 -> 38, of which waited for: 22 -> 19; matrix products, arithmetic and copies ran while one was open for 9% -> 8% of each run, Pallas kernels for 10% -> 9%
where the time goes in v10:
time: 147 us
  starting transfers between devices  62.7 us (43%)
  waiting for transfers between devices  43 us (29%)
  Pallas kernels  25.6 us (17%)
  matrix products  8.37 us (6%)
  other arithmetic  3.29 us (2%)
  local copies, waits for them, and re-layouts  2.46 us (2%)
  between operations  1.53 us (1%)
    ppermute x21, starting transfers between devices, send(): lax.ppermute(value, axis, [(i, (i + step) % SIDE) for i in range(SIDE)])  36.6 us
    ppermute x21, waiting for transfers between devices, send(): lax.ppermute(value, axis, [(i, (i + step) % SIDE) for i in range(SIDE)])  25.5 us
    ppermute x11, starting transfers between devices, swap(): return lax.ppermute(value, 'tc', [(0, 1), (1, 0)])  17.6 us
    ppermute x6, waiting for transfers between devices, crossed(): received.append(lax.ppermute(parts[step], ('vy', 'vz', 'tc'), pairs))  15.7 us
    ppermute x6, starting transfers between devices, crossed(): received.append(lax.ppermute(parts[step], ('vy', 'vz', 'tc'), pairs))  8.49 us
    dot_general x1, matrix products, shards(): jnp.dot(student_hidden, student_unembed, preferred_element_type=F32)  8.37 us
    pallas_call x2, Pallas kernels, products(): pl.pallas_call(functools.partial(product_kernel, len(pieces), later), out...  6.26 us
    pallas_call x1, Pallas kernels, staged(): pl.pallas_call(stage_kernel, out_shape=jax.ShapeDtypeStruct((depth // 2,...  4.06 us
  transfers between devices with their start and end apart: 38, of which 19 were waited for; matrix products, arithmetic and copies ran while one was open for 8% of the time, Pallas kernels for 9%

profile of v10, /device:TPU:1, one launch (start us, length us, event | category | flops | bytes accessed | tf_op | source)
XLA Modules:
  0.0 147.0 jit_solution(13312039523829183014)
XLA Ops:
  4.9 2.5 %collective-permute-start.1 = (bf16[1024,256]{1,0:T(8,128)(2,1)}, bf16[1024,256]{1,0:T(8,128)(2,1)}, u32[]{:S(2)}, u32[]{:S(2)}) collective-permute-start(bf16[1024,256]{1,0:T(8,128)(2,1)} %slice_weights.2.rest_0_), channel_id=1, source_target_pairs={{0,4},{2,6},{4,0},{6,2},{1,5},{3,7},{5,1},{7,3},{8,12},{10,14},{12... | collective-permute-start | bytes 1572872 | tf_op jit(solution)/shard_map/ppermute | solution.py:29
  12.0 8.4 %fusion.2 = (f32[256]{0:T(256)S(1)}, f32[256,2048]{1,0:T(8,128)S(1)}) fusion(bf16[256,4096]{1,0:T(8,128)(2,1)S(1)} %copy-done, bf16[4096,2048]{1,0:T(8,128)(2,1)} %unembed.1), kind=kOutput, calls=%fused_computation.4 | convolution fusion | flops 4295491584 | bytes 20972544 | tf_op jit(solution)/shard_map/dot_general | solution.py:568
  22.2 8.0 %collective-permute-done.1.refs_1_ = bf16[1024,256]{1,0:T(8,128)(2,1)} collective-permute-done((bf16[1024,256]{1,0:T(8,128)(2,1)}, bf16[1024,256]{1,0:T(8,128)(2,1)}, u32[]{:S(2)}, u32[]{:S(2)}) %collective-permute-start.1) | collective-permute-done | bytes 524320 | tf_op jit(solution)/shard_map/ppermute | solution.py:29
  36.0 3.6 %tile_products.2 = (bf16[1024,256]{1,0:T(8,128)(2,1)S(1)}, bf16[1024,256]{1,0:T(8,128)(2,1)S(1)}, bf16[1024,256]{1,0:T(8,128)(2,1)S(1)}, bf16[528,256]{1,0:T(8,1...) custom-call(s32[6]{0:T(128)S(1)} %stack.44.place, ...), custom_call_target="tpu_custom_call" | custom-call | flops 1073741824 | bytes 8388608 | tf_op jit(solution)/shard_map/tile_products/pallas_call | solution.py:182
  42.4 4.8 %collective-permute-done.7.right.refs_0_.rest_1_ = bf16[1024,256]{1,0:T(8,128)(2,1)} collective-permute-done((bf16[1024,256]{1,0:T(8,128)(2,1)S(1)}, bf16[1024,256]{1,0:T(8,128)(2,1)}, u32[]{:S(2)}, u32[]{:S(2)}) %collective-permute-start.7) | collective-permute-done | bytes 524320 | tf_op jit(solution)/shard_map/ppermute | solution.py:29
  50.8 2.4 %collective-permute-start.14 = (bf16[1024,256]{1,0:T(8,128)(2,1)S(1)}, bf16[1024,256]{1,0:T(8,128)(2,1)S(1)}, u32[]{:S(2)}, u32[]{:S(2)}) collective-permute-start(bf16[1024,256]{1,0:T(8,128)(2,1)S(1)} %get-tuple-element.62), channel_id=1, source_target_pairs={{0,96},{32,0},{64,32},{96,64},{1,97},{33,1},{65,33},{97,65},{2,98}... | collective-permute-start | bytes 1572872 | tf_op jit(solution)/shard_map/ppermute | solution.py:29
  55.9 2.9 %collective-permute-start.15 = (bf16[1024,256]{1,0:T(8,128)(2,1)S(1)}, bf16[1024,256]{1,0:T(8,128)(2,1)S(1)}, u32[]{:S(2)}, u32[]{:S(2)}) collective-permute-start(bf16[1024,256]{1,0:T(8,128)(2,1)S(1)} %slice_weights.3.rest_8_.rest_0_), channel_id=1, source_target_pairs={{0,1},{1,0},{2,3},{3,2},{4,5},{5,4},{6,7},{7,6},{8,9},{9,8},{10,11... | collective-permute-start | bytes 1572872 | tf_op jit(solution)/shard_map/ppermute | solution.py:33
  60.0 3.2 %collective-permute-start.16 = (bf16[1024,256]{1,0:T(8,128)(2,1)}, bf16[1024,256]{1,0:T(8,128)(2,1)S(1)}, u32[]{:S(2)}, u32[]{:S(2)}) collective-permute-start(bf16[1024,256]{1,0:T(8,128)(2,1)} %collective-permute-done.7.right.refs_0_.rest_1_), channel_id=1, source_target_pairs={{0,1},{1,0},{2,3},{3,2},{4,5},{5,4},{6,7},{7,6},{8,9},{9,8},{10,11... | collective-permute-start | bytes 1572872 | tf_op jit(solution)/shard_map/ppermute | solution.py:33
  66.9 2.7 %tile_products.3 = (bf16[1024,256]{1,0:T(8,128)(2,1)S(1)}, bf16[1024,256]{1,0:T(8,128)(2,1)S(1)}, bf16[1024,256]{1,0:T(8,128)(2,1)S(1)}, bf16[528,256]{1,0:T(8,128)(2,1)S(1)}, bf16[528,256]{1,0:T(8,128)(2,1)S(1)}) custom-call(s32[6]{0:T(128)S(1)} %stack.44.place, s32[16,2]{1,0:T(8,128)S(1)} %copy.14.pairs, s32[1]{0:T(128)S(6)} %copy.20.count, ...), custom_call_target="tpu_custom_call" | custom-call | flops 1073741824 | bytes 8388608 | tf_op jit(solution)/shard_map/tile_products/pallas_call | solution.py:182
  73.2 4.1 %stage_unembed.1.refs_1_.stage = bf16[2048,2048]{1,0:T(8,128)(2,1)S(1)} custom-call(s32[6]{0:T(128)S(1)} %stack.44.place, bf16[4096,2048]{1,0:T(8,128)(2,1)} %unembed.1, bf16[1024,256]{1,0:T(8,128)(2,1)S(1)} %get-tuple-element.65.refs_0_.refs_3_), custom_call_target="tpu_custom_call" | custom-call | bytes 8388608 | tf_op jit(solution)/shard_map/stage_unembed/pallas_call | solution.py:394
  77.3 2.4 %collective-permute-done.23.from_left = bf16[528,256]{1,0:T(8,128)(2,1)S(1)} collective-permute-done((bf16[528,256]{1,0:T(8,128)(2,1)S(1)}, bf16[528,256]{1,0:T(8,128)(2,1)S(1)}, u32[]{:S(2)}, u32[]{:S(2)}) %collective-permute-start.23) | collective-permute-done | bytes 270368 | tf_op jit(solution)/shard_map/ppermute | solution.py:29
  83.8 3.3 %collective-permute-start.20 = (bf16[272,256]{1,0:T(8,128)(2,1)S(1)}, bf16[272,256]{1,0:T(8,128)(2,1)S(1)}, u32[]{:S(2)}, u32[]{:S(2)}) collective-permute-start(bf16[272,256]{1,0:T(8,128)(2,1)S(1)} %get-tuple-element.68), channel_id=1, source_target_pairs={{0,8},{8,16},{16,24},{24,0},{1,9},{9,17},{17,25},{25,1},{2,10},{10... | collective-permute-start | bytes 417800 | tf_op jit(solution)/shard_map/ppermute | solution.py:29
  87.1 2.3 %collective-permute-start.21 = (bf16[272,256]{1,0:T(8,128)(2,1)S(1)}, bf16[272,256]{1,0:T(8,128)(2,1)S(1)}, u32[]{:S(2)}, u32[]{:S(2)}) collective-permute-start(bf16[272,256]{1,0:T(8,128)(2,1)S(1)} %get-tuple-element.69), channel_id=1, source_target_pairs={{0,16},{8,24},{16,0},{24,8},{1,17},{9,25},{17,1},{25,9},{2,18},{10... | collective-permute-start | bytes 417800 | tf_op jit(solution)/shard_map/ppermute | solution.py:29
  95.0 3.3 %collective-permute-start.27 = (bf16[272,256]{1,0:T(8,128)(2,1)S(1)}, bf16[272,256]{1,0:T(8,128)(2,1)S(1)}, u32[]{:S(2)}, u32[]{:S(2)}) collective-permute-start(bf16[272,256]{1,0:T(8,128)(2,1)S(1)} %get-tuple-element.82), channel_id=1, source_target_pairs={{0,8},{8,16},{16,24},{24,0},{1,9},{9,17},{17,25},{25,1},{2,10},{10... | collective-permute-start | bytes 417800 | tf_op jit(solution)/shard_map/ppermute | solution.py:29
  98.3 2.3 %collective-permute-start.28 = (bf16[272,256]{1,0:T(8,128)(2,1)S(1)}, bf16[272,256]{1,0:T(8,128)(2,1)S(1)}, u32[]{:S(2)}, u32[]{:S(2)}) collective-permute-start(bf16[272,256]{1,0:T(8,128)(2,1)S(1)} %get-tuple-element.83), channel_id=1, source_target_pairs={{0,16},{8,24},{16,0},{24,8},{1,17},{9,25},{17,1},{25,9},{2,18},{10... | collective-permute-start | bytes 417800 | tf_op jit(solution)/shard_map/ppermute | solution.py:29
  101.9 3.3 %collective-permute-done.28.refs_6_ = bf16[272,256]{1,0:T(8,128)(2,1)S(1)} collective-permute-done((bf16[272,256]{1,0:T(8,128)(2,1)S(1)}, bf16[272,256]{1,0:T(8,128)(2,1)S(1)}, u32[]{:S(2)}, u32[]{:S(2)}) %collective-permute-start.28) | collective-permute-done | bytes 139296 | tf_op jit(solution)/shard_map/ppermute | solution.py:29
  108.0 2.6 %collective-permute-start.30 = (bf16[2064,256]{1,0:T(8,128)(2,1)S(1)}, bf16[2064,256]{1,0:T(8,128)(2,1)S(1)}, u32[]{:S(2)}, u32[]{:S(2)}) collective-permute-start(bf16[2064,256]{1,0:T(8,128)(2,1)S(1)} %logit_grad.1.mine), channel_id=1, source_target_pairs={{0,1},{1,0},{2,3},{3,2},{4,5},{5,4},{6,7},{7,6},{8,9},{9,8},{10,11... | collective-permute-start | bytes 3170312 | tf_op jit(solution)/shard_map/ppermute | solution.py:33
  110.6 2.3 %own_hidden.1.own = bf16[2048,256]{1,0:T(8,128)(2,1)S(1)} custom-call(bf16[2048,2048]{1,0:T(8,128)(2,1)S(1)} %stage_unembed.1.refs_1_.stage, bf16[2064,256]{1,0:T(8,128)(2,1)S(1)} %logit_grad.1.mine), custom_call_target="tpu_custom_call" | custom-call | flops 2147483648 | bytes 8388608 | tf_op jit(solution)/shard_map/own_hidden/pallas_call | solution.py:416
  112.9 3.0 %other_hidden.1 = (bf16[528,512]{1,0:T(8,128)(2,1)S(1)}, bf16[528,512]{1,0:T(8,128)(2,1)S(1)}, bf16[528,512]{1,0:T(8,128)(2,1)S(1)}, bf16[528,512]{1,0:T(8,128)(2,1)S(1)}) custom-call(s32[6]{0:T(128)S(1)} %stack.44.place, bf16[2048,2048]{1,0:T(8,128)(2,1)S(1)} %stage_unembed.1.refs_1_.stage, bf16[2064,256]{1,0:T(8,128)(2,1)S(1)} %logit_grad.1.mine, ...), custom_call_target="tpu_custom_call" | custom-call | flops 2147483648 | bytes 8388608 | tf_op jit(solution)/shard_map/other_hidden/pallas_call | solution.py:444
  117.2 2.6 %collective-permute-start.32 = (bf16[528,512]{1,0:T(8,128)(2,1)S(1)}, bf16[528,512]{1,0:T(8,128)(2,1)S(1)}, u32[]{:S(2)}, u32[]{:S(2)}) collective-permute-start(bf16[528,512]{1,0:T(8,128)(2,1)S(1)} %get-tuple-element.87), channel_id=1, source_target_pairs={{0,64},{1,17},{8,72},{9,25},{16,80},{17,1},{24,88},{25,9},{32,96},... | collective-permute-start | bytes 1622024 | tf_op jit(solution)/shard_map/ppermute | solution.py:553
  120.5 5.4 %collective-permute-done.31.refs_1_ = bf16[528,512]{1,0:T(8,128)(2,1)S(1)} collective-permute-done((bf16[528,512]{1,0:T(8,128)(2,1)S(1)}, bf16[528,512]{1,0:T(8,128)(2,1)S(1)}, u32[]{:S(2)}, u32[]{:S(2)}) %collective-permute-start.31) | collective-permute-done | bytes 540704 | tf_op jit(solution)/shard_map/ppermute | solution.py:553
  125.9 6.7 %collective-permute-done.32.refs_2_ = bf16[528,512]{1,0:T(8,128)(2,1)S(1)} collective-permute-done((bf16[528,512]{1,0:T(8,128)(2,1)S(1)}, bf16[528,512]{1,0:T(8,128)(2,1)S(1)}, u32[]{:S(2)}, u32[]{:S(2)}) %collective-permute-start.32) | collective-permute-done | bytes 540704 | tf_op jit(solution)/shard_map/ppermute | solution.py:553
  133.6 3.3 %collective-permute-start.35 = (bf16[144,512]{1,0:T(8,128)(2,1)S(1)}, bf16[144,512]{1,0:T(8,128)(2,1)S(1)}, u32[]{:S(2)}, u32[]{:S(2)}) collective-permute-start(bf16[144,512]{1,0:T(8,128)(2,1)S(1)} %get-tuple-element.91), channel_id=1, source_target_pairs={{0,16},{1,65},{8,24},{9,73},{16,0},{17,81},{24,8},{25,89},{32,48},... | collective-permute-start | bytes 442376 | tf_op jit(solution)/shard_map/ppermute | solution.py:553
  141.7 3.1 %collective-permute-start.37 = (bf16[128,256]{1,0:T(8,128)(2,1)S(1)}, bf16[128,256]{1,0:T(8,128)(2,1)S(1)}, u32[]{:S(2)}, u32[]{:S(2)}) collective-permute-start(bf16[128,256]{1,0:T(8,128)(2,1)S(1)} %get-tuple-element.94), channel_id=1, source_target_pairs={{0,1},{1,0},{2,3},{3,2},{4,5},{5,4},{6,7},{7,6},{8,9},{9,8},{10,11... | collective-permute-start | bytes 196616 | tf_op jit(solution)/shard_map/ppermute | solution.py:33
  (96 shorter events, 56.9 us)
Async XLA Ops:
  2.9 19.3 %collective-permute-start = (bf16[1024,256]{1,0:T(8,128)(2,1)}, bf16[1024,256]{1,0:T(8,128)(2,1)S(1)}, u32[]{:S(2)}, u32[]{:S(2)}) collective-permute-start(bf16[1024,256]{1,0:T(8,128)(2,1)} %slice_weights.2.rest_0_), channel_id=1, source_target_pairs={{0,2},{2,4},{4,6},{6,0},{1,3},{3,5},{5,7},{7,1},{8,10},{10,12},{12... | collective-permute-start | bytes 1572872 | tf_op jit(solution)/shard_map/ppermute | solution.py:29
  4.9 25.3 %collective-permute-start.1 = (bf16[1024,256]{1,0:T(8,128)(2,1)}, bf16[1024,256]{1,0:T(8,128)(2,1)}, u32[]{:S(2)}, u32[]{:S(2)}) collective-permute-start(bf16[1024,256]{1,0:T(8,128)(2,1)} %slice_weights.2.rest_0_), channel_id=1, source_target_pairs={{0,4},{2,6},{4,0},{6,2},{1,5},{3,7},{5,1},{7,3},{8,12},{10,14},{12... | collective-permute-start | bytes 1572872 | tf_op jit(solution)/shard_map/ppermute | solution.py:29
  7.4 22.9 %collective-permute-start.2 = (bf16[1024,256]{1,0:T(8,128)(2,1)}, bf16[1024,256]{1,0:T(8,128)(2,1)}, u32[]{:S(2)}, u32[]{:S(2)}) collective-permute-start(bf16[1024,256]{1,0:T(8,128)(2,1)} %slice_weights.2.rest_0_), channel_id=1, source_target_pairs={{0,6},{2,0},{4,2},{6,4},{1,7},{3,1},{5,3},{7,5},{8,14},{10,8},{12,... | collective-permute-start | bytes 1572872 | tf_op jit(solution)/shard_map/ppermute | solution.py:29
  8.5 24.8 %collective-permute-start.3 = (bf16[1024,256]{1,0:T(8,128)(2,1)}, bf16[1024,256]{1,0:T(8,128)(2,1)}, u32[]{:S(2)}, u32[]{:S(2)}) collective-permute-start(bf16[1024,256]{1,0:T(8,128)(2,1)} %slice_weights.2.rest_0_), channel_id=1, source_target_pairs={{0,1},{1,0},{2,3},{3,2},{4,5},{5,4},{6,7},{7,6},{8,9},{9,8},{10,11... | collective-permute-start | bytes 1572872 | tf_op jit(solution)/shard_map/ppermute | solution.py:33
  32.3 14.9 %collective-permute-start.7 = (bf16[1024,256]{1,0:T(8,128)(2,1)S(1)}, bf16[1024,256]{1,0:T(8,128)(2,1)}, u32[]{:S(2)}, u32[]{:S(2)}) collective-permute-start(bf16[1024,256]{1,0:T(8,128)(2,1)S(1)} %slice_weights.3.rest_8_.rest_0_), channel_id=1, source_target_pairs={{0,2},{2,4},{4,6},{6,0},{1,3},{3,5},{5,7},{7,1},{8,10},{10,12},{12... | collective-permute-start | bytes 1572872 | tf_op jit(solution)/shard_map/ppermute | solution.py:29
  33.3 13.9 %collective-permute-start.8 = (bf16[1024,256]{1,0:T(8,128)(2,1)S(1)}, bf16[1024,256]{1,0:T(8,128)(2,1)}, u32[]{:S(2)}, u32[]{:S(2)}) collective-permute-start(bf16[1024,256]{1,0:T(8,128)(2,1)S(1)} %slice_weights.3.rest_8_.rest_0_), channel_id=1, source_target_pairs={{0,6},{2,0},{4,2},{6,4},{1,7},{3,1},{5,3},{7,5},{8,14},{10,8},{12,... | collective-permute-start | bytes 1572872 | tf_op jit(solution)/shard_map/ppermute | solution.py:29
  39.5 8.8 %collective-permute-start.11 = (bf16[528,256]{1,0:T(8,128)(2,1)S(1)}, bf16[528,256]{1,0:T(8,128)(2,1)S(1)}, u32[]{:S(2)}, u32[]{:S(2)}) collective-permute-start(bf16[528,256]{1,0:T(8,128)(2,1)S(1)} %get-tuple-element.59.mine), channel_id=1, source_target_pairs={{0,32},{32,64},{64,96},{96,0},{1,33},{33,65},{65,97},{97,1},{2,34}... | collective-permute-start | bytes 811016 | tf_op jit(solution)/shard_map/ppermute | solution.py:29
  41.9 7.1 %collective-permute-start.12 = (bf16[528,256]{1,0:T(8,128)(2,1)S(1)}, bf16[528,256]{1,0:T(8,128)(2,1)S(1)}, u32[]{:S(2)}, u32[]{:S(2)}) collective-permute-start(bf16[528,256]{1,0:T(8,128)(2,1)S(1)} %get-tuple-element.60), channel_id=1, source_target_pairs={{0,96},{32,0},{64,32},{96,64},{1,97},{33,1},{65,33},{97,65},{2,98}... | collective-permute-start | bytes 811016 | tf_op jit(solution)/shard_map/ppermute | solution.py:29
  49.4 13.9 %collective-permute-start.13 = (bf16[1040,256]{1,0:T(8,128)(2,1)S(1)}, bf16[1040,256]{1,0:T(8,128)(2,1)S(1)}, u32[]{:S(2)}, u32[]{:S(2)}) collective-permute-start(bf16[1040,256]{1,0:T(8,128)(2,1)S(1)} %get-tuple-element.61), channel_id=1, source_target_pairs={{0,32},{32,64},{64,96},{96,0},{1,33},{33,65},{65,97},{97,1},{2,34}... | collective-permute-start | bytes 1597448 | tf_op jit(solution)/shard_map/ppermute | solution.py:29
  50.8 12.4 %collective-permute-start.14 = (bf16[1024,256]{1,0:T(8,128)(2,1)S(1)}, bf16[1024,256]{1,0:T(8,128)(2,1)S(1)}, u32[]{:S(2)}, u32[]{:S(2)}) collective-permute-start(bf16[1024,256]{1,0:T(8,128)(2,1)S(1)} %get-tuple-element.62), channel_id=1, source_target_pairs={{0,96},{32,0},{64,32},{96,64},{1,97},{33,1},{65,33},{97,65},{2,98}... | collective-permute-start | bytes 1572872 | tf_op jit(solution)/shard_map/ppermute | solution.py:29
  53.8 9.4 %collective-permute-start.10 = (bf16[512,256]{1,0:T(8,128)(2,1)S(1)}, bf16[512,256]{1,0:T(8,128)(2,1)S(1)}, u32[]{:S(2)}, u32[]{:S(2)}) collective-permute-start(bf16[512,256]{1,0:T(8,128)(2,1)S(1)} %get-tuple-element.56), channel_id=1, source_target_pairs={{0,6},{2,0},{4,2},{6,4},{1,7},{3,1},{5,3},{7,5},{8,14},{10,8},{12,... | collective-permute-start | bytes 786440 | tf_op jit(solution)/shard_map/ppermute | solution.py:29
  55.9 9.5 %collective-permute-start.15 = (bf16[1024,256]{1,0:T(8,128)(2,1)S(1)}, bf16[1024,256]{1,0:T(8,128)(2,1)S(1)}, u32[]{:S(2)}, u32[]{:S(2)}) collective-permute-start(bf16[1024,256]{1,0:T(8,128)(2,1)S(1)} %slice_weights.3.rest_8_.rest_0_), channel_id=1, source_target_pairs={{0,1},{1,0},{2,3},{3,2},{4,5},{5,4},{6,7},{7,6},{8,9},{9,8},{10,11... | collective-permute-start | bytes 1572872 | tf_op jit(solution)/shard_map/ppermute | solution.py:33
  69.6 10.0 %collective-permute-start.23 = (bf16[528,256]{1,0:T(8,128)(2,1)S(1)}, bf16[528,256]{1,0:T(8,128)(2,1)S(1)}, u32[]{:S(2)}, u32[]{:S(2)}) collective-permute-start(bf16[528,256]{1,0:T(8,128)(2,1)S(1)} %get-tuple-element.73.mine), channel_id=1, source_target_pairs={{0,32},{32,64},{64,96},{96,0},{1,33},{33,65},{65,97},{97,1},{2,34}... | collective-permute-start | bytes 811016 | tf_op jit(solution)/shard_map/ppermute | solution.py:29
  71.5 8.1 %collective-permute-start.24 = (bf16[528,256]{1,0:T(8,128)(2,1)S(1)}, bf16[528,256]{1,0:T(8,128)(2,1)S(1)}, u32[]{:S(2)}, u32[]{:S(2)}) collective-permute-start(bf16[528,256]{1,0:T(8,128)(2,1)S(1)} %get-tuple-element.74), channel_id=1, source_target_pairs={{0,96},{32,0},{64,32},{96,64},{1,97},{33,1},{65,33},{97,65},{2,98}... | collective-permute-start | bytes 811016 | tf_op jit(solution)/shard_map/ppermute | solution.py:29
  80.0 14.0 %collective-permute-start.25 = (bf16[1040,256]{1,0:T(8,128)(2,1)S(1)}, bf16[1040,256]{1,0:T(8,128)(2,1)S(1)}, u32[]{:S(2)}, u32[]{:S(2)}) collective-permute-start(bf16[1040,256]{1,0:T(8,128)(2,1)S(1)} %get-tuple-element.77), channel_id=1, source_target_pairs={{0,32},{32,64},{64,96},{96,0},{1,33},{33,65},{65,97},{97,1},{2,34}... | collective-permute-start | bytes 1597448 | tf_op jit(solution)/shard_map/ppermute | solution.py:29
  80.6 12.2 %collective-permute-start.26 = (bf16[1024,256]{1,0:T(8,128)(2,1)S(1)}, bf16[1024,256]{1,0:T(8,128)(2,1)S(1)}, u32[]{:S(2)}, u32[]{:S(2)}) collective-permute-start(bf16[1024,256]{1,0:T(8,128)(2,1)S(1)} %get-tuple-element.78), channel_id=1, source_target_pairs={{0,96},{32,0},{64,32},{96,64},{1,97},{33,1},{65,33},{97,65},{2,98}... | collective-permute-start | bytes 1572872 | tf_op jit(solution)/shard_map/ppermute | solution.py:29
  83.8 16.8 %collective-permute-start.20 = (bf16[272,256]{1,0:T(8,128)(2,1)S(1)}, bf16[272,256]{1,0:T(8,128)(2,1)S(1)}, u32[]{:S(2)}, u32[]{:S(2)}) collective-permute-start(bf16[272,256]{1,0:T(8,128)(2,1)S(1)} %get-tuple-element.68), channel_id=1, source_target_pairs={{0,8},{8,16},{16,24},{24,0},{1,9},{9,17},{17,25},{25,1},{2,10},{10... | collective-permute-start | bytes 417800 | tf_op jit(solution)/shard_map/ppermute | solution.py:29
  87.1 14.4 %collective-permute-start.21 = (bf16[272,256]{1,0:T(8,128)(2,1)S(1)}, bf16[272,256]{1,0:T(8,128)(2,1)S(1)}, u32[]{:S(2)}, u32[]{:S(2)}) collective-permute-start(bf16[272,256]{1,0:T(8,128)(2,1)S(1)} %get-tuple-element.69), channel_id=1, source_target_pairs={{0,16},{8,24},{16,0},{24,8},{1,17},{9,25},{17,1},{25,9},{2,18},{10... | collective-permute-start | bytes 417800 | tf_op jit(solution)/shard_map/ppermute | solution.py:29
  89.5 12.1 %collective-permute-start.22 = (bf16[272,256]{1,0:T(8,128)(2,1)S(1)}, bf16[272,256]{1,0:T(8,128)(2,1)S(1)}, u32[]{:S(2)}, u32[]{:S(2)}) collective-permute-start(bf16[272,256]{1,0:T(8,128)(2,1)S(1)} %get-tuple-element.70), channel_id=1, source_target_pairs={{0,24},{8,0},{16,8},{24,16},{1,25},{9,1},{17,9},{25,17},{2,26},{10... | collective-permute-start | bytes 417800 | tf_op jit(solution)/shard_map/ppermute | solution.py:29
  98.3 6.9 %collective-permute-start.28 = (bf16[272,256]{1,0:T(8,128)(2,1)S(1)}, bf16[272,256]{1,0:T(8,128)(2,1)S(1)}, u32[]{:S(2)}, u32[]{:S(2)}) collective-permute-start(bf16[272,256]{1,0:T(8,128)(2,1)S(1)} %get-tuple-element.83), channel_id=1, source_target_pairs={{0,16},{8,24},{16,0},{24,8},{1,17},{9,25},{17,1},{25,9},{2,18},{10... | collective-permute-start | bytes 417800 | tf_op jit(solution)/shard_map/ppermute | solution.py:29
  115.9 10.0 %collective-permute-start.31 = (bf16[528,512]{1,0:T(8,128)(2,1)S(1)}, bf16[528,512]{1,0:T(8,128)(2,1)S(1)}, u32[]{:S(2)}, u32[]{:S(2)}) collective-permute-start(bf16[528,512]{1,0:T(8,128)(2,1)S(1)} %get-tuple-element.86), channel_id=1, source_target_pairs={{0,32},{1,9},{8,40},{9,17},{16,48},{17,25},{24,56},{25,1},{32,64},... | collective-permute-start | bytes 1622024 | tf_op jit(solution)/shard_map/ppermute | solution.py:553
  117.2 15.4 %collective-permute-start.32 = (bf16[528,512]{1,0:T(8,128)(2,1)S(1)}, bf16[528,512]{1,0:T(8,128)(2,1)S(1)}, u32[]{:S(2)}, u32[]{:S(2)}) collective-permute-start(bf16[528,512]{1,0:T(8,128)(2,1)S(1)} %get-tuple-element.87), channel_id=1, source_target_pairs={{0,64},{1,17},{8,72},{9,25},{16,80},{17,1},{24,88},{25,9},{32,96},... | collective-permute-start | bytes 1622024 | tf_op jit(solution)/shard_map/ppermute | solution.py:553
  119.8 12.8 %collective-permute-start.33 = (bf16[528,512]{1,0:T(8,128)(2,1)S(1)}, bf16[528,512]{1,0:T(8,128)(2,1)S(1)}, u32[]{:S(2)}, u32[]{:S(2)}) collective-permute-start(bf16[528,512]{1,0:T(8,128)(2,1)S(1)} %get-tuple-element.88), channel_id=1, source_target_pairs={{0,96},{1,25},{8,104},{9,1},{16,112},{17,9},{24,120},{25,17},{32,0... | collective-permute-start | bytes 1622024 | tf_op jit(solution)/shard_map/ppermute | solution.py:553
  133.6 7.4 %collective-permute-start.35 = (bf16[144,512]{1,0:T(8,128)(2,1)S(1)}, bf16[144,512]{1,0:T(8,128)(2,1)S(1)}, u32[]{:S(2)}, u32[]{:S(2)}) collective-permute-start(bf16[144,512]{1,0:T(8,128)(2,1)S(1)} %get-tuple-element.91), channel_id=1, source_target_pairs={{0,16},{1,65},{8,24},{9,73},{16,0},{17,81},{24,8},{25,89},{32,48},... | collective-permute-start | bytes 442376 | tf_op jit(solution)/shard_map/ppermute | solution.py:553
  (22 other events, 161.2 us)

commit v11 on v10

--- a/solution.py
+++ b/solution.py
@@ -424,64 +424,96 @@
     )(stage, mine)
 
 
-def other_kernel(steps, place, stage, mine, other, own, *refs):
-    outs = refs[-len(steps) :]
+def other_kernel(far_only, place, stage, mine, other, own, *refs):
     depth = stage.shape[1]
     rows = mine.shape[1]
     lanes = pl.ds(pl.multiple_of(place[3] * rows, rows), rows)
     other_lanes = pl.ds(pl.multiple_of((1 - place[3]) * rows, rows), rows)
-    for out, step in zip(outs, steps):
+    for index, step in enumerate((2,) if far_only else (0, 1, 3)):
         at = pl.ds(pl.multiple_of(lax.rem(place[4] + step, SIDE) * 512, 512), 512)
-        result = jnp.dot(stage[at, :], other[0:depth, :], preferred_element_type=F32)
-        out[0:512, other_lanes] = result.astype(BF16)
-        out[0:512, lanes] = own[at, :]
-        out[512:528, lanes] = mine[depth : depth + 16, :]
-        out[512:528, other_lanes] = other[depth : depth + 16, :]
-
-
-def other_hidden(steps, place, stage, mine, other, own, behind=()):
+        result = jnp.dot(stage[at, :], other[0:depth, :], preferred_element_type=F32).astype(BF16)
+        if far_only:
+            for half, out in enumerate(refs[-2:]):
+                out[0:256, other_lanes] = result[half * 256 : half * 256 + 256]
+                out[256:272, lanes] = mine[depth : depth + 16, :]
+                out[256:272, other_lanes] = other[depth : depth + 16, :]
+                at = pl.multiple_of(lax.rem(place[4] + step, SIDE) * 512 + half * 256, 256)
+                out[0:256, lanes] = own[pl.ds(at, 256), :]
+        else:
+            out = refs[index - 3]
+            out[:, other_lanes] = result
+            out[:, lanes] = own[at, :]
+
+
+def other_hidden(far_only, place, stage, mine, other, own, behind=()):
     rows = mine.shape[1]
-    return pl.pallas_call(
-        functools.partial(other_kernel, steps),
-        out_shape=[jax.ShapeDtypeStruct((528, 2 * rows), BF16)] * len(steps),
+    shapes = [(272, 2 * rows)] * 2 if far_only else [(512, 2 * rows)] * 3
+    return pl.pallas_call(
+        functools.partial(other_kernel, far_only),
+        out_shape=[jax.ShapeDtypeStruct(shape, BF16) for shape in shapes],
         in_specs=[SMEM] + [VMEM] * 4 + [ANY] * len(behind),
-        out_specs=[VMEM] * len(steps),
-        compiler_params=params(),
-        cost_estimate=cost(len(steps) * stage.size * rows // 2, 2 * stage.size),
+        out_specs=[VMEM] * len(shapes),
+        compiler_params=params(),
+        cost_estimate=cost((1 if far_only else 3) * stage.size * rows // 2, 2 * stage.size),
         name="other_hidden",
     )(place, stage, mine, other, own, *behind)
 
 
-def packed_loss(index, parts, at, ordered):
-    for step in range(SIDE):
-        ordered[lax.rem(index + SIDE - step, SIDE)] = unpack_rows(parts[step][at : at + 16, :], 1)[0]
+def pass_kernel(near, far, from_left, from_right, near_out, far_out):
+    near_out[0:256, :] = (near[0:256, :].astype(F32) + from_left[0:256, :].astype(F32)).astype(BF16)
+    near_out[256:512, :] = near[256:512, :]
+    near_out[512:528, :] = from_left[256:272, :]
+    far_out[0:256, :] = far[0:256, :]
+    far_out[256:512, :] = (far[256:512, :].astype(F32) + from_right[0:256, :].astype(F32)).astype(BF16)
+
+
+def passed(near, far, from_left, from_right):
+    rows = near.shape[1]
+    return pl.pallas_call(
+        pass_kernel,
+        out_shape=[jax.ShapeDtypeStruct((528, rows), BF16), jax.ShapeDtypeStruct((512, rows), BF16)],
+        in_specs=[VMEM] * 4,
+        out_specs=[VMEM] * 2,
+        compiler_params=params(),
+        cost_estimate=cost(512 * rows, 10 * 512 * rows),
+        name="pass_grads",
+    )(near, far, from_left, from_right)
+
+
+def ordered_loss(index, pieces, ordered):
+    for step, piece in pieces:
+        ordered[lax.rem(index + step, SIDE)] = unpack_rows(piece, 1)[0]
     return ((ordered[0] + ordered[1]) + ordered[2]) + ordered[3]
 
 
-def middle_kernel(place, *refs):
-    parts, outs, ordered = refs[:SIDE], refs[SIDE : 2 * SIDE], refs[2 * SIDE]
-    packed = pack_rows([packed_loss(place[4], parts, 512, ordered)])
+def middle_kernel(place, own, left, right, mine, from_left, from_right, *refs):
+    outs, ordered = refs[:SIDE], refs[SIDE]
+    pieces = [
+        (0, mine[256:272, :]),
+        (3, from_left[256:272, :]),
+        (1, from_right[256:272, :]),
+        (2, left[512:528, :]),
+    ]
+    packed = pack_rows([ordered_loss(place[4], pieces, ordered)])
     for step in range(SIDE):
         at = pl.ds(pl.multiple_of(lax.rem(place[5] + step, SIDE) * 128, 128), 128)
-        value = parts[0][at, :].astype(F32)
-        for part in parts[1:]:
-            value += part[at, :].astype(F32)
+        value = own[at, :].astype(F32) + left[at, :].astype(F32) + right[at, :].astype(F32)
         outs[step][0:128, :] = value.astype(BF16)
         outs[step][128:144, :] = packed
 
 
-def middle(place, parts):
-    rows = parts[0].shape[1]
+def middle(place, own, left, right, mine, from_left, from_right):
+    rows = own.shape[1]
     return pl.pallas_call(
         middle_kernel,
         out_shape=[jax.ShapeDtypeStruct((144, rows), BF16)] * SIDE,
-        in_specs=[SMEM] + [VMEM] * SIDE,
+        in_specs=[SMEM] + [VMEM] * 6,
         out_specs=[VMEM] * SIDE,
         scratch_shapes=[pltpu.VMEM((SIDE, 1, rows), F32)],
         compiler_params=params(),
         cost_estimate=cost(4 * 512 * rows, 10 * 512 * rows),
         name="merge_grads",
-    )(place, *parts)
+    )(place, own, left, right, mine, from_left, from_right)
 
 
 def total_kernel(place, *refs):
@@ -490,7 +522,8 @@
     rows = keep.shape[1]
     mine = pl.ds(pl.multiple_of(place[3] * rows, rows), rows)
     other = pl.ds(pl.multiple_of((1 - place[3]) * rows, rows), rows)
-    ordered[4] = packed_loss(place[5], parts, 128, ordered)
+    pieces = [((SIDE - step) % SIDE, part[128:144, :]) for step, part in enumerate(parts)]
+    ordered[4] = ordered_loss(place[5], pieces, ordered)
     loss[...] = jnp.broadcast_to(ordered[4, :, mine], loss.shape)
     for lanes, out in ((other, give), (mine, keep)):
         value = parts[0][0:128, lanes].astype(F32)
@@ -538,8 +571,8 @@
     return [parts[0]] + [send(parts[step], axis, step) for step in (1, 2, 3)]
 
 
-def crossed(parts, first):
-    def target(y, z, core, step):
+def cross(value, step, first):
+    def target(y, z, core):
         if (core == 0) == first:
             y = (y + step) % SIDE
         else:
@@ -547,11 +580,8 @@
         return (y * SIDE + z) * 2 + core
 
     places = [(y, z, core) for y in range(SIDE) for z in range(SIDE) for core in range(2)]
-    received = [parts[0]]
-    for step in (1, 2, 3):
-        pairs = [(i, target(*at, step)) for i, at in enumerate(places)]
-        received.append(lax.ppermute(parts[step], ("vy", "vz", "tc"), pairs))
-    return received
+    pairs = [(i, target(*at)) for i, at in enumerate(places)]
+    return lax.ppermute(value, ("vy", "vz", "tc"), pairs)
 
 
 def shards(teacher_logits, student_hidden, student_unembed, tile_weights, tile_pairs, tile_count):
@@ -571,7 +601,7 @@
 
     before = jnp.stack([peak, mass, speak, smass] * 2)
 
-    piece = sliced(tile_weights, 0)
+    piece = tile_weights[:, :, : tile_weights.shape[2] // 2].reshape(-1, tile_weights.shape[2] // 2)
     probs = held(probs)
     mine = [piece, *gated(spread([piece] * SIDE, "tx")[1:], [mass, smass, probs])]
     other = [swap(piece) for piece in mine]
@@ -604,9 +634,14 @@
 
     own = own_hidden(stage, mine)
     other = swap(mine)
-    parts = other_hidden(range(SIDE), place, stage, mine, other, own)
-    parts = middle(place, crossed(parts, True))
-    keep, give, loss = totals(place, crossed(parts, False))
+    to_right, to_left = other_hidden(True, place, stage, mine, other, own)
+    from_left, from_right = cross(to_right, 1, True), cross(to_left, 3, True)
+    here, near, far = other_hidden(False, place, stage, mine, other, own, [to_right])
+    near, far = passed(near, far, from_left, from_right)
+    near, far = cross(near, 1, True), cross(far, 3, True)
+    parts = middle(place, here, near, far, to_right, from_left, from_right)
+    parts = [parts[0], *(cross(parts[step], step, False) for step in (1, 2, 3))]
+    keep, give, loss = totals(place, parts)
     return turned(place, keep, swap(give)), loss[0]
 
 

time: 147 us -> 147 us (level)
  waiting for transfers between devices: 43 us -> 39.9 us
  starting transfers between devices: 62.7 us -> 65.6 us
    ppermute x6 -> x7, waiting for transfers between devices: 15.7 us -> 13.1 us  [cross(): return lax.ppermute(value, ('vy', 'vz', 'tc'), pairs)]
    slice x0 -> x1, local copies, waits for them, and re-layouts: none -> 2.04 us  [shards(): tile_weights[:, :, :tile_weights.shape[2] // 2]]
    ppermute x21, starting transfers between devices: 36.6 us -> 38.4 us  [send(): lax.ppermute(value, axis, [(i, (i + step) % SIDE) for i in range(SIDE)])]
    pallas_call x1 -> x3, Pallas kernels: 3 us -> 3.8 us  [the longest x2 3.65 us: other_hidden(): pl.pallas_call(functools.partial(other_kernel, far_only), out_shape=[jax....]
    ppermute x6 -> x7, starting transfers between devices: 8.49 us -> 9.12 us  [cross(): return lax.ppermute(value, ('vy', 'vz', 'tc'), pairs)]
  transfers between devices with their start and end apart: 38 -> 39, of which waited for: 19 -> 20; matrix products, arithmetic and copies ran while one was open for 8% -> 8% of each run, Pallas kernels for 9% -> 11%
where the time goes in v11:
time: 147 us
  starting transfers between devices  65.6 us (45%)
  waiting for transfers between devices  39.9 us (27%)
  Pallas kernels  25.5 us (17%)
  matrix products  8.37 us (6%)
  other arithmetic  3.29 us (2%)
  local copies, waits for them, and re-layouts  3.13 us (2%)
  between operations  1.55 us (1%)
    ppermute x21, starting transfers between devices, send(): lax.ppermute(value, axis, [(i, (i + step) % SIDE) for i in range(SIDE)])  38.4 us
    ppermute x21, waiting for transfers between devices, send(): lax.ppermute(value, axis, [(i, (i + step) % SIDE) for i in range(SIDE)])  25 us
    ppermute x11, starting transfers between devices, swap(): return lax.ppermute(value, 'tc', [(0, 1), (1, 0)])  18.1 us
    ppermute x7, waiting for transfers between devices, cross(): return lax.ppermute(value, ('vy', 'vz', 'tc'), pairs)  13.1 us
    ppermute x7, starting transfers between devices, cross(): return lax.ppermute(value, ('vy', 'vz', 'tc'), pairs)  9.12 us
    dot_general x1, matrix products, shards(): jnp.dot(student_hidden, student_unembed, preferred_element_type=F32)  8.37 us
    pallas_call x2, Pallas kernels, products(): pl.pallas_call(functools.partial(product_kernel, len(pieces), later), out...  6.28 us
    pallas_call x1, Pallas kernels, staged(): pl.pallas_call(stage_kernel, out_shape=jax.ShapeDtypeStruct((depth // 2,...  4.06 us
  transfers between devices with their start and end apart: 39, of which 20 were waited for; matrix products, arithmetic and copies ran while one was open for 8% of the time, Pallas kernels for 11%

profile of v11, /device:TPU:1, one launch (start us, length us, event | category | flops | bytes accessed | tf_op | source)
XLA Modules:
  0.0 147.3 jit_solution(2621373040231898820)
XLA Ops:
  4.7 2.5 %collective-permute-start.1 = (bf16[1024,256]{1,0:T(8,128)(2,1)}, bf16[1024,256]{1,0:T(8,128)(2,1)}, u32[]{:S(2)}, u32[]{:S(2)}) collective-permute-start(bf16[1024,256]{1,0:T(8,128)(2,1)} %bitcast.10.rest_0_), channel_id=1, source_target_pairs={{0,4},{2,6},{4,0},{6,2},{1,5},{3,7},{5,1},{7,3},{8,12},{10,14},{12... | collective-permute-start | bytes 1572872 | tf_op jit(solution)/shard_map/ppermute | solution.py:29
  11.8 8.4 %fusion.2 = (f32[256]{0:T(256)S(1)}, f32[256,2048]{1,0:T(8,128)S(1)}) fusion(bf16[256,4096]{1,0:T(8,128)(2,1)S(1)} %copy-done, bf16[4096,2048]{1,0:T(8,128)(2,1)} %unembed.1), kind=kOutput, calls=%fused_computation.4 | convolution fusion | flops 4295491584 | bytes 20972544 | tf_op jit(solution)/shard_map/dot_general | solution.py:598
  22.0 8.0 %collective-permute-done.1.refs_1_ = bf16[1024,256]{1,0:T(8,128)(2,1)} collective-permute-done((bf16[1024,256]{1,0:T(8,128)(2,1)}, bf16[1024,256]{1,0:T(8,128)(2,1)}, u32[]{:S(2)}, u32[]{:S(2)}) %collective-permute-start.1) | collective-permute-done | bytes 524320 | tf_op jit(solution)/shard_map/ppermute | solution.py:29
  35.8 3.6 %tile_products.2 = (bf16[1024,256]{1,0:T(8,128)(2,1)S(1)}, bf16[1024,256]{1,0:T(8,128)(2,1)S(1)}, bf16[1024,256]{1,0:T(8,128)(2,1)S(1)}, bf16[528,256]{1,0:T(8,1...) custom-call(s32[6]{0:T(128)S(1)} %stack.44.place, ...), custom_call_target="tpu_custom_call" | custom-call | flops 1073741824 | bytes 8388608 | tf_op jit(solution)/shard_map/tile_products/pallas_call | solution.py:182
  42.3 4.8 %collective-permute-done.7.right.refs_0_.rest_1_ = bf16[1024,256]{1,0:T(8,128)(2,1)} collective-permute-done((bf16[1024,256]{1,0:T(8,128)(2,1)S(1)}, bf16[1024,256]{1,0:T(8,128)(2,1)}, u32[]{:S(2)}, u32[]{:S(2)}) %collective-permute-start.7) | collective-permute-done | bytes 524320 | tf_op jit(solution)/shard_map/ppermute | solution.py:29
  55.3 3.0 %collective-permute-start.15 = (bf16[1024,256]{1,0:T(8,128)(2,1)S(1)}, bf16[1024,256]{1,0:T(8,128)(2,1)S(1)}, u32[]{:S(2)}, u32[]{:S(2)}) collective-permute-start(bf16[1024,256]{1,0:T(8,128)(2,1)S(1)} %slice_weights.1.rest_8_.rest_0_), channel_id=1, source_target_pairs={{0,1},{1,0},{2,3},{3,2},{4,5},{5,4},{6,7},{7,6},{8,9},{9,8},{10,11... | collective-permute-start | bytes 1572872 | tf_op jit(solution)/shard_map/ppermute | solution.py:33
  59.3 3.2 %collective-permute-start.16 = (bf16[1024,256]{1,0:T(8,128)(2,1)}, bf16[1024,256]{1,0:T(8,128)(2,1)S(1)}, u32[]{:S(2)}, u32[]{:S(2)}) collective-permute-start(bf16[1024,256]{1,0:T(8,128)(2,1)} %collective-permute-done.7.right.refs_0_.rest_1_), channel_id=1, source_target_pairs={{0,1},{1,0},{2,3},{3,2},{4,5},{5,4},{6,7},{7,6},{8,9},{9,8},{10,11... | collective-permute-start | bytes 1572872 | tf_op jit(solution)/shard_map/ppermute | solution.py:33
  62.6 2.5 %collective-permute-start.18 = (bf16[512,256]{1,0:T(8,128)(2,1)S(1)}, bf16[512,256]{1,0:T(8,128)(2,1)S(1)}, u32[]{:S(2)}, u32[]{:S(2)}) collective-permute-start(bf16[512,256]{1,0:T(8,128)(2,1)S(1)} %get-tuple-element.66.rest_3_), channel_id=1, source_target_pairs={{0,1},{1,0},{2,3},{3,2},{4,5},{5,4},{6,7},{7,6},{8,9},{9,8},{10,11... | collective-permute-start | bytes 786440 | tf_op jit(solution)/shard_map/ppermute | solution.py:33
  66.6 2.7 %tile_products.3 = (bf16[1024,256]{1,0:T(8,128)(2,1)S(1)}, bf16[1024,256]{1,0:T(8,128)(2,1)S(1)}, bf16[1024,256]{1,0:T(8,128)(2,1)S(1)}, bf16[528,256]{1,0:T(8,128)(2,1)S(1)}, bf16[528,256]{1,0:T(8,128)(2,1)S(1)}) custom-call(s32[6]{0:T(128)S(1)} %stack.44.place, s32[16,2]{1,0:T(8,128)S(1)} %copy.14.pairs, s32[1]{0:T(128)S(6)} %copy.20.count, ...), custom_call_target="tpu_custom_call" | custom-call | flops 1073741824 | bytes 8388608 | tf_op jit(solution)/shard_map/tile_products/pallas_call | solution.py:182
  72.5 4.1 %stage_unembed.1.refs_1_.stage = bf16[2048,2048]{1,0:T(8,128)(2,1)S(1)} custom-call(s32[6]{0:T(128)S(1)} %stack.44.place, bf16[4096,2048]{1,0:T(8,128)(2,1)} %unembed.1, bf16[1024,256]{1,0:T(8,128)(2,1)S(1)} %get-tuple-element.68.refs_0_.refs_3_), custom_call_target="tpu_custom_call" | custom-call | bytes 8388608 | tf_op jit(solution)/shard_map/stage_unembed/pallas_call | solution.py:394
  76.6 2.4 %collective-permute-done.23.from_left = bf16[528,256]{1,0:T(8,128)(2,1)S(1)} collective-permute-done((bf16[528,256]{1,0:T(8,128)(2,1)S(1)}, bf16[528,256]{1,0:T(8,128)(2,1)S(1)}, u32[]{:S(2)}, u32[]{:S(2)}) %collective-permute-start.23) | collective-permute-done | bytes 270368 | tf_op jit(solution)/shard_map/ppermute | solution.py:29
  79.6 2.5 %collective-permute-start.26 = (bf16[1024,256]{1,0:T(8,128)(2,1)S(1)}, bf16[1024,256]{1,0:T(8,128)(2,1)S(1)}, u32[]{:S(2)}, u32[]{:S(2)}) collective-permute-start(bf16[1024,256]{1,0:T(8,128)(2,1)S(1)} %get-tuple-element.81), channel_id=1, source_target_pairs={{0,96},{32,0},{64,32},{96,64},{1,97},{33,1},{65,33},{97,65},{2,98}... | collective-permute-start | bytes 1572872 | tf_op jit(solution)/shard_map/ppermute | solution.py:29
  84.8 6.2 %collective-permute-start.21 = (bf16[272,256]{1,0:T(8,128)(2,1)S(1)}, bf16[272,256]{1,0:T(8,128)(2,1)S(1)}, u32[]{:S(2)}, u32[]{:S(2)}) collective-permute-start(bf16[272,256]{1,0:T(8,128)(2,1)S(1)} %get-tuple-element.72), channel_id=1, source_target_pairs={{0,16},{8,24},{16,0},{24,8},{1,17},{9,25},{17,1},{25,9},{2,18},{10... | collective-permute-start | bytes 417800 | tf_op jit(solution)/shard_map/ppermute | solution.py:29
  95.9 6.2 %collective-permute-start.28 = (bf16[272,256]{1,0:T(8,128)(2,1)S(1)}, bf16[272,256]{1,0:T(8,128)(2,1)S(1)}, u32[]{:S(2)}, u32[]{:S(2)}) collective-permute-start(bf16[272,256]{1,0:T(8,128)(2,1)S(1)} %get-tuple-element.86), channel_id=1, source_target_pairs={{0,16},{8,24},{16,0},{24,8},{1,17},{9,25},{17,1},{25,9},{2,18},{10... | collective-permute-start | bytes 417800 | tf_op jit(solution)/shard_map/ppermute | solution.py:29
  103.4 3.3 %collective-permute-done.28.refs_6_ = bf16[272,256]{1,0:T(8,128)(2,1)S(1)} collective-permute-done((bf16[272,256]{1,0:T(8,128)(2,1)S(1)}, bf16[272,256]{1,0:T(8,128)(2,1)S(1)}, u32[]{:S(2)}, u32[]{:S(2)}) %collective-permute-start.28) | collective-permute-done | bytes 139296 | tf_op jit(solution)/shard_map/ppermute | solution.py:29
  109.6 2.6 %collective-permute-start.30 = (bf16[2064,256]{1,0:T(8,128)(2,1)S(1)}, bf16[2064,256]{1,0:T(8,128)(2,1)S(1)}, u32[]{:S(2)}, u32[]{:S(2)}) collective-permute-start(bf16[2064,256]{1,0:T(8,128)(2,1)S(1)} %logit_grad.1.mine), channel_id=1, source_target_pairs={{0,1},{1,0},{2,3},{3,2},{4,5},{5,4},{6,7},{7,6},{8,9},{9,8},{10,11... | collective-permute-start | bytes 3170312 | tf_op jit(solution)/shard_map/ppermute | solution.py:33
  112.1 2.3 %own_hidden.1.own = bf16[2048,256]{1,0:T(8,128)(2,1)S(1)} custom-call(bf16[2048,2048]{1,0:T(8,128)(2,1)S(1)} %stage_unembed.1.refs_1_.stage, bf16[2064,256]{1,0:T(8,128)(2,1)S(1)} %logit_grad.1.mine), custom_call_target="tpu_custom_call" | custom-call | flops 2147483648 | bytes 8388608 | tf_op jit(solution)/shard_map/own_hidden/pallas_call | solution.py:416
  115.8 2.7 %collective-permute-start.32 = (bf16[272,512]{1,0:T(8,128)(2,1)S(1)}, bf16[272,512]{1,0:T(8,128)(2,1)S(1)}, u32[]{:S(2)}, u32[]{:S(2)}) collective-permute-start(bf16[272,512]{1,0:T(8,128)(2,1)S(1)} %get-tuple-element.92), channel_id=1, source_target_pairs={{0,96},{1,25},{8,104},{9,1},{16,112},{17,9},{24,120},{25,17},{32,0... | collective-permute-start | bytes 835592 | tf_op jit(solution)/shard_map/ppermute | solution.py:584
  118.5 2.4 %other_hidden.3 = (bf16[512,512]{1,0:T(8,128)(2,1)S(1)}, bf16[512,512]{1,0:T(8,128)(2,1)S(1)}, bf16[512,512]{1,0:T(8,128)(2,1)S(1)}) custom-call(s32[6]{0:T(128)S(1)} %stack.44.place, bf16[2048,2048]{1,0:T(8,128)(2,1)S(1)} %stage_unembed.1.refs_1_.stage, bf16[2064,256]{1,0:T(8,128)(2,1)S(1)} %logit_grad.1.mine, ...), custom_call_target="tpu_custom_call" | custom-call | flops 1610612736 | bytes 8388608 | tf_op jit(solution)/shard_map/other_hidden/pallas_call | solution.py:451
  123.0 2.7 %collective-permute-start.34 = (bf16[512,512]{1,0:T(8,128)(2,1)S(1)}, bf16[512,512]{1,0:T(8,128)(2,1)S(1)}, u32[]{:S(2)}, u32[]{:S(2)}) collective-permute-start(bf16[512,512]{1,0:T(8,128)(2,1)S(1)} %get-tuple-element.94), channel_id=1, source_target_pairs={{0,96},{1,25},{8,104},{9,1},{16,112},{17,9},{24,120},{25,17},{32,0... | collective-permute-start | bytes 1572872 | tf_op jit(solution)/shard_map/ppermute | solution.py:584
  125.7 6.1 %collective-permute-done.34.right = bf16[512,512]{1,0:T(8,128)(2,1)S(1)} collective-permute-done((bf16[512,512]{1,0:T(8,128)(2,1)S(1)}, bf16[512,512]{1,0:T(8,128)(2,1)S(1)}, u32[]{:S(2)}, u32[]{:S(2)}) %collective-permute-start.34) | collective-permute-done | bytes 524320 | tf_op jit(solution)/shard_map/ppermute | solution.py:584
  133.6 3.5 %collective-permute-start.36 = (bf16[144,512]{1,0:T(8,128)(2,1)S(1)}, bf16[144,512]{1,0:T(8,128)(2,1)S(1)}, u32[]{:S(2)}, u32[]{:S(2)}) collective-permute-start(bf16[144,512]{1,0:T(8,128)(2,1)S(1)} %get-tuple-element.97), channel_id=1, source_target_pairs={{0,16},{1,65},{8,24},{9,73},{16,0},{17,81},{24,8},{25,89},{32,48},... | collective-permute-start | bytes 442376 | tf_op jit(solution)/shard_map/ppermute | solution.py:584
  138.8 2.4 %collective-permute-done.36.refs_2_ = bf16[144,512]{1,0:T(8,128)(2,1)S(1)} collective-permute-done((bf16[144,512]{1,0:T(8,128)(2,1)S(1)}, bf16[144,512]{1,0:T(8,128)(2,1)S(1)}, u32[]{:S(2)}, u32[]{:S(2)}) %collective-permute-start.36) | collective-permute-done | bytes 147488 | tf_op jit(solution)/shard_map/ppermute | solution.py:584
  142.0 3.1 %collective-permute-start.38 = (bf16[128,256]{1,0:T(8,128)(2,1)S(1)}, bf16[128,256]{1,0:T(8,128)(2,1)S(1)}, u32[]{:S(2)}, u32[]{:S(2)}) collective-permute-start(bf16[128,256]{1,0:T(8,128)(2,1)S(1)} %get-tuple-element.100), channel_id=1, source_target_pairs={{0,1},{1,0},{2,3},{3,2},{4,5},{5,4},{6,7},{7,6},{8,9},{9,8},{10,11... | collective-permute-start | bytes 196616 | tf_op jit(solution)/shard_map/ppermute | solution.py:33
  (98 shorter events, 54.7 us)
Async XLA Ops:
  2.7 19.3 %collective-permute-start = (bf16[1024,256]{1,0:T(8,128)(2,1)}, bf16[1024,256]{1,0:T(8,128)(2,1)S(1)}, u32[]{:S(2)}, u32[]{:S(2)}) collective-permute-start(bf16[1024,256]{1,0:T(8,128)(2,1)} %bitcast.10.rest_0_), channel_id=1, source_target_pairs={{0,2},{2,4},{4,6},{6,0},{1,3},{3,5},{5,7},{7,1},{8,10},{10,12},{12... | collective-permute-start | bytes 1572872 | tf_op jit(solution)/shard_map/ppermute | solution.py:29
  4.7 25.3 %collective-permute-start.1 = (bf16[1024,256]{1,0:T(8,128)(2,1)}, bf16[1024,256]{1,0:T(8,128)(2,1)}, u32[]{:S(2)}, u32[]{:S(2)}) collective-permute-start(bf16[1024,256]{1,0:T(8,128)(2,1)} %bitcast.10.rest_0_), channel_id=1, source_target_pairs={{0,4},{2,6},{4,0},{6,2},{1,5},{3,7},{5,1},{7,3},{8,12},{10,14},{12... | collective-permute-start | bytes 1572872 | tf_op jit(solution)/shard_map/ppermute | solution.py:29
  7.2 22.9 %collective-permute-start.2 = (bf16[1024,256]{1,0:T(8,128)(2,1)}, bf16[1024,256]{1,0:T(8,128)(2,1)}, u32[]{:S(2)}, u32[]{:S(2)}) collective-permute-start(bf16[1024,256]{1,0:T(8,128)(2,1)} %bitcast.10.rest_0_), channel_id=1, source_target_pairs={{0,6},{2,0},{4,2},{6,4},{1,7},{3,1},{5,3},{7,5},{8,14},{10,8},{12,... | collective-permute-start | bytes 1572872 | tf_op jit(solution)/shard_map/ppermute | solution.py:29
  8.3 24.8 %collective-permute-start.3 = (bf16[1024,256]{1,0:T(8,128)(2,1)}, bf16[1024,256]{1,0:T(8,128)(2,1)}, u32[]{:S(2)}, u32[]{:S(2)}) collective-permute-start(bf16[1024,256]{1,0:T(8,128)(2,1)} %bitcast.10.rest_0_), channel_id=1, source_target_pairs={{0,1},{1,0},{2,3},{3,2},{4,5},{5,4},{6,7},{7,6},{8,9},{9,8},{10,11... | collective-permute-start | bytes 1572872 | tf_op jit(solution)/shard_map/ppermute | solution.py:33
  32.2 14.9 %collective-permute-start.7 = (bf16[1024,256]{1,0:T(8,128)(2,1)S(1)}, bf16[1024,256]{1,0:T(8,128)(2,1)}, u32[]{:S(2)}, u32[]{:S(2)}) collective-permute-start(bf16[1024,256]{1,0:T(8,128)(2,1)S(1)} %slice_weights.1.rest_8_.rest_0_), channel_id=1, source_target_pairs={{0,2},{2,4},{4,6},{6,0},{1,3},{3,5},{5,7},{7,1},{8,10},{10,12},{12... | collective-permute-start | bytes 1572872 | tf_op jit(solution)/shard_map/ppermute | solution.py:29
  33.1 13.9 %collective-permute-start.8 = (bf16[1024,256]{1,0:T(8,128)(2,1)S(1)}, bf16[1024,256]{1,0:T(8,128)(2,1)}, u32[]{:S(2)}, u32[]{:S(2)}) collective-permute-start(bf16[1024,256]{1,0:T(8,128)(2,1)S(1)} %slice_weights.1.rest_8_.rest_0_), channel_id=1, source_target_pairs={{0,6},{2,0},{4,2},{6,4},{1,7},{3,1},{5,3},{7,5},{8,14},{10,8},{12,... | collective-permute-start | bytes 1572872 | tf_op jit(solution)/shard_map/ppermute | solution.py:29
  39.4 8.8 %collective-permute-start.11 = (bf16[528,256]{1,0:T(8,128)(2,1)S(1)}, bf16[528,256]{1,0:T(8,128)(2,1)S(1)}, u32[]{:S(2)}, u32[]{:S(2)}) collective-permute-start(bf16[528,256]{1,0:T(8,128)(2,1)S(1)} %get-tuple-element.62.mine), channel_id=1, source_target_pairs={{0,32},{32,64},{64,96},{96,0},{1,33},{33,65},{65,97},{97,1},{2,34}... | collective-permute-start | bytes 811016 | tf_op jit(solution)/shard_map/ppermute | solution.py:29
  41.2 7.1 %collective-permute-start.12 = (bf16[528,256]{1,0:T(8,128)(2,1)S(1)}, bf16[528,256]{1,0:T(8,128)(2,1)S(1)}, u32[]{:S(2)}, u32[]{:S(2)}) collective-permute-start(bf16[528,256]{1,0:T(8,128)(2,1)S(1)} %get-tuple-element.63), channel_id=1, source_target_pairs={{0,96},{32,0},{64,32},{96,64},{1,97},{33,1},{65,33},{97,65},{2,98}... | collective-permute-start | bytes 811016 | tf_op jit(solution)/shard_map/ppermute | solution.py:29
  48.7 13.9 %collective-permute-start.13 = (bf16[1040,256]{1,0:T(8,128)(2,1)S(1)}, bf16[1040,256]{1,0:T(8,128)(2,1)S(1)}, u32[]{:S(2)}, u32[]{:S(2)}) collective-permute-start(bf16[1040,256]{1,0:T(8,128)(2,1)S(1)} %get-tuple-element.64), channel_id=1, source_target_pairs={{0,32},{32,64},{64,96},{96,0},{1,33},{33,65},{65,97},{97,1},{2,34}... | collective-permute-start | bytes 1597448 | tf_op jit(solution)/shard_map/ppermute | solution.py:29
  50.7 11.9 %collective-permute-start.14 = (bf16[1024,256]{1,0:T(8,128)(2,1)S(1)}, bf16[1024,256]{1,0:T(8,128)(2,1)S(1)}, u32[]{:S(2)}, u32[]{:S(2)}) collective-permute-start(bf16[1024,256]{1,0:T(8,128)(2,1)S(1)} %get-tuple-element.65), channel_id=1, source_target_pairs={{0,96},{32,0},{64,32},{96,64},{1,97},{33,1},{65,33},{97,65},{2,98}... | collective-permute-start | bytes 1572872 | tf_op jit(solution)/shard_map/ppermute | solution.py:29
  53.2 9.4 %collective-permute-start.10 = (bf16[512,256]{1,0:T(8,128)(2,1)S(1)}, bf16[512,256]{1,0:T(8,128)(2,1)S(1)}, u32[]{:S(2)}, u32[]{:S(2)}) collective-permute-start(bf16[512,256]{1,0:T(8,128)(2,1)S(1)} %get-tuple-element.59), channel_id=1, source_target_pairs={{0,6},{2,0},{4,2},{6,4},{1,7},{3,1},{5,3},{7,5},{8,14},{10,8},{12,... | collective-permute-start | bytes 786440 | tf_op jit(solution)/shard_map/ppermute | solution.py:29
  55.3 9.9 %collective-permute-start.15 = (bf16[1024,256]{1,0:T(8,128)(2,1)S(1)}, bf16[1024,256]{1,0:T(8,128)(2,1)S(1)}, u32[]{:S(2)}, u32[]{:S(2)}) collective-permute-start(bf16[1024,256]{1,0:T(8,128)(2,1)S(1)} %slice_weights.1.rest_8_.rest_0_), channel_id=1, source_target_pairs={{0,1},{1,0},{2,3},{3,2},{4,5},{5,4},{6,7},{7,6},{8,9},{9,8},{10,11... | collective-permute-start | bytes 1572872 | tf_op jit(solution)/shard_map/ppermute | solution.py:33
  69.3 9.7 %collective-permute-start.23 = (bf16[528,256]{1,0:T(8,128)(2,1)S(1)}, bf16[528,256]{1,0:T(8,128)(2,1)S(1)}, u32[]{:S(2)}, u32[]{:S(2)}) collective-permute-start(bf16[528,256]{1,0:T(8,128)(2,1)S(1)} %get-tuple-element.76.mine), channel_id=1, source_target_pairs={{0,32},{32,64},{64,96},{96,0},{1,33},{33,65},{65,97},{97,1},{2,34}... | collective-permute-start | bytes 811016 | tf_op jit(solution)/shard_map/ppermute | solution.py:29
  70.9 8.1 %collective-permute-start.24 = (bf16[528,256]{1,0:T(8,128)(2,1)S(1)}, bf16[528,256]{1,0:T(8,128)(2,1)S(1)}, u32[]{:S(2)}, u32[]{:S(2)}) collective-permute-start(bf16[528,256]{1,0:T(8,128)(2,1)S(1)} %get-tuple-element.77), channel_id=1, source_target_pairs={{0,96},{32,0},{64,32},{96,64},{1,97},{33,1},{65,33},{97,65},{2,98}... | collective-permute-start | bytes 811016 | tf_op jit(solution)/shard_map/ppermute | solution.py:29
  79.3 14.0 %collective-permute-start.25 = (bf16[1040,256]{1,0:T(8,128)(2,1)S(1)}, bf16[1040,256]{1,0:T(8,128)(2,1)S(1)}, u32[]{:S(2)}, u32[]{:S(2)}) collective-permute-start(bf16[1040,256]{1,0:T(8,128)(2,1)S(1)} %get-tuple-element.80), channel_id=1, source_target_pairs={{0,32},{32,64},{64,96},{96,0},{1,33},{33,65},{65,97},{97,1},{2,34}... | collective-permute-start | bytes 1597448 | tf_op jit(solution)/shard_map/ppermute | solution.py:29
  79.6 12.5 %collective-permute-start.26 = (bf16[1024,256]{1,0:T(8,128)(2,1)S(1)}, bf16[1024,256]{1,0:T(8,128)(2,1)S(1)}, u32[]{:S(2)}, u32[]{:S(2)}) collective-permute-start(bf16[1024,256]{1,0:T(8,128)(2,1)S(1)} %get-tuple-element.81), channel_id=1, source_target_pairs={{0,96},{32,0},{64,32},{96,64},{1,97},{33,1},{65,33},{97,65},{2,98}... | collective-permute-start | bytes 1572872 | tf_op jit(solution)/shard_map/ppermute | solution.py:29
  83.1 19.0 %collective-permute-start.20 = (bf16[272,256]{1,0:T(8,128)(2,1)S(1)}, bf16[272,256]{1,0:T(8,128)(2,1)S(1)}, u32[]{:S(2)}, u32[]{:S(2)}) collective-permute-start(bf16[272,256]{1,0:T(8,128)(2,1)S(1)} %get-tuple-element.71), channel_id=1, source_target_pairs={{0,8},{8,16},{16,24},{24,0},{1,9},{9,17},{17,25},{25,1},{2,10},{10... | collective-permute-start | bytes 417800 | tf_op jit(solution)/shard_map/ppermute | solution.py:29
  84.8 17.4 %collective-permute-start.21 = (bf16[272,256]{1,0:T(8,128)(2,1)S(1)}, bf16[272,256]{1,0:T(8,128)(2,1)S(1)}, u32[]{:S(2)}, u32[]{:S(2)}) collective-permute-start(bf16[272,256]{1,0:T(8,128)(2,1)S(1)} %get-tuple-element.72), channel_id=1, source_target_pairs={{0,16},{8,24},{16,0},{24,8},{1,17},{9,25},{17,1},{25,9},{2,18},{10... | collective-permute-start | bytes 417800 | tf_op jit(solution)/shard_map/ppermute | solution.py:29
  91.0 11.2 %collective-permute-start.22 = (bf16[272,256]{1,0:T(8,128)(2,1)S(1)}, bf16[272,256]{1,0:T(8,128)(2,1)S(1)}, u32[]{:S(2)}, u32[]{:S(2)}) collective-permute-start(bf16[272,256]{1,0:T(8,128)(2,1)S(1)} %get-tuple-element.73), channel_id=1, source_target_pairs={{0,24},{8,0},{16,8},{24,16},{1,25},{9,1},{17,9},{25,17},{2,26},{10... | collective-permute-start | bytes 417800 | tf_op jit(solution)/shard_map/ppermute | solution.py:29
  94.3 9.1 %collective-permute-start.27 = (bf16[272,256]{1,0:T(8,128)(2,1)S(1)}, bf16[272,256]{1,0:T(8,128)(2,1)S(1)}, u32[]{:S(2)}, u32[]{:S(2)}) collective-permute-start(bf16[272,256]{1,0:T(8,128)(2,1)S(1)} %get-tuple-element.85), channel_id=1, source_target_pairs={{0,8},{8,16},{16,24},{24,0},{1,9},{9,17},{17,25},{25,1},{2,10},{10... | collective-permute-start | bytes 417800 | tf_op jit(solution)/shard_map/ppermute | solution.py:29
  95.9 10.8 %collective-permute-start.28 = (bf16[272,256]{1,0:T(8,128)(2,1)S(1)}, bf16[272,256]{1,0:T(8,128)(2,1)S(1)}, u32[]{:S(2)}, u32[]{:S(2)}) collective-permute-start(bf16[272,256]{1,0:T(8,128)(2,1)S(1)} %get-tuple-element.86), channel_id=1, source_target_pairs={{0,16},{8,24},{16,0},{24,8},{1,17},{9,25},{17,1},{25,9},{2,18},{10... | collective-permute-start | bytes 417800 | tf_op jit(solution)/shard_map/ppermute | solution.py:29
  122.9 9.8 %collective-permute-start.33 = (bf16[528,512]{1,0:T(8,128)(2,1)S(1)}, bf16[528,512]{1,0:T(8,128)(2,1)S(1)}, u32[]{:S(2)}, u32[]{:S(2)}) collective-permute-start(bf16[528,512]{1,0:T(8,128)(2,1)S(1)} %get-tuple-element.93), channel_id=1, source_target_pairs={{0,32},{1,9},{8,40},{9,17},{16,48},{17,25},{24,56},{25,1},{32,64},... | collective-permute-start | bytes 1622024 | tf_op jit(solution)/shard_map/ppermute | solution.py:584
  123.0 8.8 %collective-permute-start.34 = (bf16[512,512]{1,0:T(8,128)(2,1)S(1)}, bf16[512,512]{1,0:T(8,128)(2,1)S(1)}, u32[]{:S(2)}, u32[]{:S(2)}) collective-permute-start(bf16[512,512]{1,0:T(8,128)(2,1)S(1)} %get-tuple-element.94), channel_id=1, source_target_pairs={{0,96},{1,25},{8,104},{9,1},{16,112},{17,9},{24,120},{25,17},{32,0... | collective-permute-start | bytes 1572872 | tf_op jit(solution)/shard_map/ppermute | solution.py:584
  133.6 7.6 %collective-permute-start.36 = (bf16[144,512]{1,0:T(8,128)(2,1)S(1)}, bf16[144,512]{1,0:T(8,128)(2,1)S(1)}, u32[]{:S(2)}, u32[]{:S(2)}) collective-permute-start(bf16[144,512]{1,0:T(8,128)(2,1)S(1)} %get-tuple-element.97), channel_id=1, source_target_pairs={{0,16},{1,65},{8,24},{9,73},{16,0},{17,81},{24,8},{25,89},{32,48},... | collective-permute-start | bytes 442376 | tf_op jit(solution)/shard_map/ppermute | solution.py:584
  (22 other events, 160.4 us)

commit v12 on v11

--- a/solution.py
+++ b/solution.py
@@ -33,6 +33,11 @@
     return lax.ppermute(value, "tc", [(0, 1), (1, 0)])
 
 
+def turn(value):
+    pairs = [(x * 2 + core, (x + 1 - 2 * core) % SIDE * 2 + core) for x in range(SIDE) for core in (0, 1)]
+    return lax.ppermute(value, ("tx", "tc"), pairs)
+
+
 def thirds(value):
     high = value.astype(BF16).astype(F32)
     rest = value - high
@@ -92,31 +97,6 @@
         cost_estimate=cost(0, 4 * value.size),
         name="hold_probs",
     )(value)
-
-
-def halves_kernel(right, left, *refs):
-    top, low = refs[-2:]
-    top[...] = right[...]
-    low[...] = left[...]
-
-
-def halves(right, left, behind):
-    depth, width = right.shape
-    shape = (depth // 2, width)
-    return pl.pallas_call(
-        halves_kernel,
-        grid=(1,),
-        out_shape=[jax.ShapeDtypeStruct(shape, BF16)] * 2,
-        in_specs=[
-            pl.BlockSpec(shape, lambda i: (0, 0)),
-            pl.BlockSpec(shape, lambda i: (1, 0)),
-        ]
-        + [ANY] * len(behind),
-        out_specs=[pl.BlockSpec(shape, lambda i: (0, 0))] * 2,
-        compiler_params=params(),
-        cost_estimate=cost(0, 4 * depth * width),
-        name="take_halves",
-    )(right, left, *behind)
 
 
 def product_kernel(number, later, place, pairs, count, probs, before, *rest):
@@ -128,11 +108,10 @@
     vocab_y = place[0]
     first_block = (vocab_y * SIDE + place[1]) * (probs.shape[1] // block)
     total[...] = jnp.zeros_like(total)
-    starts = ((0, 0), (1, 0), (3, 0), (2, 0), (2, 512)) if number == 10 else ((0, 0), (1, 0), (2, 0), (3, 0))
-    for core, parts in ((place[3], pieces[: number // 2]), (1 - place[3], pieces[number // 2 :])):
-        for part, (step, start) in zip(parts, starts):
-            x = lax.rem(place[2] + SIDE - step, SIDE)
-            weights[x * 2 + core, start : start + part.shape[0]] = part[...]
+    for core, parts in ((place[3], pieces[:SIDE]), (1 - place[3], pieces[SIDE:])):
+        for step, part in enumerate(parts):
+            x = lax.rem(place[2] + step + (SIDE - 2 * step) * (1 - core), SIDE)
+            weights[x * 2 + core] = part[...]
 
     def tiles(group, carry):
         for member in range(4):
@@ -603,21 +582,23 @@
 
     piece = tile_weights[:, :, : tile_weights.shape[2] // 2].reshape(-1, tile_weights.shape[2] // 2)
     probs = held(probs)
-    mine = [piece, *gated(spread([piece] * SIDE, "tx")[1:], [mass, smass, probs])]
+    (one,) = gated([turn(piece)], [mass, probs])
+    two = turn(one)
+    mine = [piece, one, two, *gated([turn(two)], [smass])]
     other = [swap(piece) for piece in mine]
 
-    piece = sliced(tile_weights, 1, [mine[1]])
-    right, left = send(piece, "tx", 1), send(piece, "tx", 3)
+    piece = sliced(tile_weights, 1, [mine[3]])
+    one = turn(piece)
     *parts, total, probs = products(
         place, tile_pairs, tile_count, probs, before, mine, other, False, [piece]
     )
-    top, low = halves(right, left, [parts[0]])
+    (one,) = gated([one], [parts[0]])
+    two = turn(one)
     own, near, far, to_right, to_left = parts
     left_part, right_part = send(to_right, "vy", 1), send(to_left, "vy", 3)
-    near, far, given, table = relayed(near, far, left_part, right_part, to_right, [], [right, left])
+    near, far, given, table = relayed(near, far, left_part, right_part, to_right, [], [two])
     near, far = send(near, "vy", 1), send(far, "vy", 3)
-    top, low = gated([send(top, "tx", 1), send(low, "tx", 3)], [near, far])
-    mine = [piece, right, left, top, low]
+    mine = [piece, one, two, *gated([turn(two)], [near, far])]
     later = products(
         place, tile_pairs, tile_count, probs, total, mine, [swap(piece) for piece in mine], True
     )

time: 147 us -> 162 us (1.10)
  waiting for transfers between devices: 39.9 us -> 60.1 us
  starting transfers between devices: 65.6 us -> 58 us
    ppermute x21 -> x14, starting transfers between devices: 38.4 us -> 22.1 us  [send(): lax.ppermute(value, axis, [(i, (i + step) % SIDE) for i in range(SIDE)])]
    ppermute x0 -> x6, starting transfers between devices: none -> 13.8 us  [turn(): return lax.ppermute(value, ('tx', 'tc'), pairs)]
    ppermute x0 -> x6, waiting for transfers between devices: none -> 10.6 us  [turn(): return lax.ppermute(value, ('tx', 'tc'), pairs)]
    ppermute x21 -> x14, waiting for transfers between devices: 25 us -> 31.7 us  [send(): lax.ppermute(value, axis, [(i, (i + step) % SIDE) for i in range(SIDE)])]
    ppermute x11 -> x10, starting transfers between devices: 18.1 us -> 13.8 us  [swap(): return lax.ppermute(value, 'tc', [(0, 1), (1, 0)])]
    ppermute x7, waiting for transfers between devices: 13.1 us -> 15.8 us  [cross(): return lax.ppermute(value, ('vy', 'vz', 'tc'), pairs)]
  transfers between devices with their start and end apart: 39 -> 37, of which waited for: 20 -> 23; matrix products, arithmetic and copies ran while one was open for 8% -> 9% of each run, Pallas kernels for 11% -> 9%
where the time goes in v12:
time: 162 us; the launch traced here: 161 us
  waiting for transfers between devices  60.1 us (37%)
  starting transfers between devices  58 us (36%)
  Pallas kernels  24.3 us (15%)
  matrix products  8.21 us (5%)
  other arithmetic  4.88 us (3%)
  local copies, waits for them, and re-layouts  4.16 us (3%)
    ppermute x14, waiting for transfers between devices, send(): lax.ppermute(value, axis, [(i, (i + step) % SIDE) for i in range(SIDE)])  31.7 us
    ppermute x14, starting transfers between devices, send(): lax.ppermute(value, axis, [(i, (i + step) % SIDE) for i in range(SIDE)])  22.1 us
    ppermute x7, waiting for transfers between devices, cross(): return lax.ppermute(value, ('vy', 'vz', 'tc'), pairs)  15.8 us
    ppermute x10, starting transfers between devices, swap(): return lax.ppermute(value, 'tc', [(0, 1), (1, 0)])  13.8 us
    ppermute x6, starting transfers between devices, turn(): return lax.ppermute(value, ('tx', 'tc'), pairs)  13.8 us
    ppermute x6, waiting for transfers between devices, turn(): return lax.ppermute(value, ('tx', 'tc'), pairs)  10.6 us
    dot_general x1, matrix products, shards(): jnp.dot(student_hidden, student_unembed, preferred_element_type=F32)  8.21 us
    ppermute x7, starting transfers between devices, cross(): return lax.ppermute(value, ('vy', 'vz', 'tc'), pairs)  8.21 us
  transfers between devices with their start and end apart: 37, of which 23 were waited for; matrix products, arithmetic and copies ran while one was open for 9% of the time, Pallas kernels for 9%

profile of v12, /device:TPU:1, one launch (start us, length us, event | category | flops | bytes accessed | tf_op | source)
XLA Modules:
  0.0 161.1 jit_solution(8039875843033069576)
XLA Ops:
  2.7 3.3 %collective-permute-start = (bf16[1024,256]{1,0:T(8,128)(2,1)}, bf16[1024,256]{1,0:T(8,128)(2,1)}, u32[]{:S(2)}, u32[]{:S(2)}) collective-permute-start(bf16[1024,256]{1,0:T(8,128)(2,1)} %bitcast.10.rest_0_), channel_id=1, source_target_pairs={{0,2},{1,7},{2,4},{3,1},{4,6},{5,3},{6,0},{7,5},{8,10},{9,15},{10,... | collective-permute-start | bytes 1572872 | tf_op jit(solution)/shard_map/ppermute | solution.py:38
  13.8 3.1 %collective-permute-start.1 = (bf16[1024,256]{1,0:T(8,128)(2,1)}, bf16[1024,256]{1,0:T(8,128)(2,1)}, u32[]{:S(2)}, u32[]{:S(2)}) collective-permute-start(bf16[1024,256]{1,0:T(8,128)(2,1)} %gate.4.rest_1_), channel_id=1, source_target_pairs={{0,2},{1,7},{2,4},{3,1},{4,6},{5,3},{6,0},{7,5},{8,10},{9,15},{10,... | collective-permute-start | bytes 1572872 | tf_op jit(solution)/shard_map/ppermute | solution.py:38
  16.9 6.4 %collective-permute-done.1.rest_2_ = bf16[1024,256]{1,0:T(8,128)(2,1)} collective-permute-done((bf16[1024,256]{1,0:T(8,128)(2,1)}, bf16[1024,256]{1,0:T(8,128)(2,1)}, u32[]{:S(2)}, u32[]{:S(2)}) %collective-permute-start.1) | collective-permute-done | bytes 524320 | tf_op jit(solution)/shard_map/ppermute | solution.py:38
  23.3 3.1 %collective-permute-start.2 = (bf16[1024,256]{1,0:T(8,128)(2,1)}, bf16[1024,256]{1,0:T(8,128)(2,1)S(1)}, u32[]{:S(2)}, u32[]{:S(2)}) collective-permute-start(bf16[1024,256]{1,0:T(8,128)(2,1)} %collective-permute-done.1.rest_2_), channel_id=1, source_target_pairs={{0,2},{1,7},{2,4},{3,1},{4,6},{5,3},{6,0},{7,5},{8,10},{9,15},{10,... | collective-permute-start | bytes 1572872 | tf_op jit(solution)/shard_map/ppermute | solution.py:38
  26.4 8.2 %fusion.2 = (f32[256]{0:T(256)S(1)}, f32[256,2048]{1,0:T(8,128)S(1)}) fusion(bf16[256,4096]{1,0:T(8,128)(2,1)S(1)} %copy-done, bf16[4096,2048]{1,0:T(8,128)(2,1)} %unembed.1), kind=kOutput, calls=%fused_computation.4 | convolution fusion | flops 4295491584 | bytes 20972544 | tf_op jit(solution)/shard_map/dot_general | solution.py:577
  40.1 3.5 %tile_products.2 = (bf16[1024,256]{1,0:T(8,128)(2,1)S(1)}, bf16[1024,256]{1,0:T(8,128)(2,1)S(1)}, bf16[1024,256]{1,0:T(8,128)(2,1)S(1)}, bf16[528,256]{1,0:T(8,1...) custom-call(s32[6]{0:T(128)S(1)} %stack.44.place, ...), custom_call_target="tpu_custom_call" | custom-call | flops 1073741824 | bytes 8388608 | tf_op jit(solution)/shard_map/tile_products/pallas_call | solution.py:161
  48.6 2.8 %collective-permute-start.11 = (bf16[528,256]{1,0:T(8,128)(2,1)S(1)}, bf16[528,256]{1,0:T(8,128)(2,1)S(1)}, u32[]{:S(2)}, u32[]{:S(2)}) collective-permute-start(bf16[528,256]{1,0:T(8,128)(2,1)S(1)} %get-tuple-element.51), channel_id=1, source_target_pairs={{0,96},{32,0},{64,32},{96,64},{1,97},{33,1},{65,33},{97,65},{2,98}... | collective-permute-start | bytes 811016 | tf_op jit(solution)/shard_map/ppermute | solution.py:29
  51.4 6.3 %collective-permute-done.11.from_right = bf16[528,256]{1,0:T(8,128)(2,1)S(1)} collective-permute-done((bf16[528,256]{1,0:T(8,128)(2,1)S(1)}, bf16[528,256]{1,0:T(8,128)(2,1)S(1)}, u32[]{:S(2)}, u32[]{:S(2)}) %collective-permute-start.11) | collective-permute-done | bytes 270368 | tf_op jit(solution)/shard_map/ppermute | solution.py:29
  57.7 3.2 %collective-permute-done.10.from_left = bf16[528,256]{1,0:T(8,128)(2,1)S(1)} collective-permute-done((bf16[528,256]{1,0:T(8,128)(2,1)S(1)}, bf16[528,256]{1,0:T(8,128)(2,1)S(1)}, u32[]{:S(2)}, u32[]{:S(2)}) %collective-permute-start.10) | collective-permute-done | bytes 270368 | tf_op jit(solution)/shard_map/ppermute | solution.py:29
  61.4 2.7 %collective-permute-start.13 = (bf16[1024,256]{1,0:T(8,128)(2,1)S(1)}, bf16[1024,256]{1,0:T(8,128)(2,1)S(1)}, u32[]{:S(2)}, u32[]{:S(2)}) collective-permute-start(bf16[1024,256]{1,0:T(8,128)(2,1)S(1)} %get-tuple-element.53), channel_id=1, source_target_pairs={{0,96},{32,0},{64,32},{96,64},{1,97},{33,1},{65,33},{97,65},{2,98}... | collective-permute-start | bytes 1572872 | tf_op jit(solution)/shard_map/ppermute | solution.py:29
  65.2 9.1 %collective-permute-done.13.refs_2_ = bf16[1024,256]{1,0:T(8,128)(2,1)S(1)} collective-permute-done((bf16[1024,256]{1,0:T(8,128)(2,1)S(1)}, bf16[1024,256]{1,0:T(8,128)(2,1)S(1)}, u32[]{:S(2)}, u32[]{:S(2)}) %collective-permute-start.13) | collective-permute-done | bytes 524320 | tf_op jit(solution)/shard_map/ppermute | solution.py:29
  81.1 4.3 %collective-permute-start.22 = (bf16[528,256]{1,0:T(8,128)(2,1)S(1)}, bf16[528,256]{1,0:T(8,128)(2,1)S(1)}, u32[]{:S(2)}, u32[]{:S(2)}) collective-permute-start(bf16[528,256]{1,0:T(8,128)(2,1)S(1)} %get-tuple-element.63), channel_id=1, source_target_pairs={{0,96},{32,0},{64,32},{96,64},{1,97},{33,1},{65,33},{97,65},{2,98}... | collective-permute-start | bytes 811016 | tf_op jit(solution)/shard_map/ppermute | solution.py:29
  85.5 4.1 %stage_unembed.1.refs_1_.stage = bf16[2048,2048]{1,0:T(8,128)(2,1)S(1)} custom-call(s32[6]{0:T(128)S(1)} %stack.44.place, bf16[4096,2048]{1,0:T(8,128)(2,1)} %unembed.1, bf16[1024,256]{1,0:T(8,128)(2,1)S(1)} %get-tuple-element.54.refs_0_.refs_3_), custom_call_target="tpu_custom_call" | custom-call | bytes 8388608 | tf_op jit(solution)/shard_map/stage_unembed/pallas_call | solution.py:373
  90.9 3.1 %collective-permute-done.21.from_left = bf16[528,256]{1,0:T(8,128)(2,1)S(1)} collective-permute-done((bf16[528,256]{1,0:T(8,128)(2,1)S(1)}, bf16[528,256]{1,0:T(8,128)(2,1)S(1)}, u32[]{:S(2)}, u32[]{:S(2)}) %collective-permute-start.21) | collective-permute-done | bytes 270368 | tf_op jit(solution)/shard_map/ppermute | solution.py:29
  94.4 2.7 %collective-permute-start.24 = (bf16[1024,256]{1,0:T(8,128)(2,1)S(1)}, bf16[1024,256]{1,0:T(8,128)(2,1)S(1)}, u32[]{:S(2)}, u32[]{:S(2)}) collective-permute-start(bf16[1024,256]{1,0:T(8,128)(2,1)S(1)} %get-tuple-element.67), channel_id=1, source_target_pairs={{0,96},{32,0},{64,32},{96,64},{1,97},{33,1},{65,33},{97,65},{2,98}... | collective-permute-start | bytes 1572872 | tf_op jit(solution)/shard_map/ppermute | solution.py:29
  99.4 2.8 %collective-permute-start.19 = (bf16[272,256]{1,0:T(8,128)(2,1)S(1)}, bf16[272,256]{1,0:T(8,128)(2,1)S(1)}, u32[]{:S(2)}, u32[]{:S(2)}) collective-permute-start(bf16[272,256]{1,0:T(8,128)(2,1)S(1)} %get-tuple-element.58), channel_id=1, source_target_pairs={{0,16},{8,24},{16,0},{24,8},{1,17},{9,25},{17,1},{25,9},{2,18},{10... | collective-permute-start | bytes 417800 | tf_op jit(solution)/shard_map/ppermute | solution.py:29
  102.9 3.6 %collective-permute-done.24.refs_2_ = bf16[1024,256]{1,0:T(8,128)(2,1)S(1)} collective-permute-done((bf16[1024,256]{1,0:T(8,128)(2,1)S(1)}, bf16[1024,256]{1,0:T(8,128)(2,1)S(1)}, u32[]{:S(2)}, u32[]{:S(2)}) %collective-permute-start.24) | collective-permute-done | bytes 524320 | tf_op jit(solution)/shard_map/ppermute | solution.py:29
  109.9 2.8 %collective-permute-start.26 = (bf16[272,256]{1,0:T(8,128)(2,1)S(1)}, bf16[272,256]{1,0:T(8,128)(2,1)S(1)}, u32[]{:S(2)}, u32[]{:S(2)}) collective-permute-start(bf16[272,256]{1,0:T(8,128)(2,1)S(1)} %get-tuple-element.72), channel_id=1, source_target_pairs={{0,16},{8,24},{16,0},{24,8},{1,17},{9,25},{17,1},{25,9},{2,18},{10... | collective-permute-start | bytes 417800 | tf_op jit(solution)/shard_map/ppermute | solution.py:29
  114.0 2.8 %collective-permute-done.26.refs_6_ = bf16[272,256]{1,0:T(8,128)(2,1)S(1)} collective-permute-done((bf16[272,256]{1,0:T(8,128)(2,1)S(1)}, bf16[272,256]{1,0:T(8,128)(2,1)S(1)}, u32[]{:S(2)}, u32[]{:S(2)}) %collective-permute-start.26) | collective-permute-done | bytes 139296 | tf_op jit(solution)/shard_map/ppermute | solution.py:29
  119.6 3.5 %collective-permute-start.28 = (bf16[2064,256]{1,0:T(8,128)(2,1)S(1)}, bf16[2064,256]{1,0:T(8,128)(2,1)S(1)}, u32[]{:S(2)}, u32[]{:S(2)}) collective-permute-start(bf16[2064,256]{1,0:T(8,128)(2,1)S(1)} %logit_grad.1.mine), channel_id=1, source_target_pairs={{0,1},{1,0},{2,3},{3,2},{4,5},{5,4},{6,7},{7,6},{8,9},{9,8},{10,11... | collective-permute-start | bytes 3170312 | tf_op jit(solution)/shard_map/ppermute | solution.py:33
  132.5 3.2 %collective-permute-done.29.from_left = bf16[272,512]{1,0:T(8,128)(2,1)S(1)} collective-permute-done((bf16[272,512]{1,0:T(8,128)(2,1)S(1)}, bf16[272,512]{1,0:T(8,128)(2,1)S(1)}, u32[]{:S(2)}, u32[]{:S(2)}) %collective-permute-start.29) | collective-permute-done | bytes 278560 | tf_op jit(solution)/shard_map/ppermute | solution.py:563
  138.6 6.1 %collective-permute-done.32.right = bf16[512,512]{1,0:T(8,128)(2,1)S(1)} collective-permute-done((bf16[512,512]{1,0:T(8,128)(2,1)S(1)}, bf16[512,512]{1,0:T(8,128)(2,1)S(1)}, u32[]{:S(2)}, u32[]{:S(2)}) %collective-permute-start.32) | collective-permute-done | bytes 524320 | tf_op jit(solution)/shard_map/ppermute | solution.py:563
  146.5 3.4 %collective-permute-start.34 = (bf16[144,512]{1,0:T(8,128)(2,1)S(1)}, bf16[144,512]{1,0:T(8,128)(2,1)S(1)}, u32[]{:S(2)}, u32[]{:S(2)}) collective-permute-start(bf16[144,512]{1,0:T(8,128)(2,1)S(1)} %get-tuple-element.83), channel_id=1, source_target_pairs={{0,16},{1,65},{8,24},{9,73},{16,0},{17,81},{24,8},{25,89},{32,48},... | collective-permute-start | bytes 442376 | tf_op jit(solution)/shard_map/ppermute | solution.py:563
  154.8 4.1 %collective-permute-start.36 = (bf16[128,256]{1,0:T(8,128)(2,1)S(1)}, bf16[128,256]{1,0:T(8,128)(2,1)S(1)}, u32[]{:S(2)}, u32[]{:S(2)}) collective-permute-start(bf16[128,256]{1,0:T(8,128)(2,1)S(1)} %get-tuple-element.86), channel_id=1, source_target_pairs={{0,1},{1,0},{2,3},{3,2},{4,5},{5,4},{6,7},{7,6},{8,9},{9,8},{10,11... | collective-permute-start | bytes 196616 | tf_op jit(solution)/shard_map/ppermute | solution.py:33
  (97 shorter events, 61.5 us)
Async XLA Ops:
  2.7 9.8 %collective-permute-start = (bf16[1024,256]{1,0:T(8,128)(2,1)}, bf16[1024,256]{1,0:T(8,128)(2,1)}, u32[]{:S(2)}, u32[]{:S(2)}) collective-permute-start(bf16[1024,256]{1,0:T(8,128)(2,1)} %bitcast.10.rest_0_), channel_id=1, source_target_pairs={{0,2},{1,7},{2,4},{3,1},{4,6},{5,3},{6,0},{7,5},{8,10},{9,15},{10,... | collective-permute-start | bytes 1572872 | tf_op jit(solution)/shard_map/ppermute | solution.py:38
  13.8 9.6 %collective-permute-start.1 = (bf16[1024,256]{1,0:T(8,128)(2,1)}, bf16[1024,256]{1,0:T(8,128)(2,1)}, u32[]{:S(2)}, u32[]{:S(2)}) collective-permute-start(bf16[1024,256]{1,0:T(8,128)(2,1)} %gate.4.rest_1_), channel_id=1, source_target_pairs={{0,2},{1,7},{2,4},{3,1},{4,6},{5,3},{6,0},{7,5},{8,10},{9,15},{10,... | collective-permute-start | bytes 1572872 | tf_op jit(solution)/shard_map/ppermute | solution.py:38
  16.9 23.2 %collective-permute-start.3 = (bf16[1024,256]{1,0:T(8,128)(2,1)}, bf16[1024,256]{1,0:T(8,128)(2,1)}, u32[]{:S(2)}, u32[]{:S(2)}) collective-permute-start(bf16[1024,256]{1,0:T(8,128)(2,1)} %bitcast.10.rest_0_), channel_id=1, source_target_pairs={{0,1},{1,0},{2,3},{3,2},{4,5},{5,4},{6,7},{7,6},{8,9},{9,8},{10,11... | collective-permute-start | bytes 1572872 | tf_op jit(solution)/shard_map/ppermute | solution.py:33
  23.3 12.4 %collective-permute-start.2 = (bf16[1024,256]{1,0:T(8,128)(2,1)}, bf16[1024,256]{1,0:T(8,128)(2,1)S(1)}, u32[]{:S(2)}, u32[]{:S(2)}) collective-permute-start(bf16[1024,256]{1,0:T(8,128)(2,1)} %collective-permute-done.1.rest_2_), channel_id=1, source_target_pairs={{0,2},{1,7},{2,4},{3,1},{4,6},{5,3},{6,0},{7,5},{8,10},{9,15},{10,... | collective-permute-start | bytes 1572872 | tf_op jit(solution)/shard_map/ppermute | solution.py:38
  37.5 8.5 %collective-permute-start.7 = (bf16[1024,256]{1,0:T(8,128)(2,1)S(1)}, bf16[1024,256]{1,0:T(8,128)(2,1)}, u32[]{:S(2)}, u32[]{:S(2)}) collective-permute-start(bf16[1024,256]{1,0:T(8,128)(2,1)S(1)} %slice_weights.1.rest_8_.rest_0_), channel_id=1, source_target_pairs={{0,2},{1,7},{2,4},{3,1},{4,6},{5,3},{6,0},{7,5},{8,10},{9,15},{10,... | collective-permute-start | bytes 1572872 | tf_op jit(solution)/shard_map/ppermute | solution.py:38
  46.0 14.8 %collective-permute-start.8 = (bf16[1024,256]{1,0:T(8,128)(2,1)}, bf16[1024,256]{1,0:T(8,128)(2,1)S(1)}, u32[]{:S(2)}, u32[]{:S(2)}) collective-permute-start(bf16[1024,256]{1,0:T(8,128)(2,1)} %gate.6.rest_1_), channel_id=1, source_target_pairs={{0,2},{1,7},{2,4},{3,1},{4,6},{5,3},{6,0},{7,5},{8,10},{9,15},{10,... | collective-permute-start | bytes 1572872 | tf_op jit(solution)/shard_map/ppermute | solution.py:38
  48.6 9.1 %collective-permute-start.11 = (bf16[528,256]{1,0:T(8,128)(2,1)S(1)}, bf16[528,256]{1,0:T(8,128)(2,1)S(1)}, u32[]{:S(2)}, u32[]{:S(2)}) collective-permute-start(bf16[528,256]{1,0:T(8,128)(2,1)S(1)} %get-tuple-element.51), channel_id=1, source_target_pairs={{0,96},{32,0},{64,32},{96,64},{1,97},{33,1},{65,33},{97,65},{2,98}... | collective-permute-start | bytes 811016 | tf_op jit(solution)/shard_map/ppermute | solution.py:29
  51.4 9.5 %collective-permute-start.10 = (bf16[528,256]{1,0:T(8,128)(2,1)S(1)}, bf16[528,256]{1,0:T(8,128)(2,1)S(1)}, u32[]{:S(2)}, u32[]{:S(2)}) collective-permute-start(bf16[528,256]{1,0:T(8,128)(2,1)S(1)} %get-tuple-element.50.mine), channel_id=1, source_target_pairs={{0,32},{32,64},{64,96},{96,0},{1,33},{33,65},{65,97},{97,1},{2,34}... | collective-permute-start | bytes 811016 | tf_op jit(solution)/shard_map/ppermute | solution.py:29
  61.3 14.9 %collective-permute-start.12 = (bf16[1040,256]{1,0:T(8,128)(2,1)S(1)}, bf16[1040,256]{1,0:T(8,128)(2,1)S(1)}, u32[]{:S(2)}, u32[]{:S(2)}) collective-permute-start(bf16[1040,256]{1,0:T(8,128)(2,1)S(1)} %get-tuple-element.52), channel_id=1, source_target_pairs={{0,32},{32,64},{64,96},{96,0},{1,33},{33,65},{65,97},{97,1},{2,34}... | collective-permute-start | bytes 1597448 | tf_op jit(solution)/shard_map/ppermute | solution.py:29
  61.4 13.0 %collective-permute-start.13 = (bf16[1024,256]{1,0:T(8,128)(2,1)S(1)}, bf16[1024,256]{1,0:T(8,128)(2,1)S(1)}, u32[]{:S(2)}, u32[]{:S(2)}) collective-permute-start(bf16[1024,256]{1,0:T(8,128)(2,1)S(1)} %get-tuple-element.53), channel_id=1, source_target_pairs={{0,96},{32,0},{64,32},{96,64},{1,97},{33,1},{65,33},{97,65},{2,98}... | collective-permute-start | bytes 1572872 | tf_op jit(solution)/shard_map/ppermute | solution.py:29
  64.0 12.1 %collective-permute-start.9 = (bf16[1024,256]{1,0:T(8,128)(2,1)S(1)}, bf16[1024,256]{1,0:T(8,128)(2,1)S(1)}, u32[]{:S(2)}, u32[]{:S(2)}) collective-permute-start(bf16[1024,256]{1,0:T(8,128)(2,1)S(1)} %collective-permute-done.8.refs_0_.rest_2_), channel_id=1, source_target_pairs={{0,2},{1,7},{2,4},{3,1},{4,6},{5,3},{6,0},{7,5},{8,10},{9,15},{10,... | collective-permute-start | bytes 1572872 | tf_op jit(solution)/shard_map/ppermute | solution.py:38
  64.0 13.0 %collective-permute-start.14 = (bf16[1024,256]{1,0:T(8,128)(2,1)S(1)}, bf16[1024,256]{1,0:T(8,128)(2,1)S(1)}, u32[]{:S(2)}, u32[]{:S(2)}) collective-permute-start(bf16[1024,256]{1,0:T(8,128)(2,1)S(1)} %slice_weights.1.rest_8_.rest_0_), channel_id=1, source_target_pairs={{0,1},{1,0},{2,3},{3,2},{4,5},{5,4},{6,7},{7,6},{8,9},{9,8},{10,11... | collective-permute-start | bytes 1572872 | tf_op jit(solution)/shard_map/ppermute | solution.py:33
  65.2 11.8 %collective-permute-start.15 = (bf16[1024,256]{1,0:T(8,128)(2,1)}, bf16[1024,256]{1,0:T(8,128)(2,1)S(1)}, u32[]{:S(2)}, u32[]{:S(2)}) collective-permute-start(bf16[1024,256]{1,0:T(8,128)(2,1)} %gate.6.rest_1_), channel_id=1, source_target_pairs={{0,1},{1,0},{2,3},{3,2},{4,5},{5,4},{6,7},{7,6},{8,9},{9,8},{10,11... | collective-permute-start | bytes 1572872 | tf_op jit(solution)/shard_map/ppermute | solution.py:33
  81.1 9.8 %collective-permute-start.22 = (bf16[528,256]{1,0:T(8,128)(2,1)S(1)}, bf16[528,256]{1,0:T(8,128)(2,1)S(1)}, u32[]{:S(2)}, u32[]{:S(2)}) collective-permute-start(bf16[528,256]{1,0:T(8,128)(2,1)S(1)} %get-tuple-element.63), channel_id=1, source_target_pairs={{0,96},{32,0},{64,32},{96,64},{1,97},{33,1},{65,33},{97,65},{2,98}... | collective-permute-start | bytes 811016 | tf_op jit(solution)/shard_map/ppermute | solution.py:29
  85.4 8.6 %collective-permute-start.21 = (bf16[528,256]{1,0:T(8,128)(2,1)S(1)}, bf16[528,256]{1,0:T(8,128)(2,1)S(1)}, u32[]{:S(2)}, u32[]{:S(2)}) collective-permute-start(bf16[528,256]{1,0:T(8,128)(2,1)S(1)} %get-tuple-element.62.mine), channel_id=1, source_target_pairs={{0,32},{32,64},{64,96},{96,0},{1,33},{33,65},{65,97},{97,1},{2,34}... | collective-permute-start | bytes 811016 | tf_op jit(solution)/shard_map/ppermute | solution.py:29
  94.3 13.3 %collective-permute-start.23 = (bf16[1040,256]{1,0:T(8,128)(2,1)S(1)}, bf16[1040,256]{1,0:T(8,128)(2,1)S(1)}, u32[]{:S(2)}, u32[]{:S(2)}) collective-permute-start(bf16[1040,256]{1,0:T(8,128)(2,1)S(1)} %get-tuple-element.66), channel_id=1, source_target_pairs={{0,32},{32,64},{64,96},{96,0},{1,33},{33,65},{65,97},{97,1},{2,34}... | collective-permute-start | bytes 1597448 | tf_op jit(solution)/shard_map/ppermute | solution.py:29
  94.4 12.1 %collective-permute-start.24 = (bf16[1024,256]{1,0:T(8,128)(2,1)S(1)}, bf16[1024,256]{1,0:T(8,128)(2,1)S(1)}, u32[]{:S(2)}, u32[]{:S(2)}) collective-permute-start(bf16[1024,256]{1,0:T(8,128)(2,1)S(1)} %get-tuple-element.67), channel_id=1, source_target_pairs={{0,96},{32,0},{64,32},{96,64},{1,97},{33,1},{65,33},{97,65},{2,98}... | collective-permute-start | bytes 1572872 | tf_op jit(solution)/shard_map/ppermute | solution.py:29
  98.2 14.5 %collective-permute-start.18 = (bf16[272,256]{1,0:T(8,128)(2,1)S(1)}, bf16[272,256]{1,0:T(8,128)(2,1)S(1)}, u32[]{:S(2)}, u32[]{:S(2)}) collective-permute-start(bf16[272,256]{1,0:T(8,128)(2,1)S(1)} %get-tuple-element.57), channel_id=1, source_target_pairs={{0,8},{8,16},{16,24},{24,0},{1,9},{9,17},{17,25},{25,1},{2,10},{10... | collective-permute-start | bytes 417800 | tf_op jit(solution)/shard_map/ppermute | solution.py:29
  99.4 14.1 %collective-permute-start.19 = (bf16[272,256]{1,0:T(8,128)(2,1)S(1)}, bf16[272,256]{1,0:T(8,128)(2,1)S(1)}, u32[]{:S(2)}, u32[]{:S(2)}) collective-permute-start(bf16[272,256]{1,0:T(8,128)(2,1)S(1)} %get-tuple-element.58), channel_id=1, source_target_pairs={{0,16},{8,24},{16,0},{24,8},{1,17},{9,25},{17,1},{25,9},{2,18},{10... | collective-permute-start | bytes 417800 | tf_op jit(solution)/shard_map/ppermute | solution.py:29
  102.2 11.2 %collective-permute-start.20 = (bf16[272,256]{1,0:T(8,128)(2,1)S(1)}, bf16[272,256]{1,0:T(8,128)(2,1)S(1)}, u32[]{:S(2)}, u32[]{:S(2)}) collective-permute-start(bf16[272,256]{1,0:T(8,128)(2,1)S(1)} %get-tuple-element.59), channel_id=1, source_target_pairs={{0,24},{8,0},{16,8},{24,16},{1,25},{9,1},{17,9},{25,17},{2,26},{10... | collective-permute-start | bytes 417800 | tf_op jit(solution)/shard_map/ppermute | solution.py:29
  128.8 6.9 %collective-permute-start.29 = (bf16[272,512]{1,0:T(8,128)(2,1)S(1)}, bf16[272,512]{1,0:T(8,128)(2,1)S(1)}, u32[]{:S(2)}, u32[]{:S(2)}) collective-permute-start(bf16[272,512]{1,0:T(8,128)(2,1)S(1)} %get-tuple-element.74.refs_0_.mine), channel_id=1, source_target_pairs={{0,32},{1,9},{8,40},{9,17},{16,48},{17,25},{24,56},{25,1},{32,64},... | collective-permute-start | bytes 835592 | tf_op jit(solution)/shard_map/ppermute | solution.py:563
  135.8 9.8 %collective-permute-start.31 = (bf16[528,512]{1,0:T(8,128)(2,1)S(1)}, bf16[528,512]{1,0:T(8,128)(2,1)S(1)}, u32[]{:S(2)}, u32[]{:S(2)}) collective-permute-start(bf16[528,512]{1,0:T(8,128)(2,1)S(1)} %get-tuple-element.79), channel_id=1, source_target_pairs={{0,32},{1,9},{8,40},{9,17},{16,48},{17,25},{24,56},{25,1},{32,64},... | collective-permute-start | bytes 1622024 | tf_op jit(solution)/shard_map/ppermute | solution.py:563
  135.9 8.8 %collective-permute-start.32 = (bf16[512,512]{1,0:T(8,128)(2,1)S(1)}, bf16[512,512]{1,0:T(8,128)(2,1)S(1)}, u32[]{:S(2)}, u32[]{:S(2)}) collective-permute-start(bf16[512,512]{1,0:T(8,128)(2,1)S(1)} %get-tuple-element.80), channel_id=1, source_target_pairs={{0,96},{1,25},{8,104},{9,1},{16,112},{17,9},{24,120},{25,17},{32,0... | collective-permute-start | bytes 1572872 | tf_op jit(solution)/shard_map/ppermute | solution.py:563
  146.5 7.5 %collective-permute-start.34 = (bf16[144,512]{1,0:T(8,128)(2,1)S(1)}, bf16[144,512]{1,0:T(8,128)(2,1)S(1)}, u32[]{:S(2)}, u32[]{:S(2)}) collective-permute-start(bf16[144,512]{1,0:T(8,128)(2,1)S(1)} %get-tuple-element.83), channel_id=1, source_target_pairs={{0,16},{1,65},{8,24},{9,73},{16,0},{17,81},{24,8},{25,89},{32,48},... | collective-permute-start | bytes 442376 | tf_op jit(solution)/shard_map/ppermute | solution.py:563
  (21 other events, 153.5 us)

commit v13 on v11

--- a/solution.py
+++ b/solution.py
@@ -459,21 +459,21 @@
     )(place, stage, mine, other, own, *behind)
 
 
-def pass_kernel(near, far, from_left, from_right, near_out, far_out):
-    near_out[0:256, :] = (near[0:256, :].astype(F32) + from_left[0:256, :].astype(F32)).astype(BF16)
-    near_out[256:512, :] = near[256:512, :]
-    near_out[512:528, :] = from_left[256:272, :]
-    far_out[0:256, :] = far[0:256, :]
-    far_out[256:512, :] = (far[256:512, :].astype(F32) + from_right[0:256, :].astype(F32)).astype(BF16)
+def pass_kernel(near, far, from_left, from_right, near_low, near_high, far_low, far_high):
+    near_low[0:256, :] = (near[0:256, :].astype(F32) + from_left[0:256, :].astype(F32)).astype(BF16)
+    near_low[256:272, :] = from_left[256:272, :]
+    near_high[...] = near[256:512, :]
+    far_low[...] = far[0:256, :]
+    far_high[...] = (far[256:512, :].astype(F32) + from_right[0:256, :].astype(F32)).astype(BF16)
 
 
 def passed(near, far, from_left, from_right):
     rows = near.shape[1]
     return pl.pallas_call(
         pass_kernel,
-        out_shape=[jax.ShapeDtypeStruct((528, rows), BF16), jax.ShapeDtypeStruct((512, rows), BF16)],
+        out_shape=[jax.ShapeDtypeStruct((depth, rows), BF16) for depth in (272, 256, 256, 256)],
         in_specs=[VMEM] * 4,
-        out_specs=[VMEM] * 2,
+        out_specs=[VMEM] * 4,
         compiler_params=params(),
         cost_estimate=cost(512 * rows, 10 * 512 * rows),
         name="pass_grads",
@@ -486,34 +486,36 @@
     return ((ordered[0] + ordered[1]) + ordered[2]) + ordered[3]
 
 
-def middle_kernel(place, own, left, right, mine, from_left, from_right, *refs):
-    outs, ordered = refs[:SIDE], refs[SIDE]
+def middle_kernel(place, own, left_low, left_high, right_low, right_high, mine, from_left, from_right, *refs):
+    outs, ordered, summed = refs[:SIDE], refs[SIDE], refs[SIDE + 1]
     pieces = [
         (0, mine[256:272, :]),
         (3, from_left[256:272, :]),
         (1, from_right[256:272, :]),
-        (2, left[512:528, :]),
+        (2, left_low[256:272, :]),
     ]
     packed = pack_rows([ordered_loss(place[4], pieces, ordered)])
+    for start, left, right in ((0, left_low, right_low), (256, left_high, right_high)):
+        value = own[start : start + 256, :].astype(F32) + left[0:256, :].astype(F32)
+        summed[start : start + 256, :] = (value + right[...].astype(F32)).astype(BF16)
     for step in range(SIDE):
         at = pl.ds(pl.multiple_of(lax.rem(place[5] + step, SIDE) * 128, 128), 128)
-        value = own[at, :].astype(F32) + left[at, :].astype(F32) + right[at, :].astype(F32)
-        outs[step][0:128, :] = value.astype(BF16)
+        outs[step][0:128, :] = summed[at, :]
         outs[step][128:144, :] = packed
 
 
-def middle(place, own, left, right, mine, from_left, from_right):
+def middle(place, own, *parts):
     rows = own.shape[1]
     return pl.pallas_call(
         middle_kernel,
         out_shape=[jax.ShapeDtypeStruct((144, rows), BF16)] * SIDE,
-        in_specs=[SMEM] + [VMEM] * 6,
+        in_specs=[SMEM] + [VMEM] * (1 + len(parts)),
         out_specs=[VMEM] * SIDE,
-        scratch_shapes=[pltpu.VMEM((SIDE, 1, rows), F32)],
+        scratch_shapes=[pltpu.VMEM((SIDE, 1, rows), F32), pltpu.VMEM((512, rows), BF16)],
         compiler_params=params(),
         cost_estimate=cost(4 * 512 * rows, 10 * 512 * rows),
         name="merge_grads",
-    )(place, own, left, right, mine, from_left, from_right)
+    )(place, own, *parts)
 
 
 def total_kernel(place, *refs):
@@ -637,9 +639,9 @@
     to_right, to_left = other_hidden(True, place, stage, mine, other, own)
     from_left, from_right = cross(to_right, 1, True), cross(to_left, 3, True)
     here, near, far = other_hidden(False, place, stage, mine, other, own, [to_right])
-    near, far = passed(near, far, from_left, from_right)
-    near, far = cross(near, 1, True), cross(far, 3, True)
-    parts = middle(place, here, near, far, to_right, from_left, from_right)
+    sent = passed(near, far, from_left, from_right)
+    sent = [cross(part, step, True) for part, step in zip(sent, (1, 1, 3, 3))]
+    parts = middle(place, here, *sent, to_right, from_left, from_right)
     parts = [parts[0], *(cross(parts[step], step, False) for step in (1, 2, 3))]
     keep, give, loss = totals(place, parts)
     return turned(place, keep, swap(give)), loss[0]

time: 147 us -> 148 us (level)
  starting transfers between devices: 65.6 us -> 64 us
    ppermute x21, starting transfers between devices: 38.4 us -> 35.2 us  [send(): lax.ppermute(value, axis, [(i, (i + step) % SIDE) for i in range(SIDE)])]
    ppermute x7 -> x9, starting transfers between devices: 9.12 us -> 10.9 us  [cross(): return lax.ppermute(value, ('vy', 'vz', 'tc'), pairs)]
    ppermute x21, waiting for transfers between devices: 25 us -> 26.7 us  [send(): lax.ppermute(value, axis, [(i, (i + step) % SIDE) for i in range(SIDE)])]
    ppermute x7 -> x9, waiting for transfers between devices: 13.1 us -> 12 us  [cross(): return lax.ppermute(value, ('vy', 'vz', 'tc'), pairs)]
  transfers between devices with their start and end apart: 39 -> 41, of which waited for: 20 -> 20; matrix products, arithmetic and copies ran while one was open for 8% -> 8% of each run, Pallas kernels for 11% -> 11%
where the time goes in v13:
time: 148 us; the launch traced here: 147 us
  starting transfers between devices  64 us (43%)
  waiting for transfers between devices  40.5 us (27%)
  Pallas kernels  26.6 us (18%)
  matrix products  8.37 us (6%)
  other arithmetic  3.29 us (2%)
  local copies, waits for them, and re-layouts  3.12 us (2%)
  between operations  1.55 us (1%)
    ppermute x21, starting transfers between devices, send(): lax.ppermute(value, axis, [(i, (i + step) % SIDE) for i in range(SIDE)])  35.2 us
    ppermute x21, waiting for transfers between devices, send(): lax.ppermute(value, axis, [(i, (i + step) % SIDE) for i in range(SIDE)])  26.7 us
    ppermute x11, starting transfers between devices, swap(): return lax.ppermute(value, 'tc', [(0, 1), (1, 0)])  17.9 us
    ppermute x9, waiting for transfers between devices, cross(): return lax.ppermute(value, ('vy', 'vz', 'tc'), pairs)  12 us
    ppermute x9, starting transfers between devices, cross(): return lax.ppermute(value, ('vy', 'vz', 'tc'), pairs)  10.9 us
    dot_general x1, matrix products, shards(): jnp.dot(student_hidden, student_unembed, preferred_element_type=F32)  8.37 us
    pallas_call x2, Pallas kernels, products(): pl.pallas_call(functools.partial(product_kernel, len(pieces), later), out...  7.24 us
    pallas_call x1, Pallas kernels, staged(): pl.pallas_call(stage_kernel, out_shape=jax.ShapeDtypeStruct((depth // 2,...  4.06 us
  transfers between devices with their start and end apart: 41, of which 20 were waited for; matrix products, arithmetic and copies ran while one was open for 8% of the time, Pallas kernels for 11%

profile of v13, /device:TPU:1, one launch (start us, length us, event | category | flops | bytes accessed | tf_op | source)
XLA Modules:
  0.0 147.4 jit_solution(16683881015171537349)
XLA Ops:
  4.7 2.5 %collective-permute-start.1 = (bf16[1024,256]{1,0:T(8,128)(2,1)}, bf16[1024,256]{1,0:T(8,128)(2,1)}, u32[]{:S(2)}, u32[]{:S(2)}) collective-permute-start(bf16[1024,256]{1,0:T(8,128)(2,1)} %bitcast.10.rest_0_), channel_id=1, source_target_pairs={{0,4},{2,6},{4,0},{6,2},{1,5},{3,7},{5,1},{7,3},{8,12},{10,14},{12... | collective-permute-start | bytes 1572872 | tf_op jit(solution)/shard_map/ppermute | solution.py:29
  11.8 8.4 %fusion.2 = (f32[256]{0:T(256)S(1)}, f32[256,2048]{1,0:T(8,128)S(1)}) fusion(bf16[256,4096]{1,0:T(8,128)(2,1)S(1)} %copy-done, bf16[4096,2048]{1,0:T(8,128)(2,1)} %unembed.1), kind=kOutput, calls=%fused_computation.4 | convolution fusion | flops 4295491584 | bytes 20972544 | tf_op jit(solution)/shard_map/dot_general | solution.py:600
  22.0 8.0 %collective-permute-done.1.refs_1_ = bf16[1024,256]{1,0:T(8,128)(2,1)} collective-permute-done((bf16[1024,256]{1,0:T(8,128)(2,1)}, bf16[1024,256]{1,0:T(8,128)(2,1)}, u32[]{:S(2)}, u32[]{:S(2)}) %collective-permute-start.1) | collective-permute-done | bytes 524320 | tf_op jit(solution)/shard_map/ppermute | solution.py:29
  35.8 4.1 %tile_products.2 = (bf16[1024,256]{1,0:T(8,128)(2,1)S(1)}, bf16[1024,256]{1,0:T(8,128)(2,1)S(1)}, bf16[1024,256]{1,0:T(8,128)(2,1)S(1)}, bf16[528,256]{1,0:T(8,1...) custom-call(s32[6]{0:T(128)S(1)} %stack.44.place, ...), custom_call_target="tpu_custom_call" | custom-call | flops 1073741824 | bytes 8388608 | tf_op jit(solution)/shard_map/tile_products/pallas_call | solution.py:182
  42.6 4.4 %collective-permute-done.7.right.refs_0_.rest_1_ = bf16[1024,256]{1,0:T(8,128)(2,1)} collective-permute-done((bf16[1024,256]{1,0:T(8,128)(2,1)S(1)}, bf16[1024,256]{1,0:T(8,128)(2,1)}, u32[]{:S(2)}, u32[]{:S(2)}) %collective-permute-start.7) | collective-permute-done | bytes 524320 | tf_op jit(solution)/shard_map/ppermute | solution.py:29
  53.2 2.3 %collective-permute-start.10 = (bf16[512,256]{1,0:T(8,128)(2,1)S(1)}, bf16[512,256]{1,0:T(8,128)(2,1)S(1)}, u32[]{:S(2)}, u32[]{:S(2)}) collective-permute-start(bf16[512,256]{1,0:T(8,128)(2,1)S(1)} %get-tuple-element.61), channel_id=1, source_target_pairs={{0,6},{2,0},{4,2},{6,4},{1,7},{3,1},{5,3},{7,5},{8,14},{10,8},{12,... | collective-permute-start | bytes 786440 | tf_op jit(solution)/shard_map/ppermute | solution.py:29
  55.5 2.6 %collective-permute-start.15 = (bf16[1024,256]{1,0:T(8,128)(2,1)S(1)}, bf16[1024,256]{1,0:T(8,128)(2,1)S(1)}, u32[]{:S(2)}, u32[]{:S(2)}) collective-permute-start(bf16[1024,256]{1,0:T(8,128)(2,1)S(1)} %slice_weights.1.rest_8_.rest_0_), channel_id=1, source_target_pairs={{0,1},{1,0},{2,3},{3,2},{4,5},{5,4},{6,7},{7,6},{8,9},{9,8},{10,11... | collective-permute-start | bytes 1572872 | tf_op jit(solution)/shard_map/ppermute | solution.py:33
  59.8 3.0 %collective-permute-start.16 = (bf16[1024,256]{1,0:T(8,128)(2,1)}, bf16[1024,256]{1,0:T(8,128)(2,1)S(1)}, u32[]{:S(2)}, u32[]{:S(2)}) collective-permute-start(bf16[1024,256]{1,0:T(8,128)(2,1)} %collective-permute-done.7.right.refs_0_.rest_1_), channel_id=1, source_target_pairs={{0,1},{1,0},{2,3},{3,2},{4,5},{5,4},{6,7},{7,6},{8,9},{9,8},{10,11... | collective-permute-start | bytes 1572872 | tf_op jit(solution)/shard_map/ppermute | solution.py:33
  66.6 3.2 %tile_products.3 = (bf16[1024,256]{1,0:T(8,128)(2,1)S(1)}, bf16[1024,256]{1,0:T(8,128)(2,1)S(1)}, bf16[1024,256]{1,0:T(8,128)(2,1)S(1)}, bf16[528,256]{1,0:T(8,128)(2,1)S(1)}, bf16[528,256]{1,0:T(8,128)(2,1)S(1)}) custom-call(s32[6]{0:T(128)S(1)} %stack.44.place, s32[16,2]{1,0:T(8,128)S(1)} %copy.14.pairs, s32[1]{0:T(128)S(6)} %copy.20.count, ...), custom_call_target="tpu_custom_call" | custom-call | flops 1073741824 | bytes 8388608 | tf_op jit(solution)/shard_map/tile_products/pallas_call | solution.py:182
  72.8 4.1 %stage_unembed.1.refs_1_.stage = bf16[2048,2048]{1,0:T(8,128)(2,1)S(1)} custom-call(s32[6]{0:T(128)S(1)} %stack.44.place, bf16[4096,2048]{1,0:T(8,128)(2,1)} %unembed.1, bf16[1024,256]{1,0:T(8,128)(2,1)S(1)} %get-tuple-element.70.refs_0_.refs_3_), custom_call_target="tpu_custom_call" | custom-call | bytes 8388608 | tf_op jit(solution)/shard_map/stage_unembed/pallas_call | solution.py:394
  83.3 2.3 %collective-permute-start.20 = (bf16[272,256]{1,0:T(8,128)(2,1)S(1)}, bf16[272,256]{1,0:T(8,128)(2,1)S(1)}, u32[]{:S(2)}, u32[]{:S(2)}) collective-permute-start(bf16[272,256]{1,0:T(8,128)(2,1)S(1)} %get-tuple-element.73), channel_id=1, source_target_pairs={{0,8},{8,16},{16,24},{24,0},{1,9},{9,17},{17,25},{25,1},{2,10},{10... | collective-permute-start | bytes 417800 | tf_op jit(solution)/shard_map/ppermute | solution.py:29
  85.6 4.0 %collective-permute-start.21 = (bf16[272,256]{1,0:T(8,128)(2,1)S(1)}, bf16[272,256]{1,0:T(8,128)(2,1)S(1)}, u32[]{:S(2)}, u32[]{:S(2)}) collective-permute-start(bf16[272,256]{1,0:T(8,128)(2,1)S(1)} %get-tuple-element.74), channel_id=1, source_target_pairs={{0,16},{8,24},{16,0},{24,8},{1,17},{9,25},{17,1},{25,9},{2,18},{10... | collective-permute-start | bytes 417800 | tf_op jit(solution)/shard_map/ppermute | solution.py:29
  89.6 2.5 %collective-permute-done.26.refs_2_ = bf16[1024,256]{1,0:T(8,128)(2,1)S(1)} collective-permute-done((bf16[1024,256]{1,0:T(8,128)(2,1)S(1)}, bf16[1024,256]{1,0:T(8,128)(2,1)S(1)}, u32[]{:S(2)}, u32[]{:S(2)}) %collective-permute-start.26) | collective-permute-done | bytes 524320 | tf_op jit(solution)/shard_map/ppermute | solution.py:29
  96.4 4.4 %collective-permute-start.28 = (bf16[272,256]{1,0:T(8,128)(2,1)S(1)}, bf16[272,256]{1,0:T(8,128)(2,1)S(1)}, u32[]{:S(2)}, u32[]{:S(2)}) collective-permute-start(bf16[272,256]{1,0:T(8,128)(2,1)S(1)} %get-tuple-element.88), channel_id=1, source_target_pairs={{0,16},{8,24},{16,0},{24,8},{1,17},{9,25},{17,1},{25,9},{2,18},{10... | collective-permute-start | bytes 417800 | tf_op jit(solution)/shard_map/ppermute | solution.py:29
  102.0 3.3 %collective-permute-done.28.refs_6_ = bf16[272,256]{1,0:T(8,128)(2,1)S(1)} collective-permute-done((bf16[272,256]{1,0:T(8,128)(2,1)S(1)}, bf16[272,256]{1,0:T(8,128)(2,1)S(1)}, u32[]{:S(2)}, u32[]{:S(2)}) %collective-permute-start.28) | collective-permute-done | bytes 139296 | tf_op jit(solution)/shard_map/ppermute | solution.py:29
  105.9 2.3 %logit_grad.1.mine = bf16[2064,256]{1,0:T(8,128)(2,1)S(1)} custom-call(s32[6]{0:T(128)S(1)} %stack.44.place, f32[256,2048]{1,0:T(8,128)S(1)} %copy-done.3, bf16[272,256]{1,0:T(8,128)(2,1)S(1)} %get-tuple-element.72.refs_0_, bf16[272,256]{1,0:T(8,128)(2,1)S(1)} %collective-permute-done.20.refs_1_, bf16[272,256]{1,0:T(8,128)(2,1)S(1)} %collective-permute-done.21.refs_2_, ...), custom_call_target="tpu_custom_call" | custom-call | flops 31457280 | bytes 4194304 | tf_op jit(solution)/shard_map/logit_grad/pallas_call | solution.py:359
  108.2 2.6 %collective-permute-start.30 = (bf16[2064,256]{1,0:T(8,128)(2,1)S(1)}, bf16[2064,256]{1,0:T(8,128)(2,1)S(1)}, u32[]{:S(2)}, u32[]{:S(2)}) collective-permute-start(bf16[2064,256]{1,0:T(8,128)(2,1)S(1)} %logit_grad.1.mine), channel_id=1, source_target_pairs={{0,1},{1,0},{2,3},{3,2},{4,5},{5,4},{6,7},{7,6},{8,9},{9,8},{10,11... | collective-permute-start | bytes 3170312 | tf_op jit(solution)/shard_map/ppermute | solution.py:33
  110.7 2.3 %own_hidden.1.own = bf16[2048,256]{1,0:T(8,128)(2,1)S(1)} custom-call(bf16[2048,2048]{1,0:T(8,128)(2,1)S(1)} %stage_unembed.1.refs_1_.stage, bf16[2064,256]{1,0:T(8,128)(2,1)S(1)} %logit_grad.1.mine), custom_call_target="tpu_custom_call" | custom-call | flops 2147483648 | bytes 8388608 | tf_op jit(solution)/shard_map/own_hidden/pallas_call | solution.py:416
  114.4 2.7 %collective-permute-start.32 = (bf16[272,512]{1,0:T(8,128)(2,1)S(1)}, bf16[272,512]{1,0:T(8,128)(2,1)S(1)}, u32[]{:S(2)}, u32[]{:S(2)}) collective-permute-start(bf16[272,512]{1,0:T(8,128)(2,1)S(1)} %get-tuple-element.94), channel_id=1, source_target_pairs={{0,96},{1,25},{8,104},{9,1},{16,112},{17,9},{24,120},{25,17},{32,0... | collective-permute-start | bytes 835592 | tf_op jit(solution)/shard_map/ppermute | solution.py:586
  117.1 2.4 %other_hidden.3 = (bf16[512,512]{1,0:T(8,128)(2,1)S(1)}, bf16[512,512]{1,0:T(8,128)(2,1)S(1)}, bf16[512,512]{1,0:T(8,128)(2,1)S(1)}) custom-call(s32[6]{0:T(128)S(1)} %stack.44.place, bf16[2048,2048]{1,0:T(8,128)(2,1)S(1)} %stage_unembed.1.refs_1_.stage, bf16[2064,256]{1,0:T(8,128)(2,1)S(1)} %logit_grad.1.mine, ...), custom_call_target="tpu_custom_call" | custom-call | flops 1610612736 | bytes 8388608 | tf_op jit(solution)/shard_map/other_hidden/pallas_call | solution.py:451
  125.7 5.5 %collective-permute-done.34.left_high = bf16[256,512]{1,0:T(8,128)(2,1)S(1)} collective-permute-done((bf16[256,512]{1,0:T(8,128)(2,1)S(1)}, bf16[256,512]{1,0:T(8,128)(2,1)S(1)}, u32[]{:S(2)}, u32[]{:S(2)}) %collective-permute-start.34) | collective-permute-done | bytes 262176 | tf_op jit(solution)/shard_map/ppermute | solution.py:586
  133.0 3.5 %collective-permute-start.38 = (bf16[144,512]{1,0:T(8,128)(2,1)S(1)}, bf16[144,512]{1,0:T(8,128)(2,1)S(1)}, u32[]{:S(2)}, u32[]{:S(2)}) collective-permute-start(bf16[144,512]{1,0:T(8,128)(2,1)S(1)} %get-tuple-element.101), channel_id=1, source_target_pairs={{0,16},{1,65},{8,24},{9,73},{16,0},{17,81},{24,8},{25,89},{32,48},... | collective-permute-start | bytes 442376 | tf_op jit(solution)/shard_map/ppermute | solution.py:586
  138.1 2.4 %collective-permute-done.38.refs_2_ = bf16[144,512]{1,0:T(8,128)(2,1)S(1)} collective-permute-done((bf16[144,512]{1,0:T(8,128)(2,1)S(1)}, bf16[144,512]{1,0:T(8,128)(2,1)S(1)}, u32[]{:S(2)}, u32[]{:S(2)}) %collective-permute-start.38) | collective-permute-done | bytes 147488 | tf_op jit(solution)/shard_map/ppermute | solution.py:586
  141.4 3.9 %collective-permute-start.40 = (bf16[128,256]{1,0:T(8,128)(2,1)S(1)}, bf16[128,256]{1,0:T(8,128)(2,1)S(1)}, u32[]{:S(2)}, u32[]{:S(2)}) collective-permute-start(bf16[128,256]{1,0:T(8,128)(2,1)S(1)} %get-tuple-element.104), channel_id=1, source_target_pairs={{0,1},{1,0},{2,3},{3,2},{4,5},{5,4},{6,7},{7,6},{8,9},{9,8},{10,11... | collective-permute-start | bytes 196616 | tf_op jit(solution)/shard_map/ppermute | solution.py:33
  (102 shorter events, 59.3 us)
Async XLA Ops:
  2.7 19.3 %collective-permute-start = (bf16[1024,256]{1,0:T(8,128)(2,1)}, bf16[1024,256]{1,0:T(8,128)(2,1)S(1)}, u32[]{:S(2)}, u32[]{:S(2)}) collective-permute-start(bf16[1024,256]{1,0:T(8,128)(2,1)} %bitcast.10.rest_0_), channel_id=1, source_target_pairs={{0,2},{2,4},{4,6},{6,0},{1,3},{3,5},{5,7},{7,1},{8,10},{10,12},{12... | collective-permute-start | bytes 1572872 | tf_op jit(solution)/shard_map/ppermute | solution.py:29
  4.7 25.3 %collective-permute-start.1 = (bf16[1024,256]{1,0:T(8,128)(2,1)}, bf16[1024,256]{1,0:T(8,128)(2,1)}, u32[]{:S(2)}, u32[]{:S(2)}) collective-permute-start(bf16[1024,256]{1,0:T(8,128)(2,1)} %bitcast.10.rest_0_), channel_id=1, source_target_pairs={{0,4},{2,6},{4,0},{6,2},{1,5},{3,7},{5,1},{7,3},{8,12},{10,14},{12... | collective-permute-start | bytes 1572872 | tf_op jit(solution)/shard_map/ppermute | solution.py:29
  7.2 22.9 %collective-permute-start.2 = (bf16[1024,256]{1,0:T(8,128)(2,1)}, bf16[1024,256]{1,0:T(8,128)(2,1)}, u32[]{:S(2)}, u32[]{:S(2)}) collective-permute-start(bf16[1024,256]{1,0:T(8,128)(2,1)} %bitcast.10.rest_0_), channel_id=1, source_target_pairs={{0,6},{2,0},{4,2},{6,4},{1,7},{3,1},{5,3},{7,5},{8,14},{10,8},{12,... | collective-permute-start | bytes 1572872 | tf_op jit(solution)/shard_map/ppermute | solution.py:29
  8.3 24.8 %collective-permute-start.3 = (bf16[1024,256]{1,0:T(8,128)(2,1)}, bf16[1024,256]{1,0:T(8,128)(2,1)}, u32[]{:S(2)}, u32[]{:S(2)}) collective-permute-start(bf16[1024,256]{1,0:T(8,128)(2,1)} %bitcast.10.rest_0_), channel_id=1, source_target_pairs={{0,1},{1,0},{2,3},{3,2},{4,5},{5,4},{6,7},{7,6},{8,9},{9,8},{10,11... | collective-permute-start | bytes 1572872 | tf_op jit(solution)/shard_map/ppermute | solution.py:33
  32.2 14.9 %collective-permute-start.7 = (bf16[1024,256]{1,0:T(8,128)(2,1)S(1)}, bf16[1024,256]{1,0:T(8,128)(2,1)}, u32[]{:S(2)}, u32[]{:S(2)}) collective-permute-start(bf16[1024,256]{1,0:T(8,128)(2,1)S(1)} %slice_weights.1.rest_8_.rest_0_), channel_id=1, source_target_pairs={{0,2},{2,4},{4,6},{6,0},{1,3},{3,5},{5,7},{7,1},{8,10},{10,12},{12... | collective-permute-start | bytes 1572872 | tf_op jit(solution)/shard_map/ppermute | solution.py:29
  33.1 13.9 %collective-permute-start.8 = (bf16[1024,256]{1,0:T(8,128)(2,1)S(1)}, bf16[1024,256]{1,0:T(8,128)(2,1)}, u32[]{:S(2)}, u32[]{:S(2)}) collective-permute-start(bf16[1024,256]{1,0:T(8,128)(2,1)S(1)} %slice_weights.1.rest_8_.rest_0_), channel_id=1, source_target_pairs={{0,6},{2,0},{4,2},{6,4},{1,7},{3,1},{5,3},{7,5},{8,14},{10,8},{12,... | collective-permute-start | bytes 1572872 | tf_op jit(solution)/shard_map/ppermute | solution.py:29
  39.9 8.7 %collective-permute-start.11 = (bf16[528,256]{1,0:T(8,128)(2,1)S(1)}, bf16[528,256]{1,0:T(8,128)(2,1)S(1)}, u32[]{:S(2)}, u32[]{:S(2)}) collective-permute-start(bf16[528,256]{1,0:T(8,128)(2,1)S(1)} %get-tuple-element.64.mine), channel_id=1, source_target_pairs={{0,32},{32,64},{64,96},{96,0},{1,33},{33,65},{65,97},{97,1},{2,34}... | collective-permute-start | bytes 811016 | tf_op jit(solution)/shard_map/ppermute | solution.py:29
  40.7 7.8 %collective-permute-start.12 = (bf16[528,256]{1,0:T(8,128)(2,1)S(1)}, bf16[528,256]{1,0:T(8,128)(2,1)S(1)}, u32[]{:S(2)}, u32[]{:S(2)}) collective-permute-start(bf16[528,256]{1,0:T(8,128)(2,1)S(1)} %get-tuple-element.65), channel_id=1, source_target_pairs={{0,96},{32,0},{64,32},{96,64},{1,97},{33,1},{65,33},{97,65},{2,98}... | collective-permute-start | bytes 811016 | tf_op jit(solution)/shard_map/ppermute | solution.py:29
  49.0 13.8 %collective-permute-start.13 = (bf16[1040,256]{1,0:T(8,128)(2,1)S(1)}, bf16[1040,256]{1,0:T(8,128)(2,1)S(1)}, u32[]{:S(2)}, u32[]{:S(2)}) collective-permute-start(bf16[1040,256]{1,0:T(8,128)(2,1)S(1)} %get-tuple-element.66), channel_id=1, source_target_pairs={{0,32},{32,64},{64,96},{96,0},{1,33},{33,65},{65,97},{97,1},{2,34}... | collective-permute-start | bytes 1597448 | tf_op jit(solution)/shard_map/ppermute | solution.py:29
  50.7 12.1 %collective-permute-start.14 = (bf16[1024,256]{1,0:T(8,128)(2,1)S(1)}, bf16[1024,256]{1,0:T(8,128)(2,1)S(1)}, u32[]{:S(2)}, u32[]{:S(2)}) collective-permute-start(bf16[1024,256]{1,0:T(8,128)(2,1)S(1)} %get-tuple-element.67), channel_id=1, source_target_pairs={{0,96},{32,0},{64,32},{96,64},{1,97},{33,1},{65,33},{97,65},{2,98}... | collective-permute-start | bytes 1572872 | tf_op jit(solution)/shard_map/ppermute | solution.py:29
  53.2 9.6 %collective-permute-start.10 = (bf16[512,256]{1,0:T(8,128)(2,1)S(1)}, bf16[512,256]{1,0:T(8,128)(2,1)S(1)}, u32[]{:S(2)}, u32[]{:S(2)}) collective-permute-start(bf16[512,256]{1,0:T(8,128)(2,1)S(1)} %get-tuple-element.61), channel_id=1, source_target_pairs={{0,6},{2,0},{4,2},{6,4},{1,7},{3,1},{5,3},{7,5},{8,14},{10,8},{12,... | collective-permute-start | bytes 786440 | tf_op jit(solution)/shard_map/ppermute | solution.py:29
  55.5 9.6 %collective-permute-start.15 = (bf16[1024,256]{1,0:T(8,128)(2,1)S(1)}, bf16[1024,256]{1,0:T(8,128)(2,1)S(1)}, u32[]{:S(2)}, u32[]{:S(2)}) collective-permute-start(bf16[1024,256]{1,0:T(8,128)(2,1)S(1)} %slice_weights.1.rest_8_.rest_0_), channel_id=1, source_target_pairs={{0,1},{1,0},{2,3},{3,2},{4,5},{5,4},{6,7},{7,6},{8,9},{9,8},{10,11... | collective-permute-start | bytes 1572872 | tf_op jit(solution)/shard_map/ppermute | solution.py:33
  69.8 9.3 %collective-permute-start.23 = (bf16[528,256]{1,0:T(8,128)(2,1)S(1)}, bf16[528,256]{1,0:T(8,128)(2,1)S(1)}, u32[]{:S(2)}, u32[]{:S(2)}) collective-permute-start(bf16[528,256]{1,0:T(8,128)(2,1)S(1)} %get-tuple-element.78.mine), channel_id=1, source_target_pairs={{0,32},{32,64},{64,96},{96,0},{1,33},{33,65},{65,97},{97,1},{2,34}... | collective-permute-start | bytes 811016 | tf_op jit(solution)/shard_map/ppermute | solution.py:29
  70.6 8.6 %collective-permute-start.24 = (bf16[528,256]{1,0:T(8,128)(2,1)S(1)}, bf16[528,256]{1,0:T(8,128)(2,1)S(1)}, u32[]{:S(2)}, u32[]{:S(2)}) collective-permute-start(bf16[528,256]{1,0:T(8,128)(2,1)S(1)} %get-tuple-element.79), channel_id=1, source_target_pairs={{0,96},{32,0},{64,32},{96,64},{1,97},{33,1},{65,33},{97,65},{2,98}... | collective-permute-start | bytes 811016 | tf_op jit(solution)/shard_map/ppermute | solution.py:29
  79.5 13.9 %collective-permute-start.25 = (bf16[1040,256]{1,0:T(8,128)(2,1)S(1)}, bf16[1040,256]{1,0:T(8,128)(2,1)S(1)}, u32[]{:S(2)}, u32[]{:S(2)}) collective-permute-start(bf16[1040,256]{1,0:T(8,128)(2,1)S(1)} %get-tuple-element.82), channel_id=1, source_target_pairs={{0,32},{32,64},{64,96},{96,0},{1,33},{33,65},{65,97},{97,1},{2,34}... | collective-permute-start | bytes 1597448 | tf_op jit(solution)/shard_map/ppermute | solution.py:29
  79.9 12.2 %collective-permute-start.26 = (bf16[1024,256]{1,0:T(8,128)(2,1)S(1)}, bf16[1024,256]{1,0:T(8,128)(2,1)S(1)}, u32[]{:S(2)}, u32[]{:S(2)}) collective-permute-start(bf16[1024,256]{1,0:T(8,128)(2,1)S(1)} %get-tuple-element.83), channel_id=1, source_target_pairs={{0,96},{32,0},{64,32},{96,64},{1,97},{33,1},{65,33},{97,65},{2,98}... | collective-permute-start | bytes 1572872 | tf_op jit(solution)/shard_map/ppermute | solution.py:29
  83.3 17.5 %collective-permute-start.20 = (bf16[272,256]{1,0:T(8,128)(2,1)S(1)}, bf16[272,256]{1,0:T(8,128)(2,1)S(1)}, u32[]{:S(2)}, u32[]{:S(2)}) collective-permute-start(bf16[272,256]{1,0:T(8,128)(2,1)S(1)} %get-tuple-element.73), channel_id=1, source_target_pairs={{0,8},{8,16},{16,24},{24,0},{1,9},{9,17},{17,25},{25,1},{2,10},{10... | collective-permute-start | bytes 417800 | tf_op jit(solution)/shard_map/ppermute | solution.py:29
  85.6 15.1 %collective-permute-start.21 = (bf16[272,256]{1,0:T(8,128)(2,1)S(1)}, bf16[272,256]{1,0:T(8,128)(2,1)S(1)}, u32[]{:S(2)}, u32[]{:S(2)}) collective-permute-start(bf16[272,256]{1,0:T(8,128)(2,1)S(1)} %get-tuple-element.74), channel_id=1, source_target_pairs={{0,16},{8,24},{16,0},{24,8},{1,17},{9,25},{17,1},{25,9},{2,18},{10... | collective-permute-start | bytes 417800 | tf_op jit(solution)/shard_map/ppermute | solution.py:29
  89.6 11.2 %collective-permute-start.22 = (bf16[272,256]{1,0:T(8,128)(2,1)S(1)}, bf16[272,256]{1,0:T(8,128)(2,1)S(1)}, u32[]{:S(2)}, u32[]{:S(2)}) collective-permute-start(bf16[272,256]{1,0:T(8,128)(2,1)S(1)} %get-tuple-element.75), channel_id=1, source_target_pairs={{0,24},{8,0},{16,8},{24,16},{1,25},{9,1},{17,9},{25,17},{2,26},{10... | collective-permute-start | bytes 417800 | tf_op jit(solution)/shard_map/ppermute | solution.py:29
  94.3 7.7 %collective-permute-start.27 = (bf16[272,256]{1,0:T(8,128)(2,1)S(1)}, bf16[272,256]{1,0:T(8,128)(2,1)S(1)}, u32[]{:S(2)}, u32[]{:S(2)}) collective-permute-start(bf16[272,256]{1,0:T(8,128)(2,1)S(1)} %get-tuple-element.87), channel_id=1, source_target_pairs={{0,8},{8,16},{16,24},{24,0},{1,9},{9,17},{17,25},{25,1},{2,10},{10... | collective-permute-start | bytes 417800 | tf_op jit(solution)/shard_map/ppermute | solution.py:29
  96.4 9.0 %collective-permute-start.28 = (bf16[272,256]{1,0:T(8,128)(2,1)S(1)}, bf16[272,256]{1,0:T(8,128)(2,1)S(1)}, u32[]{:S(2)}, u32[]{:S(2)}) collective-permute-start(bf16[272,256]{1,0:T(8,128)(2,1)S(1)} %get-tuple-element.88), channel_id=1, source_target_pairs={{0,16},{8,24},{16,0},{24,8},{1,17},{9,25},{17,1},{25,9},{2,18},{10... | collective-permute-start | bytes 417800 | tf_op jit(solution)/shard_map/ppermute | solution.py:29
  121.5 10.5 %collective-permute-start.33 = (bf16[272,512]{1,0:T(8,128)(2,1)S(1)}, bf16[272,512]{1,0:T(8,128)(2,1)S(1)}, u32[]{:S(2)}, u32[]{:S(2)}) collective-permute-start(bf16[272,512]{1,0:T(8,128)(2,1)S(1)} %get-tuple-element.95), channel_id=1, source_target_pairs={{0,32},{1,9},{8,40},{9,17},{16,48},{17,25},{24,56},{25,1},{32,64},... | collective-permute-start | bytes 835592 | tf_op jit(solution)/shard_map/ppermute | solution.py:586
  121.6 9.7 %collective-permute-start.34 = (bf16[256,512]{1,0:T(8,128)(2,1)S(1)}, bf16[256,512]{1,0:T(8,128)(2,1)S(1)}, u32[]{:S(2)}, u32[]{:S(2)}) collective-permute-start(bf16[256,512]{1,0:T(8,128)(2,1)S(1)} %get-tuple-element.96), channel_id=1, source_target_pairs={{0,32},{1,9},{8,40},{9,17},{16,48},{17,25},{24,56},{25,1},{32,64},... | collective-permute-start | bytes 786440 | tf_op jit(solution)/shard_map/ppermute | solution.py:586
  123.0 8.2 %collective-permute-start.35 = (bf16[256,512]{1,0:T(8,128)(2,1)S(1)}, bf16[256,512]{1,0:T(8,128)(2,1)S(1)}, u32[]{:S(2)}, u32[]{:S(2)}) collective-permute-start(bf16[256,512]{1,0:T(8,128)(2,1)S(1)} %get-tuple-element.97), channel_id=1, source_target_pairs={{0,96},{1,25},{8,104},{9,1},{16,112},{17,9},{24,120},{25,17},{32,0... | collective-permute-start | bytes 786440 | tf_op jit(solution)/shard_map/ppermute | solution.py:586
  (24 other events, 175.6 us)
